TPU v7x, 32 devices: a whole 2x2x4 slice. The times are simulated.
32 devices in a mesh: az: 16 (over z, y, x), rad: 2 (over core).
Axes of the slice: x: 2, y: 2, z: 4, core: 2. Of those that a mesh axis runs over, the one named last changes fastest.
Arguments:
- density: float32 [2, 2048, 16384], P(None, 'rad', 'az'), may hold values from 0.5 to 2
- mom_r: float32 [2, 2048, 16384], P(None, 'rad', 'az'), may hold values from -1 to 1
- mom_phi: float32 [2, 2048, 16384], P(None, 'rad', 'az'), may hold values from 0.5 to 1.5
- potential_kernel: bfloat16 [64, 2048, 2048], P('az', 'rad'), may hold values from -2 to 2
- force_kernel: bfloat16 [64, 2048, 2048], P('az', 'rad'), may hold values from -2 to 2
Outputs:
- new_density: float32 [2, 2048, 16384], P(None, 'rad', 'az')
- new_mom_r: float32 [2, 2048, 16384], P(None, 'rad', 'az')
- new_mom_phi: float32 [2, 2048, 16384], P(None, 'rad', 'az')
- potential: float32 [2048, 16384], P('rad', 'az')
All inputs are finite; a program needn't handle non-finite values.
Results may differ from a plain program's by a relative error of at most 0.0015.
The roundings to bfloat16 on the way count: a program that leaves them out, or rounds other values in their place, can miss the bound.
Values may be sent and summed in bfloat16 or wider, within the bound.
No kernel may reach another device: no remote copies, remote signals or barrier semaphores. Data moves between devices by JAX's collectives and lax.ppermute only.
A program may use at most 384 MiB of HBM per device.

v0:
```python
import math

import jax
import jax.numpy as jnp
from jax import lax
from jax.sharding import PartitionSpec as P

NAZ = 16384
MODES = 64


aspect_sq = 0.0025


def extended(block, sides, width, periodic):
    for axis, dim in sides:
        count = lax.axis_size(axis)
        forward = [(i, i + 1) for i in range(count - 1)]
        if periodic:
            forward.append((count - 1, 0))
        backward = [(target, source) for source, target in forward]
        low = lax.ppermute(
            lax.slice_in_dim(block, block.shape[dim] - width, None, axis=dim), axis, forward
        )
        high = lax.ppermute(lax.slice_in_dim(block, 0, width, axis=dim), axis, backward)
        block = jnp.concatenate([low, block, high], axis=dim)
    return block


def mode_table(azimuth):
    mode_index = jnp.arange(MODES).astype(jnp.float32)
    angles = azimuth[:, None] * mode_index[None, :]
    basis = jnp.stack([jnp.cos(angles), jnp.sin(angles)], axis=-1).reshape(
        azimuth.shape[0], 2 * MODES
    )
    slope = jnp.stack(
        [-mode_index * jnp.sin(angles), mode_index * jnp.cos(angles)], axis=-1
    ).reshape(azimuth.shape[0], 2 * MODES)
    return (basis, slope)


def radial_flux(lower_side, upper_side, sound):

    def physical(fields):
        velocity = fields[1] / fields[0]
        flux = jnp.stack(
            [fields[1], fields[1] * velocity + sound * fields[0], fields[2] * velocity]
        )
        return (flux, velocity)

    flux_lower, vel_lower = physical(lower_side)
    flux_upper, vel_upper = physical(upper_side)
    wave_speed = jnp.maximum(jnp.abs(vel_lower), jnp.abs(vel_upper)) + jnp.sqrt(sound)
    return 0.5 * (flux_lower + flux_upper) - 0.5 * wave_speed * (upper_side - lower_side)


def azimuth_flux(lower_side, upper_side, sound):

    def physical(fields):
        velocity = fields[2] / fields[0]
        flux = jnp.stack(
            [fields[2], fields[1] * velocity, fields[2] * velocity + sound * fields[0]]
        )
        return (flux, velocity)

    flux_lower, vel_lower = physical(lower_side)
    flux_upper, vel_upper = physical(upper_side)
    wave_speed = jnp.maximum(jnp.abs(vel_lower), jnp.abs(vel_upper)) + jnp.sqrt(sound)
    return 0.5 * (flux_lower + flux_upper) - 0.5 * wave_speed * (upper_side - lower_side)


def tendency(fields, radial_ext, azimuth_ext, face_radius, grav_radial, grav_azimuth, cell_step):
    inner_radius = face_radius[:-1]
    outer_radius = face_radius[1:]
    mid_radius = 0.5 * (inner_radius + outer_radius)
    cell_area = 0.5 * (outer_radius * outer_radius - inner_radius * inner_radius)
    sound_face = (aspect_sq / face_radius)[:, None]
    sound_mid = (aspect_sq / mid_radius)[:, None]
    flux_rad = radial_flux(radial_ext[:, :, :-1], radial_ext[:, :, 1:], sound_face)
    flux_azi = azimuth_flux(azimuth_ext[..., :-1], azimuth_ext[..., 1:], sound_mid)
    weighted = flux_rad * face_radius[:, None]
    divergence = (weighted[:, :, 1:] - weighted[:, :, :-1]) / cell_area[:, None]
    divergence = divergence + (flux_azi[..., 1:] - flux_azi[..., :-1]) / (
        mid_radius[:, None] * cell_step
    )
    surface_now = fields[0]
    radial_mom = fields[1]
    spin_mom = fields[2]
    centre = mid_radius[:, None]
    source_rad = (spin_mom * spin_mom / surface_now + sound_mid * surface_now) / centre
    source_rad = source_rad + surface_now * (grav_radial / cell_step - 1.0 / (centre * centre))
    source_azi = -radial_mom * spin_mom / (surface_now * centre) + surface_now * (
        grav_azimuth / cell_step
    )
    source = jnp.stack([jnp.zeros_like(surface_now), source_rad, source_azi])
    return fields + 0.1 * cell_step * (source - divergence)


def local(density, mom_r, mom_phi, potential_kernel, force_kernel):
    highest = lax.Precision.HIGHEST
    row_count = density.shape[1]
    cell_count = density.shape[2]
    mode_count = potential_kernel.shape[0]
    col_count = 2 * mode_count
    cell_step = 2.0 * math.pi / NAZ
    az_index = lax.axis_index("az")
    rad_index = lax.axis_index("rad")
    azimuth = (
        (az_index * cell_count + jnp.arange(cell_count)).astype(jnp.float32) + 0.5
    ) * cell_step
    basis, slope = mode_table(azimuth)
    surface = jnp.sum(density, axis=0)
    partial_modes = jnp.dot(surface, basis, precision=highest) / NAZ
    own_modes = lax.psum_scatter(partial_modes, "az", scatter_dimension=1, tiled=True)
    own_pairs = own_modes.astype(jnp.bfloat16)
    portion = lax.all_gather(own_pairs, "rad", axis=0, tiled=True)
    count = portion.shape[0]
    pairs = portion.reshape(count, mode_count, 2)
    pot_part = jnp.einsum(
        "krs,skc->rkc", potential_kernel, pairs, preferred_element_type=jnp.float32
    ).reshape(row_count, col_count)
    force_part = jnp.einsum(
        "krs,skc->rkc", force_kernel, pairs, preferred_element_type=jnp.float32
    ).reshape(row_count, col_count)
    basis_rows = basis.T
    slope_rows = slope.T
    every_pot, every_force = (
        lax.all_gather(pot_part, "az", axis=1, tiled=True),
        lax.all_gather(force_part, "az", axis=1, tiled=True),
    )
    potential = jnp.dot(every_pot, basis_rows, precision=highest)
    grav_radial = jnp.dot(every_force, basis_rows, precision=highest)
    slope_sum = jnp.dot(every_pot, slope_rows, precision=highest)
    face_radius = jnp.exp(
        (rad_index * row_count + jnp.arange(row_count + 1)).astype(jnp.float32) * cell_step
    )
    mid_radius = 0.5 * (face_radius[:-1] + face_radius[1:])
    grav_azimuth = -slope_sum / mid_radius[:, None]
    fields = jnp.stack([density, mom_r, mom_phi])
    azimuth_ext = extended(fields.astype(jnp.bfloat16), (("az", 3),), 1, True).astype(fields.dtype)
    radial_halo = extended(fields.astype(jnp.bfloat16), (("rad", 2),), 1, False).astype(
        fields.dtype
    )
    inner_rim = jnp.where(rad_index == 0, fields[:, :, :1], radial_halo[:, :, :1])
    outer_rim = jnp.where(
        rad_index == lax.axis_size("rad") - 1, fields[:, :, -1:], radial_halo[:, :, -1:]
    )
    radial_ext = jnp.concatenate([inner_rim, fields, outer_rim], axis=2)
    result = tendency(
        fields, radial_ext, azimuth_ext, face_radius, grav_radial, grav_azimuth, cell_step
    )
    return (result[0], result[1], result[2], potential)


def solution(mesh):
    placed = (
        P(None, "rad", "az"),
        P(None, "rad", "az"),
        P(None, "rad", "az"),
        P("az", "rad", None),
        P("az", "rad", None),
    )
    return jax.shard_map(
        local,
        mesh=mesh,
        in_specs=placed,
        out_specs=(
            P(None, "rad", "az"),
            P(None, "rad", "az"),
            P(None, "rad", "az"),
            P("rad", "az"),
        ),
        check_vma=False,
    )
```

profile of v0, /device:TPU:0, one launch (start us, length us, event | category | flops | bytes accessed | tf_op | source)
XLA Modules:
  0.0 615.6 jit_solution(6261045993166330904)
XLA Ops:
  7.2 9.6 %fusion.15 = bf16[3,2,1024,1024]{3,2,1,0:T(8,128)(2,1)S(1)} fusion(f32[1,2,1024,1024]{3,2,1,0:T(8,128)} %bitcast.51, f32[1,2,1024,1024]{3,2,1,0:T(8,128)} %bitcast.58, f32[1,2,1024,1024]{3,2,1,0:T(8,128)} %bitcast.44), kind=kLoop, calls=%fused_computation.65 | loop fusion | flops 12582912 | bytes 37748736 | tf_op jit(solution)/shard_map/convert_element_type | solution.py:141
  16.8 4.6 copy-done
  23.0 3.0 collective-permute-start.2
  26.7 4.1 collective-permute-start.3
  31.8 1.5 collective-permute-start
  33.3 1.3 collective-permute-start.1
  34.6 6.7 %reduce_sum.9 = f32[1024,1024]{1,0:T(8,128)} reduce(f32[2,1024,1024]{2,1,0:T(8,128)} %param.5, f32[]{:T(128)} %constant.14.clone.1), dimensions={0}, to_apply=%region_0.0 | reduce | flops 1048576 | bytes 12582916 | tf_op jit(solution)/shard_map/reduce_sum | solution.py:112
  43.2 7.6 %convolution_multiply_fusion = f32[1024,128]{0,1:T(8,128)} fusion(f32[1024,1024]{1,0:T(8,128)} %reduce_sum.9, f32[1024,128]{0,1:T(8,128)S(1)} %reshape.285), kind=kOutput, calls=%fused_computation.41 | convolution fusion | flops 1610743808 | bytes 5242880 | tf_op jit(solution)/shard_map/dot_general | solution.py:113
  50.8 18.1 %pad_maximum_fusion.1 = f32[3,2,1024,1024]{3,2,1,0:T(8,128)} fusion(f32[1,2,1024,1024]{3,2,1,0:T(8,128)} %bitcast.52, f32[1,2,1024,1024]{3,2,1,0:T(8,128)} %bitcast.59, f32[1,2,1024,1024]{3,2,1,0:T(8,128)} %bitcast.45), kind=kLoop, calls=%fused_computation.19 | loop fusion | flops 12582912 | bytes 50331648 | tf_op jit(solution)/shard_map/stack | solution.py:139
  70.0 1.2 reshape.289
  73.8 25.5 %concatenate.16 = bf16[3,2,1024,1026]{3,2,1,0:T(8,128)(2,1)} concatenate(bf16[3,2,1024,1]{3,2,1,0:T(8,128)(2,1)S(1)} %copy.53, bf16[3,2,1024,1024]{3,2,1,0:T(8,128)(2,1)} %copy-done, bf16[3,2,1024,1]{3,2,1,0:T(8,128)(2,1)S(1)} %copy.54), dimensions={3} | concatenate | bytes 25214976 | tf_op jit(solution)/shard_map/concatenate | solution.py:26
  99.3 12.5 %fusion.16 = (f32[1,2,1024,1025]{3,2,1,0:T(8,128)}, f32[1,2,1024,1025]{3,2,1,0:T(8,128)}) fusion(bf16[3,2,1024,1026]{3,2,1,0:T(8,128)(2,1)} %concatenate.16), kind=kLoop, calls=%fused_computation.66 | loop fusion | bytes 33587200 | tf_op jit(solution)/shard_map/slice | solution.py:62
  111.7 15.2 %convert_element_type.55 = f32[3,2,1024,1026]{3,2,1,0:T(8,128)} convert(bf16[3,2,1024,1026]{3,2,1,0:T(8,128)(2,1)} %concatenate.16) | non-fusion elementwise | flops 6303744 | bytes 37822464 | tf_op jit(solution)/shard_map/convert_element_type | solution.py:140
  127.0 63.0 %concatenate.13 = bf16[3,2,1026,1024]{3,2,1,0:T(8,128)(2,1)} concatenate(bf16[3,2,1,1024]{3,2,1,0:T(2,128)(2,1)S(1)} %copy.49, bf16[3,2,1024,1024]{3,2,1,0:T(8,128)(2,1)} %copy-done, bf16[3,2,1,1024]{3,2,1,0:T(2,128)(2,1)S(1)} %copy.50), dimensions={2} | concatenate | bytes 25214976 | tf_op jit(solution)/shard_map/concatenate | solution.py:26
  190.0 7.1 %convert_element_type.54 = f32[3,2,1026,1024]{3,2,1,0:T(8,128)S(1)} convert(bf16[3,2,1026,1024]{3,2,1,0:T(8,128)(2,1)} %concatenate.13) | non-fusion elementwise | flops 6303744 | bytes 37822464 | tf_op jit(solution)/shard_map/convert_element_type | solution.py:141
  197.2 1.1 broadcast_select_fusion
  198.3 37.1 %pad_maximum_fusion = (f32[3,2,1025,1024]{3,2,1,0:T(8,128)}, f32[3,2,1025,1024]{3,2,1,0:T(8,128)}) fusion(f32[3,2,1,1024]{3,2,1,0:T(1,128)S(1)} %get-tuple-element.14, f32[1,2,1024,1024]{3,2,1,0:T(8,128)} %bitcast.53, f32[1,2,1024,1024]{3,2,1,0:T(8,128)} %bitcast.60, f32[1,2,1024,1024]{3,2,1,0:T(8,128)} %bitcast.46, f32[3,2,1,1024]{3,2,1,0:T(1,128)S(1)} %get-tuple-element.15), kind=kLoop, calls=%fused_computation.10 | loop fusion | flops 37785600 | bytes 75595776 | tf_op jit(solution)/shard_map/concatenate | solution.py:148
  235.4 33.9 %multiply_bitcast_fusion = (f32[2,1024,1025]{2,1,0:T(8,128)}, f32[1,2,1024,1025]{3,2,1,0:T(8,128)}, f32[1,2,1024,1025]{3,2,1,0:T(8,128)}, f32[1,2,1024,1025]{3,2,1,0:T(8,128)}, f32[1,2,1024,1025]{3,2,1,0:T(8,128)}) fusion(f32[1024]{0:T(1024)S(1)} %get-tuple-element.51, f32[3,2,1024,1026]{3,2,1,0:T(8,128)} %convert_element_type.55, f32[1024]{0:T(1024)S(1)} %get-tuple-element.52), kind=kLoop, calls=%fused_computation.22 | loop fusion | flops 31488000 | bytes 92372992 | tf_op jit(solution)/shard_map/mul | solution.py:69
  269.3 36.2 %multiply_bitcast_fusion.1 = (f32[2,1025,1024]{2,1,0:T(8,128)}, f32[1,2,1025,1024]{3,2,1,0:T(8,128)}, f32[1,2,1025,1024]{3,2,1,0:T(8,128)}, f32[1,2,1025,1024]{3...) fusion(f32[1025]{0:T(1024)S(1)} %get-tuple-element.54, ...), kind=kLoop, calls=%fused_computation.29 | loop fusion | flops 31488000 | bytes 109166600 | tf_op jit(solution)/shard_map/mul | solution.py:54
  305.5 49.7 %fusion.5 = f32[3,2,1025,1024]{3,2,1,0:T(8,128)} fusion(f32[1,2,1025,1024]{3,2,1,0:T(8,128)} %get-tuple-element.28, f32[1,2,1025,1024]{3,2,1,0:T(8,128)} %get-tuple-element.25, f32[1,2,1025,1024]{3,2,1,0:T(8,128)} %get-tuple-element.29, f32[1,2,1025,1024]{3,2,1,0:T(8,128)} %get-tuple-element.26, f32[1,2,1025,1024]{3,2,1,0:T(8,128)} %get-tuple-element.24, ...), kind=kLoop, calls=%fused_computation.9 | loop fusion | flops 100761600 | bytes 109187072 | tf_op jit(solution)/shard_map/mul | solution.py:81
  355.2 45.3 %fusion.1 = f32[3,2,1024,1025]{3,2,1,0:T(8,128)} fusion(f32[3,2,1024,1026]{3,2,1,0:T(8,128)} %convert_element_type.55, f32[1,2,1024,1025]{3,2,1,0:T(8,128)} %get-tuple-element.21, f32[1,2,1024,1025]{3,2,1,0:T(8,128)} %get-tuple-element.20, f32[1,2,1024,1025]{3,2,1,0:T(8,128)} %get-tuple-element.38, f32[1,2,1024,1025]{3,2,1,0:T(8,128)} %get-tuple-element.22, ...), kind=kLoop, calls=%fused_computation.2 | loop fusion | flops 56678400 | bytes 134348800 | tf_op jit(solution)/shard_map/sub | solution.py:69
  401.3 2.5 all_gather.9
  403.9 10.2 %convolution_bitcast_fusion.1 = f32[1024,4,2]{0,2,1:T(2,128)S(1)} fusion(bf16[2048,4,2]{0,2,1:T(2,128)(2,1)S(1)} %reshape.286, bf16[4,1024,2048]{2,1,0:T(8,128)(2,1)} %param.9), kind=kOutput, calls=%fused_computation.43 | convolution fusion | flops 33554432 | bytes 16842752 | tf_op jit(solution)/shard_map/krs,skc->rkc/dot_general | solution.py:122
  414.1 40.6 %all_gather.10 = f32[1024,128]{0,1:T(8,128)S(1)} all-gather(f32[1024,8]{0,1:T(8,128)S(1)} %reshape.287), channel_id=1, replica_groups=mesh['az'=16,'rad'=2] {'az'}, dimensions={1}, use_global_device_ids=true | all-gather | bytes 557056 | tf_op jit(solution)/shard_map/all_gather | solution.py:129
  454.7 10.3 %convolution_bitcast_fusion = f32[1024,4,2]{0,2,1:T(2,128)S(1)} fusion(bf16[2048,4,2]{0,2,1:T(2,128)(2,1)S(1)} %reshape.286, bf16[4,1024,2048]{2,1,0:T(8,128)(2,1)} %param.8), kind=kOutput, calls=%fused_computation.42 | convolution fusion | flops 33554432 | bytes 16842752 | tf_op jit(solution)/shard_map/krs,skc->rkc/dot_general | solution.py:119
  465.0 38.7 %all_gather.11 = f32[1024,128]{0,1:T(8,128)S(1)} all-gather(f32[1024,8]{0,1:T(8,128)S(1)} %reshape.288), channel_id=1, replica_groups=mesh['az'=16,'rad'=2] {'az'}, dimensions={1}, use_global_device_ids=true | all-gather | bytes 557056 | tf_op jit(solution)/shard_map/all_gather | solution.py:128
  503.8 5.0 fusion.19
  508.8 5.3 divide_multiply_fusion
  514.1 5.1 multiply_subtract_fusion
  519.3 15.2 %add_bitcast_fusion.1 = (f32[1,2,1024,1024]{3,2,1,0:T(8,128)}, f32[1,2,1024,1024]{3,2,1,0:T(8,128)}) fusion(f32[2,1024,1024]{2,1,0:T(8,128)S(1)} %bitcast.50, f32[2,1024,1024]{2,1,0:T(8,128)S(1)} %bitcast.57, f32[1024,1024]{1,0:T(8,128)} %multiply_subtract_fusion, f32[1024]{0:T(1024)S(1)} %copy-done.6, f32[1024]{0:T(1024)S(1)} %get-tuple-element.52, ...), kind=kLoop, calls=%fused_computation.36 | loop fusion | flops 27262976 | bytes 50339840 | tf_op jit(solution)/shard_map/stack | solution.py:95
  534.5 55.7 %fusion.10 = f32[3,2,1024,1024]{3,2,1,0:T(8,128)} fusion(f32[3,2,1024,1025]{3,2,1,0:T(8,128)} %fusion.1, f32[3,2,1025,1024]{3,2,1,0:T(8,128)} %fusion.5, f32[1,2,1024,1024]{3,2,1,0:T(8,128)} %get-tuple-element.36, f32[1,2,1024,1024]{3,2,1,0:T(8,128)} %get-tuple-element.35, f32[3]{0:T(128)S(1)} %copy-done.10, f32[1024]{0:T(1024)S(1)} %copy-done.8, ...), kind=kLoop, calls=%fused_computation.16 | loop fusion | flops 75497472 | bytes 167780368 | tf_op jit(solution)/shard_map/add | solution.py:96
  590.3 18.0 %slice_bitcast_fusion = (f32[2,1024,1024]{2,1,0:T(8,128)}, f32[2,1024,1024]{2,1,0:T(8,128)}, f32[2,1024,1024]{2,1,0:T(8,128)}) fusion(f32[3,2,1024,1024]{3,2,1,0:T(8,128)} %fusion.10), kind=kLoop, calls=%fused_computation.32 | loop fusion | bytes 50331648 | tf_op jit(solution)/shard_map/squeeze | solution.py:152
  (65 shorter events, 9.9 us)
Async XLA Ops:
  7.2 393.4 %reduce-scatter.2.cloned.1.call-start = ((), (), s32[]{:S(2)}) async-start(), calls=%async_computation.1 | async-start | bytes 557056 | tf_op jit(solution)/shard_map/reduce_scatter | solution.py:114
  16.8 4.6 copy-start
  23.0 48.8 %collective-permute-start.2 = (bf16[3,2,1024,1]{2,1,3,0:T(2,128)(2,1)S(1)}, bf16[3,2,1024,1]{2,1,3,0:T(2,128)(2,1)S(1)}, u32[]{:S(2)}, u32[]{:S(2)}) collective-permute-start(bf16[3,2,1024,1]{2,1,3,0:T(2,128)(2,1)S(1)} %copy.51), channel_id=1, source_target_pairs={{0,2},{2,4},{4,6},{6,8},{8,10},{10,12},{12,14},{14,16},{16,18},{18... | collective-permute-start | bytes 36872 | tf_op jit(solution)/shard_map/ppermute | solution.py:22
  26.7 46.1 %collective-permute-start.3 = (bf16[3,2,1024,1]{2,1,3,0:T(2,128)(2,1)S(1)}, bf16[3,2,1024,1]{2,1,3,0:T(2,128)(2,1)S(1)}, u32[]{:S(2)}, u32[]{:S(2)}) collective-permute-start(bf16[3,2,1024,1]{2,1,3,0:T(2,128)(2,1)S(1)} %copy.52), channel_id=1, source_target_pairs={{2,0},{4,2},{6,4},{8,6},{10,8},{12,10},{14,12},{16,14},{18,16},{20... | collective-permute-start | bytes 36872 | tf_op jit(solution)/shard_map/ppermute | solution.py:25
  31.8 95.2 %collective-permute-start = (bf16[3,2,1,1024]{3,1,2,0:T(2,128)(2,1)S(1)}, bf16[3,2,1,1024]{3,1,2,0:T(2,128)(2,1)S(1)}, u32[]{:S(2)}, u32[]{:S(2)}) collective-permute-start(bf16[3,2,1,1024]{3,1,2,0:T(2,128)(2,1)S(1)} %copy.47), channel_id=1, source_target_pairs={{0,1},{2,3},{4,5},{6,7},{8,9},{10,11},{12,13},{14,15},{16,17},{18,... | collective-permute-start | bytes 36872 | tf_op jit(solution)/shard_map/ppermute | solution.py:22
  33.3 93.7 %collective-permute-start.1 = (bf16[3,2,1,1024]{3,1,2,0:T(2,128)(2,1)S(1)}, bf16[3,2,1,1024]{3,1,2,0:T(2,128)(2,1)S(1)}, u32[]{:S(2)}, u32[]{:S(2)}) collective-permute-start(bf16[3,2,1,1024]{3,1,2,0:T(2,128)(2,1)S(1)} %copy.48), channel_id=1, source_target_pairs={{1,0},{3,2},{5,4},{7,6},{9,8},{11,10},{13,12},{15,14},{17,16},{19,... | collective-permute-start | bytes 36872 | tf_op jit(solution)/shard_map/ppermute | solution.py:25
  43.2 25.7 %copy-start.2 = (f32[1024,128]{0,1:T(8,128)}, f32[1024,128]{0,1:T(8,128)S(1)}, u32[]{:S(2)}) copy-start(f32[1024,128]{0,1:T(8,128)S(1)} %reshape.285) | copy-start | bytes 1572868
  69.6 3.2 copy-start.5
  305.5 49.7 %copy-start.1 = (f32[2,1024,1025]{2,1,0:T(8,128)S(1)}, f32[2,1024,1025]{2,1,0:T(8,128)}, u32[]{:S(2)}) copy-start(f32[2,1024,1025]{2,1,0:T(8,128)} %get-tuple-element.18) | copy-start | bytes 25190404
  454.7 49.1 %copy-start.3 = (f32[1024,128]{0,1:T(8,128)S(1)}, f32[1024,128]{0,1:T(8,128)}, u32[]{:S(2)}) copy-start(f32[1024,128]{0,1:T(8,128)} %copy-done.2) | copy-start | bytes 1572868
  454.7 54.1 %copy-start.4 = (f32[1024,128]{0,1:T(8,128)S(1)}, f32[1024,128]{0,1:T(8,128)}, u32[]{:S(2)}) copy-start(f32[1024,128]{0,1:T(8,128)} %reshape.289) | copy-start | bytes 1572868
  454.7 54.1 %copy-start.6 = (f32[1024]{0:T(1024)S(1)}, f32[1024]{0:T(1024)}, u32[]{:S(2)}) copy-start(f32[1024]{0:T(1024)} %copy-done.5) | copy-start | bytes 12292
  503.8 10.4 %copy-start.9 = (f32[1024]{0:T(1024)S(1)}, f32[1024]{0:T(1024)}, u32[]{:S(2)}) copy-start(f32[1024]{0:T(1024)} %get-tuple-element.45) | copy-start | bytes 12292
  503.8 15.5 %slice-start = ((s8[8388608]{0:T(1024)(128)(4,1)}), s8[4194304]{0:T(1024)(128)(4,1)S(1)}, s32[]{:S(2)}) async-start(s8[8388608]{0:T(1024)(128)(4,1)} %bitcast.49), calls=%async_computation.2 | async-start | bytes 8388608
  503.8 15.5 %slice-start.2 = ((s8[8388608]{0:T(1024)(128)(4,1)}), s8[4194304]{0:T(1024)(128)(4,1)S(1)}, s32[]{:S(2)}) async-start(s8[8388608]{0:T(1024)(128)(4,1)} %bitcast.56), calls=%async_computation.4 | async-start | bytes 8388608
  508.8 10.5 %slice-start.1 = ((s8[8388608]{0:T(1024)(128)(4,1)}), s8[4194304]{0:T(1024)(128)(4,1)S(1)}, s32[]{:S(2)}) async-start(s8[8388608]{0:T(1024)(128)(4,1)} %bitcast.49), calls=%async_computation.3 | async-start | bytes 8388608
  508.8 10.5 %slice-start.3 = ((s8[8388608]{0:T(1024)(128)(4,1)}), s8[4194304]{0:T(1024)(128)(4,1)S(1)}, s32[]{:S(2)}) async-start(s8[8388608]{0:T(1024)(128)(4,1)} %bitcast.56), calls=%async_computation.5 | async-start | bytes 8388608
  519.3 15.2 %copy-start.7 = (f32[1024]{0:T(1024)S(1)}, f32[1024]{0:T(1024)}, u32[]{:S(2)}) copy-start(f32[1024]{0:T(1024)} %get-tuple-element.43) | copy-start | bytes 12292
  519.3 15.2 %copy-start.8 = (f32[1024]{0:T(1024)S(1)}, f32[1024]{0:T(1024)}, u32[]{:S(2)}) copy-start(f32[1024]{0:T(1024)} %get-tuple-element.44) | copy-start | bytes 12292
  519.3 15.2 %copy-start.10 = (f32[3]{0:T(128)S(1)}, f32[3]{0:T(128)}, u32[]{:S(2)}) copy-start(f32[3]{0:T(128)} %pad.20.clone) | copy-start | bytes 40
Sparse Core Ops, SparseCore 0:
  50.9 74.9 reduce-scatter.1
where the time goes:
time: 625 us; the launch traced here: 616 us
  other arithmetic  334 us (53%)
  local copies, waits for them, and re-layouts  132 us (21%)
  blocking collectives  81.9 us (13%)
  matrix products  43.5 us (7%)
  between operations  14.8 us (2%)
  starting transfers between devices  9.84 us (2%)
    concatenate x2, local copies, waits for them, and re-layouts, extended(): block = jnp.concatenate([low, block, high], axis=dim)  88.5 us
    add x1, other arithmetic, tendency(): return fields + 0.1 * cell_step * (source - divergence)  55.7 us
    mul x1, other arithmetic, tendency(): weighted = flux_rad * face_radius[:, None]  49.7 us
    sub x1, other arithmetic, azimuth_flux(): 0.5 * (flux_lower + flux_upper)  45.3 us
    all_gather x1, blocking collectives, local(): lax.all_gather(force_part, 'az', axis=1, tiled=True)  40.6 us
    all_gather x1, blocking collectives, local(): lax.all_gather(pot_part, 'az', axis=1, tiled=True)  38.7 us
    concatenate x1, other arithmetic, local(): radial_ext = jnp.concatenate([inner_rim, fields, outer_rim], axis=2)  37.1 us
    mul x1, other arithmetic, radial_flux(): 0.5 * wave_speed * (upper_side - lower_side)  36.2 us
  transfers between devices with their start and end apart: 5, of which 0 were waited for; matrix products, arithmetic and copies ran while one was open for 60% of the time, Pallas kernels for 0%

commit v1 on v0

v1 whole, which is shorter than its diff:
```python
import math

import jax
import jax.numpy as jnp
from jax import lax
from jax.experimental import pallas as pl
from jax.experimental.pallas import tpu as pltpu
from jax.sharding import PartitionSpec as P

aspect_sq = 0.0025
LANES = 128
SUB = 8
MIB = 1 << 20


def split_bf16(x):
    high = x.astype(jnp.bfloat16)
    low = (x - high.astype(jnp.float32)).astype(jnp.bfloat16)
    return high, low


def modes_kernel(scale, density_ref, basis_ref, out_ref):
    surface = density_ref[0]
    for layer in range(1, density_ref.shape[0]):
        surface = surface + density_ref[layer]
    out_ref[...] = scale * lax.dot_general(
        basis_ref[...],
        surface,
        (((1,), (1,)), ((), ())),
        precision=lax.Precision.HIGHEST,
        preferred_element_type=jnp.float32,
    )


def surface_modes(density, basis, scale):
    layers, rows, cells = density.shape
    cols = basis.shape[0]
    block = min(rows, LANES)
    return pl.pallas_call(
        lambda *refs: modes_kernel(scale, *refs),
        grid=(rows // block,),
        in_specs=[
            pl.BlockSpec((layers, block, cells), lambda i: (0, i, 0)),
            pl.BlockSpec((cols, cells), lambda i: (0, 0)),
        ],
        out_specs=pl.BlockSpec((cols, block), lambda i: (0, i)),
        out_shape=jax.ShapeDtypeStruct((cols, rows), jnp.float32),
        compiler_params=pltpu.CompilerParams(vmem_limit_bytes=16 * MIB),
        cost_estimate=pl.CostEstimate(
            flops=12 * rows * cells * cols, bytes_accessed=4 * density.size, transcendentals=0
        ),
        name="surface_modes",
    )(density, basis)


def response_kernel(mode_count, pairs_ref, pot_ref, force_ref, out_ref):
    pairs = pairs_ref[...]
    row = lax.broadcasted_iota(jnp.int32, out_ref.shape[1:], 0) // 2
    for place, ref in enumerate((pot_ref, force_ref)):
        total = jnp.zeros(out_ref.shape[1:], jnp.float32)
        for mode in range(mode_count):
            part = lax.dot_general(
                pairs, ref[mode], (((1,), (1,)), ((), ())), preferred_element_type=jnp.float32
            )
            total = jnp.where(row == mode, part, total)
        out_ref[place] = total


def responses(pairs, potential_kernel, force_kernel):
    mode_count, rows, count = potential_kernel.shape
    cols = pairs.shape[0]
    block = min(rows, LANES)
    kernel_spec = pl.BlockSpec((mode_count, block, count), lambda i: (0, i, 0))
    return pl.pallas_call(
        lambda *refs: response_kernel(mode_count, *refs),
        grid=(rows // block,),
        in_specs=[pl.BlockSpec((cols, count), lambda i: (0, 0)), kernel_spec, kernel_spec],
        out_specs=pl.BlockSpec((2, cols, block), lambda i: (0, 0, i)),
        out_shape=jax.ShapeDtypeStruct((2, cols, rows), jnp.float32),
        compiler_params=pltpu.CompilerParams(vmem_limit_bytes=16 * MIB),
        cost_estimate=pl.CostEstimate(
            flops=4 * rows * count * cols * mode_count,
            bytes_accessed=4 * potential_kernel.size,
            transcendentals=0,
        ),
        name="responses",
    )(pairs, potential_kernel, force_kernel)


ROOT_FACE, SOUND_FACE, IN, OUT, ROOT_MID, SOUND_MID, AZ, SPIN, PULL = range(9)
COEFS = 16


def row_coefficients(first_row, rows, step):
    face = jnp.exp((first_row + jnp.arange(rows + SUB + 1)).astype(jnp.float32) * step)
    inner, outer = face[:-1], face[1:]
    mid = 0.5 * (inner + outer)
    area = 0.5 * (outer * outer - inner * inner)
    sound_face = aspect_sq / inner
    sound_mid = aspect_sq / mid
    radial = (0.05 * step) / area
    columns = [
        jnp.sqrt(sound_face),
        sound_face,
        radial * inner,
        radial * outer,
        jnp.sqrt(sound_mid),
        sound_mid,
        0.05 / mid,
        (0.1 * step) / mid,
        (0.1 * step) / (mid * mid),
    ]
    columns += [jnp.zeros_like(mid)] * (COEFS - len(columns))
    return jnp.stack(columns, axis=1)


def inverse(x):
    guess = pl.reciprocal(x, approx=True)
    return guess * (2.0 - x * guess)


def flux_kernel(block_count, refs):
    fields = refs[0:3]
    before = refs[3:6]
    after = refs[6:9]
    rim_in, rim_out, ghost_ref, coef_ref, coef_next = refs[9:14]
    outs = refs[-5:-2]
    above, lagged = refs[-2:]
    rows, cells = fields[0].shape
    columns = cells // LANES
    strips = rows // SUB
    index = pl.program_id(0)
    lane = lax.broadcasted_iota(jnp.int32, (SUB, LANES), 1)
    sub = lax.broadcasted_iota(jnp.int32, (SUB, LANES), 0)

    def wide(column):
        return jnp.broadcast_to(column, (SUB, LANES))

    def at(col):
        return pl.ds(col * LANES, LANES)

    def radial_state(state):
        density, mom_r, mom_phi = state
        inv = inverse(density)
        vel = mom_r * inv
        return inv, (density, mom_r, mom_phi, jnp.abs(vel), mom_r * vel, mom_phi * vel)

    def keep_above(col, values):
        for slot, value in enumerate(values):
            above[slot, :, at(col)] = pltpu.roll(value, 1, 0)

    def radial_flux(col, values, root, sound):
        lower = [
            jnp.where(sub == 0, above[slot, :, at(col)], pltpu.roll(value, 1, 0))
            for slot, value in enumerate(values)
        ]
        speed = jnp.maximum(values[3], lower[3]) + root
        return (
            (values[1] + lower[1]) - speed * (values[0] - lower[0]),
            ((values[4] + lower[4]) + sound * (values[0] + lower[0]))
            - speed * (values[1] - lower[1]),
            (values[5] + lower[5]) - speed * (values[2] - lower[2]),
        )

    def finish(rows_before, col, flux, out_coef):
        for comp in range(3):
            up = jnp.where(sub == SUB - 1, pltpu.roll(flux[comp], SUB - 1, 0), lagged[comp, :, at(col)])
            outs[comp][rows_before, at(col)] -= out_coef * up

    def azimuth_flux(values, lower, root):
        speed = jnp.maximum(values[3], lower[3]) + root
        return (
            (values[2] + lower[2]) - speed * (values[0] - lower[0]),
            (values[4] + lower[4]) - speed * (values[1] - lower[1]),
            (values[5] + lower[5]) - speed * (values[2] - lower[2]),
        )

    for col in range(columns):
        state = []
        for comp in range(3):
            row = jnp.where(index == 0, rim_in[comp : comp + 1, at(col)], before[comp][SUB - 1 :, at(col)])
            state.append(jnp.broadcast_to(row, (SUB, LANES)))
        keep_above(col, radial_state(state)[1])

    def strip(place, carry):
        here = pl.ds(pl.multiple_of(place * SUB, SUB), SUB)
        rows_before = pl.ds(pl.multiple_of(jnp.maximum(place - 1, 0) * SUB, SUB), SUB)
        coef = coef_ref[here, :]
        root_face, sound_face, in_coef, root_mid, sound_mid, az, spin, pull = (
            wide(coef[:, k : k + 1])
            for k in (ROOT_FACE, SOUND_FACE, IN, ROOT_MID, SOUND_MID, AZ, SPIN, PULL)
        )
        out_before = wide(coef_ref[rows_before, OUT : OUT + 1])
        ghost = ghost_ref[here, :]

        def azimuth_values(state, inv, cross):
            density, mom_r, mom_phi = state
            vel = mom_phi * inv
            return (
                density, mom_r, mom_phi, jnp.abs(vel), cross, mom_phi * vel + sound_mid * density
            )

        def ghost_values(side):
            state = [wide(ghost[:, 3 * side + k : 3 * side + k + 1]) for k in range(3)]
            inv = inverse(state[0])
            return azimuth_values(state, inv, state[1] * state[2] * inv)

        turned = ghost_values(0)
        held = None
        held_flux = None

        def settle(col, held, held_flux, flux):
            for comp in range(3):
                up = jnp.where(
                    lane == LANES - 1,
                    pltpu.roll(flux[comp], LANES - 1, 1),
                    pltpu.roll(held_flux[comp], LANES - 1, 1),
                )
                outs[comp][here, at(col)] = held[comp] - az * (up - held_flux[comp])

        for col in range(columns):
            state = [ref[here, at(col)] for ref in fields]
            inv, values = radial_state(state)
            flux_r = radial_flux(col, values, root_face, sound_face)
            finish(rows_before, col, flux_r, out_before)
            keep_above(col, values)
            for comp in range(3):
                lagged[comp, :, at(col)] = pltpu.roll(flux_r[comp], SUB - 1, 0)
            values = azimuth_values(state, inv, values[5])
            rolled = [pltpu.roll(value, 1, 1) for value in values]
            lower = [jnp.where(lane == 0, a, b) for a, b in zip(turned, rolled)]
            turned = rolled
            flux = azimuth_flux(values, lower, root_mid)
            if col > 0:
                settle(col - 1, held, held_flux, flux)
            held = (
                state[0] + in_coef * flux_r[0],
                state[1] + in_coef * flux_r[1] + (spin * values[5] - pull * state[0]),
                state[2] + in_coef * flux_r[2] - spin * values[4],
            )
            held_flux = flux
        values = ghost_values(1)
        lower = [wide(a[:, 0:1]) for a in turned]
        settle(columns - 1, held, held_flux, azimuth_flux(values, lower, root_mid))
        return carry

    lax.fori_loop(0, strips, strip, 0)

    last = pl.ds((strips - 1) * SUB, SUB)
    root_face = wide(coef_next[:, ROOT_FACE : ROOT_FACE + 1])
    sound_face = wide(coef_next[:, SOUND_FACE : SOUND_FACE + 1])
    out_coef = wide(coef_ref[last, OUT : OUT + 1])
    for col in range(columns):
        state = []
        for comp in range(3):
            row = jnp.where(
                index == block_count - 1,
                rim_out[comp : comp + 1, at(col)],
                after[comp][0:1, at(col)],
            )
            state.append(jnp.broadcast_to(row, (SUB, LANES)))
        finish(last, col, radial_flux(col, radial_state(state)[1], root_face, sound_face), out_coef)


def flux_layer(layer, fields, rims, ghosts, coefs, so_far):
    layers, rows, cells = fields[0].shape
    block = min(rows, 64)
    count = rows // block
    per = block // SUB
    main = pl.BlockSpec((None, block, cells), lambda i: (layer, i, 0))
    before = pl.BlockSpec((None, SUB, cells), lambda i: (layer, jnp.maximum(i * per - 1, 0), 0))
    after = pl.BlockSpec(
        (None, SUB, cells), lambda i: (layer, jnp.minimum((i + 1) * per, rows // SUB - 1), 0)
    )
    rim = pl.BlockSpec((None, 3, cells), lambda i: (layer, 0, 0))
    operands = [*fields, *fields, *fields, *rims, ghosts, coefs, coefs]
    specs = [main] * 3 + [before] * 3 + [after] * 3 + [
        rim,
        rim,
        pl.BlockSpec((None, block, ghosts.shape[2]), lambda i: (layer, i, 0)),
        pl.BlockSpec((block, COEFS), lambda i: (i, 0)),
        pl.BlockSpec((SUB, COEFS), lambda i: ((i + 1) * per, 0)),
    ]
    aliases = {}
    if so_far is not None:
        for k, array in enumerate(so_far):
            aliases[len(operands)] = k
            operands.append(array)
            specs.append(pl.BlockSpec(memory_space=pl.ANY))
    return pl.pallas_call(
        lambda *refs: flux_kernel(count, refs),
        grid=(count,),
        in_specs=specs,
        out_specs=[main] * 3,
        out_shape=[jax.ShapeDtypeStruct(f.shape, f.dtype) for f in fields],
        scratch_shapes=[
            pltpu.VMEM((6, SUB, cells), jnp.float32),
            pltpu.VMEM((3, SUB, cells), jnp.float32),
        ],
        input_output_aliases=aliases,
        compiler_params=pltpu.CompilerParams(vmem_limit_bytes=16 * MIB),
        cost_estimate=pl.CostEstimate(
            flops=100 * rows * cells, bytes_accessed=24 * rows * cells, transcendentals=rows * cells
        ),
        name="flux_layer",
    )(*operands)


def gravity_kernel(
    pot_ref, force_ref, inverse_ref, table_ref, slope_ref, density_ref, mom_r_ref, mom_phi_ref,
    out_r, out_phi, out_pot,
):
    def left(ref):
        high, low = split_bf16(ref[...])
        return jnp.concatenate([high, low, high], axis=0)

    def product(a, table):
        return lax.dot_general(
            a, table, (((0,), (0,)), ((), ())), preferred_element_type=jnp.float32
        )

    pot, force = left(pot_ref), left(force_ref)
    out_pot[...] = product(pot, table_ref[...])
    radial = product(force, table_ref[...]) * 0.1
    azimuth = product(pot, slope_ref[...]) * inverse_ref[...]
    for layer in range(density_ref.shape[0]):
        density = density_ref[layer]
        out_r[layer] = mom_r_ref[layer] + density * radial
        out_phi[layer] = mom_phi_ref[layer] + density * azimuth


def add_gravity(pot, force, inverse_mid, table, slope, density, mom_r, mom_phi):
    layers, rows, cells = density.shape
    cols = pot.shape[0]
    block = min(rows, LANES)
    modes_spec = pl.BlockSpec((cols, block), lambda i: (0, i))
    table_spec = pl.BlockSpec(table.shape, lambda i: (0, 0))
    field = pl.BlockSpec((layers, block, cells), lambda i: (0, i, 0))
    grid_shape = jax.ShapeDtypeStruct(density.shape, density.dtype)
    return pl.pallas_call(
        gravity_kernel,
        grid=(rows // block,),
        in_specs=[
            modes_spec, modes_spec, pl.BlockSpec((block, 1), lambda i: (i, 0)),
            table_spec, table_spec, field, field, field,
        ],
        out_specs=[field, field, pl.BlockSpec((block, cells), lambda i: (i, 0))],
        out_shape=[grid_shape, grid_shape, jax.ShapeDtypeStruct((rows, cells), jnp.float32)],
        input_output_aliases={6: 0, 7: 1},
        compiler_params=pltpu.CompilerParams(vmem_limit_bytes=24 * MIB),
        cost_estimate=pl.CostEstimate(
            flops=18 * rows * cells * cols, bytes_accessed=44 * rows * cells, transcendentals=0
        ),
        name="add_gravity",
    )(pot, force, inverse_mid, table, slope, density, mom_r, mom_phi)


def exchange_rims(fields, rad_index, rad_count):
    first = jnp.stack([f[:, 0] for f in fields], axis=1)
    last = jnp.stack([f[:, -1] for f in fields], axis=1)
    if rad_count == 1:
        return first, last
    first_out, last_out = first.astype(jnp.bfloat16), last.astype(jnp.bfloat16)
    if rad_count == 2:
        other = lax.ppermute(
            jnp.where(rad_index == 0, last_out, first_out), "rad", [(0, 1), (1, 0)]
        )
        low = high = other
    else:
        up = [(i, i + 1) for i in range(rad_count - 1)]
        low = lax.ppermute(last_out, "rad", up)
        high = lax.ppermute(first_out, "rad", [(b, a) for a, b in up])
    rim_in = jnp.where(rad_index == 0, first, low.astype(first.dtype))
    rim_out = jnp.where(rad_index == rad_count - 1, last, high.astype(last.dtype))
    return rim_in, rim_out


def exchange_edges(fields, az_count):
    right = [(i, (i + 1) % az_count) for i in range(az_count)]
    left = [(b, a) for a, b in right]
    low = lax.ppermute(
        jnp.stack([f[:, :, -1] for f in fields], axis=1).astype(jnp.bfloat16), "az", right
    )
    high = lax.ppermute(
        jnp.stack([f[:, :, 0] for f in fields], axis=1).astype(jnp.bfloat16), "az", left
    )
    both = jnp.concatenate([low, high], axis=1).astype(fields[0].dtype)
    return jnp.swapaxes(both, 1, 2)


def local(az_count, rad_count, density, mom_r, mom_phi, potential_kernel, force_kernel):
    layers, rows, cells = density.shape
    mode_count = potential_kernel.shape[0]
    pair_count = 2 * mode_count
    cols = az_count * pair_count
    step = 2.0 * math.pi / (az_count * cells)
    az_index = lax.axis_index("az")
    rad_index = lax.axis_index("rad")
    fields = (density, mom_r, mom_phi)

    azimuth = ((az_index * cells + jnp.arange(cells)).astype(jnp.float32) + 0.5) * step
    row = lax.broadcasted_iota(jnp.int32, (cols, cells), 0)
    mode = (row // 2).astype(jnp.float32)
    angle = azimuth[None, :] * mode
    cosine, sine = jnp.cos(angle), jnp.sin(angle)
    basis = jnp.where(row % 2 == 0, cosine, sine)
    slope = jnp.where(row % 2 == 0, -mode * sine, mode * cosine)

    rims = exchange_rims(fields, rad_index, rad_count)
    ghosts = exchange_edges(fields, az_count)
    coefs = row_coefficients(rad_index * rows, rows, step)

    partial = surface_modes(density, basis, 1.0 / (az_count * cells))
    pieces = lax.all_to_all(
        partial.reshape(az_count, pair_count, rows), "az", split_axis=0, concat_axis=0, tiled=True
    )
    results = flux_layer(0, fields, rims, ghosts, coefs, None)

    own = jnp.sum(pieces, axis=0).astype(jnp.bfloat16)
    pairs = lax.all_gather(own, "rad", axis=1, tiled=True)
    parts = responses(pairs, potential_kernel, force_kernel)
    every = lax.all_gather(parts, "az", axis=0)
    for layer in range(1, layers):
        results = flux_layer(layer, fields, rims, ghosts, coefs, results)
    pot = every[:, 0].reshape(cols, rows)
    force = every[:, 1].reshape(cols, rows)

    def table_of(x):
        high, low = split_bf16(x)
        return jnp.concatenate([high, high, low], axis=0)

    face = jnp.exp((rad_index * rows + jnp.arange(rows + 1)).astype(jnp.float32) * step)
    inverse_mid = -0.1 / (0.5 * (face[:-1] + face[1:]))
    new_r, new_phi, potential = add_gravity(
        pot, force, inverse_mid[:, None], table_of(basis), table_of(slope), density, results[1], results[2]
    )
    return results[0], new_r, new_phi, potential


def solution(mesh):
    az_count, rad_count = mesh.shape["az"], mesh.shape["rad"]
    field = P(None, "rad", "az")
    kernel = P("az", "rad", None)
    return jax.shard_map(
        lambda *args: local(az_count, rad_count, *args),
        mesh=mesh,
        in_specs=(field, field, field, kernel, kernel),
        out_specs=(field, field, field, P("rad", "az")),
        check_vma=False,
    )
```

time: 625 us -> 206 us (0.33); the launches traced: 616 us -> 205 us
  other arithmetic: 334 us -> 16.9 us
  Pallas kernels: 0 us -> 113 us
  local copies, waits for them, and re-layouts: 132 us -> 37.3 us
  blocking collectives: 81.9 us -> 1.83 us
  matrix products: 43.5 us -> 0 us
  waiting for transfers between devices: 0.03 us -> 7.04 us
    mul x6 -> x1, other arithmetic: 121 us -> 0.01 us  [local(): ((az_index * cells + jnp.arange(cells)).astype(jnp.float32) + 0.5) * step]
    pallas_call x0 -> x5, Pallas kernels: none -> 113 us  [the longest x2 78.1 us: flux_layer(): pl.pallas_call(lambda *refs: flux_kernel(count, refs), grid=(count,), in_...]
    concatenate x2 -> x0, local copies, waits for them, and re-layouts: 88.5 us -> none  [extended(): block = jnp.concatenate([low, block, high], axis=dim)]
    all_gather x3 -> x1, blocking collectives: 81.9 us -> 1.83 us  [local(): pairs = lax.all_gather(own, 'rad', axis=1, tiled=True)]
    add x1, other arithmetic: 55.7 us -> 0.01 us  [local(): basis = jnp.where(row % 2 == 0, cosine, sine)]
    sub x1, other arithmetic: 45.3 us -> 0.01 us  [local(): mode = (row // 2).astype(jnp.float32)]
    dot_general x6 -> x0, matrix products: 43.5 us -> none  [the longest x1 10.3 us: local(): jnp.einsum('krs,skc->rkc', potential_kernel, pairs, preferred_element_typ...]
    concatenate x1, other arithmetic: 37.1 us -> 0.2 us  [table_of(): return jnp.concatenate([high, high, low], axis=0)]
  transfers between devices with their start and end apart: 5 -> 5, of which waited for: 0 -> 1; matrix products, arithmetic and copies ran while one was open for 60% -> 10% of each run, Pallas kernels for 0% -> 44%
where the time goes in v1:
time: 206 us; the launch traced here: 205 us
  Pallas kernels  113 us (55%)
  local copies, waits for them, and re-layouts  37.3 us (18%)
  other arithmetic  16.9 us (8%)
  between operations  14.3 us (7%)
  starting transfers between devices  14.2 us (7%)
  waiting for transfers between devices  7.04 us (3%)
    pallas_call x2, Pallas kernels, flux_layer(): pl.pallas_call(lambda *refs: flux_kernel(count, refs), grid=(count,), in_...  78.1 us
    unnamed x16, local copies, waits for them, and re-layouts  29.5 us
    pallas_call x1, Pallas kernels, add_gravity(): pl.pallas_call(gravity_kernel, grid=(rows // block,), in_specs=[modes_spe...  16.4 us
    another operation x3, other arithmetic  14.2 us
    pallas_call x1, Pallas kernels, responses(): pl.pallas_call(lambda *refs: response_kernel(mode_count, *refs), grid=(ro...  12.4 us
    all_to_all x1, starting transfers between devices, local(): lax.all_to_all(partial.reshape(az_count, pair_count, rows), 'az', split_a...  8.31 us
    all_to_all x1, waiting for transfers between devices, local(): lax.all_to_all(partial.reshape(az_count, pair_count, rows), 'az', split_a...  7.02 us
    pallas_call x1, Pallas kernels, surface_modes(): pl.pallas_call(lambda *refs: modes_kernel(scale, *refs), grid=(rows // bl...  6.27 us
  transfers between devices with their start and end apart: 5, of which 1 were waited for; matrix products, arithmetic and copies ran while one was open for 10% of the time, Pallas kernels for 44%

profile of v1, /device:TPU:0, one launch (start us, length us, event | category | flops | bytes accessed | tf_op | source)
XLA Modules:
  0.0 204.9 jit_solution(8144539288357740354)
XLA Ops:
  7.3 2.1 %fusion.3 = (bf16[128,1024]{1,0:T(8,128)(2,1)S(1)}, bf16[128,1024]{1,0:T(8,128)(2,1)S(1)}, bf16[128,1024]{1,0:T(8,128)(2,1)S(1)}, f32[128,1024]{1,0:T(8,128)S(1)}, bf16[128,1024]{1,0:T(8,128)(2,1)S(1)}) fusion(s32[128]{0:T(128)S(1)} %iota_shift-right-logical_fusion, s32[128]{0:T(128)S(1)} %broadcast_add_fusion, f32[1024]{0:T(1024)S(1)} %add_multiply_fusion.1, ...), kind=kLoop, calls=%fused_computation.18 | loop fusion | flops 2359296 | bytes 1579264 | tf_op jit(solution)/shard_map/convert_element_type | solution.py:17
  9.4 3.4 %copy-done = f32[2,1024,1024]{2,1,0:T(8,128)S(1)} copy-done((f32[2,1024,1024]{2,1,0:T(8,128)S(1)}, f32[2,1024,1024]{2,1,0:T(8,128)}, u32[]{:S(2)}) %copy-start) | copy-done | bytes 8388632
  12.7 6.3 %surface_modes.1 = f32[128,1024]{1,0:T(8,128)} custom-call(f32[2,1024,1024]{2,1,0:T(8,128)S(1)} %copy-done, f32[128,1024]{1,0:T(8,128)S(1)} %get-tuple-element.51.refs_1_), custom_call_target="tpu_custom_call" | custom-call | flops 1610612736 | bytes 8388608 | tf_op jit(solution)/shard_map/surface_modes/pallas_call | solution.py:39
  19.0 8.3 %all-to-all-start = ((f32[16,8,1024]{2,1,0:T(8,128)}), f32[16,8,1024]{2,1,0:T(8,128)S(1)}, u32[]{:S(2)}, u32[]{:S(2)}) async-start(f32[16,8,1024]{2,1,0:T(8,128)} %bitcast.1), calls=%async_computation | async-start | bytes 1048576 | tf_op jit(solution)/shard_map/all_to_all | solution.py:414
  27.4 0.9 fusion.14
  28.3 1.0 fusion.15
  29.4 6.1 %convert.25 = bf16[2,1024,1024]{2,1,0:T(8,128)(2,1)} convert(f32[2,1024,1024]{2,1,0:T(8,128)} %density_ref.1) | non-fusion elementwise | flops 2097152 | bytes 12582912 | tf_op jit(solution)/shard_map/convert.18
  35.4 7.0 %all-to-all-done = f32[16,8,1024]{2,1,0:T(8,128)S(1)} async-done(((f32[16,8,1024]{2,1,0:T(8,128)}), f32[16,8,1024]{2,1,0:T(8,128)S(1)}, u32[]{:S(2)}, u32[]{:S(2)}) %all-to-all-start) | async-done | bytes 524320 | tf_op jit(solution)/shard_map/all_to_all | solution.py:414
  42.5 1.8 all_gather.9.refs_0_
  44.3 5.8 %copy-done.5 = bf16[4,1024,2048]{2,1,0:T(8,128)(2,1)S(1)} copy-done((bf16[4,1024,2048]{2,1,0:T(8,128)(2,1)S(1)}, bf16[4,1024,2048]{2,1,0:T(8,128)(2,1)}, u32[]{:S(2)}) %copy-start.5) | copy-done | bytes 16777240
  50.1 5.8 %copy-done.6 = bf16[4,1024,2048]{2,1,0:T(8,128)(2,1)S(1)} copy-done((bf16[4,1024,2048]{2,1,0:T(8,128)(2,1)S(1)}, bf16[4,1024,2048]{2,1,0:T(8,128)(2,1)}, u32[]{:S(2)}) %copy-start.6) | copy-done | bytes 16777240
  55.9 12.4 %responses.1 = f32[2,8,1024]{2,1,0:T(8,128)} custom-call(bf16[8,2048]{1,0:T(8,128)(2,1)S(1)} %all_gather.9.refs_0_, bf16[4,1024,2048]{2,1,0:T(8,128)(2,1)S(1)} %copy-done.5, bf16[4,1024,2048]{2,1,0:T(8,128)(2,1)S(1)} %copy-done.6), custom_call_target="tpu_custom_call" | custom-call | flops 268435456 | bytes 33554432 | tf_op jit(solution)/shard_map/responses/pallas_call | solution.py:74
  68.3 1.7 slice_reduce_fusion.5
  70.0 4.0 %convert.26 = bf16[2,1024,1024]{2,1,0:T(8,128)(2,1)S(1)} convert(f32[2,1024,1024]{2,1,0:T(8,128)} %refs_7_.3) | non-fusion elementwise | flops 2097152 | bytes 12582912 | tf_op jit(solution)/shard_map/convert.16
  74.1 4.1 %convert.27 = bf16[2,1024,1024]{2,1,0:T(8,128)(2,1)S(1)} convert(f32[2,1024,1024]{2,1,0:T(8,128)} %refs_8_.3) | non-fusion elementwise | flops 2097152 | bytes 12582912 | tf_op jit(solution)/shard_map/convert.14
  78.2 0.6 slice_reduce_fusion.4
  78.8 0.6 slice_reduce_fusion.3
  79.4 0.6 collective-permute-start.1
  80.0 5.1 %collective-permute-start.2 = (bf16[2,3,1024]{2,0,1:T(2,128)(2,1)S(1)}, bf16[2,3,1024]{2,0,1:T(2,128)(2,1)S(1)}, u32[]{:S(2)}, u32[]{:S(2)}) collective-permute-start(bf16[2,3,1024]{2,0,1:T(2,128)(2,1)S(1)} %pad_maximum_fusion.5), channel_id=1, source_target_pairs={{2,0},{4,2},{6,4},{8,6},{10,8},{12,10},{14,12},{16,14},{18,16},{20... | collective-permute-start | bytes 36872 | tf_op jit(solution)/shard_map/ppermute | solution.py:384
  85.3 0.2 pad_maximum_fusion
  85.8 0.2 copy.97.refs_12_.refs_13_
  86.0 1.0 copy.101.inverse_ref
  87.1 0.4 copy.94
  87.6 3.4 %copy-done.1 = f32[2,1024,1024]{2,1,0:T(8,128)S(1)} copy-done((f32[2,1024,1024]{2,1,0:T(8,128)S(1)}, f32[2,1024,1024]{2,1,0:T(8,128)}, u32[]{:S(2)}) %copy-start.1) | copy-done | bytes 8388632
  90.9 3.4 %copy-done.3 = f32[2,1024,1024]{2,1,0:T(8,128)S(1)} copy-done((f32[2,1024,1024]{2,1,0:T(8,128)S(1)}, f32[2,1024,1024]{2,1,0:T(8,128)}, u32[]{:S(2)}) %copy-start.3) | copy-done | bytes 8388632
  94.3 3.4 %copy-done.4 = f32[2,1024,1024]{2,1,0:T(8,128)S(1)} copy-done((f32[2,1024,1024]{2,1,0:T(8,128)S(1)}, f32[2,1024,1024]{2,1,0:T(8,128)}, u32[]{:S(2)}) %copy-start.4) | copy-done | bytes 8388632
  97.7 39.1 %flux_layer.2 = (f32[2,1024,1024]{2,1,0:T(8,128)}, f32[2,1024,1024]{2,1,0:T(8,128)}, f32[2,1024,1024]{2,1,0:T(8,128)}) custom-call(f32[2,1024,1024]{2,1,0:T(8,128)S(1)} %copy-done.1, f32[2,1024,1024]{2,1,0:T(8,128)S(1)} %copy-done.3, f32[2,1024,1024]{2,1,0:T(8,128)S(1)} %copy-done.4, f32[2,1024,1024]{2,1,0:T(8,128)S(1)} %copy-done.1, ...), custom_call_target="tpu_custom_call" | custom-call | flops 104857600 | bytes 25165824 | tf_op jit(solution)/shard_map/flux_layer/pallas_call | solution.py:290
  136.8 39.1 %flux_layer.3 = (f32[2,1024,1024]{2,1,0:T(8,128)}, f32[2,1024,1024]{2,1,0:T(8,128)}, f32[2,1024,1024]{2,1,0:T(8,128)}) custom-call(f32[2,1024,1024]{2,1,0:T(8,128)S(1)} %copy-done.1, f32[2,1024,1024]{2,1,0:T(8,128)S(1)} %copy-done.3, f32[2,1024,1024]{2,1,0:T(8,128)S(1)} %copy-done.4, ...), custom_call_target="tpu_custom_call", output_to_operand_aliasing={{0}: (14, {}), {1}: (15, {}), {2}: (16, {})} | custom-call | flops 104857600 | bytes 25165824 | tf_op jit(solution)/shard_map/flux_layer/pallas_call | solution.py:290
  175.9 1.3 slice_bitcast_fusion
  177.2 3.4 %copy-done.2 = f32[2,1024,1024]{2,1,0:T(8,128)S(1)} copy-done((f32[2,1024,1024]{2,1,0:T(8,128)S(1)}, f32[2,1024,1024]{2,1,0:T(8,128)}, u32[]{:S(2)}) %copy-start.2) | copy-done | bytes 8388632
  180.6 1.0 copy-done.7
  181.6 16.4 %add_gravity.1 = (f32[2,1024,1024]{2,1,0:T(8,128)}, f32[2,1024,1024]{2,1,0:T(8,128)}, f32[1024,1024]{1,0:T(8,128)}) custom-call(f32[128,1024]{1,0:T(8,128)S(1)} %get-tuple-element.37.pot_ref, f32[128,1024]{1,0:T(8,128)S(1)} %get-tuple-element.36.force_ref, f32[1024,1]{1,0:T(8,128)S(1)} %copy-done.7, ...), custom_call_target="tpu_custom_call", output_to_operand_aliasing={{0}: (6, {}), {1}: (7, {})} | custom-call | flops 2415919104 | bytes 46137344 | tf_op jit(solution)/shard_map/add_gravity/pallas_call | solution.py:340
  (46 shorter events, 0.8 us)
Async XLA Ops:
  9.3 3.4 %copy-start = (f32[2,1024,1024]{2,1,0:T(8,128)S(1)}, f32[2,1024,1024]{2,1,0:T(8,128)}, u32[]{:S(2)}) copy-start(f32[2,1024,1024]{2,1,0:T(8,128)} %density_ref.1) | copy-start | bytes 25165828
  19.0 23.5 %all-to-all-start = ((f32[16,8,1024]{2,1,0:T(8,128)}), f32[16,8,1024]{2,1,0:T(8,128)S(1)}, u32[]{:S(2)}, u32[]{:S(2)}) async-start(f32[16,8,1024]{2,1,0:T(8,128)} %bitcast.1), calls=%async_computation | async-start | bytes 1048576 | tf_op jit(solution)/shard_map/all_to_all | solution.py:414
  27.3 148.6 %all-gather.3.cloned.1.call-start = ((), (), s32[]{:S(2)}) async-start(), calls=%async_computation.1 | async-start | bytes 1114112 | tf_op jit(solution)/shard_map/all_gather | solution.py:422
  29.3 58.2 %collective-permute-start = (bf16[2,3,1024]{2,1,0:T(4,128)(2,1)S(1)}, bf16[2,3,1024]{2,1,0:T(4,128)(2,1)S(1)}, u32[]{:S(2)}, u32[]{:S(2)}) collective-permute-start(bf16[2,3,1024]{2,1,0:T(4,128)(2,1)S(1)} %fusion.7), channel_id=1, source_target_pairs={{0,1},{1,0},{2,3},{3,2},{4,5},{5,4},{6,7},{7,6},{8,9},{9,8},{10,11... | collective-permute-start | bytes 36872 | tf_op jit(solution)/shard_map/ppermute | solution.py:365
  44.3 5.8 %copy-start.5 = (bf16[4,1024,2048]{2,1,0:T(8,128)(2,1)S(1)}, bf16[4,1024,2048]{2,1,0:T(8,128)(2,1)}, u32[]{:S(2)}) copy-start(bf16[4,1024,2048]{2,1,0:T(8,128)(2,1)} %refs_1_.5) | copy-start | bytes 50331652
  50.1 5.8 %copy-start.6 = (bf16[4,1024,2048]{2,1,0:T(8,128)(2,1)S(1)}, bf16[4,1024,2048]{2,1,0:T(8,128)(2,1)}, u32[]{:S(2)}) copy-start(bf16[4,1024,2048]{2,1,0:T(8,128)(2,1)} %refs_2_.5) | copy-start | bytes 50331652
  79.4 7.7 %collective-permute-start.1 = (bf16[2,3,1024]{2,0,1:T(2,128)(2,1)S(1)}, bf16[2,3,1024]{2,0,1:T(2,128)(2,1)S(1)}, u32[]{:S(2)}, u32[]{:S(2)}) collective-permute-start(bf16[2,3,1024]{2,0,1:T(2,128)(2,1)S(1)} %pad_maximum_fusion.4), channel_id=1, source_target_pairs={{0,2},{2,4},{4,6},{6,8},{8,10},{10,12},{12,14},{14,16},{16,18},{18... | collective-permute-start | bytes 36872 | tf_op jit(solution)/shard_map/ppermute | solution.py:381
  80.0 7.0 %collective-permute-start.2 = (bf16[2,3,1024]{2,0,1:T(2,128)(2,1)S(1)}, bf16[2,3,1024]{2,0,1:T(2,128)(2,1)S(1)}, u32[]{:S(2)}, u32[]{:S(2)}) collective-permute-start(bf16[2,3,1024]{2,0,1:T(2,128)(2,1)S(1)} %pad_maximum_fusion.5), channel_id=1, source_target_pairs={{2,0},{4,2},{6,4},{8,6},{10,8},{12,10},{14,12},{16,14},{18,16},{20... | collective-permute-start | bytes 36872 | tf_op jit(solution)/shard_map/ppermute | solution.py:384
  87.5 3.4 %copy-start.1 = (f32[2,1024,1024]{2,1,0:T(8,128)S(1)}, f32[2,1024,1024]{2,1,0:T(8,128)}, u32[]{:S(2)}) copy-start(f32[2,1024,1024]{2,1,0:T(8,128)} %density_ref.1) | copy-start | bytes 25165828
  90.9 3.4 %copy-start.3 = (f32[2,1024,1024]{2,1,0:T(8,128)S(1)}, f32[2,1024,1024]{2,1,0:T(8,128)}, u32[]{:S(2)}) copy-start(f32[2,1024,1024]{2,1,0:T(8,128)} %refs_7_.3) | copy-start | bytes 25165828
  94.3 3.4 %copy-start.4 = (f32[2,1024,1024]{2,1,0:T(8,128)S(1)}, f32[2,1024,1024]{2,1,0:T(8,128)}, u32[]{:S(2)}) copy-start(f32[2,1024,1024]{2,1,0:T(8,128)} %refs_8_.3) | copy-start | bytes 25165828
  177.2 3.4 %copy-start.2 = (f32[2,1024,1024]{2,1,0:T(8,128)S(1)}, f32[2,1024,1024]{2,1,0:T(8,128)}, u32[]{:S(2)}) copy-start(f32[2,1024,1024]{2,1,0:T(8,128)} %density_ref.1) | copy-start | bytes 25165828
  180.6 1.0 copy-start.7
Sparse Core Ops, SparseCore 0:
  68.4 53.5 all-gather.2

commit v2 on v1

--- a/solution.py
+++ b/solution.py
@@ -10,13 +10,18 @@
 aspect_sq = 0.0025
 LANES = 128
 SUB = 8
-MIB = 1 << 20
+VMEM_BYTES = 60 << 20
 
 
 def split_bf16(x):
     high = x.astype(jnp.bfloat16)
     low = (x - high.astype(jnp.float32)).astype(jnp.bfloat16)
     return high, low
+
+
+def split_outside(x):
+    high = lax.reduce_precision(x, 8, 7)
+    return high.astype(jnp.bfloat16), (x - high).astype(jnp.bfloat16)
 
 
 def modes_kernel(scale, density_ref, basis_ref, out_ref):
@@ -45,7 +50,7 @@
         ],
         out_specs=pl.BlockSpec((cols, block), lambda i: (0, i)),
         out_shape=jax.ShapeDtypeStruct((cols, rows), jnp.float32),
-        compiler_params=pltpu.CompilerParams(vmem_limit_bytes=16 * MIB),
+        compiler_params=pltpu.CompilerParams(vmem_limit_bytes=VMEM_BYTES),
         cost_estimate=pl.CostEstimate(
             flops=12 * rows * cells * cols, bytes_accessed=4 * density.size, transcendentals=0
         ),
@@ -77,7 +82,7 @@
         in_specs=[pl.BlockSpec((cols, count), lambda i: (0, 0)), kernel_spec, kernel_spec],
         out_specs=pl.BlockSpec((2, cols, block), lambda i: (0, 0, i)),
         out_shape=jax.ShapeDtypeStruct((2, cols, rows), jnp.float32),
-        compiler_params=pltpu.CompilerParams(vmem_limit_bytes=16 * MIB),
+        compiler_params=pltpu.CompilerParams(vmem_limit_bytes=VMEM_BYTES),
         cost_estimate=pl.CostEstimate(
             flops=4 * rows * count * cols * mode_count,
             bytes_accessed=4 * potential_kernel.size,
@@ -87,7 +92,7 @@
     )(pairs, potential_kernel, force_kernel)
 
 
-ROOT_FACE, SOUND_FACE, IN, OUT, ROOT_MID, SOUND_MID, AZ, SPIN, PULL = range(9)
+ROOT_FACE, SOUND_FACE, FACE, RADIAL, ROOT_MID, SOUND_MID, AZ, SPIN, PULL = range(9)
 COEFS = 16
 
 
@@ -98,12 +103,11 @@
     area = 0.5 * (outer * outer - inner * inner)
     sound_face = aspect_sq / inner
     sound_mid = aspect_sq / mid
-    radial = (0.05 * step) / area
     columns = [
         jnp.sqrt(sound_face),
         sound_face,
-        radial * inner,
-        radial * outer,
+        inner,
+        (0.05 * step) / area,
         jnp.sqrt(sound_mid),
         sound_mid,
         0.05 / mid,
@@ -124,20 +128,22 @@
     before = refs[3:6]
     after = refs[6:9]
     rim_in, rim_out, ghost_ref, coef_ref, coef_next = refs[9:14]
-    outs = refs[-5:-2]
-    above, lagged = refs[-2:]
+    outs = refs[-6:-3]
+    cell, face, part = refs[-3:]
     rows, cells = fields[0].shape
     columns = cells // LANES
     strips = rows // SUB
     index = pl.program_id(0)
     lane = lax.broadcasted_iota(jnp.int32, (SUB, LANES), 1)
-    sub = lax.broadcasted_iota(jnp.int32, (SUB, LANES), 0)
 
     def wide(column):
         return jnp.broadcast_to(column, (SUB, LANES))
 
     def at(col):
         return pl.ds(col * LANES, LANES)
+
+    def rows_at(place):
+        return pl.ds(pl.multiple_of(place * SUB, SUB), SUB)
 
     def radial_state(state):
         density, mom_r, mom_phi = state
@@ -145,27 +151,19 @@
         vel = mom_r * inv
         return inv, (density, mom_r, mom_phi, jnp.abs(vel), mom_r * vel, mom_phi * vel)
 
-    def keep_above(col, values):
-        for slot, value in enumerate(values):
-            above[slot, :, at(col)] = pltpu.roll(value, 1, 0)
-
-    def radial_flux(col, values, root, sound):
-        lower = [
-            jnp.where(sub == 0, above[slot, :, at(col)], pltpu.roll(value, 1, 0))
-            for slot, value in enumerate(values)
-        ]
-        speed = jnp.maximum(values[3], lower[3]) + root
-        return (
-            (values[1] + lower[1]) - speed * (values[0] - lower[0]),
-            ((values[4] + lower[4]) + sound * (values[0] + lower[0]))
-            - speed * (values[1] - lower[1]),
-            (values[5] + lower[5]) - speed * (values[2] - lower[2]),
-        )
-
-    def finish(rows_before, col, flux, out_coef):
-        for comp in range(3):
-            up = jnp.where(sub == SUB - 1, pltpu.roll(flux[comp], SUB - 1, 0), lagged[comp, :, at(col)])
-            outs[comp][rows_before, at(col)] -= out_coef * up
+    for col in range(columns):
+        for place, edge, rim, near in (
+            (0, index == 0, rim_in, [ref[SUB - 1 :, at(col)] for ref in before]),
+            (rows + SUB, index == block_count - 1, rim_out, [ref[0:1, at(col)] for ref in after]),
+        ):
+            state = [
+                jnp.broadcast_to(
+                    jnp.where(edge, rim[comp : comp + 1, at(col)], near[comp]), (SUB, LANES)
+                )
+                for comp in range(3)
+            ]
+            for slot, value in enumerate(radial_state(state)[1]):
+                cell[slot, col, pl.ds(place, SUB), :] = value
 
     def azimuth_flux(values, lower, root):
         speed = jnp.maximum(values[3], lower[3]) + root
@@ -175,22 +173,13 @@
             (values[5] + lower[5]) - speed * (values[2] - lower[2]),
         )
 
-    for col in range(columns):
-        state = []
-        for comp in range(3):
-            row = jnp.where(index == 0, rim_in[comp : comp + 1, at(col)], before[comp][SUB - 1 :, at(col)])
-            state.append(jnp.broadcast_to(row, (SUB, LANES)))
-        keep_above(col, radial_state(state)[1])
-
-    def strip(place, carry):
-        here = pl.ds(pl.multiple_of(place * SUB, SUB), SUB)
-        rows_before = pl.ds(pl.multiple_of(jnp.maximum(place - 1, 0) * SUB, SUB), SUB)
+    def first_pass(place, carry):
+        here = rows_at(place)
+        inside = rows_at(place + 1)
         coef = coef_ref[here, :]
-        root_face, sound_face, in_coef, root_mid, sound_mid, az, spin, pull = (
-            wide(coef[:, k : k + 1])
-            for k in (ROOT_FACE, SOUND_FACE, IN, ROOT_MID, SOUND_MID, AZ, SPIN, PULL)
+        root_mid, sound_mid, az, spin, pull = (
+            wide(coef[:, k : k + 1]) for k in (ROOT_MID, SOUND_MID, AZ, SPIN, PULL)
         )
-        out_before = wide(coef_ref[rows_before, OUT : OUT + 1])
         ghost = ghost_ref[here, :]
 
         def azimuth_values(state, inv, cross):
@@ -204,10 +193,6 @@
             state = [wide(ghost[:, 3 * side + k : 3 * side + k + 1]) for k in range(3)]
             inv = inverse(state[0])
             return azimuth_values(state, inv, state[1] * state[2] * inv)
-
-        turned = ghost_values(0)
-        held = None
-        held_flux = None
 
         def settle(col, held, held_flux, flux):
             for comp in range(3):
@@ -216,16 +201,15 @@
                     pltpu.roll(flux[comp], LANES - 1, 1),
                     pltpu.roll(held_flux[comp], LANES - 1, 1),
                 )
-                outs[comp][here, at(col)] = held[comp] - az * (up - held_flux[comp])
-
+                part[comp, here, at(col)] = held[comp] - az * (up - held_flux[comp])
+
+        turned = ghost_values(0)
+        held = held_flux = None
         for col in range(columns):
             state = [ref[here, at(col)] for ref in fields]
             inv, values = radial_state(state)
-            flux_r = radial_flux(col, values, root_face, sound_face)
-            finish(rows_before, col, flux_r, out_before)
-            keep_above(col, values)
-            for comp in range(3):
-                lagged[comp, :, at(col)] = pltpu.roll(flux_r[comp], SUB - 1, 0)
+            for slot, value in enumerate(values):
+                cell[slot, col, inside, :] = value
             values = azimuth_values(state, inv, values[5])
             rolled = [pltpu.roll(value, 1, 1) for value in values]
             lower = [jnp.where(lane == 0, a, b) for a, b in zip(turned, rolled)]
@@ -234,9 +218,9 @@
             if col > 0:
                 settle(col - 1, held, held_flux, flux)
             held = (
-                state[0] + in_coef * flux_r[0],
-                state[1] + in_coef * flux_r[1] + (spin * values[5] - pull * state[0]),
-                state[2] + in_coef * flux_r[2] - spin * values[4],
+                state[0],
+                state[1] + (spin * values[5] - pull * state[0]),
+                state[2] - spin * values[4],
             )
             held_flux = flux
         values = ghost_values(1)
@@ -244,27 +228,50 @@
         settle(columns - 1, held, held_flux, azimuth_flux(values, lower, root_mid))
         return carry
 
-    lax.fori_loop(0, strips, strip, 0)
-
-    last = pl.ds((strips - 1) * SUB, SUB)
-    root_face = wide(coef_next[:, ROOT_FACE : ROOT_FACE + 1])
-    sound_face = wide(coef_next[:, SOUND_FACE : SOUND_FACE + 1])
-    out_coef = wide(coef_ref[last, OUT : OUT + 1])
-    for col in range(columns):
-        state = []
-        for comp in range(3):
-            row = jnp.where(
-                index == block_count - 1,
-                rim_out[comp : comp + 1, at(col)],
-                after[comp][0:1, at(col)],
-            )
-            state.append(jnp.broadcast_to(row, (SUB, LANES)))
-        finish(last, col, radial_flux(col, radial_state(state)[1], root_face, sound_face), out_coef)
+    lax.fori_loop(0, strips, first_pass, 0)
+
+    def face_flux(place, coef):
+        root, sound, radius = (wide(coef[:, k : k + 1]) for k in (ROOT_FACE, SOUND_FACE, FACE))
+        start = pl.multiple_of(place * SUB, SUB)
+        for col in range(columns):
+            upper = [cell[slot, col, pl.ds(start + SUB, SUB), :] for slot in range(6)]
+            lower = [cell[slot, col, pl.ds(start + (SUB - 1), SUB), :] for slot in range(6)]
+            speed = jnp.maximum(upper[3], lower[3]) + root
+            face[0, col, pl.ds(start, SUB), :] = radius * (
+                (upper[1] + lower[1]) - speed * (upper[0] - lower[0])
+            )
+            face[1, col, pl.ds(start, SUB), :] = radius * (
+                ((upper[4] + lower[4]) + sound * (upper[0] + lower[0]))
+                - speed * (upper[1] - lower[1])
+            )
+            face[2, col, pl.ds(start, SUB), :] = radius * (
+                (upper[5] + lower[5]) - speed * (upper[2] - lower[2])
+            )
+
+    def second_pass(place, carry):
+        face_flux(place, coef_ref[rows_at(place), :])
+        return carry
+
+    lax.fori_loop(0, strips, second_pass, 0)
+    face_flux(strips, coef_next[...])
+
+    def third_pass(place, carry):
+        here = rows_at(place)
+        start = pl.multiple_of(place * SUB, SUB)
+        scale = wide(coef_ref[here, RADIAL : RADIAL + 1])
+        for col in range(columns):
+            for comp in range(3):
+                low = face[comp, col, pl.ds(start, SUB), :]
+                high = face[comp, col, pl.ds(start + 1, SUB), :]
+                outs[comp][here, at(col)] = part[comp, here, at(col)] - scale * (high - low)
+        return carry
+
+    lax.fori_loop(0, strips, third_pass, 0)
 
 
 def flux_layer(layer, fields, rims, ghosts, coefs, so_far):
     layers, rows, cells = fields[0].shape
-    block = min(rows, 64)
+    block = min(rows, LANES)
     count = rows // block
     per = block // SUB
     main = pl.BlockSpec((None, block, cells), lambda i: (layer, i, 0))
@@ -294,11 +301,12 @@
         out_specs=[main] * 3,
         out_shape=[jax.ShapeDtypeStruct(f.shape, f.dtype) for f in fields],
         scratch_shapes=[
-            pltpu.VMEM((6, SUB, cells), jnp.float32),
-            pltpu.VMEM((3, SUB, cells), jnp.float32),
+            pltpu.VMEM((6, cells // LANES, block + 2 * SUB, LANES), jnp.float32),
+            pltpu.VMEM((3, cells // LANES, block + SUB, LANES), jnp.float32),
+            pltpu.VMEM((3, block, cells), jnp.float32),
         ],
         input_output_aliases=aliases,
-        compiler_params=pltpu.CompilerParams(vmem_limit_bytes=16 * MIB),
+        compiler_params=pltpu.CompilerParams(vmem_limit_bytes=VMEM_BYTES),
         cost_estimate=pl.CostEstimate(
             flops=100 * rows * cells, bytes_accessed=24 * rows * cells, transcendentals=rows * cells
         ),
@@ -347,7 +355,7 @@
         out_specs=[field, field, pl.BlockSpec((block, cells), lambda i: (i, 0))],
         out_shape=[grid_shape, grid_shape, jax.ShapeDtypeStruct((rows, cells), jnp.float32)],
         input_output_aliases={6: 0, 7: 1},
-        compiler_params=pltpu.CompilerParams(vmem_limit_bytes=24 * MIB),
+        compiler_params=pltpu.CompilerParams(vmem_limit_bytes=VMEM_BYTES),
         cost_estimate=pl.CostEstimate(
             flops=18 * rows * cells * cols, bytes_accessed=44 * rows * cells, transcendentals=0
         ),
@@ -378,12 +386,10 @@
 def exchange_edges(fields, az_count):
     right = [(i, (i + 1) % az_count) for i in range(az_count)]
     left = [(b, a) for a, b in right]
-    low = lax.ppermute(
-        jnp.stack([f[:, :, -1] for f in fields], axis=1).astype(jnp.bfloat16), "az", right
-    )
-    high = lax.ppermute(
-        jnp.stack([f[:, :, 0] for f in fields], axis=1).astype(jnp.bfloat16), "az", left
-    )
+    last = lax.optimization_barrier(jnp.stack([f[:, :, -1] for f in fields], axis=1))
+    first = lax.optimization_barrier(jnp.stack([f[:, :, 0] for f in fields], axis=1))
+    low = lax.ppermute(last.astype(jnp.bfloat16), "az", right)
+    high = lax.ppermute(first.astype(jnp.bfloat16), "az", left)
     both = jnp.concatenate([low, high], axis=1).astype(fields[0].dtype)
     return jnp.swapaxes(both, 1, 2)
 
@@ -415,18 +421,22 @@
         partial.reshape(az_count, pair_count, rows), "az", split_axis=0, concat_axis=0, tiled=True
     )
     results = flux_layer(0, fields, rims, ghosts, coefs, None)
+    pieces, results = lax.optimization_barrier((pieces, results))
 
     own = jnp.sum(pieces, axis=0).astype(jnp.bfloat16)
     pairs = lax.all_gather(own, "rad", axis=1, tiled=True)
     parts = responses(pairs, potential_kernel, force_kernel)
-    every = lax.all_gather(parts, "az", axis=0)
+    every = lax.all_to_all(
+        jnp.broadcast_to(parts[None], (az_count, *parts.shape)), "az", split_axis=0, concat_axis=0, tiled=True
+    )
+    coefs, parts = lax.optimization_barrier((coefs, parts))
     for layer in range(1, layers):
         results = flux_layer(layer, fields, rims, ghosts, coefs, results)
     pot = every[:, 0].reshape(cols, rows)
     force = every[:, 1].reshape(cols, rows)
 
     def table_of(x):
-        high, low = split_bf16(x)
+        high, low = split_outside(x)
         return jnp.concatenate([high, high, low], axis=0)
 
     face = jnp.exp((rad_index * rows + jnp.arange(rows + 1)).astype(jnp.float32) * step)

time: 206 us -> 220 us (1.068)
  Pallas kernels: 113 us -> 168 us
  local copies, waits for them, and re-layouts: 37.3 us -> 16.8 us
  between operations: 14.3 us -> 0.89 us
  other arithmetic: 16.9 us -> 5.58 us
  starting transfers between devices: 14.2 us -> 24.2 us
  waiting for transfers between devices: 7.04 us -> 2.14 us
    pallas_call x2, Pallas kernels: 78.1 us -> 124 us  [flux_layer(): pl.pallas_call(lambda *refs: flux_kernel(count, refs), grid=(count,), in_...]
    unnamed x16 -> x0, local copies, waits for them, and re-layouts: 29.5 us -> none
    another operation x5 -> x2, other arithmetic: 14.2 us -> 0.05 us  [the longest x1 0.02 us: exchange_edges(): jnp.stack([f[:, :, 0] for f in fields], axis=1)]
    all_to_all x0 -> x1, starting transfers between devices: none -> 9.65 us  [local(): lax.all_to_all(jnp.broadcast_to(parts[None], (az_count, *parts.shape)), '...]
    all_to_all x1, waiting for transfers between devices: 7.02 us -> 0.01 us  [local(): lax.all_to_all(partial.reshape(az_count, pair_count, rows), 'az', split_a...]
    slice x3, local copies, waits for them, and re-layouts: 2.9 us -> 7.41 us  [exchange_edges(): f[:, :, -1]]
    pallas_call x1, Pallas kernels: 12.4 us -> 16.1 us  [responses(): pl.pallas_call(lambda *refs: response_kernel(mode_count, *refs), grid=(ro...]
    pallas_call x1, Pallas kernels: 6.27 us -> 9.14 us  [surface_modes(): pl.pallas_call(lambda *refs: modes_kernel(scale, *refs), grid=(rows // bl...]
  transfers between devices with their start and end apart: 5 -> 5, of which waited for: 1 -> 1; matrix products, arithmetic and copies ran while one was open for 10% -> 8% of each run, Pallas kernels for 44% -> 60%
where the time goes in v2:
time: 220 us
  Pallas kernels  168 us (76%)
  starting transfers between devices  24.2 us (11%)
  local copies, waits for them, and re-layouts  16.8 us (8%)
  other arithmetic  5.58 us (3%)
    pallas_call x2, Pallas kernels, flux_layer(): pl.pallas_call(lambda *refs: flux_kernel(count, refs), grid=(count,), in_...  124 us
    pallas_call x1, Pallas kernels, add_gravity(): pl.pallas_call(gravity_kernel, grid=(rows // block,), in_specs=[modes_spe...  19.2 us
    pallas_call x1, Pallas kernels, responses(): pl.pallas_call(lambda *refs: response_kernel(mode_count, *refs), grid=(ro...  16.1 us
    all_to_all x1, starting transfers between devices, local(): lax.all_to_all(jnp.broadcast_to(parts[None], (az_count, *parts.shape)), '...  9.65 us
    pallas_call x1, Pallas kernels, surface_modes(): pl.pallas_call(lambda *refs: modes_kernel(scale, *refs), grid=(rows // bl...  9.14 us
    slice x3, local copies, waits for them, and re-layouts, exchange_edges(): f[:, :, -1]  7.41 us
    all_to_all x1, starting transfers between devices, local(): lax.all_to_all(partial.reshape(az_count, pair_count, rows), 'az', split_a...  5.94 us
    ppermute x1, starting transfers between devices, exchange_edges(): high = lax.ppermute(first.astype(jnp.bfloat16), 'az', left)  5.58 us
  transfers between devices with their start and end apart: 5, of which 1 were waited for; matrix products, arithmetic and copies ran while one was open for 8% of the time, Pallas kernels for 60%

profile of v2, /device:TPU:0, one launch (start us, length us, event | category | flops | bytes accessed | tf_op | source)
XLA Modules:
  0.0 219.7 jit_solution(18156674305421279578)
XLA Ops:
  0.6 0.9 fusion.12
  1.5 1.0 fusion.13
  2.5 0.1 fusion.7
  2.6 0.5 collective-permute-start
  3.1 2.5 %slice_reduce_fusion.5 = (bf16[2,1024]{1,0:T(2,128)(2,1)S(1)}, bf16[2,1024]{1,0:T(2,128)(2,1)S(1)}) fusion(f32[2,1024,1024]{2,1,0:T(8,128)} %density_ref.1), kind=kLoop, calls=%fused_computation.5 | loop fusion | bytes 24576 | tf_op jit(solution)/shard_map/slice | solution.py:389
  5.6 2.5 %slice_reduce_fusion.4 = (bf16[2,1024]{1,0:T(2,128)(2,1)S(1)}, bf16[2,1024]{1,0:T(2,128)(2,1)S(1)}) fusion(f32[2,1024,1024]{2,1,0:T(8,128)} %refs_7_.3), kind=kLoop, calls=%fused_computation.4 | loop fusion | bytes 24576 | tf_op jit(solution)/shard_map/slice | solution.py:389
  8.0 2.5 %slice_reduce_fusion.3 = (bf16[2,1024]{1,0:T(2,128)(2,1)S(1)}, bf16[2,1024]{1,0:T(2,128)(2,1)S(1)}) fusion(f32[2,1024,1024]{2,1,0:T(8,128)} %refs_8_.3), kind=kLoop, calls=%fused_computation.3 | loop fusion | bytes 24576 | tf_op jit(solution)/shard_map/slice | solution.py:389
  10.5 2.6 %collective-permute-start.1 = (bf16[2,3,1024]{2,0,1:T(2,128)(2,1)S(1)}, bf16[2,3,1024]{2,0,1:T(2,128)(2,1)S(1)}, u32[]{:S(2)}, u32[]{:S(2)}) collective-permute-start(bf16[2,3,1024]{2,0,1:T(2,128)(2,1)S(1)} %pad_maximum_fusion.4), channel_id=1, source_target_pairs={{0,2},{2,4},{4,6},{6,8},{8,10},{10,12},{12,14},{14,16},{16,18},{18... | collective-permute-start | bytes 36872 | tf_op jit(solution)/shard_map/ppermute | solution.py:391
  13.2 3.1 %reduce-precision_convert_fusion = (bf16[128,1024]{1,0:T(8,128)(2,1)S(1)}, bf16[128,1024]{1,0:T(8,128)(2,1)S(1)}, bf16[128,1024]{1,0:T(8,128)(2,1)S(1)}, f32[128,1024]{1,0:T(8,128)}, bf16[128,1024]{1,0:T(8,128)(2,1)S(1)}) fusion(s32[128]{0:T(128)S(1)} %iota_shift-right-logical_fusion, s32[128]{0:T(128)S(1)} %broadcast_add_fusion, ...), kind=kLoop, calls=%fused_computation.9 | loop fusion | flops 2359296 | bytes 1579264 | tf_op jit(solution)/shard_map/convert_element_type | solution.py:24
  16.3 9.1 %surface_modes.1 = f32[128,1024]{1,0:T(8,128)} custom-call(f32[2,1024,1024]{2,1,0:T(8,128)} %density_ref.1, f32[128,1024]{1,0:T(8,128)} %get-tuple-element.61.refs_1_), custom_call_target="tpu_custom_call" | custom-call | flops 1610612736 | bytes 8388608 | tf_op jit(solution)/shard_map/surface_modes/pallas_call | solution.py:44
  25.4 5.9 %all-to-all-start = ((f32[16,8,1024]{2,1,0:T(8,128)}), f32[16,8,1024]{2,1,0:T(8,128)S(1)}, u32[]{:S(2)}, u32[]{:S(2)}) async-start(f32[16,8,1024]{2,1,0:T(8,128)} %bitcast.15), calls=%async_computation | async-start | bytes 1048576 | tf_op jit(solution)/shard_map/all_to_all | solution.py:420
  31.4 5.6 %collective-permute-start.2 = (bf16[2,3,1024]{2,0,1:T(2,128)(2,1)S(1)}, bf16[2,3,1024]{2,0,1:T(2,128)(2,1)S(1)}, u32[]{:S(2)}, u32[]{:S(2)}) collective-permute-start(bf16[2,3,1024]{2,0,1:T(2,128)(2,1)S(1)} %pad_maximum_fusion.5), channel_id=1, source_target_pairs={{2,0},{4,2},{6,4},{8,6},{10,8},{12,10},{14,12},{16,14},{18,16},{20... | collective-permute-start | bytes 36872 | tf_op jit(solution)/shard_map/ppermute | solution.py:392
  37.0 0.1 multiply_divide_fusion
  37.3 0.1 stack.63
  37.4 1.0 copy.37.refs_12_.refs_13_
  38.4 0.0 collective-permute-done.1
  38.4 2.1 collective-permute-done.2
  40.5 1.3 copy.36
  41.9 0.0 collective-permute-done
  41.9 0.7 convert_select_fusion
  42.6 61.8 %flux_layer.2 = (f32[2,1024,1024]{2,1,0:T(8,128)}, f32[2,1024,1024]{2,1,0:T(8,128)}, f32[2,1024,1024]{2,1,0:T(8,128)}) custom-call(f32[2,1024,1024]{2,1,0:T(8,128)} %density_ref.1, f32[2,1024,1024]{2,1,0:T(8,128)} %refs_7_.3, f32[2,1024,1024]{2,1,0:T(8,128)} %refs_8_.3, f32[2,1024,1024]{2,1,0:T(8,128)} %density_ref.1, f32[2,1024,1024]{2,1,0:T(8,128)} %refs_7_.3, ...), custom_call_target="tpu_custom_call" | custom-call | flops 104857600 | bytes 25165824 | tf_op jit(solution)/shard_map/flux_layer/pallas_call | solution.py:297
  104.4 2.0 all_gather.3.refs_0_
  106.4 16.1 %responses.1 = f32[2,8,1024]{2,1,0:T(8,128)} custom-call(bf16[8,2048]{1,0:T(8,128)(2,1)} %all_gather.3.refs_0_, bf16[4,1024,2048]{2,1,0:T(8,128)(2,1)} %refs_1_.4, bf16[4,1024,2048]{2,1,0:T(8,128)(2,1)} %refs_2_.4), custom_call_target="tpu_custom_call" | custom-call | flops 268435456 | bytes 33554432 | tf_op jit(solution)/shard_map/responses/pallas_call | solution.py:79
  122.5 1.9 broadcast_in_dim.4
  124.5 9.6 %all-to-all-start.1 = ((f32[16,2,8,1024]{3,2,1,0:T(8,128)}), f32[16,2,8,1024]{3,2,1,0:T(8,128)S(1)}, u32[]{:S(2)}, u32[]{:S(2)}) async-start(f32[16,2,8,1024]{3,2,1,0:T(8,128)} %broadcast_in_dim.4), calls=%async_computation.1 | async-start | bytes 2097152 | tf_op jit(solution)/shard_map/all_to_all | solution.py:429
  134.2 0.1 fusion.9
  134.2 1.0 copy.41.inverse_ref
  135.3 1.4 pad_maximum_fusion
  136.6 1.0 copy.39.refs_12_.refs_13_
  137.6 61.8 %flux_layer.3 = (f32[2,1024,1024]{2,1,0:T(8,128)}, f32[2,1024,1024]{2,1,0:T(8,128)}, f32[2,1024,1024]{2,1,0:T(8,128)}) custom-call(f32[2,1024,1024]{2,1,0:T(8,128)} %density_ref.1, f32[2,1024,1024]{2,1,0:T(8,128)} %refs_7_.3, f32[2,1024,1024]{2,1,0:T(8,128)} %refs_8_.3, ...), custom_call_target="tpu_custom_call", output_to_operand_aliasing={{0}: (14, {}), {1}: (15, {}), {2}: (16, {})} | custom-call | flops 104857600 | bytes 25165824 | tf_op jit(solution)/shard_map/flux_layer/pallas_call | solution.py:297
  199.5 1.1 slice_bitcast_fusion
  200.5 19.2 %add_gravity.1 = (f32[2,1024,1024]{2,1,0:T(8,128)}, f32[2,1024,1024]{2,1,0:T(8,128)}, f32[1024,1024]{1,0:T(8,128)}) custom-call(f32[128,1024]{1,0:T(8,128)} %get-tuple-element.47.pot_ref, f32[128,1024]{1,0:T(8,128)} %get-tuple-element.46.force_ref, f32[1024,1]{1,0:T(8,128)} %copy.41.inverse_ref, ...), custom_call_target="tpu_custom_call", output_to_operand_aliasing={{0}: (6, {}), {1}: (7, {})} | custom-call | flops 2415919104 | bytes 46137344 | tf_op jit(solution)/shard_map/add_gravity/pallas_call | solution.py:348
  (28 shorter events, 0.2 us)
Async XLA Ops:
  2.6 39.3 %collective-permute-start = (bf16[2,3,1024]{2,1,0:T(4,128)(2,1)S(1)}, bf16[2,3,1024]{2,1,0:T(4,128)(2,1)S(1)}, u32[]{:S(2)}, u32[]{:S(2)}) collective-permute-start(bf16[2,3,1024]{2,1,0:T(4,128)(2,1)S(1)} %fusion.7), channel_id=1, source_target_pairs={{0,1},{1,0},{2,3},{3,2},{4,5},{5,4},{6,7},{7,6},{8,9},{9,8},{10,11... | collective-permute-start | bytes 36872 | tf_op jit(solution)/shard_map/ppermute | solution.py:373
  10.5 27.8 %collective-permute-start.1 = (bf16[2,3,1024]{2,0,1:T(2,128)(2,1)S(1)}, bf16[2,3,1024]{2,0,1:T(2,128)(2,1)S(1)}, u32[]{:S(2)}, u32[]{:S(2)}) collective-permute-start(bf16[2,3,1024]{2,0,1:T(2,128)(2,1)S(1)} %pad_maximum_fusion.4), channel_id=1, source_target_pairs={{0,2},{2,4},{4,6},{6,8},{8,10},{10,12},{12,14},{14,16},{16,18},{18... | collective-permute-start | bytes 36872 | tf_op jit(solution)/shard_map/ppermute | solution.py:391
  25.4 79.0 %all-to-all-start = ((f32[16,8,1024]{2,1,0:T(8,128)}), f32[16,8,1024]{2,1,0:T(8,128)S(1)}, u32[]{:S(2)}, u32[]{:S(2)}) async-start(f32[16,8,1024]{2,1,0:T(8,128)} %bitcast.15), calls=%async_computation | async-start | bytes 1048576 | tf_op jit(solution)/shard_map/all_to_all | solution.py:420
  31.4 9.1 %collective-permute-start.2 = (bf16[2,3,1024]{2,0,1:T(2,128)(2,1)S(1)}, bf16[2,3,1024]{2,0,1:T(2,128)(2,1)S(1)}, u32[]{:S(2)}, u32[]{:S(2)}) collective-permute-start(bf16[2,3,1024]{2,0,1:T(2,128)(2,1)S(1)} %pad_maximum_fusion.5), channel_id=1, source_target_pairs={{2,0},{4,2},{6,4},{8,6},{10,8},{12,10},{14,12},{16,14},{18,16},{20... | collective-permute-start | bytes 36872 | tf_op jit(solution)/shard_map/ppermute | solution.py:392
  124.5 75.0 %all-to-all-start.1 = ((f32[16,2,8,1024]{3,2,1,0:T(8,128)}), f32[16,2,8,1024]{3,2,1,0:T(8,128)S(1)}, u32[]{:S(2)}, u32[]{:S(2)}) async-start(f32[16,2,8,1024]{3,2,1,0:T(8,128)} %broadcast_in_dim.4), calls=%async_computation.1 | async-start | bytes 2097152 | tf_op jit(solution)/shard_map/all_to_all | solution.py:429

commit v3 on v1

--- a/solution.py
+++ b/solution.py
@@ -10,13 +10,18 @@
 aspect_sq = 0.0025
 LANES = 128
 SUB = 8
-MIB = 1 << 20
+VMEM_BYTES = 60 << 20
 
 
 def split_bf16(x):
     high = x.astype(jnp.bfloat16)
     low = (x - high.astype(jnp.float32)).astype(jnp.bfloat16)
     return high, low
+
+
+def split_outside(x):
+    high = lax.reduce_precision(x, 8, 7)
+    return high.astype(jnp.bfloat16), (x - high).astype(jnp.bfloat16)
 
 
 def modes_kernel(scale, density_ref, basis_ref, out_ref):
@@ -45,7 +50,7 @@
         ],
         out_specs=pl.BlockSpec((cols, block), lambda i: (0, i)),
         out_shape=jax.ShapeDtypeStruct((cols, rows), jnp.float32),
-        compiler_params=pltpu.CompilerParams(vmem_limit_bytes=16 * MIB),
+        compiler_params=pltpu.CompilerParams(vmem_limit_bytes=VMEM_BYTES),
         cost_estimate=pl.CostEstimate(
             flops=12 * rows * cells * cols, bytes_accessed=4 * density.size, transcendentals=0
         ),
@@ -55,15 +60,16 @@
 
 def response_kernel(mode_count, pairs_ref, pot_ref, force_ref, out_ref):
     pairs = pairs_ref[...]
-    row = lax.broadcasted_iota(jnp.int32, out_ref.shape[1:], 0) // 2
+    cols = pairs.shape[0]
+    mode_of = lax.broadcasted_iota(jnp.int32, (pot_ref.shape[1], cols), 1) // 2
     for place, ref in enumerate((pot_ref, force_ref)):
-        total = jnp.zeros(out_ref.shape[1:], jnp.float32)
+        total = jnp.zeros(mode_of.shape, jnp.float32)
         for mode in range(mode_count):
             part = lax.dot_general(
-                pairs, ref[mode], (((1,), (1,)), ((), ())), preferred_element_type=jnp.float32
+                ref[mode], pairs, (((1,), (1,)), ((), ())), preferred_element_type=jnp.float32
             )
-            total = jnp.where(row == mode, part, total)
-        out_ref[place] = total
+            total = jnp.where(mode_of == mode, part, total)
+        out_ref[place] = total.T
 
 
 def responses(pairs, potential_kernel, force_kernel):
@@ -77,7 +83,7 @@
         in_specs=[pl.BlockSpec((cols, count), lambda i: (0, 0)), kernel_spec, kernel_spec],
         out_specs=pl.BlockSpec((2, cols, block), lambda i: (0, 0, i)),
         out_shape=jax.ShapeDtypeStruct((2, cols, rows), jnp.float32),
-        compiler_params=pltpu.CompilerParams(vmem_limit_bytes=16 * MIB),
+        compiler_params=pltpu.CompilerParams(vmem_limit_bytes=VMEM_BYTES),
         cost_estimate=pl.CostEstimate(
             flops=4 * rows * count * cols * mode_count,
             bytes_accessed=4 * potential_kernel.size,
@@ -119,17 +125,17 @@
     return guess * (2.0 - x * guess)
 
 
-def flux_kernel(block_count, refs):
+def flux_kernel(first_block, block_count, unroll, refs):
     fields = refs[0:3]
     before = refs[3:6]
     after = refs[6:9]
     rim_in, rim_out, ghost_ref, coef_ref, coef_next = refs[9:14]
-    outs = refs[-5:-2]
-    above, lagged = refs[-2:]
-    rows, cells = fields[0].shape
+    outs = refs[-6:-3]
+    above, lagged, pending = refs[-3:]
+    layers, rows, cells = fields[0].shape
     columns = cells // LANES
     strips = rows // SUB
-    index = pl.program_id(0)
+    index = pl.program_id(0) + first_block
     lane = lax.broadcasted_iota(jnp.int32, (SUB, LANES), 1)
     sub = lax.broadcasted_iota(jnp.int32, (SUB, LANES), 0)
 
@@ -138,6 +144,9 @@
 
     def at(col):
         return pl.ds(col * LANES, LANES)
+
+    def rows_at(place):
+        return pl.ds(pl.multiple_of(place * SUB, SUB), SUB)
 
     def radial_state(state):
         density, mom_r, mom_phi = state
@@ -145,15 +154,7 @@
         vel = mom_r * inv
         return inv, (density, mom_r, mom_phi, jnp.abs(vel), mom_r * vel, mom_phi * vel)
 
-    def keep_above(col, values):
-        for slot, value in enumerate(values):
-            above[slot, :, at(col)] = pltpu.roll(value, 1, 0)
-
-    def radial_flux(col, values, root, sound):
-        lower = [
-            jnp.where(sub == 0, above[slot, :, at(col)], pltpu.roll(value, 1, 0))
-            for slot, value in enumerate(values)
-        ]
+    def radial_flux(values, lower, root, sound):
         speed = jnp.maximum(values[3], lower[3]) + root
         return (
             (values[1] + lower[1]) - speed * (values[0] - lower[0]),
@@ -162,11 +163,6 @@
             (values[5] + lower[5]) - speed * (values[2] - lower[2]),
         )
 
-    def finish(rows_before, col, flux, out_coef):
-        for comp in range(3):
-            up = jnp.where(sub == SUB - 1, pltpu.roll(flux[comp], SUB - 1, 0), lagged[comp, :, at(col)])
-            outs[comp][rows_before, at(col)] -= out_coef * up
-
     def azimuth_flux(values, lower, root):
         speed = jnp.maximum(values[3], lower[3]) + root
         return (
@@ -175,23 +171,38 @@
             (values[5] + lower[5]) - speed * (values[2] - lower[2]),
         )
 
-    for col in range(columns):
+    def finish(slot, rows_before, layer, col, turned_flux, out_coef):
+        for comp in range(3):
+            up = jnp.where(sub == SUB - 1, turned_flux[comp], lagged[slot, layer, comp, :, at(col)])
+            outs[comp][layer, rows_before, at(col)] = (
+                pending[slot, layer, comp, :, at(col)] - out_coef * up
+            )
+
+    def edge_state(layer, col, edge, rim, near, row):
         state = []
         for comp in range(3):
-            row = jnp.where(index == 0, rim_in[comp : comp + 1, at(col)], before[comp][SUB - 1 :, at(col)])
-            state.append(jnp.broadcast_to(row, (SUB, LANES)))
-        keep_above(col, radial_state(state)[1])
-
-    def strip(place, carry):
-        here = pl.ds(pl.multiple_of(place * SUB, SUB), SUB)
-        rows_before = pl.ds(pl.multiple_of(jnp.maximum(place - 1, 0) * SUB, SUB), SUB)
+            value = jnp.where(
+                edge, rim[layer, comp : comp + 1, at(col)], near[comp][layer, row : row + 1, at(col)]
+            )
+            state.append(jnp.broadcast_to(value, (SUB, LANES)))
+        return radial_state(state)[1]
+
+    for layer in range(layers):
+        for col in range(columns):
+            values = edge_state(layer, col, index == 0, rim_in, before, SUB - 1)
+            for k, value in enumerate(values):
+                above[0, layer, k, :, at(col)] = value
+
+    def strip(place, slot):
+        later = (slot + 1) % unroll
+        here = rows_at(place)
+        rows_before = rows_at(jnp.maximum(place - 1, 0))
         coef = coef_ref[here, :]
         root_face, sound_face, in_coef, root_mid, sound_mid, az, spin, pull = (
             wide(coef[:, k : k + 1])
             for k in (ROOT_FACE, SOUND_FACE, IN, ROOT_MID, SOUND_MID, AZ, SPIN, PULL)
         )
         out_before = wide(coef_ref[rows_before, OUT : OUT + 1])
-        ghost = ghost_ref[here, :]
 
         def azimuth_values(state, inv, cross):
             density, mom_r, mom_phi = state
@@ -200,86 +211,95 @@
                 density, mom_r, mom_phi, jnp.abs(vel), cross, mom_phi * vel + sound_mid * density
             )
 
-        def ghost_values(side):
+        def ghost_values(layer, side):
+            ghost = ghost_ref[layer, here, :]
             state = [wide(ghost[:, 3 * side + k : 3 * side + k + 1]) for k in range(3)]
             inv = inverse(state[0])
             return azimuth_values(state, inv, state[1] * state[2] * inv)
 
-        turned = ghost_values(0)
-        held = None
-        held_flux = None
-
-        def settle(col, held, held_flux, flux):
+        turned = [ghost_values(layer, 0) for layer in range(layers)]
+        held = [None] * layers
+        turned_held = [None] * layers
+
+        def settle(layer, col, turned_flux):
             for comp in range(3):
-                up = jnp.where(
-                    lane == LANES - 1,
-                    pltpu.roll(flux[comp], LANES - 1, 1),
-                    pltpu.roll(held_flux[comp], LANES - 1, 1),
+                up = jnp.where(lane == LANES - 1, turned_flux[comp], turned_held[layer][comp])
+                pending[later, layer, comp, :, at(col)] = held[layer][comp] - az * up
+
+        for col in range(columns):
+            for layer in range(layers):
+                state = [ref[layer, here, at(col)] for ref in fields]
+                inv, values = radial_state(state)
+                rolled = [pltpu.roll(value, 1, 0) for value in values]
+                lower = [
+                    jnp.where(sub == 0, above[slot, layer, k, :, at(col)], value)
+                    for k, value in enumerate(rolled)
+                ]
+                for k, value in enumerate(rolled):
+                    above[later, layer, k, :, at(col)] = value
+                flux_r = radial_flux(values, lower, root_face, sound_face)
+                turned_r = [pltpu.roll(value, SUB - 1, 0) for value in flux_r]
+                finish(slot, rows_before, layer, col, turned_r, out_before)
+                for comp in range(3):
+                    lagged[later, layer, comp, :, at(col)] = turned_r[comp]
+                values = azimuth_values(state, inv, values[5])
+                rolled = [pltpu.roll(value, 1, 1) for value in values]
+                lower = [jnp.where(lane == 0, a, b) for a, b in zip(turned[layer], rolled)]
+                turned[layer] = rolled
+                flux = azimuth_flux(values, lower, root_mid)
+                turned_flux = [pltpu.roll(value, LANES - 1, 1) for value in flux]
+                if col > 0:
+                    settle(layer, col - 1, turned_flux)
+                held[layer] = (
+                    state[0] + in_coef * flux_r[0] + az * flux[0],
+                    state[1] + in_coef * flux_r[1] + az * flux[1] + (spin * values[5] - pull * state[0]),
+                    state[2] + in_coef * flux_r[2] + az * flux[2] - spin * values[4],
                 )
-                outs[comp][here, at(col)] = held[comp] - az * (up - held_flux[comp])
-
-        for col in range(columns):
-            state = [ref[here, at(col)] for ref in fields]
-            inv, values = radial_state(state)
-            flux_r = radial_flux(col, values, root_face, sound_face)
-            finish(rows_before, col, flux_r, out_before)
-            keep_above(col, values)
-            for comp in range(3):
-                lagged[comp, :, at(col)] = pltpu.roll(flux_r[comp], SUB - 1, 0)
-            values = azimuth_values(state, inv, values[5])
-            rolled = [pltpu.roll(value, 1, 1) for value in values]
-            lower = [jnp.where(lane == 0, a, b) for a, b in zip(turned, rolled)]
-            turned = rolled
-            flux = azimuth_flux(values, lower, root_mid)
-            if col > 0:
-                settle(col - 1, held, held_flux, flux)
-            held = (
-                state[0] + in_coef * flux_r[0],
-                state[1] + in_coef * flux_r[1] + (spin * values[5] - pull * state[0]),
-                state[2] + in_coef * flux_r[2] - spin * values[4],
-            )
-            held_flux = flux
-        values = ghost_values(1)
-        lower = [wide(a[:, 0:1]) for a in turned]
-        settle(columns - 1, held, held_flux, azimuth_flux(values, lower, root_mid))
+                turned_held[layer] = turned_flux
+        for layer in range(layers):
+            flux = azimuth_flux(ghost_values(layer, 1), turned[layer], root_mid)
+            settle(layer, columns - 1, [pltpu.roll(value, LANES - 1, 1) for value in flux])
+
+    def strip_group(group, carry):
+        for slot in range(unroll):
+            strip(group * unroll + slot, slot)
         return carry
 
-    lax.fori_loop(0, strips, strip, 0)
+    lax.fori_loop(0, strips // unroll, strip_group, 0)
 
     last = pl.ds((strips - 1) * SUB, SUB)
     root_face = wide(coef_next[:, ROOT_FACE : ROOT_FACE + 1])
     sound_face = wide(coef_next[:, SOUND_FACE : SOUND_FACE + 1])
     out_coef = wide(coef_ref[last, OUT : OUT + 1])
-    for col in range(columns):
-        state = []
-        for comp in range(3):
-            row = jnp.where(
-                index == block_count - 1,
-                rim_out[comp : comp + 1, at(col)],
-                after[comp][0:1, at(col)],
-            )
-            state.append(jnp.broadcast_to(row, (SUB, LANES)))
-        finish(last, col, radial_flux(col, radial_state(state)[1], root_face, sound_face), out_coef)
-
-
-def flux_layer(layer, fields, rims, ghosts, coefs, so_far):
+    for layer in range(layers):
+        for col in range(columns):
+            values = edge_state(layer, col, index == block_count - 1, rim_out, after, 0)
+            lower = [above[0, layer, k, :, at(col)] for k in range(6)]
+            flux_r = radial_flux(values, lower, root_face, sound_face)
+            finish(0, last, layer, col, [pltpu.roll(value, SUB - 1, 0) for value in flux_r], out_coef)
+
+
+def flux_rows(first_block, count, fields, rims, ghosts, coefs, so_far):
     layers, rows, cells = fields[0].shape
-    block = min(rows, 64)
-    count = rows // block
+    block = flux_block(rows)
     per = block // SUB
-    main = pl.BlockSpec((None, block, cells), lambda i: (layer, i, 0))
-    before = pl.BlockSpec((None, SUB, cells), lambda i: (layer, jnp.maximum(i * per - 1, 0), 0))
+    unroll = min(2, per)
+    main = pl.BlockSpec((layers, block, cells), lambda i: (0, i + first_block, 0))
+    before = pl.BlockSpec(
+        (layers, SUB, cells), lambda i: (0, jnp.maximum((i + first_block) * per - 1, 0), 0)
+    )
     after = pl.BlockSpec(
-        (None, SUB, cells), lambda i: (layer, jnp.minimum((i + 1) * per, rows // SUB - 1), 0)
-    )
-    rim = pl.BlockSpec((None, 3, cells), lambda i: (layer, 0, 0))
+        (layers, SUB, cells),
+        lambda i: (0, jnp.minimum((i + first_block + 1) * per, rows // SUB - 1), 0),
+    )
+    rim = pl.BlockSpec((layers, 3, cells), lambda i: (0, 0, 0))
     operands = [*fields, *fields, *fields, *rims, ghosts, coefs, coefs]
     specs = [main] * 3 + [before] * 3 + [after] * 3 + [
         rim,
         rim,
-        pl.BlockSpec((None, block, ghosts.shape[2]), lambda i: (layer, i, 0)),
-        pl.BlockSpec((block, COEFS), lambda i: (i, 0)),
-        pl.BlockSpec((SUB, COEFS), lambda i: ((i + 1) * per, 0)),
+        pl.BlockSpec((layers, block, ghosts.shape[2]), lambda i: (0, i + first_block, 0)),
+        pl.BlockSpec((block, COEFS), lambda i: (i + first_block, 0)),
+        pl.BlockSpec((SUB, COEFS), lambda i: ((i + first_block + 1) * per, 0)),
     ]
     aliases = {}
     if so_far is not None:
@@ -288,22 +308,29 @@
             operands.append(array)
             specs.append(pl.BlockSpec(memory_space=pl.ANY))
     return pl.pallas_call(
-        lambda *refs: flux_kernel(count, refs),
+        lambda *refs: flux_kernel(first_block, rows // block, unroll, refs),
         grid=(count,),
         in_specs=specs,
         out_specs=[main] * 3,
         out_shape=[jax.ShapeDtypeStruct(f.shape, f.dtype) for f in fields],
         scratch_shapes=[
-            pltpu.VMEM((6, SUB, cells), jnp.float32),
-            pltpu.VMEM((3, SUB, cells), jnp.float32),
+            pltpu.VMEM((unroll, layers, 6, SUB, cells), jnp.float32),
+            pltpu.VMEM((unroll, layers, 3, SUB, cells), jnp.float32),
+            pltpu.VMEM((unroll, layers, 3, SUB, cells), jnp.float32),
         ],
         input_output_aliases=aliases,
-        compiler_params=pltpu.CompilerParams(vmem_limit_bytes=16 * MIB),
+        compiler_params=pltpu.CompilerParams(vmem_limit_bytes=VMEM_BYTES),
         cost_estimate=pl.CostEstimate(
-            flops=100 * rows * cells, bytes_accessed=24 * rows * cells, transcendentals=rows * cells
+            flops=100 * layers * count * block * cells,
+            bytes_accessed=24 * layers * count * block * cells,
+            transcendentals=layers * count * block * cells,
         ),
-        name="flux_layer",
+        name="flux_rows",
     )(*operands)
+
+
+def flux_block(rows):
+    return min(rows, 64)
 
 
 def gravity_kernel(
@@ -347,7 +374,7 @@
         out_specs=[field, field, pl.BlockSpec((block, cells), lambda i: (i, 0))],
         out_shape=[grid_shape, grid_shape, jax.ShapeDtypeStruct((rows, cells), jnp.float32)],
         input_output_aliases={6: 0, 7: 1},
-        compiler_params=pltpu.CompilerParams(vmem_limit_bytes=24 * MIB),
+        compiler_params=pltpu.CompilerParams(vmem_limit_bytes=VMEM_BYTES),
         cost_estimate=pl.CostEstimate(
             flops=18 * rows * cells * cols, bytes_accessed=44 * rows * cells, transcendentals=0
         ),
@@ -378,12 +405,10 @@
 def exchange_edges(fields, az_count):
     right = [(i, (i + 1) % az_count) for i in range(az_count)]
     left = [(b, a) for a, b in right]
-    low = lax.ppermute(
-        jnp.stack([f[:, :, -1] for f in fields], axis=1).astype(jnp.bfloat16), "az", right
-    )
-    high = lax.ppermute(
-        jnp.stack([f[:, :, 0] for f in fields], axis=1).astype(jnp.bfloat16), "az", left
-    )
+    last = lax.optimization_barrier(jnp.stack([f[:, :, -1] for f in fields], axis=1))
+    first = lax.optimization_barrier(jnp.stack([f[:, :, 0] for f in fields], axis=1))
+    low = lax.ppermute(last.astype(jnp.bfloat16), "az", right)
+    high = lax.ppermute(first.astype(jnp.bfloat16), "az", left)
     both = jnp.concatenate([low, high], axis=1).astype(fields[0].dtype)
     return jnp.swapaxes(both, 1, 2)
 
@@ -414,19 +439,25 @@
     pieces = lax.all_to_all(
         partial.reshape(az_count, pair_count, rows), "az", split_axis=0, concat_axis=0, tiled=True
     )
-    results = flux_layer(0, fields, rims, ghosts, coefs, None)
+    blocks = rows // flux_block(rows)
+    early = blocks // 2
+    results = flux_rows(0, early, fields, rims, ghosts, coefs, None) if early else None
+    if early:
+        pieces, results = lax.optimization_barrier((pieces, results))
 
     own = jnp.sum(pieces, axis=0).astype(jnp.bfloat16)
     pairs = lax.all_gather(own, "rad", axis=1, tiled=True)
     parts = responses(pairs, potential_kernel, force_kernel)
-    every = lax.all_gather(parts, "az", axis=0)
-    for layer in range(1, layers):
-        results = flux_layer(layer, fields, rims, ghosts, coefs, results)
+    every = lax.all_to_all(
+        jnp.broadcast_to(parts[None], (az_count, *parts.shape)), "az", split_axis=0, concat_axis=0, tiled=True
+    )
+    coefs, parts = lax.optimization_barrier((coefs, parts))
+    results = flux_rows(early, blocks - early, fields, rims, ghosts, coefs, results)
     pot = every[:, 0].reshape(cols, rows)
     force = every[:, 1].reshape(cols, rows)
 
     def table_of(x):
-        high, low = split_bf16(x)
+        high, low = split_outside(x)
         return jnp.concatenate([high, high, low], axis=0)
 
     face = jnp.exp((rad_index * rows + jnp.arange(rows + 1)).astype(jnp.float32) * step)

time: 206 us -> 231 us (1.12)
  Pallas kernels: 113 us -> 179 us
  local copies, waits for them, and re-layouts: 37.3 us -> 16.8 us
  between operations: 14.3 us -> 0.89 us
  other arithmetic: 16.9 us -> 5.58 us
  starting transfers between devices: 14.2 us -> 24.2 us
  waiting for transfers between devices: 7.04 us -> 2.14 us
    pallas_call x2, Pallas kernels: 78.1 us -> 134 us  [flux_rows(): pl.pallas_call(lambda *refs: flux_kernel(first_block, rows // block, unro...]
    unnamed x16 -> x0, local copies, waits for them, and re-layouts: 29.5 us -> none
    another operation x5 -> x2, other arithmetic: 14.2 us -> 0.05 us  [the longest x1 0.02 us: exchange_edges(): jnp.stack([f[:, :, -1] for f in fields], axis=1)]
    all_to_all x0 -> x1, starting transfers between devices: none -> 9.65 us  [local(): lax.all_to_all(jnp.broadcast_to(parts[None], (az_count, *parts.shape)), '...]
    all_to_all x1, waiting for transfers between devices: 7.02 us -> 0.01 us  [local(): lax.all_to_all(partial.reshape(az_count, pair_count, rows), 'az', split_a...]
    slice x3, local copies, waits for them, and re-layouts: 2.9 us -> 7.41 us  [exchange_edges(): f[:, :, -1]]
    pallas_call x1, Pallas kernels: 12.4 us -> 16.3 us  [responses(): pl.pallas_call(lambda *refs: response_kernel(mode_count, *refs), grid=(ro...]
    pallas_call x1, Pallas kernels: 6.27 us -> 9.14 us  [surface_modes(): pl.pallas_call(lambda *refs: modes_kernel(scale, *refs), grid=(rows // bl...]
  transfers between devices with their start and end apart: 5 -> 5, of which waited for: 1 -> 1; matrix products, arithmetic and copies ran while one was open for 10% -> 8% of each run, Pallas kernels for 44% -> 62%
where the time goes in v3:
time: 231 us; the launch traced here: 230 us
  Pallas kernels  179 us (77%)
  starting transfers between devices  24.2 us (10%)
  local copies, waits for them, and re-layouts  16.8 us (7%)
  other arithmetic  5.58 us (2%)
    pallas_call x2, Pallas kernels, flux_rows(): pl.pallas_call(lambda *refs: flux_kernel(first_block, rows // block, unro...  134 us
    pallas_call x1, Pallas kernels, add_gravity(): pl.pallas_call(gravity_kernel, grid=(rows // block,), in_specs=[modes_spe...  19.2 us
    pallas_call x1, Pallas kernels, responses(): pl.pallas_call(lambda *refs: response_kernel(mode_count, *refs), grid=(ro...  16.3 us
    all_to_all x1, starting transfers between devices, local(): lax.all_to_all(jnp.broadcast_to(parts[None], (az_count, *parts.shape)), '...  9.65 us
    pallas_call x1, Pallas kernels, surface_modes(): pl.pallas_call(lambda *refs: modes_kernel(scale, *refs), grid=(rows // bl...  9.14 us
    slice x3, local copies, waits for them, and re-layouts, exchange_edges(): f[:, :, -1]  7.41 us
    all_to_all x1, starting transfers between devices, local(): lax.all_to_all(partial.reshape(az_count, pair_count, rows), 'az', split_a...  5.94 us
    ppermute x1, starting transfers between devices, exchange_edges(): high = lax.ppermute(first.astype(jnp.bfloat16), 'az', left)  5.58 us
  transfers between devices with their start and end apart: 5, of which 1 were waited for; matrix products, arithmetic and copies ran while one was open for 8% of the time, Pallas kernels for 62%

profile of v3, /device:TPU:0, one launch (start us, length us, event | category | flops | bytes accessed | tf_op | source)
XLA Modules:
  0.0 230.2 jit_solution(2967260037326914418)
XLA Ops:
  0.6 0.9 fusion.14
  1.5 1.0 fusion.15
  2.5 0.1 fusion.7
  2.6 0.5 collective-permute-start
  3.1 2.5 %slice_reduce_fusion.5 = (bf16[2,1024]{1,0:T(2,128)(2,1)S(1)}, bf16[2,1024]{1,0:T(2,128)(2,1)S(1)}) fusion(f32[2,1024,1024]{2,1,0:T(8,128)} %density_ref.1), kind=kLoop, calls=%fused_computation.5 | loop fusion | bytes 24576 | tf_op jit(solution)/shard_map/slice | solution.py:408
  5.6 2.5 %slice_reduce_fusion.4 = (bf16[2,1024]{1,0:T(2,128)(2,1)S(1)}, bf16[2,1024]{1,0:T(2,128)(2,1)S(1)}) fusion(f32[2,1024,1024]{2,1,0:T(8,128)} %refs_7_.3), kind=kLoop, calls=%fused_computation.4 | loop fusion | bytes 24576 | tf_op jit(solution)/shard_map/slice | solution.py:408
  8.0 2.5 %slice_reduce_fusion.3 = (bf16[2,1024]{1,0:T(2,128)(2,1)S(1)}, bf16[2,1024]{1,0:T(2,128)(2,1)S(1)}) fusion(f32[2,1024,1024]{2,1,0:T(8,128)} %refs_8_.3), kind=kLoop, calls=%fused_computation.3 | loop fusion | bytes 24576 | tf_op jit(solution)/shard_map/slice | solution.py:408
  10.5 2.6 %collective-permute-start.1 = (bf16[2,3,1024]{2,0,1:T(2,128)(2,1)S(1)}, bf16[2,3,1024]{2,0,1:T(2,128)(2,1)S(1)}, u32[]{:S(2)}, u32[]{:S(2)}) collective-permute-start(bf16[2,3,1024]{2,0,1:T(2,128)(2,1)S(1)} %pad_maximum_fusion.4), channel_id=1, source_target_pairs={{0,2},{2,4},{4,6},{6,8},{8,10},{10,12},{12,14},{14,16},{16,18},{18... | collective-permute-start | bytes 36872 | tf_op jit(solution)/shard_map/ppermute | solution.py:410
  13.2 3.1 %reduce-precision_convert_fusion = (bf16[128,1024]{1,0:T(8,128)(2,1)S(1)}, bf16[128,1024]{1,0:T(8,128)(2,1)S(1)}, bf16[128,1024]{1,0:T(8,128)(2,1)S(1)}, f32[128,1024]{1,0:T(8,128)}, bf16[128,1024]{1,0:T(8,128)(2,1)S(1)}) fusion(s32[128]{0:T(128)S(1)} %iota_shift-right-logical_fusion, s32[128]{0:T(128)S(1)} %broadcast_add_fusion, ...), kind=kLoop, calls=%fused_computation.9 | loop fusion | flops 2359296 | bytes 1579264 | tf_op jit(solution)/shard_map/convert_element_type | solution.py:24
  16.3 9.1 %surface_modes.1 = f32[128,1024]{1,0:T(8,128)} custom-call(f32[2,1024,1024]{2,1,0:T(8,128)} %density_ref.1, f32[128,1024]{1,0:T(8,128)} %get-tuple-element.61.refs_1_), custom_call_target="tpu_custom_call" | custom-call | flops 1610612736 | bytes 8388608 | tf_op jit(solution)/shard_map/surface_modes/pallas_call | solution.py:44
  25.4 5.9 %all-to-all-start = ((f32[16,8,1024]{2,1,0:T(8,128)}), f32[16,8,1024]{2,1,0:T(8,128)S(1)}, u32[]{:S(2)}, u32[]{:S(2)}) async-start(f32[16,8,1024]{2,1,0:T(8,128)} %bitcast.15), calls=%async_computation | async-start | bytes 1048576 | tf_op jit(solution)/shard_map/all_to_all | solution.py:439
  31.4 5.6 %collective-permute-start.2 = (bf16[2,3,1024]{2,0,1:T(2,128)(2,1)S(1)}, bf16[2,3,1024]{2,0,1:T(2,128)(2,1)S(1)}, u32[]{:S(2)}, u32[]{:S(2)}) collective-permute-start(bf16[2,3,1024]{2,0,1:T(2,128)(2,1)S(1)} %pad_maximum_fusion.5), channel_id=1, source_target_pairs={{2,0},{4,2},{6,4},{8,6},{10,8},{12,10},{14,12},{16,14},{18,16},{20... | collective-permute-start | bytes 36872 | tf_op jit(solution)/shard_map/ppermute | solution.py:411
  37.0 0.1 multiply_divide_fusion
  37.3 0.1 stack.63
  37.4 1.0 copy.37.refs_12_.refs_13_
  38.4 0.0 collective-permute-done.1
  38.4 2.1 collective-permute-done.2
  40.5 1.3 copy.36
  41.9 0.0 collective-permute-done
  41.9 0.7 convert_select_fusion
  42.6 67.0 %flux_rows.2 = (f32[2,1024,1024]{2,1,0:T(8,128)}, f32[2,1024,1024]{2,1,0:T(8,128)}, f32[2,1024,1024]{2,1,0:T(8,128)}) custom-call(f32[2,1024,1024]{2,1,0:T(8,128)} %density_ref.1, f32[2,1024,1024]{2,1,0:T(8,128)} %refs_7_.3, f32[2,1024,1024]{2,1,0:T(8,128)} %refs_8_.3, f32[2,1024,1024]{2,1,0:T(8,128)} %density_ref.1, f32[2,1024,1024]{2,1,0:T(8,128)} %refs_7_.3, ...), custom_call_target="tpu_custom_call" | custom-call | flops 104857600 | bytes 25165824 | tf_op jit(solution)/shard_map/flux_rows/pallas_call | solution.py:310
  109.6 2.0 all_gather.3.refs_0_
  111.5 16.3 %responses.1 = f32[2,8,1024]{2,1,0:T(8,128)} custom-call(bf16[8,2048]{1,0:T(8,128)(2,1)} %all_gather.3.refs_0_, bf16[4,1024,2048]{2,1,0:T(8,128)(2,1)} %refs_1_.4, bf16[4,1024,2048]{2,1,0:T(8,128)(2,1)} %refs_2_.4), custom_call_target="tpu_custom_call" | custom-call | flops 268435456 | bytes 33554432 | tf_op jit(solution)/shard_map/responses/pallas_call | solution.py:80
  127.9 1.9 broadcast_in_dim.4
  129.8 9.6 %all-to-all-start.1 = ((f32[16,2,8,1024]{3,2,1,0:T(8,128)}), f32[16,2,8,1024]{3,2,1,0:T(8,128)S(1)}, u32[]{:S(2)}, u32[]{:S(2)}) async-start(f32[16,2,8,1024]{3,2,1,0:T(8,128)} %broadcast_in_dim.4), calls=%async_computation.1 | async-start | bytes 2097152 | tf_op jit(solution)/shard_map/all_to_all | solution.py:451
  139.5 0.1 fusion.11
  139.6 1.0 copy.41.inverse_ref
  140.6 1.4 pad_maximum_fusion
  142.0 1.0 copy.39.refs_12_.refs_13_
  143.0 67.0 %flux_rows.3 = (f32[2,1024,1024]{2,1,0:T(8,128)}, f32[2,1024,1024]{2,1,0:T(8,128)}, f32[2,1024,1024]{2,1,0:T(8,128)}) custom-call(f32[2,1024,1024]{2,1,0:T(8,128)} %density_ref.1, f32[2,1024,1024]{2,1,0:T(8,128)} %refs_7_.3, f32[2,1024,1024]{2,1,0:T(8,128)} %refs_8_.3, ...), custom_call_target="tpu_custom_call", output_to_operand_aliasing={{0}: (14, {}), {1}: (15, {}), {2}: (16, {})} | custom-call | flops 104857600 | bytes 25165824 | tf_op jit(solution)/shard_map/flux_rows/pallas_call | solution.py:310
  210.0 1.1 slice_bitcast_fusion
  211.0 19.2 %add_gravity.1 = (f32[2,1024,1024]{2,1,0:T(8,128)}, f32[2,1024,1024]{2,1,0:T(8,128)}, f32[1024,1024]{1,0:T(8,128)}) custom-call(f32[128,1024]{1,0:T(8,128)} %get-tuple-element.47.pot_ref, f32[128,1024]{1,0:T(8,128)} %get-tuple-element.46.force_ref, f32[1024,1]{1,0:T(8,128)} %copy.41.inverse_ref, ...), custom_call_target="tpu_custom_call", output_to_operand_aliasing={{0}: (6, {}), {1}: (7, {})} | custom-call | flops 2415919104 | bytes 46137344 | tf_op jit(solution)/shard_map/add_gravity/pallas_call | solution.py:367
  (28 shorter events, 0.2 us)
Async XLA Ops:
  2.6 39.3 %collective-permute-start = (bf16[2,3,1024]{2,1,0:T(4,128)(2,1)S(1)}, bf16[2,3,1024]{2,1,0:T(4,128)(2,1)S(1)}, u32[]{:S(2)}, u32[]{:S(2)}) collective-permute-start(bf16[2,3,1024]{2,1,0:T(4,128)(2,1)S(1)} %fusion.7), channel_id=1, source_target_pairs={{0,1},{1,0},{2,3},{3,2},{4,5},{5,4},{6,7},{7,6},{8,9},{9,8},{10,11... | collective-permute-start | bytes 36872 | tf_op jit(solution)/shard_map/ppermute | solution.py:392
  10.5 27.8 %collective-permute-start.1 = (bf16[2,3,1024]{2,0,1:T(2,128)(2,1)S(1)}, bf16[2,3,1024]{2,0,1:T(2,128)(2,1)S(1)}, u32[]{:S(2)}, u32[]{:S(2)}) collective-permute-start(bf16[2,3,1024]{2,0,1:T(2,128)(2,1)S(1)} %pad_maximum_fusion.4), channel_id=1, source_target_pairs={{0,2},{2,4},{4,6},{6,8},{8,10},{10,12},{12,14},{14,16},{16,18},{18... | collective-permute-start | bytes 36872 | tf_op jit(solution)/shard_map/ppermute | solution.py:410
  25.4 84.1 %all-to-all-start = ((f32[16,8,1024]{2,1,0:T(8,128)}), f32[16,8,1024]{2,1,0:T(8,128)S(1)}, u32[]{:S(2)}, u32[]{:S(2)}) async-start(f32[16,8,1024]{2,1,0:T(8,128)} %bitcast.15), calls=%async_computation | async-start | bytes 1048576 | tf_op jit(solution)/shard_map/all_to_all | solution.py:439
  31.4 9.1 %collective-permute-start.2 = (bf16[2,3,1024]{2,0,1:T(2,128)(2,1)S(1)}, bf16[2,3,1024]{2,0,1:T(2,128)(2,1)S(1)}, u32[]{:S(2)}, u32[]{:S(2)}) collective-permute-start(bf16[2,3,1024]{2,0,1:T(2,128)(2,1)S(1)} %pad_maximum_fusion.5), channel_id=1, source_target_pairs={{2,0},{4,2},{6,4},{8,6},{10,8},{12,10},{14,12},{16,14},{18,16},{20... | collective-permute-start | bytes 36872 | tf_op jit(solution)/shard_map/ppermute | solution.py:411
  129.8 80.1 %all-to-all-start.1 = ((f32[16,2,8,1024]{3,2,1,0:T(8,128)}), f32[16,2,8,1024]{3,2,1,0:T(8,128)S(1)}, u32[]{:S(2)}, u32[]{:S(2)}) async-start(f32[16,2,8,1024]{3,2,1,0:T(8,128)} %broadcast_in_dim.4), calls=%async_computation.1 | async-start | bytes 2097152 | tf_op jit(solution)/shard_map/all_to_all | solution.py:451

commit v4 on v3

--- a/solution.py
+++ b/solution.py
@@ -94,20 +94,21 @@
 
 
 ROOT_FACE, SOUND_FACE, IN, OUT, ROOT_MID, SOUND_MID, AZ, SPIN, PULL = range(9)
+COEFS_USED = 9
+ROOT_START, SOUND_START = 9, 10
 COEFS = 16
 
 
 def row_coefficients(first_row, rows, step):
-    face = jnp.exp((first_row + jnp.arange(rows + SUB + 1)).astype(jnp.float32) * step)
+    face = jnp.exp((first_row + jnp.arange(rows + 1)).astype(jnp.float32) * step)
     inner, outer = face[:-1], face[1:]
     mid = 0.5 * (inner + outer)
     area = 0.5 * (outer * outer - inner * inner)
-    sound_face = aspect_sq / inner
     sound_mid = aspect_sq / mid
     radial = (0.05 * step) / area
     columns = [
-        jnp.sqrt(sound_face),
-        sound_face,
+        jnp.sqrt(aspect_sq / outer),
+        aspect_sq / outer,
         radial * inner,
         radial * outer,
         jnp.sqrt(sound_mid),
@@ -115,6 +116,8 @@
         0.05 / mid,
         (0.1 * step) / mid,
         (0.1 * step) / (mid * mid),
+        jnp.sqrt(aspect_sq / inner),
+        aspect_sq / inner,
     ]
     columns += [jnp.zeros_like(mid)] * (COEFS - len(columns))
     return jnp.stack(columns, axis=1)
@@ -125,16 +128,16 @@
     return guess * (2.0 - x * guess)
 
 
-def flux_kernel(first_block, block_count, unroll, refs):
+def flux_kernel(first_block, block_count, tall, refs):
     fields = refs[0:3]
     before = refs[3:6]
     after = refs[6:9]
-    rim_in, rim_out, ghost_ref, coef_ref, coef_next = refs[9:14]
-    outs = refs[-6:-3]
-    above, lagged, pending = refs[-3:]
+    rim_in, rim_out, ghost_ref, coef_ref = refs[9:13]
+    outs = refs[-4:-1]
+    below = refs[-1]
     layers, rows, cells = fields[0].shape
     columns = cells // LANES
-    strips = rows // SUB
+    strips = rows // (SUB * tall)
     index = pl.program_id(0) + first_block
     lane = lax.broadcasted_iota(jnp.int32, (SUB, LANES), 1)
     sub = lax.broadcasted_iota(jnp.int32, (SUB, LANES), 0)
@@ -144,9 +147,6 @@
 
     def at(col):
         return pl.ds(col * LANES, LANES)
-
-    def rows_at(place):
-        return pl.ds(pl.multiple_of(place * SUB, SUB), SUB)
 
     def radial_state(state):
         density, mom_r, mom_phi = state
@@ -154,152 +154,187 @@
         vel = mom_r * inv
         return inv, (density, mom_r, mom_phi, jnp.abs(vel), mom_r * vel, mom_phi * vel)
 
-    def radial_flux(values, lower, root, sound):
-        speed = jnp.maximum(values[3], lower[3]) + root
+    def radial_flux(upper, lower, root, sound):
+        speed = jnp.maximum(upper[3], lower[3]) + root
         return (
-            (values[1] + lower[1]) - speed * (values[0] - lower[0]),
-            ((values[4] + lower[4]) + sound * (values[0] + lower[0]))
-            - speed * (values[1] - lower[1]),
-            (values[5] + lower[5]) - speed * (values[2] - lower[2]),
+            (upper[1] + lower[1]) - speed * (upper[0] - lower[0]),
+            ((upper[4] + lower[4]) + sound * (upper[0] + lower[0]))
+            - speed * (upper[1] - lower[1]),
+            (upper[5] + lower[5]) - speed * (upper[2] - lower[2]),
         )
 
-    def azimuth_flux(values, lower, root):
-        speed = jnp.maximum(values[3], lower[3]) + root
+    def azimuth_flux(upper, lower, root):
+        speed = jnp.maximum(upper[3], lower[3]) + root
         return (
-            (values[2] + lower[2]) - speed * (values[0] - lower[0]),
-            (values[4] + lower[4]) - speed * (values[1] - lower[1]),
-            (values[5] + lower[5]) - speed * (values[2] - lower[2]),
+            (upper[2] + lower[2]) - speed * (upper[0] - lower[0]),
+            (upper[4] + lower[4]) - speed * (upper[1] - lower[1]),
+            (upper[5] + lower[5]) - speed * (upper[2] - lower[2]),
         )
 
-    def finish(slot, rows_before, layer, col, turned_flux, out_coef):
-        for comp in range(3):
-            up = jnp.where(sub == SUB - 1, turned_flux[comp], lagged[slot, layer, comp, :, at(col)])
-            outs[comp][layer, rows_before, at(col)] = (
-                pending[slot, layer, comp, :, at(col)] - out_coef * up
-            )
-
-    def edge_state(layer, col, edge, rim, near, row):
-        state = []
-        for comp in range(3):
-            value = jnp.where(
-                edge, rim[layer, comp : comp + 1, at(col)], near[comp][layer, row : row + 1, at(col)]
-            )
-            state.append(jnp.broadcast_to(value, (SUB, LANES)))
-        return radial_state(state)[1]
-
-    for layer in range(layers):
-        for col in range(columns):
-            values = edge_state(layer, col, index == 0, rim_in, before, SUB - 1)
-            for k, value in enumerate(values):
-                above[0, layer, k, :, at(col)] = value
-
-    def strip(place, slot):
-        later = (slot + 1) % unroll
-        here = rows_at(place)
-        rows_before = rows_at(jnp.maximum(place - 1, 0))
-        coef = coef_ref[here, :]
-        root_face, sound_face, in_coef, root_mid, sound_mid, az, spin, pull = (
-            wide(coef[:, k : k + 1])
-            for k in (ROOT_FACE, SOUND_FACE, IN, ROOT_MID, SOUND_MID, AZ, SPIN, PULL)
-        )
-        out_before = wide(coef_ref[rows_before, OUT : OUT + 1])
-
-        def azimuth_values(state, inv, cross):
+    def face_coefs(coef):
+        return wide(coef[:, ROOT_FACE : ROOT_FACE + 1]), wide(coef[:, SOUND_FACE : SOUND_FACE + 1])
+
+    @pl.when(pl.program_id(0) == 0)
+    def _():
+        for layer in range(layers):
+            for col in range(columns):
+                pair = []
+                for comp in range(3):
+                    row = jnp.where(
+                        index == 0,
+                        rim_in[layer, comp : comp + 1, at(col)],
+                        before[comp][layer, SUB - 1 :, at(col)],
+                    )
+                    pair.append((jnp.broadcast_to(row, (SUB, LANES)), fields[comp][layer, 0:SUB, at(col)]))
+                lower = radial_state([p[0] for p in pair])[1]
+                upper = radial_state([p[1] for p in pair])[1]
+                first = coef_ref[0:SUB, :]
+                flux = radial_flux(
+                    upper,
+                    lower,
+                    wide(first[:, ROOT_START : ROOT_START + 1]),
+                    wide(first[:, SOUND_START : SOUND_START + 1]),
+                )
+                for comp in range(3):
+                    below[layer, comp, :, at(col)] = flux[comp]
+
+    def strip(layer, start, next_row):
+        tiles = [pl.ds(pl.multiple_of(start + SUB * k, SUB), SUB) for k in range(tall)]
+        raw = [
+            [[ref[layer, tile, at(col)] for ref in fields] for tile in tiles] for col in range(columns)
+        ]
+        beyond = [next_row(layer, col) for col in range(columns)]
+        lowest = [[below[layer, comp, :, at(col)] for comp in range(3)] for col in range(columns)]
+        coefs = [coef_ref[tile, :] for tile in tiles]
+        ghosts = [ghost_ref[layer, tile, :] for tile in tiles]
+        stores = []
+
+        rows_of = [
+            [wide(coef[:, k : k + 1]) for k in range(COEFS_USED)] for coef in coefs
+        ]
+
+        def azimuth_values(k, state, inv, cross):
             density, mom_r, mom_phi = state
             vel = mom_phi * inv
             return (
-                density, mom_r, mom_phi, jnp.abs(vel), cross, mom_phi * vel + sound_mid * density
+                density, mom_r, mom_phi, jnp.abs(vel), cross,
+                mom_phi * vel + rows_of[k][SOUND_MID] * density,
             )
 
-        def ghost_values(layer, side):
-            ghost = ghost_ref[layer, here, :]
-            state = [wide(ghost[:, 3 * side + k : 3 * side + k + 1]) for k in range(3)]
+        def ghost_values(k, side):
+            state = [wide(ghosts[k][:, 3 * side + c : 3 * side + c + 1]) for c in range(3)]
             inv = inverse(state[0])
-            return azimuth_values(state, inv, state[1] * state[2] * inv)
-
-        turned = [ghost_values(layer, 0) for layer in range(layers)]
-        held = [None] * layers
-        turned_held = [None] * layers
-
-        def settle(layer, col, turned_flux):
+            return azimuth_values(k, state, inv, state[1] * state[2] * inv)
+
+        turned = [ghost_values(k, 0) for k in range(tall)]
+        held = [None] * tall
+        turned_held = [None] * tall
+
+        def settle(k, col, turned_flux):
             for comp in range(3):
-                up = jnp.where(lane == LANES - 1, turned_flux[comp], turned_held[layer][comp])
-                pending[later, layer, comp, :, at(col)] = held[layer][comp] - az * up
+                up = jnp.where(lane == LANES - 1, turned_flux[comp], turned_held[k][comp])
+                stores.append((outs[comp], tiles[k], col, held[k][comp] - rows_of[k][AZ] * up))
 
         for col in range(columns):
-            for layer in range(layers):
-                state = [ref[layer, here, at(col)] for ref in fields]
-                inv, values = radial_state(state)
-                rolled = [pltpu.roll(value, 1, 0) for value in values]
-                lower = [
-                    jnp.where(sub == 0, above[slot, layer, k, :, at(col)], value)
-                    for k, value in enumerate(rolled)
+            states = [radial_state(state) for state in raw[col]]
+            last = radial_state(beyond[col])[1]
+            turned_up = [[pltpu.roll(v, SUB - 1, 0) for v in values] for _, values in states]
+            turned_up.append([pltpu.roll(v, SUB - 1, 0) for v in last])
+            earlier = lowest[col]
+            for k in range(tall):
+                c = rows_of[k]
+                inv, values = states[k]
+                upper = [
+                    jnp.where(sub == SUB - 1, b, a) for a, b in zip(turned_up[k], turned_up[k + 1])
                 ]
-                for k, value in enumerate(rolled):
-                    above[later, layer, k, :, at(col)] = value
-                flux_r = radial_flux(values, lower, root_face, sound_face)
-                turned_r = [pltpu.roll(value, SUB - 1, 0) for value in flux_r]
-                finish(slot, rows_before, layer, col, turned_r, out_before)
-                for comp in range(3):
-                    lagged[later, layer, comp, :, at(col)] = turned_r[comp]
-                values = azimuth_values(state, inv, values[5])
-                rolled = [pltpu.roll(value, 1, 1) for value in values]
-                lower = [jnp.where(lane == 0, a, b) for a, b in zip(turned[layer], rolled)]
-                turned[layer] = rolled
-                flux = azimuth_flux(values, lower, root_mid)
-                turned_flux = [pltpu.roll(value, LANES - 1, 1) for value in flux]
+                flux_r = radial_flux(upper, values, c[ROOT_FACE], c[SOUND_FACE])
+                turned_r = [pltpu.roll(v, 1, 0) for v in flux_r]
+                flux_low = [jnp.where(sub == 0, a, b) for a, b in zip(earlier, turned_r)]
+                earlier = turned_r
+
+                azimuthal = azimuth_values(k, raw[col][k], inv, values[5])
+                rolled = [pltpu.roll(v, 1, 1) for v in azimuthal]
+                lower = [jnp.where(lane == 0, a, b) for a, b in zip(turned[k], rolled)]
+                turned[k] = rolled
+                flux = azimuth_flux(azimuthal, lower, c[ROOT_MID])
+                turned_flux = [pltpu.roll(v, LANES - 1, 1) for v in flux]
                 if col > 0:
-                    settle(layer, col - 1, turned_flux)
-                held[layer] = (
-                    state[0] + in_coef * flux_r[0] + az * flux[0],
-                    state[1] + in_coef * flux_r[1] + az * flux[1] + (spin * values[5] - pull * state[0]),
-                    state[2] + in_coef * flux_r[2] + az * flux[2] - spin * values[4],
+                    settle(k, col - 1, turned_flux)
+                sums = [
+                    raw[col][k][comp]
+                    + (c[IN] * flux_low[comp] - c[OUT] * flux_r[comp])
+                    + c[AZ] * flux[comp]
+                    for comp in range(3)
+                ]
+                held[k] = (
+                    sums[0],
+                    sums[1] + (c[SPIN] * azimuthal[5] - c[PULL] * raw[col][k][0]),
+                    sums[2] - c[SPIN] * azimuthal[4],
                 )
-                turned_held[layer] = turned_flux
+                turned_held[k] = turned_flux
+            lowest[col] = earlier
+        for k in range(tall):
+            flux = azimuth_flux(ghost_values(k, 1), turned[k], rows_of[k][ROOT_MID])
+            settle(k, columns - 1, [pltpu.roll(v, LANES - 1, 1) for v in flux])
+
+        for ref, tile, col, value in stores:
+            ref[layer, tile, at(col)] = value
+        for col in range(columns):
+            for comp in range(3):
+                below[layer, comp, :, at(col)] = lowest[col][comp]
+
+    def inside(place, carry):
+        start = place * (SUB * tall)
+        following = pl.ds(pl.multiple_of(start + SUB * tall, SUB), SUB)
         for layer in range(layers):
-            flux = azimuth_flux(ghost_values(layer, 1), turned[layer], root_mid)
-            settle(layer, columns - 1, [pltpu.roll(value, LANES - 1, 1) for value in flux])
-
-    def strip_group(group, carry):
-        for slot in range(unroll):
-            strip(group * unroll + slot, slot)
+            strip(
+                layer,
+                start,
+                lambda layer, col: [ref[layer, following, at(col)] for ref in fields],
+            )
         return carry
 
-    lax.fori_loop(0, strips // unroll, strip_group, 0)
-
-    last = pl.ds((strips - 1) * SUB, SUB)
-    root_face = wide(coef_next[:, ROOT_FACE : ROOT_FACE + 1])
-    sound_face = wide(coef_next[:, SOUND_FACE : SOUND_FACE + 1])
-    out_coef = wide(coef_ref[last, OUT : OUT + 1])
+    lax.fori_loop(0, strips - 1, inside, 0)
+
+    def row_after(layer, col):
+        return [
+            jnp.broadcast_to(
+                jnp.where(
+                    index == block_count - 1,
+                    rim_out[layer, comp : comp + 1, at(col)],
+                    after[comp][layer, 0:1, at(col)],
+                ),
+                (SUB, LANES),
+            )
+            for comp in range(3)
+        ]
+
     for layer in range(layers):
-        for col in range(columns):
-            values = edge_state(layer, col, index == block_count - 1, rim_out, after, 0)
-            lower = [above[0, layer, k, :, at(col)] for k in range(6)]
-            flux_r = radial_flux(values, lower, root_face, sound_face)
-            finish(0, last, layer, col, [pltpu.roll(value, SUB - 1, 0) for value in flux_r], out_coef)
+        strip(layer, (strips - 1) * SUB * tall, row_after)
+
+
+def flux_block(rows):
+    return min(rows, LANES)
 
 
 def flux_rows(first_block, count, fields, rims, ghosts, coefs, so_far):
     layers, rows, cells = fields[0].shape
     block = flux_block(rows)
     per = block // SUB
-    unroll = min(2, per)
+    tall = min(2, per)
     main = pl.BlockSpec((layers, block, cells), lambda i: (0, i + first_block, 0))
-    before = pl.BlockSpec(
-        (layers, SUB, cells), lambda i: (0, jnp.maximum((i + first_block) * per - 1, 0), 0)
-    )
+    before = pl.BlockSpec((layers, SUB, cells), lambda i: (0, max(first_block * per - 1, 0), 0))
     after = pl.BlockSpec(
         (layers, SUB, cells),
         lambda i: (0, jnp.minimum((i + first_block + 1) * per, rows // SUB - 1), 0),
     )
     rim = pl.BlockSpec((layers, 3, cells), lambda i: (0, 0, 0))
-    operands = [*fields, *fields, *fields, *rims, ghosts, coefs, coefs]
+    operands = [*fields, *fields, *fields, *rims, ghosts, coefs]
     specs = [main] * 3 + [before] * 3 + [after] * 3 + [
         rim,
         rim,
         pl.BlockSpec((layers, block, ghosts.shape[2]), lambda i: (0, i + first_block, 0)),
         pl.BlockSpec((block, COEFS), lambda i: (i + first_block, 0)),
-        pl.BlockSpec((SUB, COEFS), lambda i: ((i + first_block + 1) * per, 0)),
     ]
     aliases = {}
     if so_far is not None:
@@ -308,16 +343,12 @@
             operands.append(array)
             specs.append(pl.BlockSpec(memory_space=pl.ANY))
     return pl.pallas_call(
-        lambda *refs: flux_kernel(first_block, rows // block, unroll, refs),
+        lambda *refs: flux_kernel(first_block, rows // block, tall, refs),
         grid=(count,),
         in_specs=specs,
         out_specs=[main] * 3,
         out_shape=[jax.ShapeDtypeStruct(f.shape, f.dtype) for f in fields],
-        scratch_shapes=[
-            pltpu.VMEM((unroll, layers, 6, SUB, cells), jnp.float32),
-            pltpu.VMEM((unroll, layers, 3, SUB, cells), jnp.float32),
-            pltpu.VMEM((unroll, layers, 3, SUB, cells), jnp.float32),
-        ],
+        scratch_shapes=[pltpu.VMEM((layers, 3, SUB, cells), jnp.float32)],
         input_output_aliases=aliases,
         compiler_params=pltpu.CompilerParams(vmem_limit_bytes=VMEM_BYTES),
         cost_estimate=pl.CostEstimate(
@@ -327,10 +358,6 @@
         ),
         name="flux_rows",
     )(*operands)
-
-
-def flux_block(rows):
-    return min(rows, 64)
 
 
 def gravity_kernel(

time: 231 us -> 235 us (1.017)
  Pallas kernels: 179 us -> 183 us
    pallas_call x2, Pallas kernels: 134 us -> 138 us  [flux_rows(): pl.pallas_call(lambda *refs: flux_kernel(first_block, rows // block, tall...]
  transfers between devices with their start and end apart: 5 -> 5, of which waited for: 1 -> 1; matrix products, arithmetic and copies ran while one was open for 8% -> 7% of each run, Pallas kernels for 62% -> 63%
where the time goes in v4:
time: 235 us; the launch traced here: 234 us
  Pallas kernels  183 us (78%)
  starting transfers between devices  24.2 us (10%)
  local copies, waits for them, and re-layouts  16.8 us (7%)
  other arithmetic  5.53 us (2%)
    pallas_call x2, Pallas kernels, flux_rows(): pl.pallas_call(lambda *refs: flux_kernel(first_block, rows // block, tall...  138 us
    pallas_call x1, Pallas kernels, add_gravity(): pl.pallas_call(gravity_kernel, grid=(rows // block,), in_specs=[modes_spe...  19.2 us
    pallas_call x1, Pallas kernels, responses(): pl.pallas_call(lambda *refs: response_kernel(mode_count, *refs), grid=(ro...  16.3 us
    all_to_all x1, starting transfers between devices, local(): lax.all_to_all(jnp.broadcast_to(parts[None], (az_count, *parts.shape)), '...  9.65 us
    pallas_call x1, Pallas kernels, surface_modes(): pl.pallas_call(lambda *refs: modes_kernel(scale, *refs), grid=(rows // bl...  9.13 us
    slice x3, local copies, waits for them, and re-layouts, exchange_edges(): f[:, :, -1]  7.41 us
    all_to_all x1, starting transfers between devices, local(): lax.all_to_all(partial.reshape(az_count, pair_count, rows), 'az', split_a...  5.94 us
    ppermute x1, starting transfers between devices, exchange_edges(): high = lax.ppermute(first.astype(jnp.bfloat16), 'az', left)  5.58 us
  transfers between devices with their start and end apart: 5, of which 1 were waited for; matrix products, arithmetic and copies ran while one was open for 7% of the time, Pallas kernels for 63%

profile of v4, /device:TPU:0, one launch (start us, length us, event | category | flops | bytes accessed | tf_op | source)
XLA Modules:
  0.0 234.4 jit_solution(1901906002327894364)
XLA Ops:
  0.6 0.9 fusion.13
  1.5 1.0 fusion.14
  2.5 0.1 fusion.7
  2.6 0.5 collective-permute-start
  3.1 2.5 %slice_reduce_fusion.5 = (bf16[2,1024]{1,0:T(2,128)(2,1)S(1)}, bf16[2,1024]{1,0:T(2,128)(2,1)S(1)}) fusion(f32[2,1024,1024]{2,1,0:T(8,128)} %density_ref.1), kind=kLoop, calls=%fused_computation.5 | loop fusion | bytes 24576 | tf_op jit(solution)/shard_map/slice | solution.py:435
  5.6 2.5 %slice_reduce_fusion.4 = (bf16[2,1024]{1,0:T(2,128)(2,1)S(1)}, bf16[2,1024]{1,0:T(2,128)(2,1)S(1)}) fusion(f32[2,1024,1024]{2,1,0:T(8,128)} %refs_7_.3), kind=kLoop, calls=%fused_computation.4 | loop fusion | bytes 24576 | tf_op jit(solution)/shard_map/slice | solution.py:435
  8.0 2.5 %slice_reduce_fusion.3 = (bf16[2,1024]{1,0:T(2,128)(2,1)S(1)}, bf16[2,1024]{1,0:T(2,128)(2,1)S(1)}) fusion(f32[2,1024,1024]{2,1,0:T(8,128)} %refs_8_.3), kind=kLoop, calls=%fused_computation.3 | loop fusion | bytes 24576 | tf_op jit(solution)/shard_map/slice | solution.py:435
  10.5 2.6 %collective-permute-start.1 = (bf16[2,3,1024]{2,0,1:T(2,128)(2,1)S(1)}, bf16[2,3,1024]{2,0,1:T(2,128)(2,1)S(1)}, u32[]{:S(2)}, u32[]{:S(2)}) collective-permute-start(bf16[2,3,1024]{2,0,1:T(2,128)(2,1)S(1)} %pad_maximum_fusion.4), channel_id=1, source_target_pairs={{0,2},{2,4},{4,6},{6,8},{8,10},{10,12},{12,14},{14,16},{16,18},{18... | collective-permute-start | bytes 36872 | tf_op jit(solution)/shard_map/ppermute | solution.py:437
  13.2 3.1 %reduce-precision_convert_fusion = (bf16[128,1024]{1,0:T(8,128)(2,1)S(1)}, bf16[128,1024]{1,0:T(8,128)(2,1)S(1)}, bf16[128,1024]{1,0:T(8,128)(2,1)S(1)}, f32[128,1024]{1,0:T(8,128)}, bf16[128,1024]{1,0:T(8,128)(2,1)S(1)}) fusion(s32[128]{0:T(128)S(1)} %iota_shift-right-logical_fusion, s32[128]{0:T(128)S(1)} %broadcast_add_fusion, ...), kind=kLoop, calls=%fused_computation.9 | loop fusion | flops 2359296 | bytes 1579264 | tf_op jit(solution)/shard_map/convert_element_type | solution.py:24
  16.3 9.1 %surface_modes.1 = f32[128,1024]{1,0:T(8,128)} custom-call(f32[2,1024,1024]{2,1,0:T(8,128)} %density_ref.1, f32[128,1024]{1,0:T(8,128)} %get-tuple-element.61.refs_1_), custom_call_target="tpu_custom_call" | custom-call | flops 1610612736 | bytes 8388608 | tf_op jit(solution)/shard_map/surface_modes/pallas_call | solution.py:44
  25.4 5.9 %all-to-all-start = ((f32[16,8,1024]{2,1,0:T(8,128)}), f32[16,8,1024]{2,1,0:T(8,128)S(1)}, u32[]{:S(2)}, u32[]{:S(2)}) async-start(f32[16,8,1024]{2,1,0:T(8,128)} %bitcast.26), calls=%async_computation | async-start | bytes 1048576 | tf_op jit(solution)/shard_map/all_to_all | solution.py:466
  31.4 5.6 %collective-permute-start.2 = (bf16[2,3,1024]{2,0,1:T(2,128)(2,1)S(1)}, bf16[2,3,1024]{2,0,1:T(2,128)(2,1)S(1)}, u32[]{:S(2)}, u32[]{:S(2)}) collective-permute-start(bf16[2,3,1024]{2,0,1:T(2,128)(2,1)S(1)} %pad_maximum_fusion.5), channel_id=1, source_target_pairs={{2,0},{4,2},{6,4},{8,6},{10,8},{12,10},{14,12},{16,14},{18,16},{20... | collective-permute-start | bytes 36872 | tf_op jit(solution)/shard_map/ppermute | solution.py:438
  37.0 0.1 slice_divide_fusion
  37.1 0.1 stack.67
  37.2 1.0 copy.39.refs_12_
  38.2 0.0 collective-permute-done.1
  38.2 2.3 collective-permute-done.2
  40.5 1.3 copy.38
  41.9 0.0 collective-permute-done
  41.9 0.7 convert_select_fusion
  42.6 69.1 %flux_rows.2 = (f32[2,1024,1024]{2,1,0:T(8,128)}, f32[2,1024,1024]{2,1,0:T(8,128)}, f32[2,1024,1024]{2,1,0:T(8,128)}) custom-call(f32[2,1024,1024]{2,1,0:T(8,128)} %density_ref.1, f32[2,1024,1024]{2,1,0:T(8,128)} %refs_7_.3, f32[2,1024,1024]{2,1,0:T(8,128)} %refs_8_.3, f32[2,1024,1024]{2,1,0:T(8,128)} %density_ref.1, f32[2,1024,1024]{2,1,0:T(8,128)} %refs_7_.3, ...), custom_call_target="tpu_custom_call" | custom-call | flops 104857600 | bytes 25165824 | tf_op jit(solution)/shard_map/flux_rows/pallas_call | solution.py:345
  111.7 0.0 all-to-all-done
  111.7 2.0 all_gather.3.refs_0_
  113.7 16.3 %responses.1 = f32[2,8,1024]{2,1,0:T(8,128)} custom-call(bf16[8,2048]{1,0:T(8,128)(2,1)} %all_gather.3.refs_0_, bf16[4,1024,2048]{2,1,0:T(8,128)(2,1)} %refs_1_.4, bf16[4,1024,2048]{2,1,0:T(8,128)(2,1)} %refs_2_.4), custom_call_target="tpu_custom_call" | custom-call | flops 268435456 | bytes 33554432 | tf_op jit(solution)/shard_map/responses/pallas_call | solution.py:80
  130.0 1.9 broadcast_in_dim.4
  132.0 9.6 %all-to-all-start.1 = ((f32[16,2,8,1024]{3,2,1,0:T(8,128)}), f32[16,2,8,1024]{3,2,1,0:T(8,128)S(1)}, u32[]{:S(2)}, u32[]{:S(2)}) async-start(f32[16,2,8,1024]{3,2,1,0:T(8,128)} %broadcast_in_dim.4), calls=%async_computation.1 | async-start | bytes 2097152 | tf_op jit(solution)/shard_map/all_to_all | solution.py:478
  141.6 1.0 copy.41.inverse_ref
  142.7 1.4 pad_maximum_fusion
  144.1 1.0 copy.40.refs_12_
  145.1 69.1 %flux_rows.3 = (f32[2,1024,1024]{2,1,0:T(8,128)}, f32[2,1024,1024]{2,1,0:T(8,128)}, f32[2,1024,1024]{2,1,0:T(8,128)}) custom-call(f32[2,1024,1024]{2,1,0:T(8,128)} %density_ref.1, f32[2,1024,1024]{2,1,0:T(8,128)} %refs_7_.3, f32[2,1024,1024]{2,1,0:T(8,128)} %refs_8_.3, ...), custom_call_target="tpu_custom_call", output_to_operand_aliasing={{0}: (13, {}), {1}: (14, {}), {2}: (15, {})} | custom-call | flops 104857600 | bytes 25165824 | tf_op jit(solution)/shard_map/flux_rows/pallas_call | solution.py:345
  214.2 1.1 slice_bitcast_fusion
  215.3 19.2 %add_gravity.1 = (f32[2,1024,1024]{2,1,0:T(8,128)}, f32[2,1024,1024]{2,1,0:T(8,128)}, f32[1024,1024]{1,0:T(8,128)}) custom-call(f32[128,1024]{1,0:T(8,128)} %get-tuple-element.47.pot_ref, f32[128,1024]{1,0:T(8,128)} %get-tuple-element.46.force_ref, f32[1024,1]{1,0:T(8,128)} %copy.41.inverse_ref, ...), custom_call_target="tpu_custom_call", output_to_operand_aliasing={{0}: (6, {}), {1}: (7, {})} | custom-call | flops 2415919104 | bytes 46137344 | tf_op jit(solution)/shard_map/add_gravity/pallas_call | solution.py:394
  (16 shorter events, 0.2 us)
Async XLA Ops:
  2.6 39.3 %collective-permute-start = (bf16[2,3,1024]{2,1,0:T(4,128)(2,1)S(1)}, bf16[2,3,1024]{2,1,0:T(4,128)(2,1)S(1)}, u32[]{:S(2)}, u32[]{:S(2)}) collective-permute-start(bf16[2,3,1024]{2,1,0:T(4,128)(2,1)S(1)} %fusion.7), channel_id=1, source_target_pairs={{0,1},{1,0},{2,3},{3,2},{4,5},{5,4},{6,7},{7,6},{8,9},{9,8},{10,11... | collective-permute-start | bytes 36872 | tf_op jit(solution)/shard_map/ppermute | solution.py:419
  10.5 27.7 %collective-permute-start.1 = (bf16[2,3,1024]{2,0,1:T(2,128)(2,1)S(1)}, bf16[2,3,1024]{2,0,1:T(2,128)(2,1)S(1)}, u32[]{:S(2)}, u32[]{:S(2)}) collective-permute-start(bf16[2,3,1024]{2,0,1:T(2,128)(2,1)S(1)} %pad_maximum_fusion.4), channel_id=1, source_target_pairs={{0,2},{2,4},{4,6},{6,8},{8,10},{10,12},{12,14},{14,16},{16,18},{18... | collective-permute-start | bytes 36872 | tf_op jit(solution)/shard_map/ppermute | solution.py:437
  25.4 86.2 %all-to-all-start = ((f32[16,8,1024]{2,1,0:T(8,128)}), f32[16,8,1024]{2,1,0:T(8,128)S(1)}, u32[]{:S(2)}, u32[]{:S(2)}) async-start(f32[16,8,1024]{2,1,0:T(8,128)} %bitcast.26), calls=%async_computation | async-start | bytes 1048576 | tf_op jit(solution)/shard_map/all_to_all | solution.py:466
  31.4 9.1 %collective-permute-start.2 = (bf16[2,3,1024]{2,0,1:T(2,128)(2,1)S(1)}, bf16[2,3,1024]{2,0,1:T(2,128)(2,1)S(1)}, u32[]{:S(2)}, u32[]{:S(2)}) collective-permute-start(bf16[2,3,1024]{2,0,1:T(2,128)(2,1)S(1)} %pad_maximum_fusion.5), channel_id=1, source_target_pairs={{2,0},{4,2},{6,4},{8,6},{10,8},{12,10},{14,12},{16,14},{18,16},{20... | collective-permute-start | bytes 36872 | tf_op jit(solution)/shard_map/ppermute | solution.py:438
  132.0 82.2 %all-to-all-start.1 = ((f32[16,2,8,1024]{3,2,1,0:T(8,128)}), f32[16,2,8,1024]{3,2,1,0:T(8,128)S(1)}, u32[]{:S(2)}, u32[]{:S(2)}) async-start(f32[16,2,8,1024]{3,2,1,0:T(8,128)} %broadcast_in_dim.4), calls=%async_computation.1 | async-start | bytes 2097152 | tf_op jit(solution)/shard_map/all_to_all | solution.py:478

commit v5 on v4

--- a/solution.py
+++ b/solution.py
@@ -19,54 +19,111 @@
     return high, low
 
 
-def split_outside(x):
-    high = lax.reduce_precision(x, 8, 7)
-    return high.astype(jnp.bfloat16), (x - high).astype(jnp.bfloat16)
-
-
-def modes_kernel(scale, density_ref, basis_ref, out_ref):
-    surface = density_ref[0]
-    for layer in range(1, density_ref.shape[0]):
-        surface = surface + density_ref[layer]
-    out_ref[...] = scale * lax.dot_general(
-        basis_ref[...],
-        surface,
-        (((1,), (1,)), ((), ())),
-        precision=lax.Precision.HIGHEST,
-        preferred_element_type=jnp.float32,
-    )
-
-
-def surface_modes(density, basis, scale):
-    layers, rows, cells = density.shape
-    cols = basis.shape[0]
+def pieces_of(x, count):
+    out = []
+    for _ in range(count - 1):
+        high = lax.reduce_precision(x, 8, 7)
+        out.append(high.astype(jnp.bfloat16))
+        x = x - high
+    return out + [x.astype(jnp.bfloat16)]
+
+
+EDGE_ROWS = 16
+
+
+def modes_kernel(scale, layers, streams, refs):
+    density = [refs[layer * streams : (layer + 1) * streams] for layer in range(layers)]
+    firsts, lasts = refs[layers * streams : layers * streams + 2], refs[layers * streams + 2 : layers * streams + 4]
+    wide_ref, thin_ref, out_ref, first_ref, last_ref = refs[layers * streams + 4 :]
+    cols = thin_ref.shape[0] // 2
+    total = None
+    for stream in range(streams):
+        x = density[0][stream][...]
+        width = x.shape[1]
+        for layer in range(1, layers):
+            x = x + density[layer][stream][...]
+        here = pl.ds(stream * width, width)
+        high = x.astype(jnp.bfloat16)
+        x = x - high.astype(jnp.float32)
+        mid = x.astype(jnp.bfloat16)
+        low = (x - mid.astype(jnp.float32)).astype(jnp.bfloat16)
+
+        def product(a, table):
+            return lax.dot_general(
+                a, table, (((1,), (1,)), ((), ())), preferred_element_type=jnp.float32
+            )
+
+        both = wide_ref[:, here]
+        major = product(high, both)
+        minor = product(mid, both)
+        small = product(low, both[:cols]) + product(high, thin_ref[:cols, here])
+        part = major[:, :cols] + (major[:, cols:] + minor[:, :cols] + (minor[:, cols:] + small))
+        total = part if total is None else total + part
+    out_ref[...] = (scale * total).T
+
+    block = out_ref.shape[1]
+    lane = lax.broadcasted_iota(jnp.int32, (block, LANES), 1)
+    edges = jnp.zeros((block, LANES), jnp.float32)
+    for layer in range(layers):
+        sides = (
+            (0, 0, (density[layer][0][:, :LANES], firsts[0][layer], firsts[1][layer])),
+            (EDGE_ROWS, LANES - 1, (density[layer][-1][:, -LANES:], lasts[0][layer], lasts[1][layer])),
+        )
+        for base, place, tiles in sides:
+            for comp, tile in enumerate(tiles):
+                edges = jnp.where(
+                    lane == base + 3 * layer + comp,
+                    jnp.broadcast_to(tile[:, place : place + 1], (block, LANES)),
+                    edges,
+                )
+    edges = edges.T
+    first_ref[...] = edges[:EDGE_ROWS].astype(jnp.bfloat16)
+    last_ref[...] = edges[EDGE_ROWS : 2 * EDGE_ROWS].astype(jnp.bfloat16)
+
+
+def surface_modes(fields, table, thin, scale):
+    layers, rows, cells = fields[0].shape
+    cols = table.shape[0] // 2
     block = min(rows, LANES)
+    streams = min(4, cells // LANES)
+    width = cells // streams
+
+    def stream(layer, place):
+        return pl.BlockSpec((None, block, width), lambda i: (layer, i, place))
+
+    first = pl.BlockSpec((layers, block, LANES), lambda i: (0, i, 0))
+    last = pl.BlockSpec((layers, block, LANES), lambda i: (0, i, cells // LANES - 1))
+    table_spec = pl.BlockSpec((2 * cols, cells), lambda i: (0, 0))
+    edge_spec = pl.BlockSpec((EDGE_ROWS, block), lambda i: (0, i))
+    edge_shape = jax.ShapeDtypeStruct((EDGE_ROWS, rows), jnp.bfloat16)
     return pl.pallas_call(
-        lambda *refs: modes_kernel(scale, *refs),
+        lambda *refs: modes_kernel(scale, layers, streams, refs),
         grid=(rows // block,),
-        in_specs=[
-            pl.BlockSpec((layers, block, cells), lambda i: (0, i, 0)),
-            pl.BlockSpec((cols, cells), lambda i: (0, 0)),
-        ],
-        out_specs=pl.BlockSpec((cols, block), lambda i: (0, i)),
-        out_shape=jax.ShapeDtypeStruct((cols, rows), jnp.float32),
+        in_specs=[stream(layer, place) for layer in range(layers) for place in range(streams)]
+        + [first, first, last, last, table_spec, table_spec],
+        out_specs=[pl.BlockSpec((cols, block), lambda i: (0, i)), edge_spec, edge_spec],
+        out_shape=[jax.ShapeDtypeStruct((cols, rows), jnp.float32), edge_shape, edge_shape],
         compiler_params=pltpu.CompilerParams(vmem_limit_bytes=VMEM_BYTES),
         cost_estimate=pl.CostEstimate(
-            flops=12 * rows * cells * cols, bytes_accessed=4 * density.size, transcendentals=0
+            flops=12 * rows * cells * cols, bytes_accessed=4 * fields[0].size, transcendentals=0
         ),
         name="surface_modes",
-    )(density, basis)
-
-
-def response_kernel(mode_count, pairs_ref, pot_ref, force_ref, out_ref):
-    pairs = pairs_ref[...]
+    )(*[fields[0]] * (layers * streams), fields[1], fields[2], fields[1], fields[2], table, thin)
+
+
+def response_kernel(mode_count, refs):
+    pairs = refs[0][...]
+    out_ref = refs[-1]
     cols = pairs.shape[0]
-    mode_of = lax.broadcasted_iota(jnp.int32, (pot_ref.shape[1], cols), 1) // 2
-    for place, ref in enumerate((pot_ref, force_ref)):
+    mode_of = lax.broadcasted_iota(jnp.int32, (refs[1].shape[0], cols), 1) // 2
+    for place in range(2):
         total = jnp.zeros(mode_of.shape, jnp.float32)
         for mode in range(mode_count):
             part = lax.dot_general(
-                ref[mode], pairs, (((1,), (1,)), ((), ())), preferred_element_type=jnp.float32
+                refs[1 + place * mode_count + mode][...],
+                pairs,
+                (((1,), (1,)), ((), ())),
+                preferred_element_type=jnp.float32,
             )
             total = jnp.where(mode_of == mode, part, total)
         out_ref[place] = total.T
@@ -76,11 +133,15 @@
     mode_count, rows, count = potential_kernel.shape
     cols = pairs.shape[0]
     block = min(rows, LANES)
-    kernel_spec = pl.BlockSpec((mode_count, block, count), lambda i: (0, i, 0))
+
+    def stream(mode):
+        return pl.BlockSpec((None, block, count), lambda i: (mode, i, 0))
+
     return pl.pallas_call(
-        lambda *refs: response_kernel(mode_count, *refs),
+        lambda *refs: response_kernel(mode_count, refs),
         grid=(rows // block,),
-        in_specs=[pl.BlockSpec((cols, count), lambda i: (0, 0)), kernel_spec, kernel_spec],
+        in_specs=[pl.BlockSpec((cols, count), lambda i: (0, 0))]
+        + [stream(mode) for mode in range(mode_count)] * 2,
         out_specs=pl.BlockSpec((2, cols, block), lambda i: (0, 0, i)),
         out_shape=jax.ShapeDtypeStruct((2, cols, rows), jnp.float32),
         compiler_params=pltpu.CompilerParams(vmem_limit_bytes=VMEM_BYTES),
@@ -90,7 +151,7 @@
             transcendentals=0,
         ),
         name="responses",
-    )(pairs, potential_kernel, force_kernel)
+    )(pairs, *[potential_kernel] * mode_count, *[force_kernel] * mode_count)
 
 
 ROOT_FACE, SOUND_FACE, IN, OUT, ROOT_MID, SOUND_MID, AZ, SPIN, PULL = range(9)
@@ -120,7 +181,7 @@
         aspect_sq / inner,
     ]
     columns += [jnp.zeros_like(mid)] * (COEFS - len(columns))
-    return jnp.stack(columns, axis=1)
+    return jnp.stack(columns, axis=0), (-0.1 / mid)[None]
 
 
 def inverse(x):
@@ -132,9 +193,9 @@
     fields = refs[0:3]
     before = refs[3:6]
     after = refs[6:9]
-    rim_in, rim_out, ghost_ref, coef_ref = refs[9:13]
-    outs = refs[-4:-1]
-    below = refs[-1]
+    rim_in, rim_out, coef_rows, low_rows, high_rows = refs[9:14]
+    outs = refs[-5:-2]
+    below, side_ref = refs[-2:]
     layers, rows, cells = fields[0].shape
     columns = cells // LANES
     strips = rows // (SUB * tall)
@@ -173,6 +234,12 @@
 
     def face_coefs(coef):
         return wide(coef[:, ROOT_FACE : ROOT_FACE + 1]), wide(coef[:, SOUND_FACE : SOUND_FACE + 1])
+
+    side_rows = jnp.concatenate(
+        [coef_rows[...], low_rows[...].astype(jnp.float32), high_rows[...].astype(jnp.float32)], axis=0
+    )
+    filler = jnp.zeros((LANES - side_rows.shape[0], rows), jnp.float32)
+    side_ref[...] = jnp.concatenate([side_rows, filler], axis=0).T
 
     @pl.when(pl.program_id(0) == 0)
     def _():
@@ -188,7 +255,7 @@
                     pair.append((jnp.broadcast_to(row, (SUB, LANES)), fields[comp][layer, 0:SUB, at(col)]))
                 lower = radial_state([p[0] for p in pair])[1]
                 upper = radial_state([p[1] for p in pair])[1]
-                first = coef_ref[0:SUB, :]
+                first = side_ref[0:SUB, :]
                 flux = radial_flux(
                     upper,
                     lower,
@@ -205,8 +272,7 @@
         ]
         beyond = [next_row(layer, col) for col in range(columns)]
         lowest = [[below[layer, comp, :, at(col)] for comp in range(3)] for col in range(columns)]
-        coefs = [coef_ref[tile, :] for tile in tiles]
-        ghosts = [ghost_ref[layer, tile, :] for tile in tiles]
+        coefs = [side_ref[tile, :] for tile in tiles]
         stores = []
 
         rows_of = [
@@ -222,7 +288,8 @@
             )
 
         def ghost_values(k, side):
-            state = [wide(ghosts[k][:, 3 * side + c : 3 * side + c + 1]) for c in range(3)]
+            base = COEFS + side * EDGE_ROWS + 3 * layer
+            state = [wide(coefs[k][:, base + c : base + c + 1]) for c in range(3)]
             inv = inverse(state[0])
             return azimuth_values(k, state, inv, state[1] * state[2] * inv)
 
@@ -317,7 +384,7 @@
     return min(rows, LANES)
 
 
-def flux_rows(first_block, count, fields, rims, ghosts, coefs, so_far):
+def flux_rows(first_block, count, fields, rims, edges, coefs, so_far):
     layers, rows, cells = fields[0].shape
     block = flux_block(rows)
     per = block // SUB
@@ -329,12 +396,13 @@
         lambda i: (0, jnp.minimum((i + first_block + 1) * per, rows // SUB - 1), 0),
     )
     rim = pl.BlockSpec((layers, 3, cells), lambda i: (0, 0, 0))
-    operands = [*fields, *fields, *fields, *rims, ghosts, coefs]
+    operands = [*fields, *fields, *fields, *rims, coefs, *edges]
     specs = [main] * 3 + [before] * 3 + [after] * 3 + [
         rim,
         rim,
-        pl.BlockSpec((layers, block, ghosts.shape[2]), lambda i: (0, i + first_block, 0)),
-        pl.BlockSpec((block, COEFS), lambda i: (i + first_block, 0)),
+        pl.BlockSpec((COEFS, block), lambda i: (0, i + first_block)),
+        pl.BlockSpec((EDGE_ROWS, block), lambda i: (0, i + first_block)),
+        pl.BlockSpec((EDGE_ROWS, block), lambda i: (0, i + first_block)),
     ]
     aliases = {}
     if so_far is not None:
@@ -348,7 +416,10 @@
         in_specs=specs,
         out_specs=[main] * 3,
         out_shape=[jax.ShapeDtypeStruct(f.shape, f.dtype) for f in fields],
-        scratch_shapes=[pltpu.VMEM((layers, 3, SUB, cells), jnp.float32)],
+        scratch_shapes=[
+            pltpu.VMEM((layers, 3, SUB, cells), jnp.float32),
+            pltpu.VMEM((block, LANES), jnp.float32),
+        ],
         input_output_aliases=aliases,
         compiler_params=pltpu.CompilerParams(vmem_limit_bytes=VMEM_BYTES),
         cost_estimate=pl.CostEstimate(
@@ -360,27 +431,28 @@
     )(*operands)
 
 
-def gravity_kernel(
-    pot_ref, force_ref, inverse_ref, table_ref, slope_ref, density_ref, mom_r_ref, mom_phi_ref,
-    out_r, out_phi, out_pot,
-):
-    def left(ref):
-        high, low = split_bf16(ref[...])
-        return jnp.concatenate([high, low, high], axis=0)
+def gravity_kernel(layers, refs):
+    pot_ref, force_ref, inverse_ref, table_ref, slope_ref = refs[:5]
+    density, mom_r, mom_phi = (refs[5 + k * layers : 5 + (k + 1) * layers] for k in range(3))
+    out_r, out_phi, out_pot = refs[5 + 3 * layers :]
 
     def product(a, table):
+        high, low = split_bf16(a)
         return lax.dot_general(
-            a, table, (((0,), (0,)), ((), ())), preferred_element_type=jnp.float32
+            jnp.concatenate([high, low, high], axis=0),
+            table,
+            (((0,), (0,)), ((), ())),
+            preferred_element_type=jnp.float32,
         )
 
-    pot, force = left(pot_ref), left(force_ref)
+    pot = pot_ref[...]
     out_pot[...] = product(pot, table_ref[...])
-    radial = product(force, table_ref[...]) * 0.1
-    azimuth = product(pot, slope_ref[...]) * inverse_ref[...]
-    for layer in range(density_ref.shape[0]):
-        density = density_ref[layer]
-        out_r[layer] = mom_r_ref[layer] + density * radial
-        out_phi[layer] = mom_phi_ref[layer] + density * azimuth
+    radial = product(force_ref[...] * 0.1, table_ref[...])
+    azimuth = product(pot * inverse_ref[...], slope_ref[...])
+    for layer in range(layers):
+        here = density[layer][...]
+        out_r[layer] = mom_r[layer][...] + here * radial
+        out_phi[layer] = mom_phi[layer][...] + here * azimuth
 
 
 def add_gravity(pot, force, inverse_mid, table, slope, density, mom_r, mom_phi):
@@ -389,24 +461,30 @@
     block = min(rows, LANES)
     modes_spec = pl.BlockSpec((cols, block), lambda i: (0, i))
     table_spec = pl.BlockSpec(table.shape, lambda i: (0, 0))
+
+    def stream(layer):
+        return pl.BlockSpec((None, block, cells), lambda i: (layer, i, 0))
+
     field = pl.BlockSpec((layers, block, cells), lambda i: (0, i, 0))
     grid_shape = jax.ShapeDtypeStruct(density.shape, density.dtype)
     return pl.pallas_call(
-        gravity_kernel,
+        lambda *refs: gravity_kernel(layers, refs),
         grid=(rows // block,),
         in_specs=[
-            modes_spec, modes_spec, pl.BlockSpec((block, 1), lambda i: (i, 0)),
-            table_spec, table_spec, field, field, field,
-        ],
+            modes_spec, modes_spec, pl.BlockSpec((1, block), lambda i: (0, i)), table_spec, table_spec,
+        ] + [stream(layer) for layer in range(layers)] * 3,
         out_specs=[field, field, pl.BlockSpec((block, cells), lambda i: (i, 0))],
         out_shape=[grid_shape, grid_shape, jax.ShapeDtypeStruct((rows, cells), jnp.float32)],
-        input_output_aliases={6: 0, 7: 1},
+        input_output_aliases={5 + layers: 0, 5 + 2 * layers: 1} if layers == 1 else {},
         compiler_params=pltpu.CompilerParams(vmem_limit_bytes=VMEM_BYTES),
         cost_estimate=pl.CostEstimate(
             flops=18 * rows * cells * cols, bytes_accessed=44 * rows * cells, transcendentals=0
         ),
         name="add_gravity",
-    )(pot, force, inverse_mid, table, slope, density, mom_r, mom_phi)
+    )(
+        pot, force, inverse_mid, table, slope,
+        *[density] * layers, *[mom_r] * layers, *[mom_phi] * layers,
+    )
 
 
 def exchange_rims(fields, rad_index, rad_count):
@@ -429,15 +507,10 @@
     return rim_in, rim_out
 
 
-def exchange_edges(fields, az_count):
+def exchange_edges(first, last, az_count):
     right = [(i, (i + 1) % az_count) for i in range(az_count)]
     left = [(b, a) for a, b in right]
-    last = lax.optimization_barrier(jnp.stack([f[:, :, -1] for f in fields], axis=1))
-    first = lax.optimization_barrier(jnp.stack([f[:, :, 0] for f in fields], axis=1))
-    low = lax.ppermute(last.astype(jnp.bfloat16), "az", right)
-    high = lax.ppermute(first.astype(jnp.bfloat16), "az", left)
-    both = jnp.concatenate([low, high], axis=1).astype(fields[0].dtype)
-    return jnp.swapaxes(both, 1, 2)
+    return lax.ppermute(last, "az", right), lax.ppermute(first, "az", left)
 
 
 def local(az_count, rad_count, density, mom_r, mom_phi, potential_kernel, force_kernel):
@@ -455,20 +528,22 @@
     mode = (row // 2).astype(jnp.float32)
     angle = azimuth[None, :] * mode
     cosine, sine = jnp.cos(angle), jnp.sin(angle)
-    basis = jnp.where(row % 2 == 0, cosine, sine)
-    slope = jnp.where(row % 2 == 0, -mode * sine, mode * cosine)
+    basis = pieces_of(jnp.where(row % 2 == 0, cosine, sine), 3)
+    slope = pieces_of(jnp.where(row % 2 == 0, -mode * sine, mode * cosine), 2)
+    wide = jnp.concatenate([basis[0], basis[1]], axis=0)
+    thin = jnp.concatenate([basis[2], basis[2]], axis=0)
 
     rims = exchange_rims(fields, rad_index, rad_count)
-    ghosts = exchange_edges(fields, az_count)
-    coefs = row_coefficients(rad_index * rows, rows, step)
-
-    partial = surface_modes(density, basis, 1.0 / (az_count * cells))
+    coefs, inverse_mid = row_coefficients(rad_index * rows, rows, step)
+
+    partial, first, last = surface_modes(fields, wide, thin, 1.0 / (az_count * cells))
+    edges = exchange_edges(first, last, az_count)
     pieces = lax.all_to_all(
         partial.reshape(az_count, pair_count, rows), "az", split_axis=0, concat_axis=0, tiled=True
     )
     blocks = rows // flux_block(rows)
     early = blocks // 2
-    results = flux_rows(0, early, fields, rims, ghosts, coefs, None) if early else None
+    results = flux_rows(0, early, fields, rims, edges, coefs, None) if early else None
     if early:
         pieces, results = lax.optimization_barrier((pieces, results))
 
@@ -479,18 +554,19 @@
         jnp.broadcast_to(parts[None], (az_count, *parts.shape)), "az", split_axis=0, concat_axis=0, tiled=True
     )
     coefs, parts = lax.optimization_barrier((coefs, parts))
-    results = flux_rows(early, blocks - early, fields, rims, ghosts, coefs, results)
+    results = flux_rows(early, blocks - early, fields, rims, edges, coefs, results)
     pot = every[:, 0].reshape(cols, rows)
     force = every[:, 1].reshape(cols, rows)
 
-    def table_of(x):
-        high, low = split_outside(x)
-        return jnp.concatenate([high, high, low], axis=0)
-
-    face = jnp.exp((rad_index * rows + jnp.arange(rows + 1)).astype(jnp.float32) * step)
-    inverse_mid = -0.1 / (0.5 * (face[:-1] + face[1:]))
     new_r, new_phi, potential = add_gravity(
-        pot, force, inverse_mid[:, None], table_of(basis), table_of(slope), density, results[1], results[2]
+        pot,
+        force,
+        inverse_mid,
+        jnp.concatenate([basis[0], basis[0], basis[1]], axis=0),
+        jnp.concatenate([slope[0], slope[0], slope[1]], axis=0),
+        density,
+        results[1],
+        results[2],
     )
     return results[0], new_r, new_phi, potential
 

time: 235 us -> 226 us (0.962)
  local copies, waits for them, and re-layouts: 16.8 us -> 6.78 us
  starting transfers between devices: 24.2 us -> 17.8 us
  Pallas kernels: 183 us -> 186 us
  waiting for transfers between devices: 2.26 us -> 4.76 us
    slice x3 -> x0, local copies, waits for them, and re-layouts: 7.41 us -> none  [exchange_edges(): f[:, :, -1]]
    all_to_all x1, starting transfers between devices: 9.65 us -> 3.7 us  [local(): lax.all_to_all(jnp.broadcast_to(parts[None], (az_count, *parts.shape)), '...]
    ppermute x2, waiting for transfers between devices: 2.25 us -> 4.75 us  [exchange_edges(): return (lax.ppermute(last, 'az', right), lax.ppermute(first, 'az', left))]
    ppermute x2, starting transfers between devices: 8.13 us -> 5.67 us  [exchange_edges(): return (lax.ppermute(last, 'az', right), lax.ppermute(first, 'az', left))]
    all_to_all x1, starting transfers between devices: 5.94 us -> 8.33 us  [local(): lax.all_to_all(partial.reshape(az_count, pair_count, rows), 'az', split_a...]
  transfers between devices with their start and end apart: 5 -> 5, of which waited for: 1 -> 1; matrix products, arithmetic and copies ran while one was open for 7% -> 3% of each run, Pallas kernels for 63% -> 62%
where the time goes in v5:
time: 226 us; the launch traced here: 225 us
  Pallas kernels  186 us (82%)
  starting transfers between devices  17.8 us (8%)
  local copies, waits for them, and re-layouts  6.78 us (3%)
  other arithmetic  6.47 us (3%)
  waiting for transfers between devices  4.76 us (2%)
    pallas_call x2, Pallas kernels, flux_rows(): pl.pallas_call(lambda *refs: flux_kernel(first_block, rows // block, tall...  140 us
    pallas_call x1, Pallas kernels, add_gravity(): pl.pallas_call(lambda *refs: gravity_kernel(layers, refs), grid=(rows //...  19.5 us
    pallas_call x1, Pallas kernels, responses(): pl.pallas_call(lambda *refs: response_kernel(mode_count, refs), grid=(row...  16.5 us
    pallas_call x1, Pallas kernels, surface_modes(): pl.pallas_call(lambda *refs: modes_kernel(scale, layers, streams, refs),...  10.6 us
    all_to_all x1, starting transfers between devices, local(): lax.all_to_all(partial.reshape(az_count, pair_count, rows), 'az', split_a...  8.33 us
    ppermute x2, starting transfers between devices, exchange_edges(): return (lax.ppermute(last, 'az', right), lax.ppermute(first, 'az', left))  5.67 us
    ppermute x2, waiting for transfers between devices, exchange_edges(): return (lax.ppermute(last, 'az', right), lax.ppermute(first, 'az', left))  4.75 us
  transfers between devices with their start and end apart: 5, of which 1 were waited for; matrix products, arithmetic and copies ran while one was open for 3% of the time, Pallas kernels for 62%

profile of v5, /device:TPU:0, one launch (start us, length us, event | category | flops | bytes accessed | tf_op | source)
XLA Modules:
  0.0 224.8 jit_solution(14059213973437611480)
XLA Ops:
  0.7 2.5 %reduce-precision_convert_fusion = (bf16[128,1024]{1,0:T(8,128)(2,1)S(1)}, bf16[128,1024]{1,0:T(8,128)(2,1)S(1)}, bf16[128,1024]{1,0:T(8,128)(2,1)S(1)}, bf16[128,1024]{1,0:T(8,128)(2,1)S(1)}, bf16[128,1024]{1,0:T(8,128)(2,1)S(1)}) fusion(s32[128]{0:T(128)S(1)} %iota_shift-right-logical_fusion, s32[128]{0:T(128)S(1)} %broadcast_add_fusion, ...), kind=kLoop, calls=%fused_computation.3 | loop fusion | flops 2752512 | bytes 1317120 | tf_op jit(solution)/shard_map/convert_element_type | solution.py:26
  3.2 1.1 pad_maximum_fusion.2
  4.3 10.6 %surface_modes.1 = (f32[128,1024]{1,0:T(8,128)}, bf16[16,1024]{1,0:T(8,128)(2,1)}, bf16[16,1024]{1,0:T(8,128)(2,1)}) custom-call(f32[2,1024,1024]{2,1,0:T(8,128)} %refs_6_.9, f32[2,1024,1024]{2,1,0:T(8,128)} %refs_6_.9, f32[2,1024,1024]{2,1,0:T(8,128)} %refs_6_.9, f32[2,1024,1024]{2,1,0:T(8,128)} %refs_6_.9, f32[2,1024,1024]{2,1,0:T(8,128)} %refs_6_.9, ...), custom_call_target="tpu_custom_call" | custom-call | flops 1610612736 | bytes 8388608 | tf_op jit(solution)/shard_map/surface_modes/pallas_call | solution.py:99
  15.0 8.3 %all-to-all-start = ((f32[16,8,1024]{2,1,0:T(8,128)}), f32[16,8,1024]{2,1,0:T(8,128)S(1)}, u32[]{:S(2)}, u32[]{:S(2)}) async-start(f32[16,8,1024]{2,1,0:T(8,128)} %bitcast.17), calls=%async_computation | async-start | bytes 1048576 | tf_op jit(solution)/shard_map/all_to_all | solution.py:541
  23.3 1.0 fusion.13
  24.3 0.9 fusion.15
  25.2 0.1 fusion.7
  25.2 0.1 collective-permute-start
  25.3 2.0 collective-permute-start.1
  27.3 3.7 %collective-permute-start.2 = (bf16[16,1024]{1,0:T(8,128)(2,1)}, bf16[16,1024]{1,0:T(8,128)(2,1)S(1)}, u32[]{:S(2)}, u32[]{:S(2)}) collective-permute-start(bf16[16,1024]{1,0:T(8,128)(2,1)} %get-tuple-element.23), channel_id=1, source_target_pairs={{2,0},{4,2},{6,4},{8,6},{10,8},{12,10},{14,12},{16,14},{18,16},{20... | collective-permute-start | bytes 98312 | tf_op jit(solution)/shard_map/ppermute | solution.py:513
  31.0 0.7 slice_divide_fusion
  31.7 1.3 stack.59.refs_11_
  33.0 0.0 collective-permute-done
  33.0 0.7 convert_select_fusion
  33.7 4.7 %collective-permute-done.1.refs_12_ = bf16[16,1024]{1,0:T(8,128)(2,1)S(1)} collective-permute-done((bf16[16,1024]{1,0:T(8,128)(2,1)}, bf16[16,1024]{1,0:T(8,128)(2,1)S(1)}, u32[]{:S(2)}, u32[]{:S(2)}) %collective-permute-start.1) | collective-permute-done | bytes 32800 | tf_op jit(solution)/shard_map/ppermute | solution.py:513
  38.4 0.0 copy-start
  38.4 0.0 collective-permute-done.2.refs_13_
  38.4 0.0 copy-start.1
  38.4 0.6 copy-done
  39.0 0.0 copy-done.1
  39.1 69.8 %flux_rows.2 = (f32[2,1024,1024]{2,1,0:T(8,128)}, f32[2,1024,1024]{2,1,0:T(8,128)}, f32[2,1024,1024]{2,1,0:T(8,128)}) custom-call(f32[2,1024,1024]{2,1,0:T(8,128)} %refs_6_.9, f32[2,1024,1024]{2,1,0:T(8,128)} %refs_7_.7, f32[2,1024,1024]{2,1,0:T(8,128)} %refs_8_.7, f32[2,1024,1024]{2,1,0:T(8,128)} %refs_6_.9, f32[2,1024,1024]{2,1,0:T(8,128)} %refs_7_.7, ...), custom_call_target="tpu_custom_call" | custom-call | flops 104857600 | bytes 25165824 | tf_op jit(solution)/shard_map/flux_rows/pallas_call | solution.py:413
  108.9 0.0 all-to-all-done
  108.9 2.0 all_gather.3.refs_0_
  110.9 16.5 %responses.1 = f32[2,8,1024]{2,1,0:T(8,128)} custom-call(bf16[8,2048]{1,0:T(8,128)(2,1)} %all_gather.3.refs_0_, bf16[4,1024,2048]{2,1,0:T(8,128)(2,1)} %refs_4_.6, bf16[4,1024,2048]{2,1,0:T(8,128)(2,1)} %refs_4_.6, bf16[4,1024,2048]{2,1,0:T(8,128)(2,1)} %refs_4_.6, bf16[4,1024,2048]{2,1,0:T(8,128)(2,1)} %refs_4_.6, bf16[4,1024,2048]{2,1,0:T(8,128)(2,1)} %refs_8_.6, ...), custom_call_target="tpu_custom_call" | custom-call | flops 268435456 | bytes 33554432 | tf_op jit(solution)/shard_map/responses/pallas_call | solution.py:140
  127.4 1.9 broadcast_in_dim.4
  129.3 3.7 %all-to-all-start.1 = ((f32[16,2,8,1024]{3,2,1,0:T(8,128)}), f32[16,2,8,1024]{3,2,1,0:T(8,128)S(1)}, u32[]{:S(2)}, u32[]{:S(2)}) async-start(f32[16,2,8,1024]{3,2,1,0:T(8,128)} %broadcast_in_dim.4), calls=%async_computation.1 | async-start | bytes 2097152 | tf_op jit(solution)/shard_map/all_to_all | solution.py:553
  133.0 1.4 pad_maximum_fusion
  134.4 69.9 %flux_rows.3 = (f32[2,1024,1024]{2,1,0:T(8,128)}, f32[2,1024,1024]{2,1,0:T(8,128)}, f32[2,1024,1024]{2,1,0:T(8,128)}) custom-call(f32[2,1024,1024]{2,1,0:T(8,128)} %refs_6_.9, f32[2,1024,1024]{2,1,0:T(8,128)} %refs_7_.7, f32[2,1024,1024]{2,1,0:T(8,128)} %refs_8_.7, ...), custom_call_target="tpu_custom_call", output_to_operand_aliasing={{0}: (14, {}), {1}: (15, {}), {2}: (16, {})} | custom-call | flops 104857600 | bytes 25165824 | tf_op jit(solution)/shard_map/flux_rows/pallas_call | solution.py:413
  204.3 0.0 all-to-all-done.1
  204.3 1.1 slice_bitcast_fusion
  205.4 19.5 %add_gravity.1 = (f32[2,1024,1024]{2,1,0:T(8,128)}, f32[2,1024,1024]{2,1,0:T(8,128)}, f32[1024,1024]{1,0:T(8,128)}) custom-call(f32[128,1024]{1,0:T(8,128)} %get-tuple-element.47.refs_0_, f32[128,1024]{1,0:T(8,128)} %get-tuple-element.46.refs_1_, f32[1,1024]{1,0:T(1,128)} %bitcast.29, bf16[384,1024]{1,0:T(8,128)(2,1)} %get-tuple-element.70.refs_3_, ...), custom_call_target="tpu_custom_call" | custom-call | flops 2415919104 | bytes 46137344 | tf_op jit(solution)/shard_map/add_gravity/pallas_call | solution.py:470
  (12 shorter events, 0.1 us)
Async XLA Ops:
  15.0 93.9 %all-to-all-start = ((f32[16,8,1024]{2,1,0:T(8,128)}), f32[16,8,1024]{2,1,0:T(8,128)S(1)}, u32[]{:S(2)}, u32[]{:S(2)}) async-start(f32[16,8,1024]{2,1,0:T(8,128)} %bitcast.17), calls=%async_computation | async-start | bytes 1048576 | tf_op jit(solution)/shard_map/all_to_all | solution.py:541
  25.2 7.8 %collective-permute-start = (bf16[2,3,1024]{2,1,0:T(4,128)(2,1)S(1)}, bf16[2,3,1024]{2,1,0:T(4,128)(2,1)S(1)}, u32[]{:S(2)}, u32[]{:S(2)}) collective-permute-start(bf16[2,3,1024]{2,1,0:T(4,128)(2,1)S(1)} %fusion.7), channel_id=1, source_target_pairs={{0,1},{1,0},{2,3},{3,2},{4,5},{5,4},{6,7},{7,6},{8,9},{9,8},{10,11... | collective-permute-start | bytes 36872 | tf_op jit(solution)/shard_map/ppermute | solution.py:497
  25.3 13.1 %collective-permute-start.1 = (bf16[16,1024]{1,0:T(8,128)(2,1)}, bf16[16,1024]{1,0:T(8,128)(2,1)S(1)}, u32[]{:S(2)}, u32[]{:S(2)}) collective-permute-start(bf16[16,1024]{1,0:T(8,128)(2,1)} %get-tuple-element.22), channel_id=1, source_target_pairs={{0,2},{2,4},{4,6},{6,8},{8,10},{10,12},{12,14},{14,16},{16,18},{18... | collective-permute-start | bytes 98312 | tf_op jit(solution)/shard_map/ppermute | solution.py:513
  27.3 11.2 %collective-permute-start.2 = (bf16[16,1024]{1,0:T(8,128)(2,1)}, bf16[16,1024]{1,0:T(8,128)(2,1)S(1)}, u32[]{:S(2)}, u32[]{:S(2)}) collective-permute-start(bf16[16,1024]{1,0:T(8,128)(2,1)} %get-tuple-element.23), channel_id=1, source_target_pairs={{2,0},{4,2},{6,4},{8,6},{10,8},{12,10},{14,12},{16,14},{18,16},{20... | collective-permute-start | bytes 98312 | tf_op jit(solution)/shard_map/ppermute | solution.py:513
  38.4 0.6 copy-start
  38.4 0.6 copy-start.1
  129.3 75.0 %all-to-all-start.1 = ((f32[16,2,8,1024]{3,2,1,0:T(8,128)}), f32[16,2,8,1024]{3,2,1,0:T(8,128)S(1)}, u32[]{:S(2)}, u32[]{:S(2)}) async-start(f32[16,2,8,1024]{3,2,1,0:T(8,128)} %broadcast_in_dim.4), calls=%async_computation.1 | async-start | bytes 2097152 | tf_op jit(solution)/shard_map/all_to_all | solution.py:553

commit v6 on v1

v6 whole, which is shorter than its diff:
```python
import math

import jax
import jax.numpy as jnp
from jax import lax
from jax.experimental import pallas as pl
from jax.experimental.pallas import tpu as pltpu
from jax.sharding import PartitionSpec as P

aspect_sq = 0.0025
LANES = 128
SUB = 8
VMEM_BYTES = 60 << 20


def fetch_rows(refs, buffers, sems, steps):
    block = refs[0].shape[1] // steps

    def copy(k, place):
        if isinstance(place, int):
            rows = pl.ds(place * block, block)
        else:
            rows = pl.ds(pl.multiple_of(place * block, block), block)
        return pltpu.make_async_copy(refs[k].at[:, rows], buffers[k].at[:, rows], sems.at[k, place])

    @pl.when(pl.program_id(0) == 0)
    def _():
        for place in range(steps):
            for k in range(len(refs)):
                copy(k, place).start()

    for k in range(len(refs)):
        copy(k, pl.program_id(0)).wait()
    return pl.ds(pl.multiple_of(pl.program_id(0) * block, block), block)


def split_bf16(x):
    high = x.astype(jnp.bfloat16)
    low = (x - high.astype(jnp.float32)).astype(jnp.bfloat16)
    return high, low


def pieces_of(x, count):
    out = []
    for _ in range(count - 1):
        high = lax.reduce_precision(x, 8, 7)
        out.append(high.astype(jnp.bfloat16))
        x = x - high
    return out + [x.astype(jnp.bfloat16)]


EDGE_ROWS = 16


def modes_kernel(scale, steps, refs):
    firsts, lasts = refs[1:3], refs[3:5]
    *tables, out_ref, first_ref, last_ref, wide_ref, density, sems = refs[5:]
    thin_ref = tables[2]
    layers, _, cells = density.shape
    streams = min(4, cells // LANES)
    width = cells // streams
    rows_here = fetch_rows(refs[:1], [density], sems, steps)
    cols = thin_ref.shape[0]

    @pl.when(pl.program_id(0) == 0)
    def _():
        wide_ref[:cols] = tables[0][...]
        wide_ref[cols:] = tables[1][...]

    total = None
    for stream in range(streams):
        here = pl.ds(stream * width, width)
        x = density[0, rows_here, here]
        for layer in range(1, layers):
            x = x + density[layer, rows_here, here]
        high = x.astype(jnp.bfloat16)
        x = x - high.astype(jnp.float32)
        mid = x.astype(jnp.bfloat16)
        low = (x - mid.astype(jnp.float32)).astype(jnp.bfloat16)

        def product(a, table):
            return lax.dot_general(
                a, table, (((1,), (1,)), ((), ())), preferred_element_type=jnp.float32
            )

        both = wide_ref[:, here]
        major = product(high, both)
        minor = product(mid, both)
        small = product(low, both[:cols]) + product(high, thin_ref[:, here])
        part = major[:, :cols] + (major[:, cols:] + minor[:, :cols] + (minor[:, cols:] + small))
        total = part if total is None else total + part
    out_ref[...] = (scale * total).T

    block = out_ref.shape[1]
    lane = lax.broadcasted_iota(jnp.int32, (block, LANES), 1)
    edges = jnp.zeros((block, LANES), jnp.float32)
    for layer in range(layers):
        sides = (
            (0, 0, (density[layer, rows_here, :LANES], firsts[0][layer], firsts[1][layer])),
            (
                EDGE_ROWS,
                LANES - 1,
                (density[layer, rows_here, cells - LANES :], lasts[0][layer], lasts[1][layer]),
            ),
        )
        for base, place, tiles in sides:
            for comp, tile in enumerate(tiles):
                edges = jnp.where(
                    lane == base + 3 * layer + comp,
                    jnp.broadcast_to(tile[:, place : place + 1], (block, LANES)),
                    edges,
                )
    edges = edges.T
    first_ref[...] = edges[:EDGE_ROWS].astype(jnp.bfloat16)
    last_ref[...] = edges[EDGE_ROWS : 2 * EDGE_ROWS].astype(jnp.bfloat16)


def surface_modes(fields, tables, scale):
    layers, rows, cells = fields[0].shape
    cols = tables[0].shape[0]
    block = min(rows, LANES)
    first = pl.BlockSpec((layers, block, LANES), lambda i: (0, i, 0))
    last = pl.BlockSpec((layers, block, LANES), lambda i: (0, i, cells // LANES - 1))
    table_spec = pl.BlockSpec((cols, cells), lambda i: (0, 0))
    edge_spec = pl.BlockSpec((EDGE_ROWS, block), lambda i: (0, i))
    edge_shape = jax.ShapeDtypeStruct((EDGE_ROWS, rows), jnp.bfloat16)
    return pl.pallas_call(
        lambda *refs: modes_kernel(scale, rows // block, refs),
        grid=(rows // block,),
        in_specs=[pl.BlockSpec(memory_space=pl.ANY)]
        + [first, first, last, last] + [table_spec] * 3,
        out_specs=[pl.BlockSpec((cols, block), lambda i: (0, i)), edge_spec, edge_spec],
        out_shape=[jax.ShapeDtypeStruct((cols, rows), jnp.float32), edge_shape, edge_shape],
        scratch_shapes=[
            pltpu.VMEM((2 * cols, cells), jnp.bfloat16),
            pltpu.VMEM(fields[0].shape, jnp.float32),
            pltpu.SemaphoreType.DMA((1, rows // block)),
        ],
        compiler_params=pltpu.CompilerParams(vmem_limit_bytes=VMEM_BYTES),
        cost_estimate=pl.CostEstimate(
            flops=12 * rows * cells * cols, bytes_accessed=4 * fields[0].size, transcendentals=0
        ),
        name="surface_modes",
    )(*fields, fields[1], fields[2], *tables)


def response_kernel(steps, refs):
    pairs_ref, pot_ref, force_ref, out_ref, pot_buffer, force_buffer, sems = refs
    pairs = pairs_ref[...]
    buffers = (pot_buffer, force_buffer)
    rows_here = fetch_rows((pot_ref, force_ref), buffers, sems, steps)
    block, cols = out_ref.shape[3], pairs.shape[0]
    mode_of = lax.broadcasted_iota(jnp.int32, (block, cols), 1) // 2
    for place, buffer in enumerate(buffers):
        total = jnp.zeros(mode_of.shape, jnp.float32)
        for mode in range(buffer.shape[0]):
            part = lax.dot_general(
                buffer[mode, rows_here, :],
                pairs,
                (((1,), (1,)), ((), ())),
                preferred_element_type=jnp.float32,
            )
            total = jnp.where(mode_of == mode, part, total)
        out_ref[:, place] = jnp.broadcast_to(total.T[None], (out_ref.shape[0], cols, block))


def responses(pairs, potential_kernel, force_kernel, copies):
    mode_count, rows, count = potential_kernel.shape
    cols = pairs.shape[0]
    block = min(rows, LANES)
    steps = rows // block
    whole = pl.BlockSpec(memory_space=pl.ANY)
    return pl.pallas_call(
        lambda *refs: response_kernel(steps, refs),
        grid=(steps,),
        in_specs=[pl.BlockSpec((cols, count), lambda i: (0, 0)), whole, whole],
        out_specs=pl.BlockSpec((copies, 2, cols, block), lambda i: (0, 0, 0, i)),
        out_shape=jax.ShapeDtypeStruct((copies, 2, cols, rows), jnp.float32),
        scratch_shapes=[
            pltpu.VMEM(potential_kernel.shape, potential_kernel.dtype),
            pltpu.VMEM(force_kernel.shape, force_kernel.dtype),
            pltpu.SemaphoreType.DMA((2, steps)),
        ],
        compiler_params=pltpu.CompilerParams(vmem_limit_bytes=VMEM_BYTES),
        cost_estimate=pl.CostEstimate(
            flops=4 * rows * count * cols * mode_count,
            bytes_accessed=4 * potential_kernel.size,
            transcendentals=0,
        ),
        name="responses",
    )(pairs, potential_kernel, force_kernel)


ROOT_FACE, SOUND_FACE, IN, OUT, ROOT_MID, SOUND_MID, AZ, SPIN, PULL = range(9)
COEFS = 16


def row_coefficients(first_row, rows, step):
    face = jnp.exp((first_row + jnp.arange(rows + LANES + 1)).astype(jnp.float32) * step)
    inner, outer = face[:-1], face[1:]
    mid = 0.5 * (inner + outer)
    area = 0.5 * (outer * outer - inner * inner)
    sound_face = aspect_sq / inner
    sound_mid = aspect_sq / mid
    radial = (0.05 * step) / area
    columns = [
        jnp.sqrt(sound_face),
        sound_face,
        radial * inner,
        radial * outer,
        jnp.sqrt(sound_mid),
        sound_mid,
        0.05 / mid,
        (0.1 * step) / mid,
        (0.1 * step) / (mid * mid),
    ]
    columns += [jnp.zeros_like(mid)] * (COEFS - len(columns))
    return jnp.stack(columns, axis=0), (-0.1 / mid)[None, :rows]


def inverse(x):
    guess = pl.reciprocal(x, approx=True)
    return guess * (2.0 - x * guess)


class FluxBlock:
    def __init__(self, block_count, refs):
        self.fields = refs[0:3]
        self.before = refs[3:6]
        self.after = refs[6:9]
        self.rim_in, self.rim_out, coef_rows, low_rows, high_rows, coef_after = refs[9:15]
        self.block_count = block_count
        self.rows, cells = self.fields[0].shape
        self.columns = cells // LANES
        self.strips = self.rows // SUB
        self.index = pl.program_id(0)
        self.lane = lax.broadcasted_iota(jnp.int32, (SUB, LANES), 1)
        self.sub = lax.broadcasted_iota(jnp.int32, (SUB, LANES), 0)
        side_rows = jnp.concatenate(
            [coef_rows[...], low_rows[...].astype(jnp.float32), high_rows[...].astype(jnp.float32)], axis=0
        )
        filler = jnp.zeros((LANES - side_rows.shape[0], self.rows), jnp.float32)
        self.side = jnp.concatenate([side_rows, filler], axis=0).T
        self.coef_after = coef_after

    def wide(self, column):
        return jnp.broadcast_to(column, (SUB, LANES))

    def at(self, col):
        return pl.ds(col * LANES, LANES)

    def rows_at(self, place):
        return pl.ds(pl.multiple_of(place * SUB, SUB), SUB)

    def radial_state(self, state):
        density, mom_r, mom_phi = state
        inv = inverse(density)
        vel = mom_r * inv
        return inv, (density, mom_r, mom_phi, jnp.abs(vel), mom_r * vel, mom_phi * vel)

    def radial_flux(self, upper, lower, root, sound):
        speed = jnp.maximum(upper[3], lower[3]) + root
        return (
            (upper[1] + lower[1]) - speed * (upper[0] - lower[0]),
            ((upper[4] + lower[4]) + sound * (upper[0] + lower[0]))
            - speed * (upper[1] - lower[1]),
            (upper[5] + lower[5]) - speed * (upper[2] - lower[2]),
        )

    def azimuth_flux(self, upper, lower, root):
        speed = jnp.maximum(upper[3], lower[3]) + root
        return (
            (upper[2] + lower[2]) - speed * (upper[0] - lower[0]),
            (upper[4] + lower[4]) - speed * (upper[1] - lower[1]),
            (upper[5] + lower[5]) - speed * (upper[2] - lower[2]),
        )

    def azimuth_values(self, state, inv, cross, sound):
        density, mom_r, mom_phi = state
        vel = mom_phi * inv
        return density, mom_r, mom_phi, jnp.abs(vel), cross, mom_phi * vel + sound * density

    def ghost_values(self, layer, coef, side, sound):
        base = COEFS + side * EDGE_ROWS + 3 * layer
        state = [self.wide(coef[:, base + c : base + c + 1]) for c in range(3)]
        inv = inverse(state[0])
        return self.azimuth_values(state, inv, state[1] * state[2] * inv, sound)

    def row_before(self, col):
        return self.edge_row(col, self.index == 0, self.rim_in, self.before, SUB - 1)

    def row_after(self, col):
        return self.edge_row(col, self.index == self.block_count - 1, self.rim_out, self.after, 0)

    def edge_row(self, col, edge, rim, near, row):
        state = []
        for comp in range(3):
            value = jnp.where(
                edge, rim[comp : comp + 1, self.at(col)], near[comp][row : row + 1, self.at(col)]
            )
            state.append(jnp.broadcast_to(value, (SUB, LANES)))
        return self.radial_state(state)[1]

    def columns_of(self, coef, names):
        return [self.wide(coef[:, k : k + 1]) for k in names]


def joint_flux(layer, block_count, refs):
    block = FluxBlock(block_count, refs)
    outs = refs[-6:-3]
    above, lagged, side = refs[-3:]
    side[...] = block.side
    lane, sub, at, fields = block.lane, block.sub, block.at, block.fields
    columns = block.columns

    def keep_above(col, rolled):
        for slot, value in enumerate(rolled):
            above[slot, :, at(col)] = value

    def finish(rows_before, col, turned, out_coef):
        for comp in range(3):
            up = jnp.where(sub == SUB - 1, turned[comp], lagged[comp, :, at(col)])
            outs[comp][rows_before, at(col)] -= out_coef * up

    for col in range(columns):
        keep_above(col, block.row_before(col))

    def strip(place, carry):
        here = block.rows_at(place)
        rows_before = block.rows_at(jnp.maximum(place - 1, 0))
        coef = side[here, :]
        root_face, sound_face, in_coef, root_mid, sound_mid, az, spin, pull = block.columns_of(
            coef, (ROOT_FACE, SOUND_FACE, IN, ROOT_MID, SOUND_MID, AZ, SPIN, PULL)
        )
        (out_before,) = block.columns_of(side[rows_before, :], (OUT,))
        turned = block.ghost_values(layer, coef, 0, sound_mid)
        held = held_flux = None

        def settle(col, held, held_flux, flux):
            for comp in range(3):
                up = jnp.where(
                    lane == LANES - 1,
                    pltpu.roll(flux[comp], LANES - 1, 1),
                    pltpu.roll(held_flux[comp], LANES - 1, 1),
                )
                outs[comp][here, at(col)] = held[comp] - az * (up - held_flux[comp])

        for col in range(columns):
            state = [ref[here, at(col)] for ref in fields]
            inv, values = block.radial_state(state)
            rolled = [pltpu.roll(value, 1, 0) for value in values]
            lower = [
                jnp.where(sub == 0, above[slot, :, at(col)], value)
                for slot, value in enumerate(rolled)
            ]
            flux_r = block.radial_flux(values, lower, root_face, sound_face)
            turned_r = [pltpu.roll(value, SUB - 1, 0) for value in flux_r]
            finish(rows_before, col, turned_r, out_before)
            keep_above(col, rolled)
            for comp in range(3):
                lagged[comp, :, at(col)] = turned_r[comp]
            values = block.azimuth_values(state, inv, values[5], sound_mid)
            rolled = [pltpu.roll(value, 1, 1) for value in values]
            lower = [jnp.where(lane == 0, a, b) for a, b in zip(turned, rolled)]
            turned = rolled
            flux = block.azimuth_flux(values, lower, root_mid)
            if col > 0:
                settle(col - 1, held, held_flux, flux)
            held = (
                state[0] + in_coef * flux_r[0],
                state[1] + in_coef * flux_r[1] + (spin * values[5] - pull * state[0]),
                state[2] + in_coef * flux_r[2] - spin * values[4],
            )
            held_flux = flux
        values = block.ghost_values(layer, coef, 1, sound_mid)
        settle(columns - 1, held, held_flux, block.azimuth_flux(values, turned, root_mid))
        return carry

    lax.fori_loop(0, block.strips, strip, 0)

    last = pl.ds((block.strips - 1) * SUB, SUB)
    after = block.coef_after[...].T
    root_face, sound_face = block.columns_of(after[:SUB], (ROOT_FACE, SOUND_FACE))
    (out_coef,) = block.columns_of(side[last, :], (OUT,))
    for col in range(columns):
        lower = [above[slot, :, at(col)] for slot in range(6)]
        flux_r = block.radial_flux(block.row_after(col), lower, root_face, sound_face)
        finish(last, col, [pltpu.roll(value, SUB - 1, 0) for value in flux_r], out_coef)


def split_flux(layer, block_count, refs):
    block = FluxBlock(block_count, refs)
    outs = refs[-7:-4]
    above, lagged, side, part = refs[-4:]
    side[...] = block.side
    lane, sub, at, fields = block.lane, block.sub, block.at, block.fields
    columns = block.columns

    def azimuth_strip(place, carry):
        here = block.rows_at(place)
        coef = side[here, :]
        root_mid, sound_mid, az, spin, pull = block.columns_of(
            coef, (ROOT_MID, SOUND_MID, AZ, SPIN, PULL)
        )
        turned = block.ghost_values(layer, coef, 0, sound_mid)
        held = turned_held = None

        def settle(col, turned_flux):
            for comp in range(3):
                up = jnp.where(lane == LANES - 1, turned_flux[comp], turned_held[comp])
                part[comp, here, at(col)] = held[comp] - az * up

        for col in range(columns):
            state = [ref[here, at(col)] for ref in fields]
            inv = inverse(state[0])
            vel = state[2] * inv
            values = (
                *state, jnp.abs(vel), state[1] * vel, state[2] * vel + sound_mid * state[0]
            )
            rolled = [pltpu.roll(value, 1, 1) for value in values]
            lower = [jnp.where(lane == 0, a, b) for a, b in zip(turned, rolled)]
            turned = rolled
            flux = block.azimuth_flux(values, lower, root_mid)
            turned_flux = [pltpu.roll(value, LANES - 1, 1) for value in flux]
            if col > 0:
                settle(col - 1, turned_flux)
            held = (
                state[0] + az * flux[0],
                state[1] + az * flux[1] + (spin * values[5] - pull * state[0]),
                state[2] + az * flux[2] - spin * values[4],
            )
            turned_held = turned_flux
        flux = block.azimuth_flux(block.ghost_values(layer, coef, 1, sound_mid), turned, root_mid)
        settle(columns - 1, [pltpu.roll(value, LANES - 1, 1) for value in flux])
        return carry

    lax.fori_loop(0, block.strips, azimuth_strip, 0)

    for col in range(columns):
        for slot, value in enumerate(block.row_before(col)):
            above[slot, :, at(col)] = value

    def finish(place, col, turned, in_coef, out_coef):
        here = block.rows_at(place)
        for comp in range(3):
            low = lagged[comp, :, at(col)]
            up = jnp.where(sub == SUB - 1, turned[comp], pltpu.roll(low, SUB - 1, 0))
            outs[comp][here, at(col)] = part[comp, here, at(col)] + (in_coef * low - out_coef * up)

    def radial_strip(place, carry):
        here = block.rows_at(place)
        earlier = jnp.maximum(place - 1, 0)
        root_face, sound_face = block.columns_of(side[here, :], (ROOT_FACE, SOUND_FACE))
        in_coef, out_coef = block.columns_of(side[block.rows_at(earlier), :], (IN, OUT))
        for col in range(columns):
            values = block.radial_state([ref[here, at(col)] for ref in fields])[1]
            rolled = [pltpu.roll(value, 1, 0) for value in values]
            lower = [
                jnp.where(sub == 0, above[slot, :, at(col)], value)
                for slot, value in enumerate(rolled)
            ]
            for slot, value in enumerate(rolled):
                above[slot, :, at(col)] = value
            flux = block.radial_flux(values, lower, root_face, sound_face)
            finish(earlier, col, [pltpu.roll(value, SUB - 1, 0) for value in flux], in_coef, out_coef)
            for comp in range(3):
                lagged[comp, :, at(col)] = flux[comp]
        return carry

    lax.fori_loop(0, block.strips, radial_strip, 0)

    after = block.coef_after[...].T
    root_face, sound_face = block.columns_of(after[:SUB], (ROOT_FACE, SOUND_FACE))
    in_coef, out_coef = block.columns_of(
        side[(block.strips - 1) * SUB : block.strips * SUB, :], (IN, OUT)
    )
    for col in range(columns):
        lower = [above[slot, :, at(col)] for slot in range(6)]
        flux = block.radial_flux(block.row_after(col), lower, root_face, sound_face)
        turned = [pltpu.roll(value, SUB - 1, 0) for value in flux]
        finish(block.strips - 1, col, turned, in_coef, out_coef)


def flux_layer(layer, kernel, fields, rims, edges, coefs, so_far):
    layers, rows, cells = fields[0].shape
    block = min(rows, LANES)
    count = rows // block
    per = block // SUB
    main = pl.BlockSpec((None, block, cells), lambda i: (layer, i, 0))
    before = pl.BlockSpec((None, SUB, cells), lambda i: (layer, jnp.maximum(i * per - 1, 0), 0))
    after = pl.BlockSpec(
        (None, SUB, cells), lambda i: (layer, jnp.minimum((i + 1) * per, rows // SUB - 1), 0)
    )
    rim = pl.BlockSpec((None, 3, cells), lambda i: (layer, 0, 0))
    operands = [*fields, *fields, *fields, *rims, coefs, *edges, coefs]
    specs = [main] * 3 + [before] * 3 + [after] * 3 + [
        rim,
        rim,
        pl.BlockSpec((COEFS, block), lambda i: (0, i)),
        pl.BlockSpec((EDGE_ROWS, block), lambda i: (0, i)),
        pl.BlockSpec((EDGE_ROWS, block), lambda i: (0, i)),
        pl.BlockSpec((COEFS, LANES), lambda i: (0, (i + 1) * (block // LANES))),
    ]
    aliases = {}
    if so_far is not None:
        for k, array in enumerate(so_far):
            aliases[len(operands)] = k
            operands.append(array)
            specs.append(pl.BlockSpec(memory_space=pl.ANY))
    scratch = [
        pltpu.VMEM((6, SUB, cells), jnp.float32),
        pltpu.VMEM((3, SUB, cells), jnp.float32),
        pltpu.VMEM((block, LANES), jnp.float32),
    ]
    if kernel is split_flux:
        scratch.append(pltpu.VMEM((3, block, cells), jnp.float32))
    return pl.pallas_call(
        lambda *refs: kernel(layer, count, refs),
        grid=(count,),
        in_specs=specs,
        out_specs=[main] * 3,
        out_shape=[jax.ShapeDtypeStruct(f.shape, f.dtype) for f in fields],
        scratch_shapes=scratch,
        input_output_aliases=aliases,
        compiler_params=pltpu.CompilerParams(vmem_limit_bytes=VMEM_BYTES),
        cost_estimate=pl.CostEstimate(
            flops=100 * rows * cells, bytes_accessed=24 * rows * cells, transcendentals=rows * cells
        ),
        name=kernel.__name__,
    )(*operands)


def gravity_kernel(steps, refs):
    pot_ref, force_ref, inverse_ref = refs[:3]
    halves = refs[3:7]
    out_r, out_phi, out_pot, table_ref, slope_ref, *buffers, sems = refs[10:]
    density, mom_r, mom_phi = buffers
    rows_here = fetch_rows(refs[7:10], buffers, sems, steps)
    cols = pot_ref.shape[0]

    @pl.when(pl.program_id(0) == 0)
    def _():
        for ref, (high, low) in ((table_ref, halves[:2]), (slope_ref, halves[2:])):
            ref[:cols] = high[...]
            ref[cols : 2 * cols] = high[...]
            ref[2 * cols :] = low[...]


    def product(a, table):
        high, low = split_bf16(a)
        return lax.dot_general(
            jnp.concatenate([high, low, high], axis=0),
            table,
            (((0,), (0,)), ((), ())),
            preferred_element_type=jnp.float32,
        )

    pot = pot_ref[...]
    out_pot[...] = product(pot, table_ref[...])
    radial = product(force_ref[...] * 0.1, table_ref[...])
    azimuth = product(pot * inverse_ref[...], slope_ref[...])
    for layer in range(density.shape[0]):
        here = density[layer, rows_here, :]
        out_r[layer] = mom_r[layer, rows_here, :] + here * radial
        out_phi[layer] = mom_phi[layer, rows_here, :] + here * azimuth


def add_gravity(pot, force, inverse_mid, tables, density, mom_r, mom_phi):
    layers, rows, cells = density.shape
    cols = pot.shape[0]
    block = min(rows, LANES)
    modes_spec = pl.BlockSpec((cols, block), lambda i: (0, i))
    table_spec = pl.BlockSpec((cols, cells), lambda i: (0, 0))

    field = pl.BlockSpec((layers, block, cells), lambda i: (0, i, 0))
    grid_shape = jax.ShapeDtypeStruct(density.shape, density.dtype)
    return pl.pallas_call(
        lambda *refs: gravity_kernel(rows // block, refs),
        grid=(rows // block,),
        in_specs=[
            modes_spec, modes_spec, pl.BlockSpec((1, block), lambda i: (0, i)),
        ] + [table_spec] * 4 + [pl.BlockSpec(memory_space=pl.ANY)] * 3,
        out_specs=[field, field, pl.BlockSpec((block, cells), lambda i: (i, 0))],
        out_shape=[grid_shape, grid_shape, jax.ShapeDtypeStruct((rows, cells), jnp.float32)],
        scratch_shapes=[pltpu.VMEM((3 * cols, cells), jnp.bfloat16)] * 2
        + [pltpu.VMEM(density.shape, density.dtype)] * 3
        + [pltpu.SemaphoreType.DMA((3, rows // block))],
        compiler_params=pltpu.CompilerParams(vmem_limit_bytes=VMEM_BYTES),
        cost_estimate=pl.CostEstimate(
            flops=18 * rows * cells * cols, bytes_accessed=44 * rows * cells, transcendentals=0
        ),
        name="add_gravity",
    )(
        pot, force, inverse_mid, *tables,
        density, mom_r, mom_phi,
    )


def exchange_rims(fields, rad_index, rad_count):
    first = jnp.stack([f[:, 0] for f in fields], axis=1)
    last = jnp.stack([f[:, -1] for f in fields], axis=1)
    if rad_count == 1:
        return first, last
    first_out, last_out = first.astype(jnp.bfloat16), last.astype(jnp.bfloat16)
    if rad_count == 2:
        other = lax.ppermute(
            jnp.where(rad_index == 0, last_out, first_out), "rad", [(0, 1), (1, 0)]
        )
        low = high = other
    else:
        up = [(i, i + 1) for i in range(rad_count - 1)]
        low = lax.ppermute(last_out, "rad", up)
        high = lax.ppermute(first_out, "rad", [(b, a) for a, b in up])
    rim_in = jnp.where(rad_index == 0, first, low.astype(first.dtype))
    rim_out = jnp.where(rad_index == rad_count - 1, last, high.astype(last.dtype))
    return rim_in, rim_out


def exchange_edges(first, last, az_count):
    right = [(i, (i + 1) % az_count) for i in range(az_count)]
    left = [(b, a) for a, b in right]
    return lax.ppermute(last, "az", right), lax.ppermute(first, "az", left)


def local(az_count, rad_count, density, mom_r, mom_phi, potential_kernel, force_kernel):
    layers, rows, cells = density.shape
    mode_count = potential_kernel.shape[0]
    pair_count = 2 * mode_count
    cols = az_count * pair_count
    step = 2.0 * math.pi / (az_count * cells)
    az_index = lax.axis_index("az")
    rad_index = lax.axis_index("rad")
    fields = (density, mom_r, mom_phi)

    azimuth = ((az_index * cells + jnp.arange(cells)).astype(jnp.float32) + 0.5) * step
    row = lax.broadcasted_iota(jnp.int32, (cols, cells), 0)
    mode = (row // 2).astype(jnp.float32)
    angle = azimuth[None, :] * mode
    cosine, sine = jnp.cos(angle), jnp.sin(angle)
    basis = pieces_of(jnp.where(row % 2 == 0, cosine, sine), 3)
    slope = pieces_of(jnp.where(row % 2 == 0, -mode * sine, mode * cosine), 2)

    rims = exchange_rims(fields, rad_index, rad_count)
    coefs, inverse_mid = row_coefficients(rad_index * rows, rows, step)

    partial, first, last = surface_modes(fields, basis, 1.0 / (az_count * cells))
    edges = exchange_edges(first, last, az_count)
    pieces = lax.all_to_all(
        partial.reshape(az_count, pair_count, rows), "az", split_axis=0, concat_axis=0, tiled=True
    )
    results = flux_layer(0, joint_flux, fields, rims, edges, coefs, None)
    pieces, results = lax.optimization_barrier((pieces, results))

    own = jnp.sum(pieces, axis=0).astype(jnp.bfloat16)
    pairs = lax.all_gather(own, "rad", axis=1, tiled=True)
    parts = responses(pairs, potential_kernel, force_kernel, az_count)
    every = lax.all_to_all(parts, "az", split_axis=0, concat_axis=0, tiled=True)
    coefs, parts = lax.optimization_barrier((coefs, parts))
    for layer in range(1, layers):
        results = flux_layer(layer, split_flux, fields, rims, edges, coefs, results)
    pot = every[:, 0].reshape(cols, rows)
    force = every[:, 1].reshape(cols, rows)

    new_r, new_phi, potential = add_gravity(
        pot,
        force,
        inverse_mid,
        (basis[0], basis[1], *slope),
        density,
        results[1],
        results[2],
    )
    return results[0], new_r, new_phi, potential


def solution(mesh):
    az_count, rad_count = mesh.shape["az"], mesh.shape["rad"]
    field = P(None, "rad", "az")
    kernel = P("az", "rad", None)
    return jax.shard_map(
        lambda *args: local(az_count, rad_count, *args),
        mesh=mesh,
        in_specs=(field, field, field, kernel, kernel),
        out_specs=(field, field, field, P("rad", "az")),
        check_vma=False,
    )
```

time: 206 us -> 170 us (0.83)
  local copies, waits for them, and re-layouts: 37.3 us -> 4.92 us
  Pallas kernels: 113 us -> 133 us
  between operations: 14.3 us -> 0.87 us
  other arithmetic: 16.9 us -> 4.75 us
  starting transfers between devices: 14.2 us -> 17.8 us
    unnamed x16 -> x4, local copies, waits for them, and re-layouts: 29.5 us -> 0.62 us
    pallas_call x5, Pallas kernels: 113 us -> 133 us  [the longest x2 89.3 us: flux_layer(): pl.pallas_call(lambda *refs: kernel(layer, count, refs), grid=(count,), i...]
    another operation x5 -> x0, other arithmetic: 14.2 us -> none
    all_to_all x1, waiting for transfers between devices: 7.02 us -> 0.01 us  [local(): lax.all_to_all(partial.reshape(az_count, pair_count, rows), 'az', split_a...]
    ppermute x2, waiting for transfers between devices: 0.01 us -> 5.18 us  [exchange_edges(): return (lax.ppermute(last, 'az', right), lax.ppermute(first, 'az', left))]
    all_to_all x0 -> x1, starting transfers between devices: none -> 3.71 us  [local(): every = lax.all_to_all(parts, 'az', split_axis=0, concat_axis=0, tiled=True)]
    slice x3 -> x0, local copies, waits for them, and re-layouts: 2.9 us -> none  [exchange_edges(): f[:, :, -1]]
  transfers between devices with their start and end apart: 5 -> 5, of which waited for: 1 -> 1; matrix products, arithmetic and copies ran while one was open for 10% -> 3% of each run, Pallas kernels for 44% -> 53%
where the time goes in v6:
time: 170 us; the launch traced here: 169 us
  Pallas kernels  133 us (78%)
  starting transfers between devices  17.8 us (10%)
  waiting for transfers between devices  5.19 us (3%)
  local copies, waits for them, and re-layouts  4.92 us (3%)
  other arithmetic  4.75 us (3%)
  blocking collectives  1.96 us (1%)
    pallas_call x2, Pallas kernels, flux_layer(): pl.pallas_call(lambda *refs: kernel(layer, count, refs), grid=(count,), i...  89.3 us
    pallas_call x1, Pallas kernels, add_gravity(): pl.pallas_call(lambda *refs: gravity_kernel(rows // block, refs), grid=(r...  19 us
    pallas_call x1, Pallas kernels, responses(): pl.pallas_call(lambda *refs: response_kernel(steps, refs), grid=(steps,),...  13.9 us
    pallas_call x1, Pallas kernels, surface_modes(): pl.pallas_call(lambda *refs: modes_kernel(scale, rows // block, refs), gr...  11.1 us
    all_to_all x1, starting transfers between devices, local(): lax.all_to_all(partial.reshape(az_count, pair_count, rows), 'az', split_a...  8.32 us
    ppermute x2, starting transfers between devices, exchange_edges(): return (lax.ppermute(last, 'az', right), lax.ppermute(first, 'az', left))  5.67 us
    ppermute x2, waiting for transfers between devices, exchange_edges(): return (lax.ppermute(last, 'az', right), lax.ppermute(first, 'az', left))  5.18 us
    all_to_all x1, starting transfers between devices, local(): every = lax.all_to_all(parts, 'az', split_axis=0, concat_axis=0, tiled=True)  3.71 us
  transfers between devices with their start and end apart: 5, of which 1 were waited for; matrix products, arithmetic and copies ran while one was open for 3% of the time, Pallas kernels for 53%

profile of v6, /device:TPU:0, one launch (start us, length us, event | category | flops | bytes accessed | tf_op | source)
XLA Modules:
  0.0 168.8 jit_solution(2291885859166928844)
XLA Ops:
  0.7 3.3 %fusion.1 = (bf16[128,1024]{1,0:T(8,128)(2,1)}, bf16[128,1024]{1,0:T(8,128)(2,1)}, bf16[128,1024]{1,0:T(8,128)(2,1)}, bf16[128,1024]{1,0:T(8,128)(2,1)}, bf16[128,1024]{1,0:T(8,128)(2,1)}) fusion(s32[128]{0:T(128)S(1)} %get-tuple-element.67, s32[128]{0:T(128)S(1)} %get-tuple-element.69, f32[1024]{0:T(1024)S(1)} %add_multiply_fusion.1, ...), kind=kLoop, calls=%fused_computation.7 | loop fusion | flops 2752512 | bytes 1317120 | tf_op jit(solution)/shard_map/convert_element_type | solution.py:49
  4.0 11.1 %surface_modes.1 = (f32[128,1024]{1,0:T(8,128)}, bf16[16,1024]{1,0:T(8,128)(2,1)}, bf16[16,1024]{1,0:T(8,128)(2,1)}) custom-call(f32[2,1024,1024]{2,1,0:T(8,128)} %refs_7_.5, f32[2,1024,1024]{2,1,0:T(8,128)} %refs_7_.4, f32[2,1024,1024]{2,1,0:T(8,128)} %refs_8_.3, f32[2,1024,1024]{2,1,0:T(8,128)} %refs_7_.4, f32[2,1024,1024]{2,1,0:T(8,128)} %refs_8_.3, ...), custom_call_target="tpu_custom_call" | custom-call | flops 1610612736 | bytes 8388608 | tf_op jit(solution)/shard_map/surface_modes/pallas_call | solution.py:127
  15.0 8.3 %all-to-all-start = ((f32[16,8,1024]{2,1,0:T(8,128)}), f32[16,8,1024]{2,1,0:T(8,128)S(1)}, u32[]{:S(2)}, u32[]{:S(2)}) async-start(f32[16,8,1024]{2,1,0:T(8,128)} %bitcast.6), calls=%async_computation | async-start | bytes 1048576 | tf_op jit(solution)/shard_map/all_to_all | solution.py:648
  23.4 1.0 fusion.12
  24.3 0.9 fusion.14
  25.2 0.1 fusion.7
  25.3 0.1 collective-permute-start
  25.4 2.0 %collective-permute-start.1 = (bf16[16,1024]{1,0:T(8,128)(2,1)}, bf16[16,1024]{1,0:T(8,128)(2,1)S(1)}, u32[]{:S(2)}, u32[]{:S(2)}) collective-permute-start(bf16[16,1024]{1,0:T(8,128)(2,1)} %get-tuple-element.22), channel_id=1, source_target_pairs={{0,2},{2,4},{4,6},{6,8},{8,10},{10,12},{12,14},{14,16},{16,18},{18... | collective-permute-start | bytes 98312 | tf_op jit(solution)/shard_map/ppermute | solution.py:622
  27.3 3.7 %collective-permute-start.2 = (bf16[16,1024]{1,0:T(8,128)(2,1)}, bf16[16,1024]{1,0:T(8,128)(2,1)S(1)}, u32[]{:S(2)}, u32[]{:S(2)}) collective-permute-start(bf16[16,1024]{1,0:T(8,128)(2,1)} %get-tuple-element.23), channel_id=1, source_target_pairs={{2,0},{4,2},{6,4},{8,6},{10,8},{12,10},{14,12},{16,14},{18,16},{20... | collective-permute-start | bytes 98312 | tf_op jit(solution)/shard_map/ppermute | solution.py:622
  31.0 0.1 multiply_divide_fusion
  31.3 1.3 stack.55.refs_11_.refs_14_
  32.6 0.0 collective-permute-done
  32.6 0.7 convert_select_fusion
  33.3 5.2 %collective-permute-done.1.refs_12_ = bf16[16,1024]{1,0:T(8,128)(2,1)S(1)} collective-permute-done((bf16[16,1024]{1,0:T(8,128)(2,1)}, bf16[16,1024]{1,0:T(8,128)(2,1)S(1)}, u32[]{:S(2)}, u32[]{:S(2)}) %collective-permute-start.1) | collective-permute-done | bytes 32800 | tf_op jit(solution)/shard_map/ppermute | solution.py:622
  38.5 0.0 copy-start
  38.5 0.0 collective-permute-done.2.refs_13_
  38.5 0.0 copy-start.1
  38.5 0.6 copy-done
  39.1 0.0 copy-done.1
  39.1 39.6 %joint_flux.1 = (f32[2,1024,1024]{2,1,0:T(8,128)}, f32[2,1024,1024]{2,1,0:T(8,128)}, f32[2,1024,1024]{2,1,0:T(8,128)}) custom-call(f32[2,1024,1024]{2,1,0:T(8,128)} %refs_7_.5, f32[2,1024,1024]{2,1,0:T(8,128)} %refs_7_.4, f32[2,1024,1024]{2,1,0:T(8,128)} %refs_8_.3, f32[2,1024,1024]{2,1,0:T(8,128)} %refs_7_.5, f32[2,1024,1024]{2,1,0:T(8,128)} %refs_7_.4, ...), custom_call_target="tpu_custom_call" | custom-call | flops 104857600 | bytes 25165824 | tf_op jit(solution)/shard_map/joint_flux/pallas_call | solution.py:517
  78.7 0.0 all-to-all-done
  78.8 2.0 %all_gather.3.refs_0_ = bf16[8,2048]{1,0:T(8,128)(2,1)} all-gather(bf16[8,1024]{1,0:T(8,128)(2,1)S(1)} %reduce_sum.9), channel_id=1, replica_groups=mesh['az'=16,'rad'=2] {'rad'}, dimensions={1}, use_global_device_ids=true | all-gather | bytes 49152 | tf_op jit(solution)/shard_map/all_gather | solution.py:655
  80.7 13.9 %responses.1 = f32[16,2,8,1024]{3,2,1,0:T(8,128)} custom-call(bf16[8,2048]{1,0:T(8,128)(2,1)} %all_gather.3.refs_0_, bf16[4,1024,2048]{2,1,0:T(8,128)(2,1)} %refs_1_.6, bf16[4,1024,2048]{2,1,0:T(8,128)(2,1)} %refs_2_.6), custom_call_target="tpu_custom_call" | custom-call | flops 268435456 | bytes 33554432 | tf_op jit(solution)/shard_map/responses/pallas_call | solution.py:173
  94.6 3.7 %all-to-all-start.1 = ((f32[16,2,8,1024]{3,2,1,0:T(8,128)}), f32[16,2,8,1024]{3,2,1,0:T(8,128)S(1)}, u32[]{:S(2)}, u32[]{:S(2)}) async-start(f32[16,2,8,1024]{3,2,1,0:T(8,128)} %responses.1), calls=%async_computation.1 | async-start | bytes 2097152 | tf_op jit(solution)/shard_map/all_to_all | solution.py:657
  98.4 0.6 slice_divide_fusion.1
  99.0 49.7 %split_flux.1 = (f32[2,1024,1024]{2,1,0:T(8,128)}, f32[2,1024,1024]{2,1,0:T(8,128)}, f32[2,1024,1024]{2,1,0:T(8,128)}) custom-call(f32[2,1024,1024]{2,1,0:T(8,128)} %refs_7_.5, f32[2,1024,1024]{2,1,0:T(8,128)} %refs_7_.4, f32[2,1024,1024]{2,1,0:T(8,128)} %refs_8_.3, ...), custom_call_target="tpu_custom_call", output_to_operand_aliasing={{0}: (15, {}), {1}: (16, {}), {2}: (17, {})} | custom-call | flops 104857600 | bytes 25165824 | tf_op jit(solution)/shard_map/split_flux/pallas_call | solution.py:517
  148.7 0.0 all-to-all-done.1
  148.7 1.1 slice_bitcast_fusion
  149.7 19.0 %add_gravity.1 = (f32[2,1024,1024]{2,1,0:T(8,128)}, f32[2,1024,1024]{2,1,0:T(8,128)}, f32[1024,1024]{1,0:T(8,128)}) custom-call(f32[128,1024]{1,0:T(8,128)} %get-tuple-element.47.refs_0_, f32[128,1024]{1,0:T(8,128)} %get-tuple-element.46.refs_1_, f32[1,1024]{1,0:T(1,128)} %bitcast.7, bf16[128,1024]{1,0:T(8,128)(2,1)} %get-tuple-element.61.refs_5_.refs_3_, ...), custom_call_target="tpu_custom_call" | custom-call | flops 2415919104 | bytes 46137344 | tf_op jit(solution)/shard_map/add_gravity/pallas_call | solution.py:577
  (19 shorter events, 0.1 us)
Async XLA Ops:
  15.0 63.7 %all-to-all-start = ((f32[16,8,1024]{2,1,0:T(8,128)}), f32[16,8,1024]{2,1,0:T(8,128)S(1)}, u32[]{:S(2)}, u32[]{:S(2)}) async-start(f32[16,8,1024]{2,1,0:T(8,128)} %bitcast.6), calls=%async_computation | async-start | bytes 1048576 | tf_op jit(solution)/shard_map/all_to_all | solution.py:648
  25.3 7.4 %collective-permute-start = (bf16[2,3,1024]{2,1,0:T(4,128)(2,1)S(1)}, bf16[2,3,1024]{2,1,0:T(4,128)(2,1)S(1)}, u32[]{:S(2)}, u32[]{:S(2)}) collective-permute-start(bf16[2,3,1024]{2,1,0:T(4,128)(2,1)S(1)} %fusion.7), channel_id=1, source_target_pairs={{0,1},{1,0},{2,3},{3,2},{4,5},{5,4},{6,7},{7,6},{8,9},{9,8},{10,11... | collective-permute-start | bytes 36872 | tf_op jit(solution)/shard_map/ppermute | solution.py:606
  25.4 13.1 %collective-permute-start.1 = (bf16[16,1024]{1,0:T(8,128)(2,1)}, bf16[16,1024]{1,0:T(8,128)(2,1)S(1)}, u32[]{:S(2)}, u32[]{:S(2)}) collective-permute-start(bf16[16,1024]{1,0:T(8,128)(2,1)} %get-tuple-element.22), channel_id=1, source_target_pairs={{0,2},{2,4},{4,6},{6,8},{8,10},{10,12},{12,14},{14,16},{16,18},{18... | collective-permute-start | bytes 98312 | tf_op jit(solution)/shard_map/ppermute | solution.py:622
  27.3 11.2 %collective-permute-start.2 = (bf16[16,1024]{1,0:T(8,128)(2,1)}, bf16[16,1024]{1,0:T(8,128)(2,1)S(1)}, u32[]{:S(2)}, u32[]{:S(2)}) collective-permute-start(bf16[16,1024]{1,0:T(8,128)(2,1)} %get-tuple-element.23), channel_id=1, source_target_pairs={{2,0},{4,2},{6,4},{8,6},{10,8},{12,10},{14,12},{16,14},{18,16},{20... | collective-permute-start | bytes 98312 | tf_op jit(solution)/shard_map/ppermute | solution.py:622
  38.5 0.6 copy-start
  38.5 0.6 copy-start.1
  94.6 54.0 %all-to-all-start.1 = ((f32[16,2,8,1024]{3,2,1,0:T(8,128)}), f32[16,2,8,1024]{3,2,1,0:T(8,128)S(1)}, u32[]{:S(2)}, u32[]{:S(2)}) async-start(f32[16,2,8,1024]{3,2,1,0:T(8,128)} %responses.1), calls=%async_computation.1 | async-start | bytes 2097152 | tf_op jit(solution)/shard_map/all_to_all | solution.py:657

commit v7 on v6

--- a/solution.py
+++ b/solution.py
@@ -57,8 +57,6 @@
     *tables, out_ref, first_ref, last_ref, wide_ref, density, sems = refs[5:]
     thin_ref = tables[2]
     layers, _, cells = density.shape
-    streams = min(4, cells // LANES)
-    width = cells // streams
     rows_here = fetch_rows(refs[:1], [density], sems, steps)
     cols = thin_ref.shape[0]
 
@@ -67,28 +65,25 @@
         wide_ref[:cols] = tables[0][...]
         wide_ref[cols:] = tables[1][...]
 
-    total = None
-    for stream in range(streams):
-        here = pl.ds(stream * width, width)
-        x = density[0, rows_here, here]
-        for layer in range(1, layers):
-            x = x + density[layer, rows_here, here]
-        high = x.astype(jnp.bfloat16)
-        x = x - high.astype(jnp.float32)
-        mid = x.astype(jnp.bfloat16)
-        low = (x - mid.astype(jnp.float32)).astype(jnp.bfloat16)
-
-        def product(a, table):
-            return lax.dot_general(
-                a, table, (((1,), (1,)), ((), ())), preferred_element_type=jnp.float32
-            )
-
-        both = wide_ref[:, here]
-        major = product(high, both)
-        minor = product(mid, both)
-        small = product(low, both[:cols]) + product(high, thin_ref[:, here])
-        part = major[:, :cols] + (major[:, cols:] + minor[:, :cols] + (minor[:, cols:] + small))
-        total = part if total is None else total + part
+    x = density[0, rows_here, :]
+    for layer in range(1, layers):
+        x = x + density[layer, rows_here, :]
+    high = x.astype(jnp.bfloat16)
+    x = x - high.astype(jnp.float32)
+    mid = x.astype(jnp.bfloat16)
+    low = (x - mid.astype(jnp.float32)).astype(jnp.bfloat16)
+
+    def product(a, table):
+        return lax.dot_general(
+            a, table, (((1,), (1,)), ((), ())), preferred_element_type=jnp.float32
+        )
+
+    rows = high.shape[0]
+    major = product(jnp.concatenate([high, mid, low], axis=0), wide_ref[...])
+    small = major[2 * rows :, :cols] + product(high, thin_ref[...])
+    total = major[:rows, :cols] + (
+        major[:rows, cols:] + major[rows : 2 * rows, :cols] + (major[rows : 2 * rows, cols:] + small)
+    )
     out_ref[...] = (scale * total).T
 
     block = out_ref.shape[1]
@@ -118,7 +113,7 @@
 def surface_modes(fields, tables, scale):
     layers, rows, cells = fields[0].shape
     cols = tables[0].shape[0]
-    block = min(rows, LANES)
+    block = min(rows, 2 * LANES)
     first = pl.BlockSpec((layers, block, LANES), lambda i: (0, i, 0))
     last = pl.BlockSpec((layers, block, LANES), lambda i: (0, i, cells // LANES - 1))
     table_spec = pl.BlockSpec((cols, cells), lambda i: (0, 0))
@@ -305,7 +300,7 @@
         return [self.wide(coef[:, k : k + 1]) for k in names]
 
 
-def joint_flux(layer, block_count, refs):
+def joint_flux(group, layer, block_count, refs):
     block = FluxBlock(block_count, refs)
     outs = refs[-6:-3]
     above, lagged, side = refs[-3:]
@@ -333,47 +328,59 @@
             coef, (ROOT_FACE, SOUND_FACE, IN, ROOT_MID, SOUND_MID, AZ, SPIN, PULL)
         )
         (out_before,) = block.columns_of(side[rows_before, :], (OUT,))
-        turned = block.ghost_values(layer, coef, 0, sound_mid)
-        held = held_flux = None
-
-        def settle(col, held, held_flux, flux):
+        zero = jnp.zeros((SUB, LANES), jnp.float32)
+
+        def settle(col, held, turned_held, turned_flux):
             for comp in range(3):
-                up = jnp.where(
-                    lane == LANES - 1,
-                    pltpu.roll(flux[comp], LANES - 1, 1),
-                    pltpu.roll(held_flux[comp], LANES - 1, 1),
+                up = jnp.where(lane == LANES - 1, turned_flux[comp], turned_held[comp])
+                outs[comp][here, col] = held[comp] - az * up
+
+        def some_columns(place, carry):
+            turned, held, turned_held = carry
+            for k in range(group):
+                first = place * (group * LANES) + k * LANES
+                col = pl.ds(pl.multiple_of(first, LANES), LANES)
+                before = pl.ds(pl.multiple_of(jnp.maximum(first - LANES, 0), LANES), LANES)
+                state = [ref[here, col] for ref in fields]
+                inv, values = block.radial_state(state)
+                rolled = [pltpu.roll(value, 1, 0) for value in values]
+                lower = [
+                    jnp.where(sub == 0, above[slot, :, col], value) for slot, value in enumerate(rolled)
+                ]
+                flux_r = block.radial_flux(values, lower, root_face, sound_face)
+                turned_r = [pltpu.roll(value, SUB - 1, 0) for value in flux_r]
+                for comp in range(3):
+                    up = jnp.where(sub == SUB - 1, turned_r[comp], lagged[comp, :, col])
+                    outs[comp][rows_before, col] -= out_before * up
+                for slot, value in enumerate(rolled):
+                    above[slot, :, col] = value
+                for comp in range(3):
+                    lagged[comp, :, col] = turned_r[comp]
+                values = block.azimuth_values(state, inv, values[5], sound_mid)
+                rolled = [pltpu.roll(value, 1, 1) for value in values]
+                lower = [jnp.where(lane == 0, a, b) for a, b in zip(turned, rolled)]
+                turned = rolled
+                flux = block.azimuth_flux(values, lower, root_mid)
+                turned_flux = [pltpu.roll(value, LANES - 1, 1) for value in flux]
+                settle(before, held, turned_held, turned_flux)
+                held = (
+                    state[0] + in_coef * flux_r[0] + az * flux[0],
+                    state[1] + in_coef * flux_r[1] + az * flux[1] + (spin * values[5] - pull * state[0]),
+                    state[2] + in_coef * flux_r[2] + az * flux[2] - spin * values[4],
                 )
-                outs[comp][here, at(col)] = held[comp] - az * (up - held_flux[comp])
-
-        for col in range(columns):
-            state = [ref[here, at(col)] for ref in fields]
-            inv, values = block.radial_state(state)
-            rolled = [pltpu.roll(value, 1, 0) for value in values]
-            lower = [
-                jnp.where(sub == 0, above[slot, :, at(col)], value)
-                for slot, value in enumerate(rolled)
-            ]
-            flux_r = block.radial_flux(values, lower, root_face, sound_face)
-            turned_r = [pltpu.roll(value, SUB - 1, 0) for value in flux_r]
-            finish(rows_before, col, turned_r, out_before)
-            keep_above(col, rolled)
-            for comp in range(3):
-                lagged[comp, :, at(col)] = turned_r[comp]
-            values = block.azimuth_values(state, inv, values[5], sound_mid)
-            rolled = [pltpu.roll(value, 1, 1) for value in values]
-            lower = [jnp.where(lane == 0, a, b) for a, b in zip(turned, rolled)]
-            turned = rolled
-            flux = block.azimuth_flux(values, lower, root_mid)
-            if col > 0:
-                settle(col - 1, held, held_flux, flux)
-            held = (
-                state[0] + in_coef * flux_r[0],
-                state[1] + in_coef * flux_r[1] + (spin * values[5] - pull * state[0]),
-                state[2] + in_coef * flux_r[2] - spin * values[4],
-            )
-            held_flux = flux
-        values = block.ghost_values(layer, coef, 1, sound_mid)
-        settle(columns - 1, held, held_flux, block.azimuth_flux(values, turned, root_mid))
+                turned_held = turned_flux
+            return tuple(turned), held, tuple(turned_held)
+
+        turned, held, turned_held = lax.fori_loop(
+            0,
+            columns // group,
+            some_columns,
+            (block.ghost_values(layer, coef, 0, sound_mid), (zero,) * 3, (zero,) * 3),
+        )
+        flux = block.azimuth_flux(block.ghost_values(layer, coef, 1, sound_mid), turned, root_mid)
+        settle(
+            at(columns - 1), held, turned_held, [pltpu.roll(value, LANES - 1, 1) for value in flux]
+        )
         return carry
 
     lax.fori_loop(0, block.strips, strip, 0)
@@ -388,100 +395,7 @@
         finish(last, col, [pltpu.roll(value, SUB - 1, 0) for value in flux_r], out_coef)
 
 
-def split_flux(layer, block_count, refs):
-    block = FluxBlock(block_count, refs)
-    outs = refs[-7:-4]
-    above, lagged, side, part = refs[-4:]
-    side[...] = block.side
-    lane, sub, at, fields = block.lane, block.sub, block.at, block.fields
-    columns = block.columns
-
-    def azimuth_strip(place, carry):
-        here = block.rows_at(place)
-        coef = side[here, :]
-        root_mid, sound_mid, az, spin, pull = block.columns_of(
-            coef, (ROOT_MID, SOUND_MID, AZ, SPIN, PULL)
-        )
-        turned = block.ghost_values(layer, coef, 0, sound_mid)
-        held = turned_held = None
-
-        def settle(col, turned_flux):
-            for comp in range(3):
-                up = jnp.where(lane == LANES - 1, turned_flux[comp], turned_held[comp])
-                part[comp, here, at(col)] = held[comp] - az * up
-
-        for col in range(columns):
-            state = [ref[here, at(col)] for ref in fields]
-            inv = inverse(state[0])
-            vel = state[2] * inv
-            values = (
-                *state, jnp.abs(vel), state[1] * vel, state[2] * vel + sound_mid * state[0]
-            )
-            rolled = [pltpu.roll(value, 1, 1) for value in values]
-            lower = [jnp.where(lane == 0, a, b) for a, b in zip(turned, rolled)]
-            turned = rolled
-            flux = block.azimuth_flux(values, lower, root_mid)
-            turned_flux = [pltpu.roll(value, LANES - 1, 1) for value in flux]
-            if col > 0:
-                settle(col - 1, turned_flux)
-            held = (
-                state[0] + az * flux[0],
-                state[1] + az * flux[1] + (spin * values[5] - pull * state[0]),
-                state[2] + az * flux[2] - spin * values[4],
-            )
-            turned_held = turned_flux
-        flux = block.azimuth_flux(block.ghost_values(layer, coef, 1, sound_mid), turned, root_mid)
-        settle(columns - 1, [pltpu.roll(value, LANES - 1, 1) for value in flux])
-        return carry
-
-    lax.fori_loop(0, block.strips, azimuth_strip, 0)
-
-    for col in range(columns):
-        for slot, value in enumerate(block.row_before(col)):
-            above[slot, :, at(col)] = value
-
-    def finish(place, col, turned, in_coef, out_coef):
-        here = block.rows_at(place)
-        for comp in range(3):
-            low = lagged[comp, :, at(col)]
-            up = jnp.where(sub == SUB - 1, turned[comp], pltpu.roll(low, SUB - 1, 0))
-            outs[comp][here, at(col)] = part[comp, here, at(col)] + (in_coef * low - out_coef * up)
-
-    def radial_strip(place, carry):
-        here = block.rows_at(place)
-        earlier = jnp.maximum(place - 1, 0)
-        root_face, sound_face = block.columns_of(side[here, :], (ROOT_FACE, SOUND_FACE))
-        in_coef, out_coef = block.columns_of(side[block.rows_at(earlier), :], (IN, OUT))
-        for col in range(columns):
-            values = block.radial_state([ref[here, at(col)] for ref in fields])[1]
-            rolled = [pltpu.roll(value, 1, 0) for value in values]
-            lower = [
-                jnp.where(sub == 0, above[slot, :, at(col)], value)
-                for slot, value in enumerate(rolled)
-            ]
-            for slot, value in enumerate(rolled):
-                above[slot, :, at(col)] = value
-            flux = block.radial_flux(values, lower, root_face, sound_face)
-            finish(earlier, col, [pltpu.roll(value, SUB - 1, 0) for value in flux], in_coef, out_coef)
-            for comp in range(3):
-                lagged[comp, :, at(col)] = flux[comp]
-        return carry
-
-    lax.fori_loop(0, block.strips, radial_strip, 0)
-
-    after = block.coef_after[...].T
-    root_face, sound_face = block.columns_of(after[:SUB], (ROOT_FACE, SOUND_FACE))
-    in_coef, out_coef = block.columns_of(
-        side[(block.strips - 1) * SUB : block.strips * SUB, :], (IN, OUT)
-    )
-    for col in range(columns):
-        lower = [above[slot, :, at(col)] for slot in range(6)]
-        flux = block.radial_flux(block.row_after(col), lower, root_face, sound_face)
-        turned = [pltpu.roll(value, SUB - 1, 0) for value in flux]
-        finish(block.strips - 1, col, turned, in_coef, out_coef)
-
-
-def flux_layer(layer, kernel, fields, rims, edges, coefs, so_far):
+def flux_layer(layer, group, fields, rims, edges, coefs, so_far):
     layers, rows, cells = fields[0].shape
     block = min(rows, LANES)
     count = rows // block
@@ -512,10 +426,9 @@
         pltpu.VMEM((3, SUB, cells), jnp.float32),
         pltpu.VMEM((block, LANES), jnp.float32),
     ]
-    if kernel is split_flux:
-        scratch.append(pltpu.VMEM((3, block, cells), jnp.float32))
+    group = min(group, cells // LANES)
     return pl.pallas_call(
-        lambda *refs: kernel(layer, count, refs),
+        lambda *refs: joint_flux(group, layer, count, refs),
         grid=(count,),
         in_specs=specs,
         out_specs=[main] * 3,
@@ -526,49 +439,50 @@
         cost_estimate=pl.CostEstimate(
             flops=100 * rows * cells, bytes_accessed=24 * rows * cells, transcendentals=rows * cells
         ),
-        name=kernel.__name__,
+        name="joint_flux",
     )(*operands)
 
 
 def gravity_kernel(steps, refs):
     pot_ref, force_ref, inverse_ref = refs[:3]
-    halves = refs[3:7]
-    out_r, out_phi, out_pot, table_ref, slope_ref, *buffers, sems = refs[10:]
+    halves = refs[3:5]
+    out_r, out_phi, out_pot, table_ref, *buffers, sems = refs[8:]
     density, mom_r, mom_phi = buffers
-    rows_here = fetch_rows(refs[7:10], buffers, sems, steps)
-    cols = pot_ref.shape[0]
+    rows_here = fetch_rows(refs[5:8], buffers, sems, steps)
+    cols, block = pot_ref.shape
 
     @pl.when(pl.program_id(0) == 0)
     def _():
-        for ref, (high, low) in ((table_ref, halves[:2]), (slope_ref, halves[2:])):
-            ref[:cols] = high[...]
-            ref[cols : 2 * cols] = high[...]
-            ref[2 * cols :] = low[...]
-
-
-    def product(a, table):
-        high, low = split_bf16(a)
-        return lax.dot_general(
-            jnp.concatenate([high, low, high], axis=0),
-            table,
-            (((0,), (0,)), ((), ())),
-            preferred_element_type=jnp.float32,
-        )
+        table_ref[:cols] = halves[0][...]
+        table_ref[cols : 2 * cols] = halves[0][...]
+        table_ref[2 * cols :] = halves[1][...]
 
     pot = pot_ref[...]
-    out_pot[...] = product(pot, table_ref[...])
-    radial = product(force_ref[...] * 0.1, table_ref[...])
-    azimuth = product(pot * inverse_ref[...], slope_ref[...])
+    row = lax.broadcasted_iota(jnp.int32, pot.shape, 0)
+    even = row % 2 == 0
+    mode = (row // 2).astype(jnp.float32)
+    swapped = jnp.where(even, pltpu.roll(pot, cols - 1, 0), -pltpu.roll(pot, 1, 0))
+    left = jnp.concatenate(
+        [pot, 0.1 * force_ref[...], swapped * (mode * inverse_ref[...])], axis=1
+    )
+    high, low = split_bf16(left)
+    grid = lax.dot_general(
+        jnp.concatenate([high, low, high], axis=0),
+        table_ref[...],
+        (((0,), (0,)), ((), ())),
+        preferred_element_type=jnp.float32,
+    )
+    out_pot[...] = grid[:block]
     for layer in range(density.shape[0]):
         here = density[layer, rows_here, :]
-        out_r[layer] = mom_r[layer, rows_here, :] + here * radial
-        out_phi[layer] = mom_phi[layer, rows_here, :] + here * azimuth
+        out_r[layer] = mom_r[layer, rows_here, :] + here * grid[block : 2 * block]
+        out_phi[layer] = mom_phi[layer, rows_here, :] + here * grid[2 * block :]
 
 
 def add_gravity(pot, force, inverse_mid, tables, density, mom_r, mom_phi):
     layers, rows, cells = density.shape
     cols = pot.shape[0]
-    block = min(rows, LANES)
+    block = min(rows, 2 * LANES)
     modes_spec = pl.BlockSpec((cols, block), lambda i: (0, i))
     table_spec = pl.BlockSpec((cols, cells), lambda i: (0, 0))
 
@@ -579,10 +493,10 @@
         grid=(rows // block,),
         in_specs=[
             modes_spec, modes_spec, pl.BlockSpec((1, block), lambda i: (0, i)),
-        ] + [table_spec] * 4 + [pl.BlockSpec(memory_space=pl.ANY)] * 3,
+        ] + [table_spec] * 2 + [pl.BlockSpec(memory_space=pl.ANY)] * 3,
         out_specs=[field, field, pl.BlockSpec((block, cells), lambda i: (i, 0))],
         out_shape=[grid_shape, grid_shape, jax.ShapeDtypeStruct((rows, cells), jnp.float32)],
-        scratch_shapes=[pltpu.VMEM((3 * cols, cells), jnp.bfloat16)] * 2
+        scratch_shapes=[pltpu.VMEM((3 * cols, cells), jnp.bfloat16)]
         + [pltpu.VMEM(density.shape, density.dtype)] * 3
         + [pltpu.SemaphoreType.DMA((3, rows // block))],
         compiler_params=pltpu.CompilerParams(vmem_limit_bytes=VMEM_BYTES),
@@ -638,17 +552,17 @@
     angle = azimuth[None, :] * mode
     cosine, sine = jnp.cos(angle), jnp.sin(angle)
     basis = pieces_of(jnp.where(row % 2 == 0, cosine, sine), 3)
-    slope = pieces_of(jnp.where(row % 2 == 0, -mode * sine, mode * cosine), 2)
 
     rims = exchange_rims(fields, rad_index, rad_count)
     coefs, inverse_mid = row_coefficients(rad_index * rows, rows, step)
 
     partial, first, last = surface_modes(fields, basis, 1.0 / (az_count * cells))
     edges = exchange_edges(first, last, az_count)
+    partial, edges, rims = lax.optimization_barrier((partial, edges, rims))
     pieces = lax.all_to_all(
         partial.reshape(az_count, pair_count, rows), "az", split_axis=0, concat_axis=0, tiled=True
     )
-    results = flux_layer(0, joint_flux, fields, rims, edges, coefs, None)
+    results = flux_layer(0, 4, fields, rims, edges, coefs, None)
     pieces, results = lax.optimization_barrier((pieces, results))
 
     own = jnp.sum(pieces, axis=0).astype(jnp.bfloat16)
@@ -657,7 +571,7 @@
     every = lax.all_to_all(parts, "az", split_axis=0, concat_axis=0, tiled=True)
     coefs, parts = lax.optimization_barrier((coefs, parts))
     for layer in range(1, layers):
-        results = flux_layer(layer, split_flux, fields, rims, edges, coefs, results)
+        results = flux_layer(layer, 2, fields, rims, edges, coefs, results)
     pot = every[:, 0].reshape(cols, rows)
     force = every[:, 1].reshape(cols, rows)
 
@@ -665,7 +579,7 @@
         pot,
         force,
         inverse_mid,
-        (basis[0], basis[1], *slope),
+        basis[:2],
         density,
         results[1],
         results[2],

time: 170 us -> 280 us (1.65)
  Pallas kernels: 133 us -> 245 us
  waiting for transfers between devices: 5.19 us -> 1.52 us
  starting transfers between devices: 17.8 us -> 21 us
    pallas_call x2, Pallas kernels: 89.3 us -> 204 us  [flux_layer(): pl.pallas_call(lambda *refs: joint_flux(group, layer, count, refs), grid=...]
    ppermute x2, waiting for transfers between devices: 5.18 us -> 1.51 us  [exchange_edges(): return (lax.ppermute(last, 'az', right), lax.ppermute(first, 'az', left))]
    all_to_all x1, starting transfers between devices: 3.71 us -> 6.89 us  [local(): every = lax.all_to_all(parts, 'az', split_axis=0, concat_axis=0, tiled=True)]
    pallas_call x1, Pallas kernels: 11.1 us -> 8.1 us  [surface_modes(): pl.pallas_call(lambda *refs: modes_kernel(scale, rows // block, refs), gr...]
  transfers between devices with their start and end apart: 5 -> 5, of which waited for: 1 -> 1; matrix products, arithmetic and copies ran while one was open for 3% -> 2% of each run, Pallas kernels for 53% -> 76%
where the time goes in v7:
time: 280 us; the launch traced here: 279 us
  Pallas kernels  245 us (88%)
  starting transfers between devices  21 us (8%)
  other arithmetic  4.62 us (2%)
  local copies, waits for them, and re-layouts  4.31 us (2%)
    pallas_call x2, Pallas kernels, flux_layer(): pl.pallas_call(lambda *refs: joint_flux(group, layer, count, refs), grid=...  204 us
    pallas_call x1, Pallas kernels, add_gravity(): pl.pallas_call(lambda *refs: gravity_kernel(rows // block, refs), grid=(r...  18.4 us
    pallas_call x1, Pallas kernels, responses(): pl.pallas_call(lambda *refs: response_kernel(steps, refs), grid=(steps,),...  13.9 us
    pallas_call x1, Pallas kernels, surface_modes(): pl.pallas_call(lambda *refs: modes_kernel(scale, rows // block, refs), gr...  8.1 us
    all_to_all x1, starting transfers between devices, local(): lax.all_to_all(partial.reshape(az_count, pair_count, rows), 'az', split_a...  6.91 us
    all_to_all x1, starting transfers between devices, local(): every = lax.all_to_all(parts, 'az', split_axis=0, concat_axis=0, tiled=True)  6.89 us
    ppermute x2, starting transfers between devices, exchange_edges(): return (lax.ppermute(last, 'az', right), lax.ppermute(first, 'az', left))  6.63 us
  transfers between devices with their start and end apart: 5, of which 1 were waited for; matrix products, arithmetic and copies ran while one was open for 2% of the time, Pallas kernels for 76%

profile of v7, /device:TPU:0, one launch (start us, length us, event | category | flops | bytes accessed | tf_op | source)
XLA Modules:
  0.0 279.0 jit_solution(17129821992329843705)
XLA Ops:
  0.6 0.9 fusion.10
  1.5 1.0 fusion.8
  2.5 0.1 fusion.3
  2.6 0.5 collective-permute-start.2
  3.1 3.1 %fusion = (bf16[128,1024]{1,0:T(8,128)(2,1)}, bf16[128,1024]{1,0:T(8,128)(2,1)}, bf16[128,1024]{1,0:T(8,128)(2,1)}) fusion(s32[128]{0:T(128)S(1)} %get-tuple-element.73, s32[128]{0:T(128)S(1)} %get-tuple-element.75, f32[1024]{0:T(1024)S(1)} %add_multiply_fusion.1, s32[128]{0:T(128)S(1)} %get-tuple-element.74, s32[128]{0:T(128)S(1)} %get-tuple-element.76, ...), kind=kLoop, calls=%fused_computation.4 | loop fusion | flops 1703936 | bytes 792832 | tf_op jit(solution)/shard_map/convert_element_type | solution.py:49
  6.3 8.1 %surface_modes.1 = (f32[128,1024]{1,0:T(8,128)}, bf16[16,1024]{1,0:T(8,128)(2,1)}, bf16[16,1024]{1,0:T(8,128)(2,1)}) custom-call(f32[2,1024,1024]{2,1,0:T(8,128)} %refs_5_.5, f32[2,1024,1024]{2,1,0:T(8,128)} %refs_7_.3, f32[2,1024,1024]{2,1,0:T(8,128)} %refs_8_.3, f32[2,1024,1024]{2,1,0:T(8,128)} %refs_7_.3, f32[2,1024,1024]{2,1,0:T(8,128)} %refs_8_.3, ...), custom_call_target="tpu_custom_call" | custom-call | flops 1610612736 | bytes 8388608 | tf_op jit(solution)/shard_map/surface_modes/pallas_call | solution.py:122
  14.4 2.6 collective-permute-start
  16.9 4.1 %collective-permute-start.1 = (bf16[16,1024]{1,0:T(8,128)(2,1)}, bf16[16,1024]{1,0:T(8,128)(2,1)S(1)}, u32[]{:S(2)}, u32[]{:S(2)}) collective-permute-start(bf16[16,1024]{1,0:T(8,128)(2,1)} %get-tuple-element.28), channel_id=1, source_target_pairs={{2,0},{4,2},{6,4},{8,6},{10,8},{12,10},{14,12},{16,14},{18,16},{20... | collective-permute-start | bytes 98312 | tf_op jit(solution)/shard_map/ppermute | solution.py:536
  21.0 0.0 collective-permute-done.2
  21.0 0.7 convert_select_fusion
  21.7 1.5 collective-permute-done.refs_12_
  23.2 0.0 copy-start
  23.2 0.0 collective-permute-done.1.refs_13_
  23.2 0.0 copy-start.1
  23.2 6.9 %all-to-all-start = ((f32[16,8,1024]{2,1,0:T(8,128)}), f32[16,8,1024]{2,1,0:T(8,128)S(1)}, u32[]{:S(2)}, u32[]{:S(2)}) async-start(f32[16,8,1024]{2,1,0:T(8,128)} %bitcast.6), calls=%async_computation | async-start | bytes 1048576 | tf_op jit(solution)/shard_map/all_to_all | solution.py:562
  30.1 0.1 multiply_divide_fusion
  30.4 1.3 stack.55.refs_11_.refs_14_
  31.7 0.0 copy-done
  31.7 0.0 copy-done.1
  31.7 83.4 %joint_flux.2 = (f32[2,1024,1024]{2,1,0:T(8,128)}, f32[2,1024,1024]{2,1,0:T(8,128)}, f32[2,1024,1024]{2,1,0:T(8,128)}) custom-call(f32[2,1024,1024]{2,1,0:T(8,128)} %refs_5_.5, f32[2,1024,1024]{2,1,0:T(8,128)} %refs_7_.3, f32[2,1024,1024]{2,1,0:T(8,128)} %refs_8_.3, f32[2,1024,1024]{2,1,0:T(8,128)} %refs_5_.5, f32[2,1024,1024]{2,1,0:T(8,128)} %refs_7_.3, ...), custom_call_target="tpu_custom_call" | custom-call | flops 104857600 | bytes 25165824 | tf_op jit(solution)/shard_map/joint_flux/pallas_call | solution.py:430
  115.1 0.0 all-to-all-done
  115.1 2.0 all_gather.3.refs_0_
  117.1 13.9 %responses.1 = f32[16,2,8,1024]{3,2,1,0:T(8,128)} custom-call(bf16[8,2048]{1,0:T(8,128)(2,1)} %all_gather.3.refs_0_, bf16[4,1024,2048]{2,1,0:T(8,128)(2,1)} %refs_1_.6, bf16[4,1024,2048]{2,1,0:T(8,128)(2,1)} %refs_2_.6), custom_call_target="tpu_custom_call" | custom-call | flops 268435456 | bytes 33554432 | tf_op jit(solution)/shard_map/responses/pallas_call | solution.py:168
  131.0 6.9 %all-to-all-start.1 = ((f32[16,2,8,1024]{3,2,1,0:T(8,128)}), f32[16,2,8,1024]{3,2,1,0:T(8,128)S(1)}, u32[]{:S(2)}, u32[]{:S(2)}) async-start(f32[16,2,8,1024]{3,2,1,0:T(8,128)} %responses.1), calls=%async_computation.1 | async-start | bytes 2097152 | tf_op jit(solution)/shard_map/all_to_all | solution.py:571
  137.9 0.6 slice_divide_fusion.1
  138.5 121.1 %joint_flux.3 = (f32[2,1024,1024]{2,1,0:T(8,128)}, f32[2,1024,1024]{2,1,0:T(8,128)}, f32[2,1024,1024]{2,1,0:T(8,128)}) custom-call(f32[2,1024,1024]{2,1,0:T(8,128)} %refs_5_.5, f32[2,1024,1024]{2,1,0:T(8,128)} %refs_7_.3, f32[2,1024,1024]{2,1,0:T(8,128)} %refs_8_.3, ...), custom_call_target="tpu_custom_call", output_to_operand_aliasing={{0}: (15, {}), {1}: (16, {}), {2}: (17, {})} | custom-call | flops 104857600 | bytes 25165824 | tf_op jit(solution)/shard_map/joint_flux/pallas_call | solution.py:430
  259.6 0.0 all-to-all-done.1
  259.6 1.1 slice_bitcast_fusion
  260.7 18.4 %add_gravity.1 = (f32[2,1024,1024]{2,1,0:T(8,128)}, f32[2,1024,1024]{2,1,0:T(8,128)}, f32[1024,1024]{1,0:T(8,128)}) custom-call(f32[128,1024]{1,0:T(8,128)} %get-tuple-element.57.refs_0_, f32[128,1024]{1,0:T(8,128)} %get-tuple-element.56.refs_1_, f32[1,1024]{1,0:T(1,128)} %bitcast.7, bf16[128,1024]{1,0:T(8,128)(2,1)} %get-tuple-element.69.refs_5_.refs_3_, ...), custom_call_target="tpu_custom_call" | custom-call | flops 2415919104 | bytes 46137344 | tf_op jit(solution)/shard_map/add_gravity/pallas_call | solution.py:491
  (19 shorter events, 0.1 us)
Async XLA Ops:
  2.6 18.4 %collective-permute-start.2 = (bf16[2,3,1024]{2,1,0:T(4,128)(2,1)S(1)}, bf16[2,3,1024]{2,1,0:T(4,128)(2,1)S(1)}, u32[]{:S(2)}, u32[]{:S(2)}) collective-permute-start(bf16[2,3,1024]{2,1,0:T(4,128)(2,1)S(1)} %fusion.3), channel_id=1, source_target_pairs={{0,1},{1,0},{2,3},{3,2},{4,5},{5,4},{6,7},{7,6},{8,9},{9,8},{10,11... | collective-permute-start | bytes 36872 | tf_op jit(solution)/shard_map/ppermute | solution.py:520
  14.4 8.8 %collective-permute-start = (bf16[16,1024]{1,0:T(8,128)(2,1)}, bf16[16,1024]{1,0:T(8,128)(2,1)S(1)}, u32[]{:S(2)}, u32[]{:S(2)}) collective-permute-start(bf16[16,1024]{1,0:T(8,128)(2,1)} %get-tuple-element.27), channel_id=1, source_target_pairs={{0,2},{2,4},{4,6},{6,8},{8,10},{10,12},{12,14},{14,16},{16,18},{18... | collective-permute-start | bytes 98312 | tf_op jit(solution)/shard_map/ppermute | solution.py:536
  16.9 6.2 %collective-permute-start.1 = (bf16[16,1024]{1,0:T(8,128)(2,1)}, bf16[16,1024]{1,0:T(8,128)(2,1)S(1)}, u32[]{:S(2)}, u32[]{:S(2)}) collective-permute-start(bf16[16,1024]{1,0:T(8,128)(2,1)} %get-tuple-element.28), channel_id=1, source_target_pairs={{2,0},{4,2},{6,4},{8,6},{10,8},{12,10},{14,12},{16,14},{18,16},{20... | collective-permute-start | bytes 98312 | tf_op jit(solution)/shard_map/ppermute | solution.py:536
  23.2 8.5 %copy-start = (bf16[16,1024]{1,0:T(8,128)(2,1)}, bf16[16,1024]{1,0:T(8,128)(2,1)S(1)}, u32[]{:S(2)}) copy-start(bf16[16,1024]{1,0:T(8,128)(2,1)S(1)} %collective-permute-done.refs_12_) | copy-start | bytes 98308
  23.2 8.5 %copy-start.1 = (bf16[16,1024]{1,0:T(8,128)(2,1)}, bf16[16,1024]{1,0:T(8,128)(2,1)S(1)}, u32[]{:S(2)}) copy-start(bf16[16,1024]{1,0:T(8,128)(2,1)S(1)} %collective-permute-done.1.refs_13_) | copy-start | bytes 98308
  23.2 91.9 %all-to-all-start = ((f32[16,8,1024]{2,1,0:T(8,128)}), f32[16,8,1024]{2,1,0:T(8,128)S(1)}, u32[]{:S(2)}, u32[]{:S(2)}) async-start(f32[16,8,1024]{2,1,0:T(8,128)} %bitcast.6), calls=%async_computation | async-start | bytes 1048576 | tf_op jit(solution)/shard_map/all_to_all | solution.py:562
  131.0 128.6 %all-to-all-start.1 = ((f32[16,2,8,1024]{3,2,1,0:T(8,128)}), f32[16,2,8,1024]{3,2,1,0:T(8,128)S(1)}, u32[]{:S(2)}, u32[]{:S(2)}) async-start(f32[16,2,8,1024]{3,2,1,0:T(8,128)} %responses.1), calls=%async_computation.1 | async-start | bytes 2097152 | tf_op jit(solution)/shard_map/all_to_all | solution.py:571

commit v8 on v7

--- a/solution.py
+++ b/solution.py
@@ -300,104 +300,101 @@
         return [self.wide(coef[:, k : k + 1]) for k in names]
 
 
-def joint_flux(group, layer, block_count, refs):
+CELL_VALUES = 8
+
+
+def flux_kernel(layer, block_count, refs):
     block = FluxBlock(block_count, refs)
-    outs = refs[-6:-3]
-    above, lagged, side = refs[-3:]
+    outs = refs[-8:-5]
+    side, cell, faces, sides, held = refs[-5:]
     side[...] = block.side
-    lane, sub, at, fields = block.lane, block.sub, block.at, block.fields
-    columns = block.columns
-
-    def keep_above(col, rolled):
-        for slot, value in enumerate(rolled):
-            above[slot, :, at(col)] = value
-
-    def finish(rows_before, col, turned, out_coef):
+    lane, sub, at, fields, rows_at = block.lane, block.sub, block.at, block.fields, block.rows_at
+    columns, strips, rows = block.columns, block.strips, block.rows
+
+    after = block.coef_after[...].T
+    root_face, sound_face = block.columns_of(after[:SUB], (ROOT_FACE, SOUND_FACE))
+    for col in range(columns):
+        for slot, value in enumerate(block.row_before(col)):
+            cell[slot, 0:SUB, at(col)] = value
+        last = [
+            jnp.broadcast_to(ref[rows - 1 : rows, at(col)], (SUB, LANES)) for ref in fields
+        ]
+        flux = block.radial_flux(
+            block.row_after(col), block.radial_state(last)[1], root_face, sound_face
+        )
         for comp in range(3):
-            up = jnp.where(sub == SUB - 1, turned[comp], lagged[comp, :, at(col)])
-            outs[comp][rows_before, at(col)] -= out_coef * up
-
-    for col in range(columns):
-        keep_above(col, block.row_before(col))
-
-    def strip(place, carry):
-        here = block.rows_at(place)
-        rows_before = block.rows_at(jnp.maximum(place - 1, 0))
+            faces[comp, rows : rows + SUB, at(col)] = flux[comp]
+
+    def update(place):
+        here, above = rows_at(place), rows_at(place + 1)
+        out_coef, az = block.columns_of(side[here, :], (OUT, AZ))
+        for col in range(columns):
+            for comp in range(3):
+                face = jnp.where(sub == 0, faces[comp, above, at(col)], faces[comp, here, at(col)])
+                edge = jnp.where(lane == 0, sides[comp, here, at(col + 1)], sides[comp, here, at(col)])
+                outs[comp][here, at(col)] = held[comp, here, at(col)] - (
+                    out_coef * pltpu.roll(face, SUB - 1, 0) + az * pltpu.roll(edge, LANES - 1, 1)
+                )
+
+    def face_fluxes(place):
+        here, inside = rows_at(place), rows_at(place + 1)
         coef = side[here, :]
         root_face, sound_face, in_coef, root_mid, sound_mid, az, spin, pull = block.columns_of(
             coef, (ROOT_FACE, SOUND_FACE, IN, ROOT_MID, SOUND_MID, AZ, SPIN, PULL)
         )
-        (out_before,) = block.columns_of(side[rows_before, :], (OUT,))
-        zero = jnp.zeros((SUB, LANES), jnp.float32)
-
-        def settle(col, held, turned_held, turned_flux):
+        left = block.ghost_values(layer, coef, 0, sound_mid)
+        for col in range(columns):
+            now = [cell[slot, inside, at(col)] for slot in range(CELL_VALUES)]
+            lower = [
+                pltpu.roll(jnp.where(sub == SUB - 1, cell[slot, here, at(col)], now[slot]), 1, 0)
+                for slot in range(6)
+            ]
+            flux_r = block.radial_flux(now[:6], lower, root_face, sound_face)
+            values = (*now[:3], now[6], now[5], now[7])
+            lower = [
+                pltpu.roll(jnp.where(lane == LANES - 1, a, b), 1, 1) for a, b in zip(left, values)
+            ]
+            left = values
+            flux = block.azimuth_flux(values, lower, root_mid)
             for comp in range(3):
-                up = jnp.where(lane == LANES - 1, turned_flux[comp], turned_held[comp])
-                outs[comp][here, col] = held[comp] - az * up
-
-        def some_columns(place, carry):
-            turned, held, turned_held = carry
-            for k in range(group):
-                first = place * (group * LANES) + k * LANES
-                col = pl.ds(pl.multiple_of(first, LANES), LANES)
-                before = pl.ds(pl.multiple_of(jnp.maximum(first - LANES, 0), LANES), LANES)
-                state = [ref[here, col] for ref in fields]
-                inv, values = block.radial_state(state)
-                rolled = [pltpu.roll(value, 1, 0) for value in values]
-                lower = [
-                    jnp.where(sub == 0, above[slot, :, col], value) for slot, value in enumerate(rolled)
-                ]
-                flux_r = block.radial_flux(values, lower, root_face, sound_face)
-                turned_r = [pltpu.roll(value, SUB - 1, 0) for value in flux_r]
-                for comp in range(3):
-                    up = jnp.where(sub == SUB - 1, turned_r[comp], lagged[comp, :, col])
-                    outs[comp][rows_before, col] -= out_before * up
-                for slot, value in enumerate(rolled):
-                    above[slot, :, col] = value
-                for comp in range(3):
-                    lagged[comp, :, col] = turned_r[comp]
-                values = block.azimuth_values(state, inv, values[5], sound_mid)
-                rolled = [pltpu.roll(value, 1, 1) for value in values]
-                lower = [jnp.where(lane == 0, a, b) for a, b in zip(turned, rolled)]
-                turned = rolled
-                flux = block.azimuth_flux(values, lower, root_mid)
-                turned_flux = [pltpu.roll(value, LANES - 1, 1) for value in flux]
-                settle(before, held, turned_held, turned_flux)
-                held = (
-                    state[0] + in_coef * flux_r[0] + az * flux[0],
-                    state[1] + in_coef * flux_r[1] + az * flux[1] + (spin * values[5] - pull * state[0]),
-                    state[2] + in_coef * flux_r[2] + az * flux[2] - spin * values[4],
-                )
-                turned_held = turned_flux
-            return tuple(turned), held, tuple(turned_held)
-
-        turned, held, turned_held = lax.fori_loop(
-            0,
-            columns // group,
-            some_columns,
-            (block.ghost_values(layer, coef, 0, sound_mid), (zero,) * 3, (zero,) * 3),
-        )
-        flux = block.azimuth_flux(block.ghost_values(layer, coef, 1, sound_mid), turned, root_mid)
-        settle(
-            at(columns - 1), held, turned_held, [pltpu.roll(value, LANES - 1, 1) for value in flux]
-        )
+                faces[comp, here, at(col)] = flux_r[comp]
+                sides[comp, here, at(col)] = flux[comp]
+            held[0, here, at(col)] = now[0] + (in_coef * flux_r[0] + az * flux[0])
+            held[1, here, at(col)] = (now[1] + (in_coef * flux_r[1] + az * flux[1])) + (
+                spin * now[7] - pull * now[0]
+            )
+            held[2, here, at(col)] = (now[2] + (in_coef * flux_r[2] + az * flux[2])) - spin * now[5]
+        values = block.ghost_values(layer, coef, 1, sound_mid)
+        lower = [pltpu.roll(a, 1, 1) for a in left]
+        for comp, value in enumerate(block.azimuth_flux(values, lower, root_mid)):
+            sides[comp, here, at(columns)] = value
+
+    def cell_values(place):
+        here, inside = rows_at(place), rows_at(place + 1)
+        (sound_mid,) = block.columns_of(side[here, :], (SOUND_MID,))
+        for col in range(columns):
+            state = [ref[here, at(col)] for ref in fields]
+            inv, values = block.radial_state(state)
+            vel = state[2] * inv
+            values = (*values, jnp.abs(vel), state[2] * vel + sound_mid * state[0])
+            for slot, value in enumerate(values):
+                cell[slot, inside, at(col)] = value
+
+    def iteration(place, carry):
+        def clamped(late):
+            return jnp.clip(place - late, 0, strips - 1)
+
+        update(clamped(3))
+        face_fluxes(clamped(1))
+        cell_values(clamped(0))
         return carry
 
-    lax.fori_loop(0, block.strips, strip, 0)
-
-    last = pl.ds((block.strips - 1) * SUB, SUB)
-    after = block.coef_after[...].T
-    root_face, sound_face = block.columns_of(after[:SUB], (ROOT_FACE, SOUND_FACE))
-    (out_coef,) = block.columns_of(side[last, :], (OUT,))
-    for col in range(columns):
-        lower = [above[slot, :, at(col)] for slot in range(6)]
-        flux_r = block.radial_flux(block.row_after(col), lower, root_face, sound_face)
-        finish(last, col, [pltpu.roll(value, SUB - 1, 0) for value in flux_r], out_coef)
-
-
-def flux_layer(layer, group, fields, rims, edges, coefs, so_far):
+    lax.fori_loop(0, strips + 3, iteration, 0)
+
+
+def flux_layer(layer, fields, rims, edges, coefs, so_far):
     layers, rows, cells = fields[0].shape
-    block = min(rows, LANES)
+    block = min(rows, 2 * LANES)
     count = rows // block
     per = block // SUB
     main = pl.BlockSpec((None, block, cells), lambda i: (layer, i, 0))
@@ -422,13 +419,14 @@
             operands.append(array)
             specs.append(pl.BlockSpec(memory_space=pl.ANY))
     scratch = [
-        pltpu.VMEM((6, SUB, cells), jnp.float32),
-        pltpu.VMEM((3, SUB, cells), jnp.float32),
         pltpu.VMEM((block, LANES), jnp.float32),
+        pltpu.VMEM((CELL_VALUES, block + SUB, cells), jnp.float32),
+        pltpu.VMEM((3, block + SUB, cells), jnp.float32),
+        pltpu.VMEM((3, block, cells + LANES), jnp.float32),
+        pltpu.VMEM((3, block, cells), jnp.float32),
     ]
-    group = min(group, cells // LANES)
     return pl.pallas_call(
-        lambda *refs: joint_flux(group, layer, count, refs),
+        lambda *refs: flux_kernel(layer, count, refs),
         grid=(count,),
         in_specs=specs,
         out_specs=[main] * 3,
@@ -439,7 +437,7 @@
         cost_estimate=pl.CostEstimate(
             flops=100 * rows * cells, bytes_accessed=24 * rows * cells, transcendentals=rows * cells
         ),
-        name="joint_flux",
+        name="flux_layer",
     )(*operands)
 
 
@@ -562,7 +560,7 @@
     pieces = lax.all_to_all(
         partial.reshape(az_count, pair_count, rows), "az", split_axis=0, concat_axis=0, tiled=True
     )
-    results = flux_layer(0, 4, fields, rims, edges, coefs, None)
+    results = flux_layer(0, fields, rims, edges, coefs, None)
     pieces, results = lax.optimization_barrier((pieces, results))
 
     own = jnp.sum(pieces, axis=0).astype(jnp.bfloat16)
@@ -571,7 +569,7 @@
     every = lax.all_to_all(parts, "az", split_axis=0, concat_axis=0, tiled=True)
     coefs, parts = lax.optimization_barrier((coefs, parts))
     for layer in range(1, layers):
-        results = flux_layer(layer, 2, fields, rims, edges, coefs, results)
+        results = flux_layer(layer, fields, rims, edges, coefs, results)
     pot = every[:, 0].reshape(cols, rows)
     force = every[:, 1].reshape(cols, rows)
 

time: 280 us -> 151 us (0.54)
  Pallas kernels: 245 us -> 117 us
    pallas_call x2, Pallas kernels: 204 us -> 76.2 us  [flux_layer(): pl.pallas_call(lambda *refs: flux_kernel(layer, count, refs), grid=(count...]
  transfers between devices with their start and end apart: 5 -> 5, of which waited for: 1 -> 1; matrix products, arithmetic and copies ran while one was open for 2% -> 4% of each run, Pallas kernels for 76% -> 56%
where the time goes in v8:
time: 151 us
  Pallas kernels  117 us (77%)
  starting transfers between devices  21 us (14%)
  other arithmetic  4.62 us (3%)
  local copies, waits for them, and re-layouts  4.31 us (3%)
  blocking collectives  1.96 us (1%)
  waiting for transfers between devices  1.52 us (1%)
    pallas_call x2, Pallas kernels, flux_layer(): pl.pallas_call(lambda *refs: flux_kernel(layer, count, refs), grid=(count...  76.2 us
    pallas_call x1, Pallas kernels, add_gravity(): pl.pallas_call(lambda *refs: gravity_kernel(rows // block, refs), grid=(r...  18.4 us
    pallas_call x1, Pallas kernels, responses(): pl.pallas_call(lambda *refs: response_kernel(steps, refs), grid=(steps,),...  13.9 us
    pallas_call x1, Pallas kernels, surface_modes(): pl.pallas_call(lambda *refs: modes_kernel(scale, rows // block, refs), gr...  8.1 us
    all_to_all x1, starting transfers between devices, local(): lax.all_to_all(partial.reshape(az_count, pair_count, rows), 'az', split_a...  6.91 us
    all_to_all x1, starting transfers between devices, local(): every = lax.all_to_all(parts, 'az', split_axis=0, concat_axis=0, tiled=True)  6.91 us
    ppermute x2, starting transfers between devices, exchange_edges(): return (lax.ppermute(last, 'az', right), lax.ppermute(first, 'az', left))  6.63 us
    convert_element_type x1, other arithmetic, pieces_of(): return out + [x.astype(jnp.bfloat16)]  3.14 us
  transfers between devices with their start and end apart: 5, of which 1 were waited for; matrix products, arithmetic and copies ran while one was open for 4% of the time, Pallas kernels for 56%

profile of v8, /device:TPU:0, one launch (start us, length us, event | category | flops | bytes accessed | tf_op | source)
XLA Modules:
  0.0 150.8 jit_solution(5334336657878717858)
XLA Ops:
  0.6 0.9 fusion.10
  1.5 1.0 fusion.8
  2.5 0.1 fusion.3
  2.6 0.5 collective-permute-start.2
  3.1 3.1 %fusion = (bf16[128,1024]{1,0:T(8,128)(2,1)}, bf16[128,1024]{1,0:T(8,128)(2,1)}, bf16[128,1024]{1,0:T(8,128)(2,1)}) fusion(s32[128]{0:T(128)S(1)} %get-tuple-element.73, s32[128]{0:T(128)S(1)} %get-tuple-element.75, f32[1024]{0:T(1024)S(1)} %add_multiply_fusion.1, s32[128]{0:T(128)S(1)} %get-tuple-element.74, s32[128]{0:T(128)S(1)} %get-tuple-element.76, ...), kind=kLoop, calls=%fused_computation.4 | loop fusion | flops 1703936 | bytes 792832 | tf_op jit(solution)/shard_map/convert_element_type | solution.py:49
  6.3 8.1 %surface_modes.1 = (f32[128,1024]{1,0:T(8,128)}, bf16[16,1024]{1,0:T(8,128)(2,1)}, bf16[16,1024]{1,0:T(8,128)(2,1)}) custom-call(f32[2,1024,1024]{2,1,0:T(8,128)} %refs_5_.5, f32[2,1024,1024]{2,1,0:T(8,128)} %refs_7_.3, f32[2,1024,1024]{2,1,0:T(8,128)} %refs_8_.3, f32[2,1024,1024]{2,1,0:T(8,128)} %refs_7_.3, f32[2,1024,1024]{2,1,0:T(8,128)} %refs_8_.3, ...), custom_call_target="tpu_custom_call" | custom-call | flops 1610612736 | bytes 8388608 | tf_op jit(solution)/shard_map/surface_modes/pallas_call | solution.py:122
  14.4 2.6 %collective-permute-start = (bf16[16,1024]{1,0:T(8,128)(2,1)}, bf16[16,1024]{1,0:T(8,128)(2,1)S(1)}, u32[]{:S(2)}, u32[]{:S(2)}) collective-permute-start(bf16[16,1024]{1,0:T(8,128)(2,1)} %get-tuple-element.27), channel_id=1, source_target_pairs={{0,2},{2,4},{4,6},{6,8},{8,10},{10,12},{12,14},{14,16},{16,18},{18... | collective-permute-start | bytes 98312 | tf_op jit(solution)/shard_map/ppermute | solution.py:534
  16.9 4.1 %collective-permute-start.1 = (bf16[16,1024]{1,0:T(8,128)(2,1)}, bf16[16,1024]{1,0:T(8,128)(2,1)S(1)}, u32[]{:S(2)}, u32[]{:S(2)}) collective-permute-start(bf16[16,1024]{1,0:T(8,128)(2,1)} %get-tuple-element.28), channel_id=1, source_target_pairs={{2,0},{4,2},{6,4},{8,6},{10,8},{12,10},{14,12},{16,14},{18,16},{20... | collective-permute-start | bytes 98312 | tf_op jit(solution)/shard_map/ppermute | solution.py:534
  21.0 0.0 collective-permute-done.2
  21.0 0.7 convert_select_fusion
  21.7 1.5 %collective-permute-done.refs_12_ = bf16[16,1024]{1,0:T(8,128)(2,1)S(1)} collective-permute-done((bf16[16,1024]{1,0:T(8,128)(2,1)}, bf16[16,1024]{1,0:T(8,128)(2,1)S(1)}, u32[]{:S(2)}, u32[]{:S(2)}) %collective-permute-start) | collective-permute-done | bytes 32800 | tf_op jit(solution)/shard_map/ppermute | solution.py:534
  23.2 0.0 copy-start
  23.2 0.0 collective-permute-done.1.refs_13_
  23.2 0.0 copy-start.1
  23.2 6.9 %all-to-all-start = ((f32[16,8,1024]{2,1,0:T(8,128)}), f32[16,8,1024]{2,1,0:T(8,128)S(1)}, u32[]{:S(2)}, u32[]{:S(2)}) async-start(f32[16,8,1024]{2,1,0:T(8,128)} %bitcast.6), calls=%async_computation | async-start | bytes 1048576 | tf_op jit(solution)/shard_map/all_to_all | solution.py:560
  30.1 0.1 multiply_divide_fusion
  30.4 1.3 stack.55.refs_11_.refs_14_
  31.7 0.0 copy-done
  31.7 0.0 copy-done.1
  31.7 38.1 %flux_layer.2 = (f32[2,1024,1024]{2,1,0:T(8,128)}, f32[2,1024,1024]{2,1,0:T(8,128)}, f32[2,1024,1024]{2,1,0:T(8,128)}) custom-call(f32[2,1024,1024]{2,1,0:T(8,128)} %refs_5_.5, f32[2,1024,1024]{2,1,0:T(8,128)} %refs_7_.3, f32[2,1024,1024]{2,1,0:T(8,128)} %refs_8_.3, f32[2,1024,1024]{2,1,0:T(8,128)} %refs_5_.5, f32[2,1024,1024]{2,1,0:T(8,128)} %refs_7_.3, ...), custom_call_target="tpu_custom_call" | custom-call | flops 104857600 | bytes 25165824 | tf_op jit(solution)/shard_map/flux_layer/pallas_call | solution.py:428
  69.8 0.0 all-to-all-done
  69.9 2.0 %all_gather.3.refs_0_ = bf16[8,2048]{1,0:T(8,128)(2,1)} all-gather(bf16[8,1024]{1,0:T(8,128)(2,1)S(1)} %reduce_sum.9), channel_id=1, replica_groups=mesh['az'=16,'rad'=2] {'rad'}, dimensions={1}, use_global_device_ids=true | all-gather | bytes 49152 | tf_op jit(solution)/shard_map/all_gather | solution.py:567
  71.9 13.9 %responses.1 = f32[16,2,8,1024]{3,2,1,0:T(8,128)} custom-call(bf16[8,2048]{1,0:T(8,128)(2,1)} %all_gather.3.refs_0_, bf16[4,1024,2048]{2,1,0:T(8,128)(2,1)} %refs_1_.6, bf16[4,1024,2048]{2,1,0:T(8,128)(2,1)} %refs_2_.6), custom_call_target="tpu_custom_call" | custom-call | flops 268435456 | bytes 33554432 | tf_op jit(solution)/shard_map/responses/pallas_call | solution.py:168
  85.8 6.9 %all-to-all-start.1 = ((f32[16,2,8,1024]{3,2,1,0:T(8,128)}), f32[16,2,8,1024]{3,2,1,0:T(8,128)S(1)}, u32[]{:S(2)}, u32[]{:S(2)}) async-start(f32[16,2,8,1024]{3,2,1,0:T(8,128)} %responses.1), calls=%async_computation.1 | async-start | bytes 2097152 | tf_op jit(solution)/shard_map/all_to_all | solution.py:569
  92.7 0.6 slice_divide_fusion.1
  93.3 38.1 %flux_layer.3 = (f32[2,1024,1024]{2,1,0:T(8,128)}, f32[2,1024,1024]{2,1,0:T(8,128)}, f32[2,1024,1024]{2,1,0:T(8,128)}) custom-call(f32[2,1024,1024]{2,1,0:T(8,128)} %refs_5_.5, f32[2,1024,1024]{2,1,0:T(8,128)} %refs_7_.3, f32[2,1024,1024]{2,1,0:T(8,128)} %refs_8_.3, ...), custom_call_target="tpu_custom_call", output_to_operand_aliasing={{0}: (15, {}), {1}: (16, {}), {2}: (17, {})} | custom-call | flops 104857600 | bytes 25165824 | tf_op jit(solution)/shard_map/flux_layer/pallas_call | solution.py:428
  131.3 0.0 all-to-all-done.1
  131.4 1.1 slice_bitcast_fusion
  132.4 18.4 %add_gravity.1 = (f32[2,1024,1024]{2,1,0:T(8,128)}, f32[2,1024,1024]{2,1,0:T(8,128)}, f32[1024,1024]{1,0:T(8,128)}) custom-call(f32[128,1024]{1,0:T(8,128)} %get-tuple-element.57.refs_0_, f32[128,1024]{1,0:T(8,128)} %get-tuple-element.56.refs_1_, f32[1,1024]{1,0:T(1,128)} %bitcast.7, bf16[128,1024]{1,0:T(8,128)(2,1)} %get-tuple-element.69.refs_5_.refs_3_, ...), custom_call_target="tpu_custom_call" | custom-call | flops 2415919104 | bytes 46137344 | tf_op jit(solution)/shard_map/add_gravity/pallas_call | solution.py:489
  (19 shorter events, 0.1 us)
Async XLA Ops:
  2.6 18.4 %collective-permute-start.2 = (bf16[2,3,1024]{2,1,0:T(4,128)(2,1)S(1)}, bf16[2,3,1024]{2,1,0:T(4,128)(2,1)S(1)}, u32[]{:S(2)}, u32[]{:S(2)}) collective-permute-start(bf16[2,3,1024]{2,1,0:T(4,128)(2,1)S(1)} %fusion.3), channel_id=1, source_target_pairs={{0,1},{1,0},{2,3},{3,2},{4,5},{5,4},{6,7},{7,6},{8,9},{9,8},{10,11... | collective-permute-start | bytes 36872 | tf_op jit(solution)/shard_map/ppermute | solution.py:518
  14.4 8.8 %collective-permute-start = (bf16[16,1024]{1,0:T(8,128)(2,1)}, bf16[16,1024]{1,0:T(8,128)(2,1)S(1)}, u32[]{:S(2)}, u32[]{:S(2)}) collective-permute-start(bf16[16,1024]{1,0:T(8,128)(2,1)} %get-tuple-element.27), channel_id=1, source_target_pairs={{0,2},{2,4},{4,6},{6,8},{8,10},{10,12},{12,14},{14,16},{16,18},{18... | collective-permute-start | bytes 98312 | tf_op jit(solution)/shard_map/ppermute | solution.py:534
  16.9 6.2 %collective-permute-start.1 = (bf16[16,1024]{1,0:T(8,128)(2,1)}, bf16[16,1024]{1,0:T(8,128)(2,1)S(1)}, u32[]{:S(2)}, u32[]{:S(2)}) collective-permute-start(bf16[16,1024]{1,0:T(8,128)(2,1)} %get-tuple-element.28), channel_id=1, source_target_pairs={{2,0},{4,2},{6,4},{8,6},{10,8},{12,10},{14,12},{16,14},{18,16},{20... | collective-permute-start | bytes 98312 | tf_op jit(solution)/shard_map/ppermute | solution.py:534
  23.2 8.5 %copy-start = (bf16[16,1024]{1,0:T(8,128)(2,1)}, bf16[16,1024]{1,0:T(8,128)(2,1)S(1)}, u32[]{:S(2)}) copy-start(bf16[16,1024]{1,0:T(8,128)(2,1)S(1)} %collective-permute-done.refs_12_) | copy-start | bytes 98308
  23.2 8.5 %copy-start.1 = (bf16[16,1024]{1,0:T(8,128)(2,1)}, bf16[16,1024]{1,0:T(8,128)(2,1)S(1)}, u32[]{:S(2)}) copy-start(bf16[16,1024]{1,0:T(8,128)(2,1)S(1)} %collective-permute-done.1.refs_13_) | copy-start | bytes 98308
  23.2 46.7 %all-to-all-start = ((f32[16,8,1024]{2,1,0:T(8,128)}), f32[16,8,1024]{2,1,0:T(8,128)S(1)}, u32[]{:S(2)}, u32[]{:S(2)}) async-start(f32[16,8,1024]{2,1,0:T(8,128)} %bitcast.6), calls=%async_computation | async-start | bytes 1048576 | tf_op jit(solution)/shard_map/all_to_all | solution.py:560
  85.8 45.6 %all-to-all-start.1 = ((f32[16,2,8,1024]{3,2,1,0:T(8,128)}), f32[16,2,8,1024]{3,2,1,0:T(8,128)S(1)}, u32[]{:S(2)}, u32[]{:S(2)}) async-start(f32[16,2,8,1024]{3,2,1,0:T(8,128)} %responses.1), calls=%async_computation.1 | async-start | bytes 2097152 | tf_op jit(solution)/shard_map/all_to_all | solution.py:569

commit v9 on v8

--- a/solution.py
+++ b/solution.py
@@ -230,7 +230,6 @@
         self.strips = self.rows // SUB
         self.index = pl.program_id(0)
         self.lane = lax.broadcasted_iota(jnp.int32, (SUB, LANES), 1)
-        self.sub = lax.broadcasted_iota(jnp.int32, (SUB, LANES), 0)
         side_rows = jnp.concatenate(
             [coef_rows[...], low_rows[...].astype(jnp.float32), high_rows[...].astype(jnp.float32)], axis=0
         )
@@ -308,14 +307,14 @@
     outs = refs[-8:-5]
     side, cell, faces, sides, held = refs[-5:]
     side[...] = block.side
-    lane, sub, at, fields, rows_at = block.lane, block.sub, block.at, block.fields, block.rows_at
+    lane, at, fields, rows_at = block.lane, block.at, block.fields, block.rows_at
     columns, strips, rows = block.columns, block.strips, block.rows
 
     after = block.coef_after[...].T
     root_face, sound_face = block.columns_of(after[:SUB], (ROOT_FACE, SOUND_FACE))
     for col in range(columns):
         for slot, value in enumerate(block.row_before(col)):
-            cell[slot, 0:SUB, at(col)] = value
+            cell[slot, col, 0:SUB, :] = value
         last = [
             jnp.broadcast_to(ref[rows - 1 : rows, at(col)], (SUB, LANES)) for ref in fields
         ]
@@ -323,32 +322,31 @@
             block.row_after(col), block.radial_state(last)[1], root_face, sound_face
         )
         for comp in range(3):
-            faces[comp, rows : rows + SUB, at(col)] = flux[comp]
+            faces[comp, col, rows : rows + SUB, :] = flux[comp]
+
+    def shifted(place, by):
+        return pl.ds(pl.multiple_of(place * SUB, SUB) + by, SUB)
 
     def update(place):
-        here, above = rows_at(place), rows_at(place + 1)
+        here, above = rows_at(place), shifted(place, 1)
         out_coef, az = block.columns_of(side[here, :], (OUT, AZ))
         for col in range(columns):
             for comp in range(3):
-                face = jnp.where(sub == 0, faces[comp, above, at(col)], faces[comp, here, at(col)])
                 edge = jnp.where(lane == 0, sides[comp, here, at(col + 1)], sides[comp, here, at(col)])
                 outs[comp][here, at(col)] = held[comp, here, at(col)] - (
-                    out_coef * pltpu.roll(face, SUB - 1, 0) + az * pltpu.roll(edge, LANES - 1, 1)
+                    out_coef * faces[comp, col, above, :] + az * pltpu.roll(edge, LANES - 1, 1)
                 )
 
     def face_fluxes(place):
-        here, inside = rows_at(place), rows_at(place + 1)
+        here, inside, below = rows_at(place), rows_at(place + 1), shifted(place, SUB - 1)
         coef = side[here, :]
         root_face, sound_face, in_coef, root_mid, sound_mid, az, spin, pull = block.columns_of(
             coef, (ROOT_FACE, SOUND_FACE, IN, ROOT_MID, SOUND_MID, AZ, SPIN, PULL)
         )
         left = block.ghost_values(layer, coef, 0, sound_mid)
         for col in range(columns):
-            now = [cell[slot, inside, at(col)] for slot in range(CELL_VALUES)]
-            lower = [
-                pltpu.roll(jnp.where(sub == SUB - 1, cell[slot, here, at(col)], now[slot]), 1, 0)
-                for slot in range(6)
-            ]
+            now = [cell[slot, col, inside, :] for slot in range(CELL_VALUES)]
+            lower = [cell[slot, col, below, :] for slot in range(6)]
             flux_r = block.radial_flux(now[:6], lower, root_face, sound_face)
             values = (*now[:3], now[6], now[5], now[7])
             lower = [
@@ -357,7 +355,7 @@
             left = values
             flux = block.azimuth_flux(values, lower, root_mid)
             for comp in range(3):
-                faces[comp, here, at(col)] = flux_r[comp]
+                faces[comp, col, here, :] = flux_r[comp]
                 sides[comp, here, at(col)] = flux[comp]
             held[0, here, at(col)] = now[0] + (in_coef * flux_r[0] + az * flux[0])
             held[1, here, at(col)] = (now[1] + (in_coef * flux_r[1] + az * flux[1])) + (
@@ -378,7 +376,7 @@
             vel = state[2] * inv
             values = (*values, jnp.abs(vel), state[2] * vel + sound_mid * state[0])
             for slot, value in enumerate(values):
-                cell[slot, inside, at(col)] = value
+                cell[slot, col, inside, :] = value
 
     def iteration(place, carry):
         def clamped(late):
@@ -420,8 +418,8 @@
             specs.append(pl.BlockSpec(memory_space=pl.ANY))
     scratch = [
         pltpu.VMEM((block, LANES), jnp.float32),
-        pltpu.VMEM((CELL_VALUES, block + SUB, cells), jnp.float32),
-        pltpu.VMEM((3, block + SUB, cells), jnp.float32),
+        pltpu.VMEM((CELL_VALUES, cells // LANES, block + SUB, LANES), jnp.float32),
+        pltpu.VMEM((3, cells // LANES, block + SUB, LANES), jnp.float32),
         pltpu.VMEM((3, block, cells + LANES), jnp.float32),
         pltpu.VMEM((3, block, cells), jnp.float32),
     ]

time: 151 us -> 149 us (0.987)
  Pallas kernels: 117 us -> 115 us
    pallas_call x2, Pallas kernels: 76.2 us -> 74.3 us  [flux_layer(): pl.pallas_call(lambda *refs: flux_kernel(layer, count, refs), grid=(count...]
  transfers between devices with their start and end apart: 5 -> 5, of which waited for: 1 -> 1; matrix products, arithmetic and copies ran while one was open for 4% -> 4% of each run, Pallas kernels for 56% -> 55%
where the time goes in v9:
time: 149 us
  Pallas kernels  115 us (77%)
  starting transfers between devices  21 us (14%)
  other arithmetic  4.62 us (3%)
  local copies, waits for them, and re-layouts  4.31 us (3%)
  blocking collectives  1.96 us (1%)
  waiting for transfers between devices  1.52 us (1%)
    pallas_call x2, Pallas kernels, flux_layer(): pl.pallas_call(lambda *refs: flux_kernel(layer, count, refs), grid=(count...  74.3 us
    pallas_call x1, Pallas kernels, add_gravity(): pl.pallas_call(lambda *refs: gravity_kernel(rows // block, refs), grid=(r...  18.4 us
    pallas_call x1, Pallas kernels, responses(): pl.pallas_call(lambda *refs: response_kernel(steps, refs), grid=(steps,),...  13.9 us
    pallas_call x1, Pallas kernels, surface_modes(): pl.pallas_call(lambda *refs: modes_kernel(scale, rows // block, refs), gr...  8.1 us
    all_to_all x1, starting transfers between devices, local(): every = lax.all_to_all(parts, 'az', split_axis=0, concat_axis=0, tiled=True)  6.92 us
    all_to_all x1, starting transfers between devices, local(): lax.all_to_all(partial.reshape(az_count, pair_count, rows), 'az', split_a...  6.91 us
    ppermute x2, starting transfers between devices, exchange_edges(): return (lax.ppermute(last, 'az', right), lax.ppermute(first, 'az', left))  6.63 us
    convert_element_type x1, other arithmetic, pieces_of(): return out + [x.astype(jnp.bfloat16)]  3.14 us
  transfers between devices with their start and end apart: 5, of which 1 were waited for; matrix products, arithmetic and copies ran while one was open for 4% of the time, Pallas kernels for 55%

profile of v9, /device:TPU:0, one launch (start us, length us, event | category | flops | bytes accessed | tf_op | source)
XLA Modules:
  0.0 148.9 jit_solution(12854490546886545741)
XLA Ops:
  0.6 0.9 fusion.10
  1.5 1.0 fusion.8
  2.5 0.1 fusion.3
  2.6 0.5 collective-permute-start.2
  3.1 3.1 %fusion = (bf16[128,1024]{1,0:T(8,128)(2,1)}, bf16[128,1024]{1,0:T(8,128)(2,1)}, bf16[128,1024]{1,0:T(8,128)(2,1)}) fusion(s32[128]{0:T(128)S(1)} %get-tuple-element.73, s32[128]{0:T(128)S(1)} %get-tuple-element.75, f32[1024]{0:T(1024)S(1)} %add_multiply_fusion.1, s32[128]{0:T(128)S(1)} %get-tuple-element.74, s32[128]{0:T(128)S(1)} %get-tuple-element.76, ...), kind=kLoop, calls=%fused_computation.4 | loop fusion | flops 1703936 | bytes 792832 | tf_op jit(solution)/shard_map/convert_element_type | solution.py:49
  6.3 8.1 %surface_modes.1 = (f32[128,1024]{1,0:T(8,128)}, bf16[16,1024]{1,0:T(8,128)(2,1)}, bf16[16,1024]{1,0:T(8,128)(2,1)}) custom-call(f32[2,1024,1024]{2,1,0:T(8,128)} %refs_5_.5, f32[2,1024,1024]{2,1,0:T(8,128)} %refs_7_.3, f32[2,1024,1024]{2,1,0:T(8,128)} %refs_8_.3, f32[2,1024,1024]{2,1,0:T(8,128)} %refs_7_.3, f32[2,1024,1024]{2,1,0:T(8,128)} %refs_8_.3, ...), custom_call_target="tpu_custom_call" | custom-call | flops 1610612736 | bytes 8388608 | tf_op jit(solution)/shard_map/surface_modes/pallas_call | solution.py:122
  14.4 2.6 %collective-permute-start = (bf16[16,1024]{1,0:T(8,128)(2,1)}, bf16[16,1024]{1,0:T(8,128)(2,1)S(1)}, u32[]{:S(2)}, u32[]{:S(2)}) collective-permute-start(bf16[16,1024]{1,0:T(8,128)(2,1)} %get-tuple-element.27), channel_id=1, source_target_pairs={{0,2},{2,4},{4,6},{6,8},{8,10},{10,12},{12,14},{14,16},{16,18},{18... | collective-permute-start | bytes 98312 | tf_op jit(solution)/shard_map/ppermute | solution.py:532
  16.9 4.1 %collective-permute-start.1 = (bf16[16,1024]{1,0:T(8,128)(2,1)}, bf16[16,1024]{1,0:T(8,128)(2,1)S(1)}, u32[]{:S(2)}, u32[]{:S(2)}) collective-permute-start(bf16[16,1024]{1,0:T(8,128)(2,1)} %get-tuple-element.28), channel_id=1, source_target_pairs={{2,0},{4,2},{6,4},{8,6},{10,8},{12,10},{14,12},{16,14},{18,16},{20... | collective-permute-start | bytes 98312 | tf_op jit(solution)/shard_map/ppermute | solution.py:532
  21.0 0.0 collective-permute-done.2
  21.0 0.7 convert_select_fusion
  21.7 1.5 %collective-permute-done.refs_12_ = bf16[16,1024]{1,0:T(8,128)(2,1)S(1)} collective-permute-done((bf16[16,1024]{1,0:T(8,128)(2,1)}, bf16[16,1024]{1,0:T(8,128)(2,1)S(1)}, u32[]{:S(2)}, u32[]{:S(2)}) %collective-permute-start) | collective-permute-done | bytes 32800 | tf_op jit(solution)/shard_map/ppermute | solution.py:532
  23.2 0.0 copy-start
  23.2 0.0 collective-permute-done.1.refs_13_
  23.2 0.0 copy-start.1
  23.2 6.9 %all-to-all-start = ((f32[16,8,1024]{2,1,0:T(8,128)}), f32[16,8,1024]{2,1,0:T(8,128)S(1)}, u32[]{:S(2)}, u32[]{:S(2)}) async-start(f32[16,8,1024]{2,1,0:T(8,128)} %bitcast.6), calls=%async_computation | async-start | bytes 1048576 | tf_op jit(solution)/shard_map/all_to_all | solution.py:558
  30.1 0.1 multiply_divide_fusion
  30.4 1.3 stack.55.refs_11_.refs_14_
  31.7 0.0 copy-done
  31.7 0.0 copy-done.1
  31.7 37.2 %flux_layer.2 = (f32[2,1024,1024]{2,1,0:T(8,128)}, f32[2,1024,1024]{2,1,0:T(8,128)}, f32[2,1024,1024]{2,1,0:T(8,128)}) custom-call(f32[2,1024,1024]{2,1,0:T(8,128)} %refs_5_.5, f32[2,1024,1024]{2,1,0:T(8,128)} %refs_7_.3, f32[2,1024,1024]{2,1,0:T(8,128)} %refs_8_.3, f32[2,1024,1024]{2,1,0:T(8,128)} %refs_5_.5, f32[2,1024,1024]{2,1,0:T(8,128)} %refs_7_.3, ...), custom_call_target="tpu_custom_call" | custom-call | flops 104857600 | bytes 25165824 | tf_op jit(solution)/shard_map/flux_layer/pallas_call | solution.py:426
  68.9 0.0 all-to-all-done
  68.9 2.0 %all_gather.3.refs_0_ = bf16[8,2048]{1,0:T(8,128)(2,1)} all-gather(bf16[8,1024]{1,0:T(8,128)(2,1)S(1)} %reduce_sum.9), channel_id=1, replica_groups=mesh['az'=16,'rad'=2] {'rad'}, dimensions={1}, use_global_device_ids=true | all-gather | bytes 49152 | tf_op jit(solution)/shard_map/all_gather | solution.py:565
  70.9 13.9 %responses.1 = f32[16,2,8,1024]{3,2,1,0:T(8,128)} custom-call(bf16[8,2048]{1,0:T(8,128)(2,1)} %all_gather.3.refs_0_, bf16[4,1024,2048]{2,1,0:T(8,128)(2,1)} %refs_1_.6, bf16[4,1024,2048]{2,1,0:T(8,128)(2,1)} %refs_2_.6), custom_call_target="tpu_custom_call" | custom-call | flops 268435456 | bytes 33554432 | tf_op jit(solution)/shard_map/responses/pallas_call | solution.py:168
  84.8 6.9 %all-to-all-start.1 = ((f32[16,2,8,1024]{3,2,1,0:T(8,128)}), f32[16,2,8,1024]{3,2,1,0:T(8,128)S(1)}, u32[]{:S(2)}, u32[]{:S(2)}) async-start(f32[16,2,8,1024]{3,2,1,0:T(8,128)} %responses.1), calls=%async_computation.1 | async-start | bytes 2097152 | tf_op jit(solution)/shard_map/all_to_all | solution.py:567
  91.7 0.6 slice_divide_fusion.1
  92.3 37.1 %flux_layer.3 = (f32[2,1024,1024]{2,1,0:T(8,128)}, f32[2,1024,1024]{2,1,0:T(8,128)}, f32[2,1024,1024]{2,1,0:T(8,128)}) custom-call(f32[2,1024,1024]{2,1,0:T(8,128)} %refs_5_.5, f32[2,1024,1024]{2,1,0:T(8,128)} %refs_7_.3, f32[2,1024,1024]{2,1,0:T(8,128)} %refs_8_.3, ...), custom_call_target="tpu_custom_call", output_to_operand_aliasing={{0}: (15, {}), {1}: (16, {}), {2}: (17, {})} | custom-call | flops 104857600 | bytes 25165824 | tf_op jit(solution)/shard_map/flux_layer/pallas_call | solution.py:426
  129.4 0.0 all-to-all-done.1
  129.4 1.1 slice_bitcast_fusion
  130.5 18.4 %add_gravity.1 = (f32[2,1024,1024]{2,1,0:T(8,128)}, f32[2,1024,1024]{2,1,0:T(8,128)}, f32[1024,1024]{1,0:T(8,128)}) custom-call(f32[128,1024]{1,0:T(8,128)} %get-tuple-element.57.refs_0_, f32[128,1024]{1,0:T(8,128)} %get-tuple-element.56.refs_1_, f32[1,1024]{1,0:T(1,128)} %bitcast.7, bf16[128,1024]{1,0:T(8,128)(2,1)} %get-tuple-element.69.refs_5_.refs_3_, ...), custom_call_target="tpu_custom_call" | custom-call | flops 2415919104 | bytes 46137344 | tf_op jit(solution)/shard_map/add_gravity/pallas_call | solution.py:487
  (19 shorter events, 0.1 us)
Async XLA Ops:
  2.6 18.4 %collective-permute-start.2 = (bf16[2,3,1024]{2,1,0:T(4,128)(2,1)S(1)}, bf16[2,3,1024]{2,1,0:T(4,128)(2,1)S(1)}, u32[]{:S(2)}, u32[]{:S(2)}) collective-permute-start(bf16[2,3,1024]{2,1,0:T(4,128)(2,1)S(1)} %fusion.3), channel_id=1, source_target_pairs={{0,1},{1,0},{2,3},{3,2},{4,5},{5,4},{6,7},{7,6},{8,9},{9,8},{10,11... | collective-permute-start | bytes 36872 | tf_op jit(solution)/shard_map/ppermute | solution.py:516
  14.4 8.8 %collective-permute-start = (bf16[16,1024]{1,0:T(8,128)(2,1)}, bf16[16,1024]{1,0:T(8,128)(2,1)S(1)}, u32[]{:S(2)}, u32[]{:S(2)}) collective-permute-start(bf16[16,1024]{1,0:T(8,128)(2,1)} %get-tuple-element.27), channel_id=1, source_target_pairs={{0,2},{2,4},{4,6},{6,8},{8,10},{10,12},{12,14},{14,16},{16,18},{18... | collective-permute-start | bytes 98312 | tf_op jit(solution)/shard_map/ppermute | solution.py:532
  16.9 6.2 %collective-permute-start.1 = (bf16[16,1024]{1,0:T(8,128)(2,1)}, bf16[16,1024]{1,0:T(8,128)(2,1)S(1)}, u32[]{:S(2)}, u32[]{:S(2)}) collective-permute-start(bf16[16,1024]{1,0:T(8,128)(2,1)} %get-tuple-element.28), channel_id=1, source_target_pairs={{2,0},{4,2},{6,4},{8,6},{10,8},{12,10},{14,12},{16,14},{18,16},{20... | collective-permute-start | bytes 98312 | tf_op jit(solution)/shard_map/ppermute | solution.py:532
  23.2 8.5 %copy-start = (bf16[16,1024]{1,0:T(8,128)(2,1)}, bf16[16,1024]{1,0:T(8,128)(2,1)S(1)}, u32[]{:S(2)}) copy-start(bf16[16,1024]{1,0:T(8,128)(2,1)S(1)} %collective-permute-done.refs_12_) | copy-start | bytes 98308
  23.2 8.5 %copy-start.1 = (bf16[16,1024]{1,0:T(8,128)(2,1)}, bf16[16,1024]{1,0:T(8,128)(2,1)S(1)}, u32[]{:S(2)}) copy-start(bf16[16,1024]{1,0:T(8,128)(2,1)S(1)} %collective-permute-done.1.refs_13_) | copy-start | bytes 98308
  23.2 45.7 %all-to-all-start = ((f32[16,8,1024]{2,1,0:T(8,128)}), f32[16,8,1024]{2,1,0:T(8,128)S(1)}, u32[]{:S(2)}, u32[]{:S(2)}) async-start(f32[16,8,1024]{2,1,0:T(8,128)} %bitcast.6), calls=%async_computation | async-start | bytes 1048576 | tf_op jit(solution)/shard_map/all_to_all | solution.py:558
  84.8 44.6 %all-to-all-start.1 = ((f32[16,2,8,1024]{3,2,1,0:T(8,128)}), f32[16,2,8,1024]{3,2,1,0:T(8,128)S(1)}, u32[]{:S(2)}, u32[]{:S(2)}) async-start(f32[16,2,8,1024]{3,2,1,0:T(8,128)} %responses.1), calls=%async_computation.1 | async-start | bytes 2097152 | tf_op jit(solution)/shard_map/all_to_all | solution.py:567

commit v10 on v9

--- a/solution.py
+++ b/solution.py
@@ -53,10 +53,9 @@
 
 
 def modes_kernel(scale, steps, refs):
-    firsts, lasts = refs[1:3], refs[3:5]
-    *tables, out_ref, first_ref, last_ref, wide_ref, density, sems = refs[5:]
+    *tables, out_ref, wide_ref, density, sems = refs[1:]
     thin_ref = tables[2]
-    layers, _, cells = density.shape
+    layers = density.shape[0]
     rows_here = fetch_rows(refs[:1], [density], sems, steps)
     cols = thin_ref.shape[0]
 
@@ -86,23 +85,19 @@
     )
     out_ref[...] = (scale * total).T
 
-    block = out_ref.shape[1]
+
+def edge_kernel(refs):
+    firsts, lasts = refs[:3], refs[3:6]
+    first_ref, last_ref = refs[6:]
+    layers, block, _ = firsts[0].shape
     lane = lax.broadcasted_iota(jnp.int32, (block, LANES), 1)
     edges = jnp.zeros((block, LANES), jnp.float32)
     for layer in range(layers):
-        sides = (
-            (0, 0, (density[layer, rows_here, :LANES], firsts[0][layer], firsts[1][layer])),
-            (
-                EDGE_ROWS,
-                LANES - 1,
-                (density[layer, rows_here, cells - LANES :], lasts[0][layer], lasts[1][layer]),
-            ),
-        )
-        for base, place, tiles in sides:
+        for base, place, tiles in ((0, 0, firsts), (EDGE_ROWS, LANES - 1, lasts)):
             for comp, tile in enumerate(tiles):
                 edges = jnp.where(
                     lane == base + 3 * layer + comp,
-                    jnp.broadcast_to(tile[:, place : place + 1], (block, LANES)),
+                    jnp.broadcast_to(tile[layer, :, place : place + 1], (block, LANES)),
                     edges,
                 )
     edges = edges.T
@@ -110,33 +105,49 @@
     last_ref[...] = edges[EDGE_ROWS : 2 * EDGE_ROWS].astype(jnp.bfloat16)
 
 
-def surface_modes(fields, tables, scale):
+def edge_cells(fields):
     layers, rows, cells = fields[0].shape
-    cols = tables[0].shape[0]
     block = min(rows, 2 * LANES)
     first = pl.BlockSpec((layers, block, LANES), lambda i: (0, i, 0))
     last = pl.BlockSpec((layers, block, LANES), lambda i: (0, i, cells // LANES - 1))
-    table_spec = pl.BlockSpec((cols, cells), lambda i: (0, 0))
     edge_spec = pl.BlockSpec((EDGE_ROWS, block), lambda i: (0, i))
     edge_shape = jax.ShapeDtypeStruct((EDGE_ROWS, rows), jnp.bfloat16)
     return pl.pallas_call(
+        lambda *refs: edge_kernel(refs),
+        grid=(rows // block,),
+        in_specs=[first] * 3 + [last] * 3,
+        out_specs=[edge_spec, edge_spec],
+        out_shape=[edge_shape, edge_shape],
+        compiler_params=pltpu.CompilerParams(vmem_limit_bytes=VMEM_BYTES),
+        cost_estimate=pl.CostEstimate(
+            flops=40 * rows * LANES, bytes_accessed=24 * layers * rows * LANES, transcendentals=0
+        ),
+        name="edge_cells",
+    )(*fields, *fields)
+
+
+def surface_modes(density, tables, scale):
+    layers, rows, cells = density.shape
+    cols = tables[0].shape[0]
+    block = min(rows, 2 * LANES)
+    table_spec = pl.BlockSpec((cols, cells), lambda i: (0, 0))
+    return pl.pallas_call(
         lambda *refs: modes_kernel(scale, rows // block, refs),
         grid=(rows // block,),
-        in_specs=[pl.BlockSpec(memory_space=pl.ANY)]
-        + [first, first, last, last] + [table_spec] * 3,
-        out_specs=[pl.BlockSpec((cols, block), lambda i: (0, i)), edge_spec, edge_spec],
-        out_shape=[jax.ShapeDtypeStruct((cols, rows), jnp.float32), edge_shape, edge_shape],
+        in_specs=[pl.BlockSpec(memory_space=pl.ANY)] + [table_spec] * 3,
+        out_specs=pl.BlockSpec((cols, block), lambda i: (0, i)),
+        out_shape=jax.ShapeDtypeStruct((cols, rows), jnp.float32),
         scratch_shapes=[
             pltpu.VMEM((2 * cols, cells), jnp.bfloat16),
-            pltpu.VMEM(fields[0].shape, jnp.float32),
+            pltpu.VMEM(density.shape, jnp.float32),
             pltpu.SemaphoreType.DMA((1, rows // block)),
         ],
         compiler_params=pltpu.CompilerParams(vmem_limit_bytes=VMEM_BYTES),
         cost_estimate=pl.CostEstimate(
-            flops=12 * rows * cells * cols, bytes_accessed=4 * fields[0].size, transcendentals=0
+            flops=12 * rows * cells * cols, bytes_accessed=4 * density.size, transcendentals=0
         ),
         name="surface_modes",
-    )(*fields, fields[1], fields[2], *tables)
+    )(density, *tables)
 
 
 def response_kernel(steps, refs):
@@ -302,7 +313,7 @@
 CELL_VALUES = 8
 
 
-def flux_kernel(layer, block_count, refs):
+def flux_kernel(together, layer, block_count, refs):
     block = FluxBlock(block_count, refs)
     outs = refs[-8:-5]
     side, cell, faces, sides, held = refs[-5:]
@@ -330,11 +341,24 @@
     def update(place):
         here, above = rows_at(place), shifted(place, 1)
         out_coef, az = block.columns_of(side[here, :], (OUT, AZ))
+        if together:
+            side_row, held_row, face_row = sides[:, here, :], held[:, here, :], faces[:, :, above, :]
+
         for col in range(columns):
             for comp in range(3):
-                edge = jnp.where(lane == 0, sides[comp, here, at(col + 1)], sides[comp, here, at(col)])
-                outs[comp][here, at(col)] = held[comp, here, at(col)] - (
-                    out_coef * faces[comp, col, above, :] + az * pltpu.roll(edge, LANES - 1, 1)
+                if together:
+                    parts = [
+                        row[comp, :, k * LANES : (k + 1) * LANES]
+                        for row, k in ((side_row, col + 1), (side_row, col), (held_row, col))
+                    ] + [face_row[comp, col]]
+                else:
+                    parts = [
+                        sides[comp, here, at(col + 1)], sides[comp, here, at(col)],
+                        held[comp, here, at(col)], faces[comp, col, above, :],
+                    ]
+                edge = jnp.where(lane == 0, parts[0], parts[1])
+                outs[comp][here, at(col)] = parts[2] - (
+                    out_coef * parts[3] + az * pltpu.roll(edge, LANES - 1, 1)
                 )
 
     def face_fluxes(place):
@@ -344,9 +368,15 @@
             coef, (ROOT_FACE, SOUND_FACE, IN, ROOT_MID, SOUND_MID, AZ, SPIN, PULL)
         )
         left = block.ghost_values(layer, coef, 0, sound_mid)
+        if together:
+            now_row, low_row = cell[:, :, inside, :], cell[:6, :, below, :]
         for col in range(columns):
-            now = [cell[slot, col, inside, :] for slot in range(CELL_VALUES)]
-            lower = [cell[slot, col, below, :] for slot in range(6)]
+            if together:
+                now = [now_row[slot, col] for slot in range(CELL_VALUES)]
+                lower = [low_row[slot, col] for slot in range(6)]
+            else:
+                now = [cell[slot, col, inside, :] for slot in range(CELL_VALUES)]
+                lower = [cell[slot, col, below, :] for slot in range(6)]
             flux_r = block.radial_flux(now[:6], lower, root_face, sound_face)
             values = (*now[:3], now[6], now[5], now[7])
             lower = [
@@ -390,7 +420,7 @@
     lax.fori_loop(0, strips + 3, iteration, 0)
 
 
-def flux_layer(layer, fields, rims, edges, coefs, so_far):
+def flux_layer(layer, together, fields, rims, edges, coefs, so_far):
     layers, rows, cells = fields[0].shape
     block = min(rows, 2 * LANES)
     count = rows // block
@@ -424,7 +454,7 @@
         pltpu.VMEM((3, block, cells), jnp.float32),
     ]
     return pl.pallas_call(
-        lambda *refs: flux_kernel(layer, count, refs),
+        lambda *refs: flux_kernel(together, layer, count, refs),
         grid=(count,),
         in_specs=specs,
         out_specs=[main] * 3,
@@ -440,12 +470,13 @@
 
 
 def gravity_kernel(steps, refs):
-    pot_ref, force_ref, inverse_ref = refs[:3]
-    halves = refs[3:5]
-    out_r, out_phi, out_pot, table_ref, *buffers, sems = refs[8:]
+    every_ref, inverse_ref = refs[:2]
+    halves = refs[2:4]
+    out_r, out_phi, out_pot, table_ref, *buffers, sems = refs[7:]
     density, mom_r, mom_phi = buffers
-    rows_here = fetch_rows(refs[5:8], buffers, sems, steps)
-    cols, block = pot_ref.shape
+    rows_here = fetch_rows(refs[4:7], buffers, sems, steps)
+    copies, _, part, block = every_ref.shape
+    cols = copies * part
 
     @pl.when(pl.program_id(0) == 0)
     def _():
@@ -453,13 +484,14 @@
         table_ref[cols : 2 * cols] = halves[0][...]
         table_ref[2 * cols :] = halves[1][...]
 
-    pot = pot_ref[...]
+    pot = every_ref[:, 0].reshape(cols, block)
+    force = every_ref[:, 1].reshape(cols, block)
     row = lax.broadcasted_iota(jnp.int32, pot.shape, 0)
     even = row % 2 == 0
     mode = (row // 2).astype(jnp.float32)
     swapped = jnp.where(even, pltpu.roll(pot, cols - 1, 0), -pltpu.roll(pot, 1, 0))
     left = jnp.concatenate(
-        [pot, 0.1 * force_ref[...], swapped * (mode * inverse_ref[...])], axis=1
+        [pot, 0.1 * force, swapped * (mode * inverse_ref[...])], axis=1
     )
     high, low = split_bf16(left)
     grid = lax.dot_general(
@@ -475,11 +507,11 @@
         out_phi[layer] = mom_phi[layer, rows_here, :] + here * grid[2 * block :]
 
 
-def add_gravity(pot, force, inverse_mid, tables, density, mom_r, mom_phi):
+def add_gravity(every, inverse_mid, tables, density, mom_r, mom_phi):
     layers, rows, cells = density.shape
-    cols = pot.shape[0]
+    cols = every.shape[0] * every.shape[2]
     block = min(rows, 2 * LANES)
-    modes_spec = pl.BlockSpec((cols, block), lambda i: (0, i))
+    modes_spec = pl.BlockSpec((*every.shape[:3], block), lambda i: (0, 0, 0, i))
     table_spec = pl.BlockSpec((cols, cells), lambda i: (0, 0))
 
     field = pl.BlockSpec((layers, block, cells), lambda i: (0, i, 0))
@@ -488,7 +520,7 @@
         lambda *refs: gravity_kernel(rows // block, refs),
         grid=(rows // block,),
         in_specs=[
-            modes_spec, modes_spec, pl.BlockSpec((1, block), lambda i: (0, i)),
+            modes_spec, pl.BlockSpec((1, block), lambda i: (0, i)),
         ] + [table_spec] * 2 + [pl.BlockSpec(memory_space=pl.ANY)] * 3,
         out_specs=[field, field, pl.BlockSpec((block, cells), lambda i: (i, 0))],
         out_shape=[grid_shape, grid_shape, jax.ShapeDtypeStruct((rows, cells), jnp.float32)],
@@ -501,7 +533,7 @@
         ),
         name="add_gravity",
     )(
-        pot, force, inverse_mid, *tables,
+        every, inverse_mid, *tables,
         density, mom_r, mom_phi,
     )
 
@@ -552,13 +584,15 @@
     rims = exchange_rims(fields, rad_index, rad_count)
     coefs, inverse_mid = row_coefficients(rad_index * rows, rows, step)
 
-    partial, first, last = surface_modes(fields, basis, 1.0 / (az_count * cells))
+    first, last = edge_cells(fields)
+    basis, first, last = lax.optimization_barrier((basis, first, last))
     edges = exchange_edges(first, last, az_count)
+    partial = surface_modes(density, basis, 1.0 / (az_count * cells))
     partial, edges, rims = lax.optimization_barrier((partial, edges, rims))
     pieces = lax.all_to_all(
         partial.reshape(az_count, pair_count, rows), "az", split_axis=0, concat_axis=0, tiled=True
     )
-    results = flux_layer(0, fields, rims, edges, coefs, None)
+    results = flux_layer(0, True, fields, rims, edges, coefs, None)
     pieces, results = lax.optimization_barrier((pieces, results))
 
     own = jnp.sum(pieces, axis=0).astype(jnp.bfloat16)
@@ -567,13 +601,12 @@
     every = lax.all_to_all(parts, "az", split_axis=0, concat_axis=0, tiled=True)
     coefs, parts = lax.optimization_barrier((coefs, parts))
     for layer in range(1, layers):
-        results = flux_layer(layer, fields, rims, edges, coefs, results)
-    pot = every[:, 0].reshape(cols, rows)
-    force = every[:, 1].reshape(cols, rows)
+        results = flux_layer(layer, False, fields, rims, edges, coefs, results)
+    if pair_count % SUB:
+        every = jnp.swapaxes(every, 0, 1).reshape(1, 2, cols, rows)
 
     new_r, new_phi, potential = add_gravity(
-        pot,
-        force,
+        every,
         inverse_mid,
         basis[:2],
         density,

time: 149 us -> 148 us (level)
  starting transfers between devices: 21 us -> 17.5 us
  Pallas kernels: 115 us -> 118 us
  waiting for transfers between devices: 1.52 us -> 0.01 us
    pallas_call x2 -> x3, Pallas kernels: 74.3 us -> 79 us  [the longest x2 74.2 us: flux_layer(): pl.pallas_call(lambda *refs: flux_kernel(together, layer, count, refs), g...]
    all_to_all x1, starting transfers between devices: 6.91 us -> 3.59 us  [local(): lax.all_to_all(partial.reshape(az_count, pair_count, rows), 'az', split_a...]
    ppermute x2, waiting for transfers between devices: 1.51 us -> 0.01 us  [exchange_edges(): return (lax.ppermute(last, 'az', right), lax.ppermute(first, 'az', left))]
  transfers between devices with their start and end apart: 5 -> 5, of which waited for: 1 -> 0; matrix products, arithmetic and copies ran while one was open for 4% -> 4% of each run, Pallas kernels for 55% -> 58%
where the time goes in v10:
time: 148 us; the launch traced here: 147 us
  Pallas kernels  118 us (80%)
  starting transfers between devices  17.5 us (12%)
  other arithmetic  4.62 us (3%)
  local copies, waits for them, and re-layouts  4.23 us (3%)
  blocking collectives  1.96 us (1%)
    pallas_call x2, Pallas kernels, flux_layer(): pl.pallas_call(lambda *refs: flux_kernel(together, layer, count, refs), g...  74.2 us
    pallas_call x1, Pallas kernels, add_gravity(): pl.pallas_call(lambda *refs: gravity_kernel(rows // block, refs), grid=(r...  18.2 us
    pallas_call x1, Pallas kernels, responses(): pl.pallas_call(lambda *refs: response_kernel(steps, refs), grid=(steps,),...  13.9 us
    all_to_all x1, starting transfers between devices, local(): every = lax.all_to_all(parts, 'az', split_axis=0, concat_axis=0, tiled=True)  6.89 us
    pallas_call x1, Pallas kernels, surface_modes(): pl.pallas_call(lambda *refs: modes_kernel(scale, rows // block, refs), gr...  6.79 us
    ppermute x2, starting transfers between devices, exchange_edges(): return (lax.ppermute(last, 'az', right), lax.ppermute(first, 'az', left))  6.52 us
    pallas_call x1, Pallas kernels, edge_cells(): pl.pallas_call(lambda *refs: edge_kernel(refs), grid=(rows // block,), in...  4.78 us
    all_to_all x1, starting transfers between devices, local(): lax.all_to_all(partial.reshape(az_count, pair_count, rows), 'az', split_a...  3.59 us
  transfers between devices with their start and end apart: 5, of which 0 were waited for; matrix products, arithmetic and copies ran while one was open for 4% of the time, Pallas kernels for 58%

profile of v10, /device:TPU:0, one launch (start us, length us, event | category | flops | bytes accessed | tf_op | source)
XLA Modules:
  0.0 147.1 jit_solution(14902379244471821706)
XLA Ops:
  0.6 0.9 fusion.10
  1.5 1.0 fusion.8
  2.5 0.1 fusion.3
  2.6 0.5 collective-permute-start.2
  3.1 4.8 %edge_cells.1 = (bf16[16,1024]{1,0:T(8,128)(2,1)}, bf16[16,1024]{1,0:T(8,128)(2,1)}) custom-call(f32[2,1024,1024]{2,1,0:T(8,128)} %refs_4_.7, f32[2,1024,1024]{2,1,0:T(8,128)} %refs_7_.3, f32[2,1024,1024]{2,1,0:T(8,128)} %refs_8_.3, f32[2,1024,1024]{2,1,0:T(8,128)} %refs_4_.7, f32[2,1024,1024]{2,1,0:T(8,128)} %refs_7_.3, f32[2,1024,1024]{2,1,0:T(8,128)} %refs_8_.3), custom_call_target="tpu_custom_call" | custom-call | flops 5242880 | bytes 6291456 | tf_op jit(solution)/shard_map/edge_cells/pallas_call | solution.py:115
  7.9 3.1 %fusion = (bf16[128,1024]{1,0:T(8,128)(2,1)}, bf16[128,1024]{1,0:T(8,128)(2,1)}, bf16[128,1024]{1,0:T(8,128)(2,1)}) fusion(s32[128]{0:T(128)S(1)} %get-tuple-element.79, s32[128]{0:T(128)S(1)} %get-tuple-element.81, f32[1024]{0:T(1024)S(1)} %add_multiply_fusion.1, s32[128]{0:T(128)S(1)} %get-tuple-element.80, s32[128]{0:T(128)S(1)} %get-tuple-element.82, ...), kind=kLoop, calls=%fused_computation.4 | loop fusion | flops 1703936 | bytes 792832 | tf_op jit(solution)/shard_map/convert_element_type | solution.py:49
  11.0 2.5 %collective-permute-start = (bf16[16,1024]{1,0:T(8,128)(2,1)}, bf16[16,1024]{1,0:T(8,128)(2,1)S(1)}, u32[]{:S(2)}, u32[]{:S(2)}) collective-permute-start(bf16[16,1024]{1,0:T(8,128)(2,1)} %get-tuple-element.35), channel_id=1, source_target_pairs={{0,2},{2,4},{4,6},{6,8},{8,10},{10,12},{12,14},{14,16},{16,18},{18... | collective-permute-start | bytes 98312 | tf_op jit(solution)/shard_map/ppermute | solution.py:564
  13.5 4.0 %collective-permute-start.1 = (bf16[16,1024]{1,0:T(8,128)(2,1)}, bf16[16,1024]{1,0:T(8,128)(2,1)S(1)}, u32[]{:S(2)}, u32[]{:S(2)}) collective-permute-start(bf16[16,1024]{1,0:T(8,128)(2,1)} %get-tuple-element.36), channel_id=1, source_target_pairs={{2,0},{4,2},{6,4},{8,6},{10,8},{12,10},{14,12},{16,14},{18,16},{20... | collective-permute-start | bytes 98312 | tf_op jit(solution)/shard_map/ppermute | solution.py:564
  17.5 6.8 %surface_modes.1 = f32[128,1024]{1,0:T(8,128)} custom-call(f32[2,1024,1024]{2,1,0:T(8,128)} %refs_4_.7, bf16[128,1024]{1,0:T(8,128)(2,1)} %get-tuple-element.32.refs_1_.refs_2_, bf16[128,1024]{1,0:T(8,128)(2,1)} %get-tuple-element.33.refs_2_.refs_3_, bf16[128,1024]{1,0:T(8,128)(2,1)} %get-tuple-element.34.refs_3_), custom_call_target="tpu_custom_call" | custom-call | flops 1610612736 | bytes 8388608 | tf_op jit(solution)/shard_map/surface_modes/pallas_call | solution.py:134
  24.3 0.0 collective-permute-done.2
  24.4 0.7 convert_select_fusion
  25.0 0.0 collective-permute-done.refs_12_
  25.0 0.0 copy-start.1
  25.0 0.0 collective-permute-done.1.refs_13_
  25.0 0.0 copy-start.2
  25.0 3.6 %all-to-all-start = ((f32[16,8,1024]{2,1,0:T(8,128)}), f32[16,8,1024]{2,1,0:T(8,128)S(1)}, u32[]{:S(2)}, u32[]{:S(2)}) async-start(f32[16,8,1024]{2,1,0:T(8,128)} %bitcast.2), calls=%async_computation | async-start | bytes 1048576 | tf_op jit(solution)/shard_map/all_to_all | solution.py:592
  28.7 0.1 multiply_divide_fusion
  28.9 1.3 stack.55.refs_11_.refs_14_
  30.2 0.0 copy-done.1
  30.2 0.0 copy-done.2
  30.3 37.1 %flux_layer.2 = (f32[2,1024,1024]{2,1,0:T(8,128)}, f32[2,1024,1024]{2,1,0:T(8,128)}, f32[2,1024,1024]{2,1,0:T(8,128)}) custom-call(f32[2,1024,1024]{2,1,0:T(8,128)} %refs_4_.7, f32[2,1024,1024]{2,1,0:T(8,128)} %refs_7_.3, f32[2,1024,1024]{2,1,0:T(8,128)} %refs_8_.3, f32[2,1024,1024]{2,1,0:T(8,128)} %refs_4_.7, f32[2,1024,1024]{2,1,0:T(8,128)} %refs_7_.3, ...), custom_call_target="tpu_custom_call" | custom-call | flops 104857600 | bytes 25165824 | tf_op jit(solution)/shard_map/flux_layer/pallas_call | solution.py:456
  67.4 0.0 all-to-all-done
  67.4 2.0 %all_gather.3.refs_0_ = bf16[8,2048]{1,0:T(8,128)(2,1)} all-gather(bf16[8,1024]{1,0:T(8,128)(2,1)S(1)} %reduce_sum.9), channel_id=1, replica_groups=mesh['az'=16,'rad'=2] {'rad'}, dimensions={1}, use_global_device_ids=true | all-gather | bytes 49152 | tf_op jit(solution)/shard_map/all_gather | solution.py:599
  69.4 13.9 %responses.1 = f32[16,2,8,1024]{3,2,1,0:T(8,128)} custom-call(bf16[8,2048]{1,0:T(8,128)(2,1)} %all_gather.3.refs_0_, bf16[4,1024,2048]{2,1,0:T(8,128)(2,1)} %refs_1_.6, bf16[4,1024,2048]{2,1,0:T(8,128)(2,1)} %refs_2_.6), custom_call_target="tpu_custom_call" | custom-call | flops 268435456 | bytes 33554432 | tf_op jit(solution)/shard_map/responses/pallas_call | solution.py:179
  83.3 6.9 %all-to-all-start.1 = ((f32[16,2,8,1024]{3,2,1,0:T(8,128)}), f32[16,2,8,1024]{3,2,1,0:T(8,128)S(1)}, u32[]{:S(2)}, u32[]{:S(2)}) async-start(f32[16,2,8,1024]{3,2,1,0:T(8,128)} %responses.1), calls=%async_computation.1 | async-start | bytes 2097152 | tf_op jit(solution)/shard_map/all_to_all | solution.py:601
  90.2 0.6 slice_divide_fusion.1
  90.8 37.1 %flux_layer.3 = (f32[2,1024,1024]{2,1,0:T(8,128)}, f32[2,1024,1024]{2,1,0:T(8,128)}, f32[2,1024,1024]{2,1,0:T(8,128)}) custom-call(f32[2,1024,1024]{2,1,0:T(8,128)} %refs_4_.7, f32[2,1024,1024]{2,1,0:T(8,128)} %refs_7_.3, f32[2,1024,1024]{2,1,0:T(8,128)} %refs_8_.3, ...), custom_call_target="tpu_custom_call", output_to_operand_aliasing={{0}: (15, {}), {1}: (16, {}), {2}: (17, {})} | custom-call | flops 104857600 | bytes 25165824 | tf_op jit(solution)/shard_map/flux_layer/pallas_call | solution.py:456
  127.9 0.0 all-to-all-done.1.refs_0_
  127.9 0.0 copy-start
  127.9 1.0 copy-done
  128.9 18.2 %add_gravity.1 = (f32[2,1024,1024]{2,1,0:T(8,128)}, f32[2,1024,1024]{2,1,0:T(8,128)}, f32[1024,1024]{1,0:T(8,128)}) custom-call(f32[16,2,8,1024]{3,2,1,0:T(8,128)} %copy-done, f32[1,1024]{1,0:T(1,128)} %bitcast.3, bf16[128,1024]{1,0:T(8,128)(2,1)} %get-tuple-element.32.refs_1_.refs_2_, bf16[128,1024]{1,0:T(8,128)(2,1)} %get-tuple-element.33.refs_2_.refs_3_, ...), custom_call_target="tpu_custom_call" | custom-call | flops 2415919104 | bytes 46137344 | tf_op jit(solution)/shard_map/add_gravity/pallas_call | solution.py:519
  (19 shorter events, 0.1 us)
Async XLA Ops:
  2.6 21.8 %collective-permute-start.2 = (bf16[2,3,1024]{2,1,0:T(4,128)(2,1)S(1)}, bf16[2,3,1024]{2,1,0:T(4,128)(2,1)S(1)}, u32[]{:S(2)}, u32[]{:S(2)}) collective-permute-start(bf16[2,3,1024]{2,1,0:T(4,128)(2,1)S(1)} %fusion.3), channel_id=1, source_target_pairs={{0,1},{1,0},{2,3},{3,2},{4,5},{5,4},{6,7},{7,6},{8,9},{9,8},{10,11... | collective-permute-start | bytes 36872 | tf_op jit(solution)/shard_map/ppermute | solution.py:548
  11.0 14.0 %collective-permute-start = (bf16[16,1024]{1,0:T(8,128)(2,1)}, bf16[16,1024]{1,0:T(8,128)(2,1)S(1)}, u32[]{:S(2)}, u32[]{:S(2)}) collective-permute-start(bf16[16,1024]{1,0:T(8,128)(2,1)} %get-tuple-element.35), channel_id=1, source_target_pairs={{0,2},{2,4},{4,6},{6,8},{8,10},{10,12},{12,14},{14,16},{16,18},{18... | collective-permute-start | bytes 98312 | tf_op jit(solution)/shard_map/ppermute | solution.py:564
  13.5 11.5 %collective-permute-start.1 = (bf16[16,1024]{1,0:T(8,128)(2,1)}, bf16[16,1024]{1,0:T(8,128)(2,1)S(1)}, u32[]{:S(2)}, u32[]{:S(2)}) collective-permute-start(bf16[16,1024]{1,0:T(8,128)(2,1)} %get-tuple-element.36), channel_id=1, source_target_pairs={{2,0},{4,2},{6,4},{8,6},{10,8},{12,10},{14,12},{16,14},{18,16},{20... | collective-permute-start | bytes 98312 | tf_op jit(solution)/shard_map/ppermute | solution.py:564
  25.0 5.2 %copy-start.1 = (bf16[16,1024]{1,0:T(8,128)(2,1)}, bf16[16,1024]{1,0:T(8,128)(2,1)S(1)}, u32[]{:S(2)}) copy-start(bf16[16,1024]{1,0:T(8,128)(2,1)S(1)} %collective-permute-done.refs_12_) | copy-start | bytes 98308
  25.0 5.2 %copy-start.2 = (bf16[16,1024]{1,0:T(8,128)(2,1)}, bf16[16,1024]{1,0:T(8,128)(2,1)S(1)}, u32[]{:S(2)}) copy-start(bf16[16,1024]{1,0:T(8,128)(2,1)S(1)} %collective-permute-done.1.refs_13_) | copy-start | bytes 98308
  25.0 42.3 %all-to-all-start = ((f32[16,8,1024]{2,1,0:T(8,128)}), f32[16,8,1024]{2,1,0:T(8,128)S(1)}, u32[]{:S(2)}, u32[]{:S(2)}) async-start(f32[16,8,1024]{2,1,0:T(8,128)} %bitcast.2), calls=%async_computation | async-start | bytes 1048576 | tf_op jit(solution)/shard_map/all_to_all | solution.py:592
  83.3 44.6 %all-to-all-start.1 = ((f32[16,2,8,1024]{3,2,1,0:T(8,128)}), f32[16,2,8,1024]{3,2,1,0:T(8,128)S(1)}, u32[]{:S(2)}, u32[]{:S(2)}) async-start(f32[16,2,8,1024]{3,2,1,0:T(8,128)} %responses.1), calls=%async_computation.1 | async-start | bytes 2097152 | tf_op jit(solution)/shard_map/all_to_all | solution.py:601
  127.9 1.0 copy-start

commit v11 on v10

--- a/solution.py
+++ b/solution.py
@@ -313,10 +313,10 @@
 CELL_VALUES = 8
 
 
-def flux_kernel(together, layer, block_count, refs):
+def flux_kernel(lag, layer, block_count, refs):
     block = FluxBlock(block_count, refs)
-    outs = refs[-8:-5]
-    side, cell, faces, sides, held = refs[-5:]
+    outs = refs[-7:-4]
+    side, cell, faces, sides = refs[-4:]
     side[...] = block.side
     lane, at, fields, rows_at = block.lane, block.at, block.fields, block.rows_at
     columns, strips, rows = block.columns, block.strips, block.rows
@@ -339,44 +339,33 @@
         return pl.ds(pl.multiple_of(place * SUB, SUB) + by, SUB)
 
     def update(place):
-        here, above = rows_at(place), shifted(place, 1)
-        out_coef, az = block.columns_of(side[here, :], (OUT, AZ))
-        if together:
-            side_row, held_row, face_row = sides[:, here, :], held[:, here, :], faces[:, :, above, :]
-
+        here, inside, above = rows_at(place), rows_at(place + 1), shifted(place, 1)
+        in_coef, out_coef, spin, pull = block.columns_of(side[here, :], (IN, OUT, SPIN, PULL))
         for col in range(columns):
+            density, mom_r, mom_phi, cross, push = (
+                cell[slot, col, inside, :] for slot in (0, 1, 2, 5, 7)
+            )
+            base = (
+                density, mom_r + (spin * push - pull * density), mom_phi - spin * cross
+            )
             for comp in range(3):
-                if together:
-                    parts = [
-                        row[comp, :, k * LANES : (k + 1) * LANES]
-                        for row, k in ((side_row, col + 1), (side_row, col), (held_row, col))
-                    ] + [face_row[comp, col]]
-                else:
-                    parts = [
-                        sides[comp, here, at(col + 1)], sides[comp, here, at(col)],
-                        held[comp, here, at(col)], faces[comp, col, above, :],
-                    ]
-                edge = jnp.where(lane == 0, parts[0], parts[1])
-                outs[comp][here, at(col)] = parts[2] - (
-                    out_coef * parts[3] + az * pltpu.roll(edge, LANES - 1, 1)
+                low = sides[comp, here, at(col)]
+                edge = jnp.where(lane == 0, sides[comp, here, at(col + 1)], low)
+                outs[comp][here, at(col)] = base[comp] + (
+                    (in_coef * faces[comp, col, here, :] - out_coef * faces[comp, col, above, :])
+                    + (low - pltpu.roll(edge, LANES - 1, 1))
                 )
 
     def face_fluxes(place):
         here, inside, below = rows_at(place), rows_at(place + 1), shifted(place, SUB - 1)
         coef = side[here, :]
-        root_face, sound_face, in_coef, root_mid, sound_mid, az, spin, pull = block.columns_of(
-            coef, (ROOT_FACE, SOUND_FACE, IN, ROOT_MID, SOUND_MID, AZ, SPIN, PULL)
+        root_face, sound_face, root_mid, sound_mid, az = block.columns_of(
+            coef, (ROOT_FACE, SOUND_FACE, ROOT_MID, SOUND_MID, AZ)
         )
         left = block.ghost_values(layer, coef, 0, sound_mid)
-        if together:
-            now_row, low_row = cell[:, :, inside, :], cell[:6, :, below, :]
         for col in range(columns):
-            if together:
-                now = [now_row[slot, col] for slot in range(CELL_VALUES)]
-                lower = [low_row[slot, col] for slot in range(6)]
-            else:
-                now = [cell[slot, col, inside, :] for slot in range(CELL_VALUES)]
-                lower = [cell[slot, col, below, :] for slot in range(6)]
+            now = [cell[slot, col, inside, :] for slot in range(CELL_VALUES)]
+            lower = [cell[slot, col, below, :] for slot in range(6)]
             flux_r = block.radial_flux(now[:6], lower, root_face, sound_face)
             values = (*now[:3], now[6], now[5], now[7])
             lower = [
@@ -386,16 +375,11 @@
             flux = block.azimuth_flux(values, lower, root_mid)
             for comp in range(3):
                 faces[comp, col, here, :] = flux_r[comp]
-                sides[comp, here, at(col)] = flux[comp]
-            held[0, here, at(col)] = now[0] + (in_coef * flux_r[0] + az * flux[0])
-            held[1, here, at(col)] = (now[1] + (in_coef * flux_r[1] + az * flux[1])) + (
-                spin * now[7] - pull * now[0]
-            )
-            held[2, here, at(col)] = (now[2] + (in_coef * flux_r[2] + az * flux[2])) - spin * now[5]
+                sides[comp, here, at(col)] = az * flux[comp]
         values = block.ghost_values(layer, coef, 1, sound_mid)
         lower = [pltpu.roll(a, 1, 1) for a in left]
         for comp, value in enumerate(block.azimuth_flux(values, lower, root_mid)):
-            sides[comp, here, at(columns)] = value
+            sides[comp, here, at(columns)] = az * value
 
     def cell_values(place):
         here, inside = rows_at(place), rows_at(place + 1)
@@ -412,15 +396,18 @@
         def clamped(late):
             return jnp.clip(place - late, 0, strips - 1)
 
-        update(clamped(3))
-        face_fluxes(clamped(1))
-        cell_values(clamped(0))
+        if lag == 0:
+            cell_values(clamped(0))
+        face_fluxes(clamped(lag))
+        update(clamped(lag + 1))
+        if lag > 0:
+            cell_values(clamped(0))
         return carry
 
-    lax.fori_loop(0, strips + 3, iteration, 0)
-
-
-def flux_layer(layer, together, fields, rims, edges, coefs, so_far):
+    lax.fori_loop(0, strips + lag + 1, iteration, 0)
+
+
+def flux_layer(layer, lag, fields, rims, edges, coefs, so_far):
     layers, rows, cells = fields[0].shape
     block = min(rows, 2 * LANES)
     count = rows // block
@@ -451,10 +438,9 @@
         pltpu.VMEM((CELL_VALUES, cells // LANES, block + SUB, LANES), jnp.float32),
         pltpu.VMEM((3, cells // LANES, block + SUB, LANES), jnp.float32),
         pltpu.VMEM((3, block, cells + LANES), jnp.float32),
-        pltpu.VMEM((3, block, cells), jnp.float32),
     ]
     return pl.pallas_call(
-        lambda *refs: flux_kernel(together, layer, count, refs),
+        lambda *refs: flux_kernel(lag, layer, count, refs),
         grid=(count,),
         in_specs=specs,
         out_specs=[main] * 3,
@@ -510,7 +496,7 @@
 def add_gravity(every, inverse_mid, tables, density, mom_r, mom_phi):
     layers, rows, cells = density.shape
     cols = every.shape[0] * every.shape[2]
-    block = min(rows, 2 * LANES)
+    block = min(rows, LANES)
     modes_spec = pl.BlockSpec((*every.shape[:3], block), lambda i: (0, 0, 0, i))
     table_spec = pl.BlockSpec((cols, cells), lambda i: (0, 0))
 
@@ -592,7 +578,7 @@
     pieces = lax.all_to_all(
         partial.reshape(az_count, pair_count, rows), "az", split_axis=0, concat_axis=0, tiled=True
     )
-    results = flux_layer(0, True, fields, rims, edges, coefs, None)
+    results = flux_layer(0, 1, fields, rims, edges, coefs, None)
     pieces, results = lax.optimization_barrier((pieces, results))
 
     own = jnp.sum(pieces, axis=0).astype(jnp.bfloat16)
@@ -601,7 +587,7 @@
     every = lax.all_to_all(parts, "az", split_axis=0, concat_axis=0, tiled=True)
     coefs, parts = lax.optimization_barrier((coefs, parts))
     for layer in range(1, layers):
-        results = flux_layer(layer, False, fields, rims, edges, coefs, results)
+        results = flux_layer(layer, 0, fields, rims, edges, coefs, results)
     if pair_count % SUB:
         every = jnp.swapaxes(every, 0, 1).reshape(1, 2, cols, rows)
 

time: 148 us -> 158 us (1.068)
  Pallas kernels: 118 us -> 128 us
    pallas_call x2, Pallas kernels: 74.2 us -> 83.5 us  [flux_layer(): pl.pallas_call(lambda *refs: flux_kernel(lag, layer, count, refs), grid=(...]
  transfers between devices with their start and end apart: 5 -> 5, of which waited for: 0 -> 0; matrix products, arithmetic and copies ran while one was open for 4% -> 4% of each run, Pallas kernels for 58% -> 61%
where the time goes in v11:
time: 158 us; the launch traced here: 157 us
  Pallas kernels  128 us (81%)
  starting transfers between devices  17.5 us (11%)
  other arithmetic  4.62 us (3%)
  local copies, waits for them, and re-layouts  4.23 us (3%)
  blocking collectives  1.96 us (1%)
    pallas_call x2, Pallas kernels, flux_layer(): pl.pallas_call(lambda *refs: flux_kernel(lag, layer, count, refs), grid=(...  83.5 us
    pallas_call x1, Pallas kernels, add_gravity(): pl.pallas_call(lambda *refs: gravity_kernel(rows // block, refs), grid=(r...  18.9 us
    pallas_call x1, Pallas kernels, responses(): pl.pallas_call(lambda *refs: response_kernel(steps, refs), grid=(steps,),...  13.9 us
    all_to_all x1, starting transfers between devices, local(): every = lax.all_to_all(parts, 'az', split_axis=0, concat_axis=0, tiled=True)  6.89 us
    pallas_call x1, Pallas kernels, surface_modes(): pl.pallas_call(lambda *refs: modes_kernel(scale, rows // block, refs), gr...  6.79 us
    ppermute x2, starting transfers between devices, exchange_edges(): return (lax.ppermute(last, 'az', right), lax.ppermute(first, 'az', left))  6.52 us
    pallas_call x1, Pallas kernels, edge_cells(): pl.pallas_call(lambda *refs: edge_kernel(refs), grid=(rows // block,), in...  4.78 us
    all_to_all x1, starting transfers between devices, local(): lax.all_to_all(partial.reshape(az_count, pair_count, rows), 'az', split_a...  3.59 us
  transfers between devices with their start and end apart: 5, of which 0 were waited for; matrix products, arithmetic and copies ran while one was open for 4% of the time, Pallas kernels for 61%

profile of v11, /device:TPU:0, one launch (start us, length us, event | category | flops | bytes accessed | tf_op | source)
XLA Modules:
  0.0 157.1 jit_solution(16617918634643672114)
XLA Ops:
  0.6 0.9 fusion.10
  1.5 1.0 fusion.8
  2.5 0.1 fusion.3
  2.6 0.5 collective-permute-start.2
  3.1 4.8 %edge_cells.1 = (bf16[16,1024]{1,0:T(8,128)(2,1)}, bf16[16,1024]{1,0:T(8,128)(2,1)}) custom-call(f32[2,1024,1024]{2,1,0:T(8,128)} %refs_4_.7, f32[2,1024,1024]{2,1,0:T(8,128)} %refs_7_.3, f32[2,1024,1024]{2,1,0:T(8,128)} %refs_8_.3, f32[2,1024,1024]{2,1,0:T(8,128)} %refs_4_.7, f32[2,1024,1024]{2,1,0:T(8,128)} %refs_7_.3, f32[2,1024,1024]{2,1,0:T(8,128)} %refs_8_.3), custom_call_target="tpu_custom_call" | custom-call | flops 5242880 | bytes 6291456 | tf_op jit(solution)/shard_map/edge_cells/pallas_call | solution.py:115
  7.9 3.1 %fusion = (bf16[128,1024]{1,0:T(8,128)(2,1)}, bf16[128,1024]{1,0:T(8,128)(2,1)}, bf16[128,1024]{1,0:T(8,128)(2,1)}) fusion(s32[128]{0:T(128)S(1)} %get-tuple-element.79, s32[128]{0:T(128)S(1)} %get-tuple-element.81, f32[1024]{0:T(1024)S(1)} %add_multiply_fusion.1, s32[128]{0:T(128)S(1)} %get-tuple-element.80, s32[128]{0:T(128)S(1)} %get-tuple-element.82, ...), kind=kLoop, calls=%fused_computation.4 | loop fusion | flops 1703936 | bytes 792832 | tf_op jit(solution)/shard_map/convert_element_type | solution.py:49
  11.0 2.5 %collective-permute-start = (bf16[16,1024]{1,0:T(8,128)(2,1)}, bf16[16,1024]{1,0:T(8,128)(2,1)S(1)}, u32[]{:S(2)}, u32[]{:S(2)}) collective-permute-start(bf16[16,1024]{1,0:T(8,128)(2,1)} %get-tuple-element.35), channel_id=1, source_target_pairs={{0,2},{2,4},{4,6},{6,8},{8,10},{10,12},{12,14},{14,16},{16,18},{18... | collective-permute-start | bytes 98312 | tf_op jit(solution)/shard_map/ppermute | solution.py:550
  13.5 4.0 %collective-permute-start.1 = (bf16[16,1024]{1,0:T(8,128)(2,1)}, bf16[16,1024]{1,0:T(8,128)(2,1)S(1)}, u32[]{:S(2)}, u32[]{:S(2)}) collective-permute-start(bf16[16,1024]{1,0:T(8,128)(2,1)} %get-tuple-element.36), channel_id=1, source_target_pairs={{2,0},{4,2},{6,4},{8,6},{10,8},{12,10},{14,12},{16,14},{18,16},{20... | collective-permute-start | bytes 98312 | tf_op jit(solution)/shard_map/ppermute | solution.py:550
  17.5 6.8 %surface_modes.1 = f32[128,1024]{1,0:T(8,128)} custom-call(f32[2,1024,1024]{2,1,0:T(8,128)} %refs_4_.7, bf16[128,1024]{1,0:T(8,128)(2,1)} %get-tuple-element.32.refs_1_.refs_2_, bf16[128,1024]{1,0:T(8,128)(2,1)} %get-tuple-element.33.refs_2_.refs_3_, bf16[128,1024]{1,0:T(8,128)(2,1)} %get-tuple-element.34.refs_3_), custom_call_target="tpu_custom_call" | custom-call | flops 1610612736 | bytes 8388608 | tf_op jit(solution)/shard_map/surface_modes/pallas_call | solution.py:134
  24.3 0.0 collective-permute-done.2
  24.4 0.7 convert_select_fusion
  25.0 0.0 collective-permute-done.refs_12_
  25.0 0.0 copy-start.1
  25.0 0.0 collective-permute-done.1.refs_13_
  25.0 0.0 copy-start.2
  25.0 3.6 %all-to-all-start = ((f32[16,8,1024]{2,1,0:T(8,128)}), f32[16,8,1024]{2,1,0:T(8,128)S(1)}, u32[]{:S(2)}, u32[]{:S(2)}) async-start(f32[16,8,1024]{2,1,0:T(8,128)} %bitcast.2), calls=%async_computation | async-start | bytes 1048576 | tf_op jit(solution)/shard_map/all_to_all | solution.py:578
  28.7 0.1 multiply_divide_fusion
  28.9 1.3 stack.55.refs_11_.refs_14_
  30.2 0.0 copy-done.1
  30.2 0.0 copy-done.2
  30.3 42.7 %flux_layer.2 = (f32[2,1024,1024]{2,1,0:T(8,128)}, f32[2,1024,1024]{2,1,0:T(8,128)}, f32[2,1024,1024]{2,1,0:T(8,128)}) custom-call(f32[2,1024,1024]{2,1,0:T(8,128)} %refs_4_.7, f32[2,1024,1024]{2,1,0:T(8,128)} %refs_7_.3, f32[2,1024,1024]{2,1,0:T(8,128)} %refs_8_.3, f32[2,1024,1024]{2,1,0:T(8,128)} %refs_4_.7, f32[2,1024,1024]{2,1,0:T(8,128)} %refs_7_.3, ...), custom_call_target="tpu_custom_call" | custom-call | flops 104857600 | bytes 25165824 | tf_op jit(solution)/shard_map/flux_layer/pallas_call | solution.py:442
  72.9 0.0 all-to-all-done
  73.0 2.0 %all_gather.3.refs_0_ = bf16[8,2048]{1,0:T(8,128)(2,1)} all-gather(bf16[8,1024]{1,0:T(8,128)(2,1)S(1)} %reduce_sum.9), channel_id=1, replica_groups=mesh['az'=16,'rad'=2] {'rad'}, dimensions={1}, use_global_device_ids=true | all-gather | bytes 49152 | tf_op jit(solution)/shard_map/all_gather | solution.py:585
  74.9 13.9 %responses.1 = f32[16,2,8,1024]{3,2,1,0:T(8,128)} custom-call(bf16[8,2048]{1,0:T(8,128)(2,1)} %all_gather.3.refs_0_, bf16[4,1024,2048]{2,1,0:T(8,128)(2,1)} %refs_1_.6, bf16[4,1024,2048]{2,1,0:T(8,128)(2,1)} %refs_2_.6), custom_call_target="tpu_custom_call" | custom-call | flops 268435456 | bytes 33554432 | tf_op jit(solution)/shard_map/responses/pallas_call | solution.py:179
  88.8 6.9 %all-to-all-start.1 = ((f32[16,2,8,1024]{3,2,1,0:T(8,128)}), f32[16,2,8,1024]{3,2,1,0:T(8,128)S(1)}, u32[]{:S(2)}, u32[]{:S(2)}) async-start(f32[16,2,8,1024]{3,2,1,0:T(8,128)} %responses.1), calls=%async_computation.1 | async-start | bytes 2097152 | tf_op jit(solution)/shard_map/all_to_all | solution.py:587
  95.7 0.6 slice_divide_fusion.1
  96.3 40.9 %flux_layer.3 = (f32[2,1024,1024]{2,1,0:T(8,128)}, f32[2,1024,1024]{2,1,0:T(8,128)}, f32[2,1024,1024]{2,1,0:T(8,128)}) custom-call(f32[2,1024,1024]{2,1,0:T(8,128)} %refs_4_.7, f32[2,1024,1024]{2,1,0:T(8,128)} %refs_7_.3, f32[2,1024,1024]{2,1,0:T(8,128)} %refs_8_.3, ...), custom_call_target="tpu_custom_call", output_to_operand_aliasing={{0}: (15, {}), {1}: (16, {}), {2}: (17, {})} | custom-call | flops 104857600 | bytes 25165824 | tf_op jit(solution)/shard_map/flux_layer/pallas_call | solution.py:442
  137.2 0.0 all-to-all-done.1.refs_0_
  137.2 0.0 copy-start
  137.2 1.0 copy-done
  138.2 18.9 %add_gravity.1 = (f32[2,1024,1024]{2,1,0:T(8,128)}, f32[2,1024,1024]{2,1,0:T(8,128)}, f32[1024,1024]{1,0:T(8,128)}) custom-call(f32[16,2,8,1024]{3,2,1,0:T(8,128)} %copy-done, f32[1,1024]{1,0:T(1,128)} %bitcast.3, bf16[128,1024]{1,0:T(8,128)(2,1)} %get-tuple-element.32.refs_1_.refs_2_, bf16[128,1024]{1,0:T(8,128)(2,1)} %get-tuple-element.33.refs_2_.refs_3_, ...), custom_call_target="tpu_custom_call" | custom-call | flops 2415919104 | bytes 46137344 | tf_op jit(solution)/shard_map/add_gravity/pallas_call | solution.py:505
  (19 shorter events, 0.1 us)
Async XLA Ops:
  2.6 21.8 %collective-permute-start.2 = (bf16[2,3,1024]{2,1,0:T(4,128)(2,1)S(1)}, bf16[2,3,1024]{2,1,0:T(4,128)(2,1)S(1)}, u32[]{:S(2)}, u32[]{:S(2)}) collective-permute-start(bf16[2,3,1024]{2,1,0:T(4,128)(2,1)S(1)} %fusion.3), channel_id=1, source_target_pairs={{0,1},{1,0},{2,3},{3,2},{4,5},{5,4},{6,7},{7,6},{8,9},{9,8},{10,11... | collective-permute-start | bytes 36872 | tf_op jit(solution)/shard_map/ppermute | solution.py:534
  11.0 14.0 %collective-permute-start = (bf16[16,1024]{1,0:T(8,128)(2,1)}, bf16[16,1024]{1,0:T(8,128)(2,1)S(1)}, u32[]{:S(2)}, u32[]{:S(2)}) collective-permute-start(bf16[16,1024]{1,0:T(8,128)(2,1)} %get-tuple-element.35), channel_id=1, source_target_pairs={{0,2},{2,4},{4,6},{6,8},{8,10},{10,12},{12,14},{14,16},{16,18},{18... | collective-permute-start | bytes 98312 | tf_op jit(solution)/shard_map/ppermute | solution.py:550
  13.5 11.5 %collective-permute-start.1 = (bf16[16,1024]{1,0:T(8,128)(2,1)}, bf16[16,1024]{1,0:T(8,128)(2,1)S(1)}, u32[]{:S(2)}, u32[]{:S(2)}) collective-permute-start(bf16[16,1024]{1,0:T(8,128)(2,1)} %get-tuple-element.36), channel_id=1, source_target_pairs={{2,0},{4,2},{6,4},{8,6},{10,8},{12,10},{14,12},{16,14},{18,16},{20... | collective-permute-start | bytes 98312 | tf_op jit(solution)/shard_map/ppermute | solution.py:550
  25.0 5.2 %copy-start.1 = (bf16[16,1024]{1,0:T(8,128)(2,1)}, bf16[16,1024]{1,0:T(8,128)(2,1)S(1)}, u32[]{:S(2)}) copy-start(bf16[16,1024]{1,0:T(8,128)(2,1)S(1)} %collective-permute-done.refs_12_) | copy-start | bytes 98308
  25.0 5.2 %copy-start.2 = (bf16[16,1024]{1,0:T(8,128)(2,1)}, bf16[16,1024]{1,0:T(8,128)(2,1)S(1)}, u32[]{:S(2)}) copy-start(bf16[16,1024]{1,0:T(8,128)(2,1)S(1)} %collective-permute-done.1.refs_13_) | copy-start | bytes 98308
  25.0 47.9 %all-to-all-start = ((f32[16,8,1024]{2,1,0:T(8,128)}), f32[16,8,1024]{2,1,0:T(8,128)S(1)}, u32[]{:S(2)}, u32[]{:S(2)}) async-start(f32[16,8,1024]{2,1,0:T(8,128)} %bitcast.2), calls=%async_computation | async-start | bytes 1048576 | tf_op jit(solution)/shard_map/all_to_all | solution.py:578
  88.8 48.4 %all-to-all-start.1 = ((f32[16,2,8,1024]{3,2,1,0:T(8,128)}), f32[16,2,8,1024]{3,2,1,0:T(8,128)S(1)}, u32[]{:S(2)}, u32[]{:S(2)}) async-start(f32[16,2,8,1024]{3,2,1,0:T(8,128)} %responses.1), calls=%async_computation.1 | async-start | bytes 2097152 | tf_op jit(solution)/shard_map/all_to_all | solution.py:587
  137.2 1.0 copy-start

commit v12 on v10

--- a/solution.py
+++ b/solution.py
@@ -107,7 +107,7 @@
 
 def edge_cells(fields):
     layers, rows, cells = fields[0].shape
-    block = min(rows, 2 * LANES)
+    block = min(rows, 4 * LANES)
     first = pl.BlockSpec((layers, block, LANES), lambda i: (0, i, 0))
     last = pl.BlockSpec((layers, block, LANES), lambda i: (0, i, cells // LANES - 1))
     edge_spec = pl.BlockSpec((EDGE_ROWS, block), lambda i: (0, i))
@@ -313,7 +313,7 @@
 CELL_VALUES = 8
 
 
-def flux_kernel(together, layer, block_count, refs):
+def flux_kernel(unroll, layer, block_count, refs):
     block = FluxBlock(block_count, refs)
     outs = refs[-8:-5]
     side, cell, faces, sides, held = refs[-5:]
@@ -341,24 +341,14 @@
     def update(place):
         here, above = rows_at(place), shifted(place, 1)
         out_coef, az = block.columns_of(side[here, :], (OUT, AZ))
-        if together:
-            side_row, held_row, face_row = sides[:, here, :], held[:, here, :], faces[:, :, above, :]
-
-        for col in range(columns):
-            for comp in range(3):
-                if together:
-                    parts = [
-                        row[comp, :, k * LANES : (k + 1) * LANES]
-                        for row, k in ((side_row, col + 1), (side_row, col), (held_row, col))
-                    ] + [face_row[comp, col]]
-                else:
-                    parts = [
-                        sides[comp, here, at(col + 1)], sides[comp, here, at(col)],
-                        held[comp, here, at(col)], faces[comp, col, above, :],
-                    ]
-                edge = jnp.where(lane == 0, parts[0], parts[1])
-                outs[comp][here, at(col)] = parts[2] - (
-                    out_coef * parts[3] + az * pltpu.roll(edge, LANES - 1, 1)
+        for comp in range(3):
+            low = sides[comp, here, at(0)]
+            for col in range(columns):
+                beyond = sides[comp, here, at(col + 1)]
+                edge = jnp.where(lane == 0, beyond, low)
+                low = beyond
+                outs[comp][here, at(col)] = held[comp, here, at(col)] - (
+                    out_coef * faces[comp, col, above, :] + az * pltpu.roll(edge, LANES - 1, 1)
                 )
 
     def face_fluxes(place):
@@ -368,15 +358,9 @@
             coef, (ROOT_FACE, SOUND_FACE, IN, ROOT_MID, SOUND_MID, AZ, SPIN, PULL)
         )
         left = block.ghost_values(layer, coef, 0, sound_mid)
-        if together:
-            now_row, low_row = cell[:, :, inside, :], cell[:6, :, below, :]
         for col in range(columns):
-            if together:
-                now = [now_row[slot, col] for slot in range(CELL_VALUES)]
-                lower = [low_row[slot, col] for slot in range(6)]
-            else:
-                now = [cell[slot, col, inside, :] for slot in range(CELL_VALUES)]
-                lower = [cell[slot, col, below, :] for slot in range(6)]
+            now = [cell[slot, col, inside, :] for slot in range(CELL_VALUES)]
+            lower = [cell[slot, col, below, :] for slot in range(6)]
             flux_r = block.radial_flux(now[:6], lower, root_face, sound_face)
             values = (*now[:3], now[6], now[5], now[7])
             lower = [
@@ -409,18 +393,16 @@
                 cell[slot, col, inside, :] = value
 
     def iteration(place, carry):
-        def clamped(late):
-            return jnp.clip(place - late, 0, strips - 1)
-
-        update(clamped(3))
-        face_fluxes(clamped(1))
-        cell_values(clamped(0))
+        for stage, late in ((update, 3), (face_fluxes, 1), (cell_values, 0)):
+            first = jnp.clip(place - late, 0, strips // unroll - 1) * unroll
+            for k in range(unroll):
+                stage(first + k)
         return carry
 
-    lax.fori_loop(0, strips + 3, iteration, 0)
-
-
-def flux_layer(layer, together, fields, rims, edges, coefs, so_far):
+    lax.fori_loop(0, strips // unroll + 3, iteration, 0)
+
+
+def flux_layer(layer, unroll, fields, rims, edges, coefs, so_far):
     layers, rows, cells = fields[0].shape
     block = min(rows, 2 * LANES)
     count = rows // block
@@ -454,7 +436,7 @@
         pltpu.VMEM((3, block, cells), jnp.float32),
     ]
     return pl.pallas_call(
-        lambda *refs: flux_kernel(together, layer, count, refs),
+        lambda *refs: flux_kernel(unroll, layer, count, refs),
         grid=(count,),
         in_specs=specs,
         out_specs=[main] * 3,
@@ -592,7 +574,7 @@
     pieces = lax.all_to_all(
         partial.reshape(az_count, pair_count, rows), "az", split_axis=0, concat_axis=0, tiled=True
     )
-    results = flux_layer(0, True, fields, rims, edges, coefs, None)
+    results = flux_layer(0, 1, fields, rims, edges, coefs, None)
     pieces, results = lax.optimization_barrier((pieces, results))
 
     own = jnp.sum(pieces, axis=0).astype(jnp.bfloat16)
@@ -601,7 +583,7 @@
     every = lax.all_to_all(parts, "az", split_axis=0, concat_axis=0, tiled=True)
     coefs, parts = lax.optimization_barrier((coefs, parts))
     for layer in range(1, layers):
-        results = flux_layer(layer, False, fields, rims, edges, coefs, results)
+        results = flux_layer(layer, 2, fields, rims, edges, coefs, results)
     if pair_count % SUB:
         every = jnp.swapaxes(every, 0, 1).reshape(1, 2, cols, rows)
 

time: 148 us -> 148 us (level)
  transfers between devices with their start and end apart: 5 -> 5, of which waited for: 0 -> 0; matrix products, arithmetic and copies ran while one was open for 4% -> 4% of each run, Pallas kernels for 58% -> 59%
where the time goes in v12:
time: 148 us
  Pallas kernels  119 us (80%)
  starting transfers between devices  17.5 us (12%)
  other arithmetic  4.62 us (3%)
  local copies, waits for them, and re-layouts  4.23 us (3%)
  blocking collectives  1.96 us (1%)
    pallas_call x2, Pallas kernels, flux_layer(): pl.pallas_call(lambda *refs: flux_kernel(unroll, layer, count, refs), gri...  75.6 us
    pallas_call x1, Pallas kernels, add_gravity(): pl.pallas_call(lambda *refs: gravity_kernel(rows // block, refs), grid=(r...  18.2 us
    pallas_call x1, Pallas kernels, responses(): pl.pallas_call(lambda *refs: response_kernel(steps, refs), grid=(steps,),...  13.9 us
    all_to_all x1, starting transfers between devices, local(): every = lax.all_to_all(parts, 'az', split_axis=0, concat_axis=0, tiled=True)  6.89 us
    pallas_call x1, Pallas kernels, surface_modes(): pl.pallas_call(lambda *refs: modes_kernel(scale, rows // block, refs), gr...  6.79 us
    ppermute x2, starting transfers between devices, exchange_edges(): return (lax.ppermute(last, 'az', right), lax.ppermute(first, 'az', left))  6.52 us
    pallas_call x1, Pallas kernels, edge_cells(): pl.pallas_call(lambda *refs: edge_kernel(refs), grid=(rows // block,), in...  4.1 us
    all_to_all x1, starting transfers between devices, local(): lax.all_to_all(partial.reshape(az_count, pair_count, rows), 'az', split_a...  3.59 us
  transfers between devices with their start and end apart: 5, of which 0 were waited for; matrix products, arithmetic and copies ran while one was open for 4% of the time, Pallas kernels for 59%

profile of v12, /device:TPU:0, one launch (start us, length us, event | category | flops | bytes accessed | tf_op | source)
XLA Modules:
  0.0 147.8 jit_solution(2654120075813435706)
XLA Ops:
  0.6 0.9 fusion.10
  1.5 1.0 fusion.8
  2.5 0.1 fusion.3
  2.6 0.5 collective-permute-start.2
  3.1 4.1 %edge_cells.1 = (bf16[16,1024]{1,0:T(8,128)(2,1)}, bf16[16,1024]{1,0:T(8,128)(2,1)}) custom-call(f32[2,1024,1024]{2,1,0:T(8,128)} %refs_4_.7, f32[2,1024,1024]{2,1,0:T(8,128)} %refs_7_.3, f32[2,1024,1024]{2,1,0:T(8,128)} %refs_8_.3, f32[2,1024,1024]{2,1,0:T(8,128)} %refs_4_.7, f32[2,1024,1024]{2,1,0:T(8,128)} %refs_7_.3, f32[2,1024,1024]{2,1,0:T(8,128)} %refs_8_.3), custom_call_target="tpu_custom_call" | custom-call | flops 5242880 | bytes 6291456 | tf_op jit(solution)/shard_map/edge_cells/pallas_call | solution.py:115
  7.2 3.1 %fusion = (bf16[128,1024]{1,0:T(8,128)(2,1)}, bf16[128,1024]{1,0:T(8,128)(2,1)}, bf16[128,1024]{1,0:T(8,128)(2,1)}) fusion(s32[128]{0:T(128)S(1)} %get-tuple-element.79, s32[128]{0:T(128)S(1)} %get-tuple-element.81, f32[1024]{0:T(1024)S(1)} %add_multiply_fusion.1, s32[128]{0:T(128)S(1)} %get-tuple-element.80, s32[128]{0:T(128)S(1)} %get-tuple-element.82, ...), kind=kLoop, calls=%fused_computation.4 | loop fusion | flops 1703936 | bytes 792832 | tf_op jit(solution)/shard_map/convert_element_type | solution.py:49
  10.3 2.5 %collective-permute-start = (bf16[16,1024]{1,0:T(8,128)(2,1)}, bf16[16,1024]{1,0:T(8,128)(2,1)S(1)}, u32[]{:S(2)}, u32[]{:S(2)}) collective-permute-start(bf16[16,1024]{1,0:T(8,128)(2,1)} %get-tuple-element.35), channel_id=1, source_target_pairs={{0,2},{2,4},{4,6},{6,8},{8,10},{10,12},{12,14},{14,16},{16,18},{18... | collective-permute-start | bytes 98312 | tf_op jit(solution)/shard_map/ppermute | solution.py:546
  12.9 4.0 %collective-permute-start.1 = (bf16[16,1024]{1,0:T(8,128)(2,1)}, bf16[16,1024]{1,0:T(8,128)(2,1)S(1)}, u32[]{:S(2)}, u32[]{:S(2)}) collective-permute-start(bf16[16,1024]{1,0:T(8,128)(2,1)} %get-tuple-element.36), channel_id=1, source_target_pairs={{2,0},{4,2},{6,4},{8,6},{10,8},{12,10},{14,12},{16,14},{18,16},{20... | collective-permute-start | bytes 98312 | tf_op jit(solution)/shard_map/ppermute | solution.py:546
  16.9 6.8 %surface_modes.1 = f32[128,1024]{1,0:T(8,128)} custom-call(f32[2,1024,1024]{2,1,0:T(8,128)} %refs_4_.7, bf16[128,1024]{1,0:T(8,128)(2,1)} %get-tuple-element.32.refs_1_.refs_2_, bf16[128,1024]{1,0:T(8,128)(2,1)} %get-tuple-element.33.refs_2_.refs_3_, bf16[128,1024]{1,0:T(8,128)(2,1)} %get-tuple-element.34.refs_3_), custom_call_target="tpu_custom_call" | custom-call | flops 1610612736 | bytes 8388608 | tf_op jit(solution)/shard_map/surface_modes/pallas_call | solution.py:134
  23.7 0.0 collective-permute-done.2
  23.7 0.7 convert_select_fusion
  24.3 0.0 collective-permute-done.refs_12_
  24.3 0.0 copy-start.1
  24.3 0.0 collective-permute-done.1.refs_13_
  24.4 0.0 copy-start.2
  24.4 3.6 %all-to-all-start = ((f32[16,8,1024]{2,1,0:T(8,128)}), f32[16,8,1024]{2,1,0:T(8,128)S(1)}, u32[]{:S(2)}, u32[]{:S(2)}) async-start(f32[16,8,1024]{2,1,0:T(8,128)} %bitcast.2), calls=%async_computation | async-start | bytes 1048576 | tf_op jit(solution)/shard_map/all_to_all | solution.py:574
  28.0 0.1 multiply_divide_fusion
  28.2 1.3 stack.55.refs_11_.refs_14_
  29.6 0.0 copy-done.1
  29.6 0.0 copy-done.2
  29.6 37.1 %flux_layer.2 = (f32[2,1024,1024]{2,1,0:T(8,128)}, f32[2,1024,1024]{2,1,0:T(8,128)}, f32[2,1024,1024]{2,1,0:T(8,128)}) custom-call(f32[2,1024,1024]{2,1,0:T(8,128)} %refs_4_.7, f32[2,1024,1024]{2,1,0:T(8,128)} %refs_7_.3, f32[2,1024,1024]{2,1,0:T(8,128)} %refs_8_.3, f32[2,1024,1024]{2,1,0:T(8,128)} %refs_4_.7, f32[2,1024,1024]{2,1,0:T(8,128)} %refs_7_.3, ...), custom_call_target="tpu_custom_call" | custom-call | flops 104857600 | bytes 25165824 | tf_op jit(solution)/shard_map/flux_layer/pallas_call | solution.py:438
  66.6 0.0 all-to-all-done
  66.7 2.0 %all_gather.3.refs_0_ = bf16[8,2048]{1,0:T(8,128)(2,1)} all-gather(bf16[8,1024]{1,0:T(8,128)(2,1)S(1)} %reduce_sum.9), channel_id=1, replica_groups=mesh['az'=16,'rad'=2] {'rad'}, dimensions={1}, use_global_device_ids=true | all-gather | bytes 49152 | tf_op jit(solution)/shard_map/all_gather | solution.py:581
  68.6 13.9 %responses.1 = f32[16,2,8,1024]{3,2,1,0:T(8,128)} custom-call(bf16[8,2048]{1,0:T(8,128)(2,1)} %all_gather.3.refs_0_, bf16[4,1024,2048]{2,1,0:T(8,128)(2,1)} %refs_1_.6, bf16[4,1024,2048]{2,1,0:T(8,128)(2,1)} %refs_2_.6), custom_call_target="tpu_custom_call" | custom-call | flops 268435456 | bytes 33554432 | tf_op jit(solution)/shard_map/responses/pallas_call | solution.py:179
  82.5 6.9 %all-to-all-start.1 = ((f32[16,2,8,1024]{3,2,1,0:T(8,128)}), f32[16,2,8,1024]{3,2,1,0:T(8,128)S(1)}, u32[]{:S(2)}, u32[]{:S(2)}) async-start(f32[16,2,8,1024]{3,2,1,0:T(8,128)} %responses.1), calls=%async_computation.1 | async-start | bytes 2097152 | tf_op jit(solution)/shard_map/all_to_all | solution.py:583
  89.4 0.6 slice_divide_fusion.1
  90.0 38.6 %flux_layer.3 = (f32[2,1024,1024]{2,1,0:T(8,128)}, f32[2,1024,1024]{2,1,0:T(8,128)}, f32[2,1024,1024]{2,1,0:T(8,128)}) custom-call(f32[2,1024,1024]{2,1,0:T(8,128)} %refs_4_.7, f32[2,1024,1024]{2,1,0:T(8,128)} %refs_7_.3, f32[2,1024,1024]{2,1,0:T(8,128)} %refs_8_.3, ...), custom_call_target="tpu_custom_call", output_to_operand_aliasing={{0}: (15, {}), {1}: (16, {}), {2}: (17, {})} | custom-call | flops 104857600 | bytes 25165824 | tf_op jit(solution)/shard_map/flux_layer/pallas_call | solution.py:438
  128.6 0.0 all-to-all-done.1.refs_0_
  128.6 0.0 copy-start
  128.6 1.0 copy-done
  129.6 18.2 %add_gravity.1 = (f32[2,1024,1024]{2,1,0:T(8,128)}, f32[2,1024,1024]{2,1,0:T(8,128)}, f32[1024,1024]{1,0:T(8,128)}) custom-call(f32[16,2,8,1024]{3,2,1,0:T(8,128)} %copy-done, f32[1,1024]{1,0:T(1,128)} %bitcast.3, bf16[128,1024]{1,0:T(8,128)(2,1)} %get-tuple-element.32.refs_1_.refs_2_, bf16[128,1024]{1,0:T(8,128)(2,1)} %get-tuple-element.33.refs_2_.refs_3_, ...), custom_call_target="tpu_custom_call" | custom-call | flops 2415919104 | bytes 46137344 | tf_op jit(solution)/shard_map/add_gravity/pallas_call | solution.py:501
  (19 shorter events, 0.1 us)
Async XLA Ops:
  2.6 21.1 %collective-permute-start.2 = (bf16[2,3,1024]{2,1,0:T(4,128)(2,1)S(1)}, bf16[2,3,1024]{2,1,0:T(4,128)(2,1)S(1)}, u32[]{:S(2)}, u32[]{:S(2)}) collective-permute-start(bf16[2,3,1024]{2,1,0:T(4,128)(2,1)S(1)} %fusion.3), channel_id=1, source_target_pairs={{0,1},{1,0},{2,3},{3,2},{4,5},{5,4},{6,7},{7,6},{8,9},{9,8},{10,11... | collective-permute-start | bytes 36872 | tf_op jit(solution)/shard_map/ppermute | solution.py:530
  10.3 14.0 %collective-permute-start = (bf16[16,1024]{1,0:T(8,128)(2,1)}, bf16[16,1024]{1,0:T(8,128)(2,1)S(1)}, u32[]{:S(2)}, u32[]{:S(2)}) collective-permute-start(bf16[16,1024]{1,0:T(8,128)(2,1)} %get-tuple-element.35), channel_id=1, source_target_pairs={{0,2},{2,4},{4,6},{6,8},{8,10},{10,12},{12,14},{14,16},{16,18},{18... | collective-permute-start | bytes 98312 | tf_op jit(solution)/shard_map/ppermute | solution.py:546
  12.9 11.5 %collective-permute-start.1 = (bf16[16,1024]{1,0:T(8,128)(2,1)}, bf16[16,1024]{1,0:T(8,128)(2,1)S(1)}, u32[]{:S(2)}, u32[]{:S(2)}) collective-permute-start(bf16[16,1024]{1,0:T(8,128)(2,1)} %get-tuple-element.36), channel_id=1, source_target_pairs={{2,0},{4,2},{6,4},{8,6},{10,8},{12,10},{14,12},{16,14},{18,16},{20... | collective-permute-start | bytes 98312 | tf_op jit(solution)/shard_map/ppermute | solution.py:546
  24.3 5.2 %copy-start.1 = (bf16[16,1024]{1,0:T(8,128)(2,1)}, bf16[16,1024]{1,0:T(8,128)(2,1)S(1)}, u32[]{:S(2)}) copy-start(bf16[16,1024]{1,0:T(8,128)(2,1)S(1)} %collective-permute-done.refs_12_) | copy-start | bytes 98308
  24.4 5.2 %copy-start.2 = (bf16[16,1024]{1,0:T(8,128)(2,1)}, bf16[16,1024]{1,0:T(8,128)(2,1)S(1)}, u32[]{:S(2)}) copy-start(bf16[16,1024]{1,0:T(8,128)(2,1)S(1)} %collective-permute-done.1.refs_13_) | copy-start | bytes 98308
  24.4 42.3 %all-to-all-start = ((f32[16,8,1024]{2,1,0:T(8,128)}), f32[16,8,1024]{2,1,0:T(8,128)S(1)}, u32[]{:S(2)}, u32[]{:S(2)}) async-start(f32[16,8,1024]{2,1,0:T(8,128)} %bitcast.2), calls=%async_computation | async-start | bytes 1048576 | tf_op jit(solution)/shard_map/all_to_all | solution.py:574
  82.5 46.1 %all-to-all-start.1 = ((f32[16,2,8,1024]{3,2,1,0:T(8,128)}), f32[16,2,8,1024]{3,2,1,0:T(8,128)S(1)}, u32[]{:S(2)}, u32[]{:S(2)}) async-start(f32[16,2,8,1024]{3,2,1,0:T(8,128)} %responses.1), calls=%async_computation.1 | async-start | bytes 2097152 | tf_op jit(solution)/shard_map/all_to_all | solution.py:583
  128.6 1.0 copy-start

commit v13 on v12

--- a/solution.py
+++ b/solution.py
@@ -255,6 +255,8 @@
         return pl.ds(col * LANES, LANES)
 
     def rows_at(self, place):
+        if isinstance(place, int):
+            return pl.ds(place * SUB, SUB)
         return pl.ds(pl.multiple_of(place * SUB, SUB), SUB)
 
     def radial_state(self, state):
@@ -336,6 +338,8 @@
             faces[comp, col, rows : rows + SUB, :] = flux[comp]
 
     def shifted(place, by):
+        if isinstance(place, int):
+            return pl.ds(place * SUB + by, SUB)
         return pl.ds(pl.multiple_of(place * SUB, SUB) + by, SUB)
 
     def update(place):
@@ -392,14 +396,27 @@
             for slot, value in enumerate(values):
                 cell[slot, col, inside, :] = value
 
-    def iteration(place, carry):
-        for stage, late in ((update, 3), (face_fluxes, 1), (cell_values, 0)):
-            first = jnp.clip(place - late, 0, strips // unroll - 1) * unroll
-            for k in range(unroll):
-                stage(first + k)
+    groups = strips // unroll
+
+    def run(stage, group):
+        for k in range(unroll):
+            stage(group * unroll + k)
+
+    def iteration(group, carry):
+        run(update, group - 3)
+        run(face_fluxes, group - 1)
+        run(cell_values, group)
         return carry
 
-    lax.fori_loop(0, strips // unroll + 3, iteration, 0)
+    run(cell_values, 0)
+    for group in (1, 2):
+        run(face_fluxes, group - 1)
+        run(cell_values, group)
+    lax.fori_loop(3, groups, iteration, 0)
+    run(update, groups - 3)
+    run(face_fluxes, groups - 1)
+    run(update, groups - 2)
+    run(update, groups - 1)
 
 
 def flux_layer(layer, unroll, fields, rims, edges, coefs, so_far):
@@ -574,7 +591,7 @@
     pieces = lax.all_to_all(
         partial.reshape(az_count, pair_count, rows), "az", split_axis=0, concat_axis=0, tiled=True
     )
-    results = flux_layer(0, 1, fields, rims, edges, coefs, None)
+    results = flux_layer(0, 2, fields, rims, edges, coefs, None)
     pieces, results = lax.optimization_barrier((pieces, results))
 
     own = jnp.sum(pieces, axis=0).astype(jnp.bfloat16)

time: 148 us -> 139 us (0.939)
  Pallas kernels: 119 us -> 109 us
    pallas_call x2, Pallas kernels: 75.6 us -> 65.9 us  [flux_layer(): pl.pallas_call(lambda *refs: flux_kernel(unroll, layer, count, refs), gri...]
  transfers between devices with their start and end apart: 5 -> 5, of which waited for: 0 -> 0; matrix products, arithmetic and copies ran while one was open for 4% -> 4% of each run, Pallas kernels for 59% -> 56%
where the time goes in v13:
time: 139 us; the launch traced here: 138 us
  Pallas kernels  109 us (78%)
  starting transfers between devices  17.5 us (13%)
  other arithmetic  4.62 us (3%)
  local copies, waits for them, and re-layouts  4.23 us (3%)
  blocking collectives  1.96 us (1%)
    pallas_call x2, Pallas kernels, flux_layer(): pl.pallas_call(lambda *refs: flux_kernel(unroll, layer, count, refs), gri...  65.9 us
    pallas_call x1, Pallas kernels, add_gravity(): pl.pallas_call(lambda *refs: gravity_kernel(rows // block, refs), grid=(r...  18.2 us
    pallas_call x1, Pallas kernels, responses(): pl.pallas_call(lambda *refs: response_kernel(steps, refs), grid=(steps,),...  13.9 us
    all_to_all x1, starting transfers between devices, local(): every = lax.all_to_all(parts, 'az', split_axis=0, concat_axis=0, tiled=True)  6.89 us
    pallas_call x1, Pallas kernels, surface_modes(): pl.pallas_call(lambda *refs: modes_kernel(scale, rows // block, refs), gr...  6.79 us
    ppermute x2, starting transfers between devices, exchange_edges(): return (lax.ppermute(last, 'az', right), lax.ppermute(first, 'az', left))  6.52 us
    pallas_call x1, Pallas kernels, edge_cells(): pl.pallas_call(lambda *refs: edge_kernel(refs), grid=(rows // block,), in...  4.1 us
    all_to_all x1, starting transfers between devices, local(): lax.all_to_all(partial.reshape(az_count, pair_count, rows), 'az', split_a...  3.59 us
  transfers between devices with their start and end apart: 5, of which 0 were waited for; matrix products, arithmetic and copies ran while one was open for 4% of the time, Pallas kernels for 56%

profile of v13, /device:TPU:0, one launch (start us, length us, event | category | flops | bytes accessed | tf_op | source)
XLA Modules:
  0.0 138.1 jit_solution(10506651337929849082)
XLA Ops:
  0.6 0.9 fusion.10
  1.5 1.0 fusion.8
  2.5 0.1 fusion.3
  2.6 0.5 collective-permute-start.2
  3.1 4.1 %edge_cells.1 = (bf16[16,1024]{1,0:T(8,128)(2,1)}, bf16[16,1024]{1,0:T(8,128)(2,1)}) custom-call(f32[2,1024,1024]{2,1,0:T(8,128)} %refs_4_.7, f32[2,1024,1024]{2,1,0:T(8,128)} %refs_7_.3, f32[2,1024,1024]{2,1,0:T(8,128)} %refs_8_.3, f32[2,1024,1024]{2,1,0:T(8,128)} %refs_4_.7, f32[2,1024,1024]{2,1,0:T(8,128)} %refs_7_.3, f32[2,1024,1024]{2,1,0:T(8,128)} %refs_8_.3), custom_call_target="tpu_custom_call" | custom-call | flops 5242880 | bytes 6291456 | tf_op jit(solution)/shard_map/edge_cells/pallas_call | solution.py:115
  7.2 3.1 %fusion = (bf16[128,1024]{1,0:T(8,128)(2,1)}, bf16[128,1024]{1,0:T(8,128)(2,1)}, bf16[128,1024]{1,0:T(8,128)(2,1)}) fusion(s32[128]{0:T(128)S(1)} %get-tuple-element.79, s32[128]{0:T(128)S(1)} %get-tuple-element.81, f32[1024]{0:T(1024)S(1)} %add_multiply_fusion.1, s32[128]{0:T(128)S(1)} %get-tuple-element.80, s32[128]{0:T(128)S(1)} %get-tuple-element.82, ...), kind=kLoop, calls=%fused_computation.4 | loop fusion | flops 1703936 | bytes 792832 | tf_op jit(solution)/shard_map/convert_element_type | solution.py:49
  10.3 2.5 %collective-permute-start = (bf16[16,1024]{1,0:T(8,128)(2,1)}, bf16[16,1024]{1,0:T(8,128)(2,1)S(1)}, u32[]{:S(2)}, u32[]{:S(2)}) collective-permute-start(bf16[16,1024]{1,0:T(8,128)(2,1)} %get-tuple-element.35), channel_id=1, source_target_pairs={{0,2},{2,4},{4,6},{6,8},{8,10},{10,12},{12,14},{14,16},{16,18},{18... | collective-permute-start | bytes 98312 | tf_op jit(solution)/shard_map/ppermute | solution.py:563
  12.9 4.0 %collective-permute-start.1 = (bf16[16,1024]{1,0:T(8,128)(2,1)}, bf16[16,1024]{1,0:T(8,128)(2,1)S(1)}, u32[]{:S(2)}, u32[]{:S(2)}) collective-permute-start(bf16[16,1024]{1,0:T(8,128)(2,1)} %get-tuple-element.36), channel_id=1, source_target_pairs={{2,0},{4,2},{6,4},{8,6},{10,8},{12,10},{14,12},{16,14},{18,16},{20... | collective-permute-start | bytes 98312 | tf_op jit(solution)/shard_map/ppermute | solution.py:563
  16.9 6.8 %surface_modes.1 = f32[128,1024]{1,0:T(8,128)} custom-call(f32[2,1024,1024]{2,1,0:T(8,128)} %refs_4_.7, bf16[128,1024]{1,0:T(8,128)(2,1)} %get-tuple-element.32.refs_1_.refs_2_, bf16[128,1024]{1,0:T(8,128)(2,1)} %get-tuple-element.33.refs_2_.refs_3_, bf16[128,1024]{1,0:T(8,128)(2,1)} %get-tuple-element.34.refs_3_), custom_call_target="tpu_custom_call" | custom-call | flops 1610612736 | bytes 8388608 | tf_op jit(solution)/shard_map/surface_modes/pallas_call | solution.py:134
  23.7 0.0 collective-permute-done.2
  23.7 0.7 convert_select_fusion
  24.3 0.0 collective-permute-done.refs_12_
  24.3 0.0 copy-start.1
  24.3 0.0 collective-permute-done.1.refs_13_
  24.4 0.0 copy-start.2
  24.4 3.6 %all-to-all-start = ((f32[16,8,1024]{2,1,0:T(8,128)}), f32[16,8,1024]{2,1,0:T(8,128)S(1)}, u32[]{:S(2)}, u32[]{:S(2)}) async-start(f32[16,8,1024]{2,1,0:T(8,128)} %bitcast.2), calls=%async_computation | async-start | bytes 1048576 | tf_op jit(solution)/shard_map/all_to_all | solution.py:591
  28.0 0.1 multiply_divide_fusion
  28.2 1.3 stack.55.refs_11_.refs_14_
  29.6 0.0 copy-done.1
  29.6 0.0 copy-done.2
  29.6 33.0 %flux_layer.2 = (f32[2,1024,1024]{2,1,0:T(8,128)}, f32[2,1024,1024]{2,1,0:T(8,128)}, f32[2,1024,1024]{2,1,0:T(8,128)}) custom-call(f32[2,1024,1024]{2,1,0:T(8,128)} %refs_4_.7, f32[2,1024,1024]{2,1,0:T(8,128)} %refs_7_.3, f32[2,1024,1024]{2,1,0:T(8,128)} %refs_8_.3, f32[2,1024,1024]{2,1,0:T(8,128)} %refs_4_.7, f32[2,1024,1024]{2,1,0:T(8,128)} %refs_7_.3, ...), custom_call_target="tpu_custom_call" | custom-call | flops 104857600 | bytes 25165824 | tf_op jit(solution)/shard_map/flux_layer/pallas_call | solution.py:455
  62.6 0.0 all-to-all-done
  62.6 2.0 %all_gather.3.refs_0_ = bf16[8,2048]{1,0:T(8,128)(2,1)} all-gather(bf16[8,1024]{1,0:T(8,128)(2,1)S(1)} %reduce_sum.9), channel_id=1, replica_groups=mesh['az'=16,'rad'=2] {'rad'}, dimensions={1}, use_global_device_ids=true | all-gather | bytes 49152 | tf_op jit(solution)/shard_map/all_gather | solution.py:598
  64.6 13.9 %responses.1 = f32[16,2,8,1024]{3,2,1,0:T(8,128)} custom-call(bf16[8,2048]{1,0:T(8,128)(2,1)} %all_gather.3.refs_0_, bf16[4,1024,2048]{2,1,0:T(8,128)(2,1)} %refs_1_.6, bf16[4,1024,2048]{2,1,0:T(8,128)(2,1)} %refs_2_.6), custom_call_target="tpu_custom_call" | custom-call | flops 268435456 | bytes 33554432 | tf_op jit(solution)/shard_map/responses/pallas_call | solution.py:179
  78.5 6.9 %all-to-all-start.1 = ((f32[16,2,8,1024]{3,2,1,0:T(8,128)}), f32[16,2,8,1024]{3,2,1,0:T(8,128)S(1)}, u32[]{:S(2)}, u32[]{:S(2)}) async-start(f32[16,2,8,1024]{3,2,1,0:T(8,128)} %responses.1), calls=%async_computation.1 | async-start | bytes 2097152 | tf_op jit(solution)/shard_map/all_to_all | solution.py:600
  85.4 0.6 slice_divide_fusion.1
  86.0 32.9 %flux_layer.3 = (f32[2,1024,1024]{2,1,0:T(8,128)}, f32[2,1024,1024]{2,1,0:T(8,128)}, f32[2,1024,1024]{2,1,0:T(8,128)}) custom-call(f32[2,1024,1024]{2,1,0:T(8,128)} %refs_4_.7, f32[2,1024,1024]{2,1,0:T(8,128)} %refs_7_.3, f32[2,1024,1024]{2,1,0:T(8,128)} %refs_8_.3, ...), custom_call_target="tpu_custom_call", output_to_operand_aliasing={{0}: (15, {}), {1}: (16, {}), {2}: (17, {})} | custom-call | flops 104857600 | bytes 25165824 | tf_op jit(solution)/shard_map/flux_layer/pallas_call | solution.py:455
  118.9 0.0 all-to-all-done.1.refs_0_
  118.9 0.0 copy-start
  118.9 1.0 copy-done
  119.9 18.2 %add_gravity.1 = (f32[2,1024,1024]{2,1,0:T(8,128)}, f32[2,1024,1024]{2,1,0:T(8,128)}, f32[1024,1024]{1,0:T(8,128)}) custom-call(f32[16,2,8,1024]{3,2,1,0:T(8,128)} %copy-done, f32[1,1024]{1,0:T(1,128)} %bitcast.3, bf16[128,1024]{1,0:T(8,128)(2,1)} %get-tuple-element.32.refs_1_.refs_2_, bf16[128,1024]{1,0:T(8,128)(2,1)} %get-tuple-element.33.refs_2_.refs_3_, ...), custom_call_target="tpu_custom_call" | custom-call | flops 2415919104 | bytes 46137344 | tf_op jit(solution)/shard_map/add_gravity/pallas_call | solution.py:518
  (19 shorter events, 0.1 us)
Async XLA Ops:
  2.6 21.1 %collective-permute-start.2 = (bf16[2,3,1024]{2,1,0:T(4,128)(2,1)S(1)}, bf16[2,3,1024]{2,1,0:T(4,128)(2,1)S(1)}, u32[]{:S(2)}, u32[]{:S(2)}) collective-permute-start(bf16[2,3,1024]{2,1,0:T(4,128)(2,1)S(1)} %fusion.3), channel_id=1, source_target_pairs={{0,1},{1,0},{2,3},{3,2},{4,5},{5,4},{6,7},{7,6},{8,9},{9,8},{10,11... | collective-permute-start | bytes 36872 | tf_op jit(solution)/shard_map/ppermute | solution.py:547
  10.3 14.0 %collective-permute-start = (bf16[16,1024]{1,0:T(8,128)(2,1)}, bf16[16,1024]{1,0:T(8,128)(2,1)S(1)}, u32[]{:S(2)}, u32[]{:S(2)}) collective-permute-start(bf16[16,1024]{1,0:T(8,128)(2,1)} %get-tuple-element.35), channel_id=1, source_target_pairs={{0,2},{2,4},{4,6},{6,8},{8,10},{10,12},{12,14},{14,16},{16,18},{18... | collective-permute-start | bytes 98312 | tf_op jit(solution)/shard_map/ppermute | solution.py:563
  12.9 11.5 %collective-permute-start.1 = (bf16[16,1024]{1,0:T(8,128)(2,1)}, bf16[16,1024]{1,0:T(8,128)(2,1)S(1)}, u32[]{:S(2)}, u32[]{:S(2)}) collective-permute-start(bf16[16,1024]{1,0:T(8,128)(2,1)} %get-tuple-element.36), channel_id=1, source_target_pairs={{2,0},{4,2},{6,4},{8,6},{10,8},{12,10},{14,12},{16,14},{18,16},{20... | collective-permute-start | bytes 98312 | tf_op jit(solution)/shard_map/ppermute | solution.py:563
  24.3 5.2 %copy-start.1 = (bf16[16,1024]{1,0:T(8,128)(2,1)}, bf16[16,1024]{1,0:T(8,128)(2,1)S(1)}, u32[]{:S(2)}) copy-start(bf16[16,1024]{1,0:T(8,128)(2,1)S(1)} %collective-permute-done.refs_12_) | copy-start | bytes 98308
  24.4 5.2 %copy-start.2 = (bf16[16,1024]{1,0:T(8,128)(2,1)}, bf16[16,1024]{1,0:T(8,128)(2,1)S(1)}, u32[]{:S(2)}) copy-start(bf16[16,1024]{1,0:T(8,128)(2,1)S(1)} %collective-permute-done.1.refs_13_) | copy-start | bytes 98308
  24.4 38.2 %all-to-all-start = ((f32[16,8,1024]{2,1,0:T(8,128)}), f32[16,8,1024]{2,1,0:T(8,128)S(1)}, u32[]{:S(2)}, u32[]{:S(2)}) async-start(f32[16,8,1024]{2,1,0:T(8,128)} %bitcast.2), calls=%async_computation | async-start | bytes 1048576 | tf_op jit(solution)/shard_map/all_to_all | solution.py:591
  78.5 40.4 %all-to-all-start.1 = ((f32[16,2,8,1024]{3,2,1,0:T(8,128)}), f32[16,2,8,1024]{3,2,1,0:T(8,128)S(1)}, u32[]{:S(2)}, u32[]{:S(2)}) async-start(f32[16,2,8,1024]{3,2,1,0:T(8,128)} %responses.1), calls=%async_computation.1 | async-start | bytes 2097152 | tf_op jit(solution)/shard_map/all_to_all | solution.py:600
  118.9 1.0 copy-start
